TPU v7x, 512 devices: a whole 4x8x8 slice. The times are simulated.
512 devices in a mesh: dom: 128 (over y_hi, x, z), rep: 4 (over y_lo, core).
Axes of the slice: x: 4, y: 8 (y_hi: 4, y_lo: 2; y = y_hi * 2 + y_lo), z: 8, core: 2. Of those that a mesh axis runs over, the one named last changes fastest.
Arguments:
- features: bfloat16 [256, 131072], P('rep', 'dom'), may hold values from -6 to 6
- hub_weight: bfloat16 [128, 128, 64, 128], P('dom'), may hold values from -0.25 to 0.25
- hub_block: int32 [128, 128], P('dom'), may hold values from 0 to 7
- hub_mask: int32 [128, 128], P('dom'), may hold values from 0 to 1, as said below
- tail_rows: int32 [128, 128, 32], P('dom'), may hold values from 0 to 1023
- tail_count: int32 [128, 128], P('dom'), may hold values from 1 to 32, as said below
- tail_target: int32 [128, 128, 32], P('dom'), may hold values from 0 to 1023
- degree: int32 [131072], P('dom'), may hold values from 1 to 8
- w_self: bfloat16 [256, 256], P(None, 'rep'), may hold values from -0.375 to 0.375
- w_neigh: bfloat16 [256, 256], P(None, 'rep'), may hold values from -0.375 to 0.375
- out_bias: float32 [256], P('rep'), may hold values from -3 to 3
- cotangent: bfloat16 [256, 131072], P('rep', 'dom'), may hold values from -6 to 6
Outputs:
- output: bfloat16 [256, 131072], P('rep', 'dom')
- grad_features: float32 [256, 131072], P('rep', 'dom')
- grad_w_self: float32 [256, 256], P(None, 'rep')
- grad_w_neigh: float32 [256, 256], P(None, 'rep')
- grad_bias: float32 [256], P('rep')
Inputs may be any that keep to these rules, and one draw needn't show every extreme that they name: `hub_mask`: 1 where the pair's hub tile holds edges, else 0. `tail_count`: every partition sends 32 live rows to some partition, and some partition receives 32 live rows from every partition; slots at or past the count are padding.
All inputs are finite; a program needn't handle non-finite values.
Results may differ from a plain program's by a relative error of at most 0.007.
Values may be sent and summed in bfloat16 or wider, within the bound.
No kernel may reach another device: no remote copies, remote signals or barrier semaphores. Data moves between devices by JAX's collectives and lax.ppermute only.
A program may use at most 64 MiB of HBM per device.

v0:
```python
from functools import partial
import math

import jax
import jax.numpy as jnp
from jax import lax
from jax.sharding import PartitionSpec as P


def block_width(slot_total):
    return math.gcd(slot_total, 1024)


def silu_slope(pre):
    sigma = jax.nn.sigmoid(pre)
    return sigma * (1.0 + pre * (1.0 - sigma))


def pick_columns(sources, indices, is_live, row_total):
    slot_total = indices.shape[0]
    block_len = block_width(slot_total)
    row_ids = jnp.arange(row_total, dtype=jnp.int32)[:, None]
    collected = [[] for source in sources]
    for offset in range(0, slot_total, block_len):
        hits = (row_ids == indices[None, offset : offset + block_len]) & is_live[
            None, offset : offset + block_len
        ]
        hits = hits.astype(jnp.bfloat16)
        for place, source in enumerate(sources):
            collected[place].append(jnp.dot(source, hits, preferred_element_type=jnp.float32))
    return [jnp.concatenate(pieces_list, axis=1) for pieces_list in collected]


def spread_columns(values, indices, row_total, is_live, exact_float):
    slot_total = indices.shape[0]
    block_len = block_width(slot_total)
    row_ids = jnp.arange(row_total, dtype=jnp.int32)[None, :]
    summed = jnp.zeros((values.shape[0], row_total), jnp.float32)
    for offset in range(0, slot_total, block_len):
        hits = (indices[offset : offset + block_len, None] == row_ids) & is_live[
            offset : offset + block_len, None
        ]
        value_block = values[:, offset : offset + block_len]
        if exact_float:
            summed = summed + jnp.dot(
                value_block, hits.astype(jnp.float32), precision=lax.Precision.HIGHEST
            )
        else:
            summed = summed + jnp.dot(
                value_block, hits.astype(value_block.dtype), preferred_element_type=jnp.float32
            )
    return summed


def fold_hubs(carry, piece, start, tiles, hub_rows, hub_live):
    hub_total = tiles.shape[1]
    tile_len = tiles.shape[2]
    piece_len = piece.shape[1]
    step_len = math.gcd(piece_len, hub_total)
    flat_tiles = tiles.reshape(-1, tile_len)

    def one_step(summed, step_index):
        local_first = step_index * step_len
        owner = local_first // hub_total
        columns = lax.dynamic_slice_in_dim(piece, local_first, step_len, 1)
        weights = lax.dynamic_slice_in_dim(flat_tiles, local_first, step_len, 0)
        target = hub_rows[owner] * tile_len

        def add_tile(current):
            product = jnp.dot(columns, weights, preferred_element_type=jnp.float32)
            window = lax.dynamic_slice_in_dim(current, target, tile_len, 1)
            return lax.dynamic_update_slice_in_dim(current, window + product, target, 1)

        def keep_tile(current):
            return current

        return (lax.cond(hub_live[owner] > 0, add_tile, keep_tile, summed), None)

    summed, unused = lax.scan(one_step, carry, jnp.arange(piece_len // step_len, dtype=jnp.int32))
    return summed


def hub_terms(mixed_grad, tiles, hub_rows, hub_live, form):
    own_width, node_total = mixed_grad.shape
    tile_len = tiles.shape[2]
    grouped = mixed_grad.reshape(own_width, node_total // tile_len, tile_len)
    live_sel = hub_live.astype(jnp.bfloat16)
    chosen = jnp.take(grouped, hub_rows, axis=1) * live_sel[None, :, None]
    return jnp.einsum(form, chosen, tiles, preferred_element_type=jnp.float32)


def local(
    features,
    hub_weight,
    hub_block,
    hub_mask,
    tail_rows,
    tail_count,
    tail_target,
    degree,
    w_self,
    w_neigh,
    out_bias,
    cotangent,
):
    own_width, node_total = features.shape
    hub_total = hub_weight.shape[2]
    slot_total = tail_rows.shape[2]
    tiles = hub_weight[0]
    hub_rows = hub_block[0]
    hub_live = hub_mask[0]
    hub_part = features[:, :hub_total]
    send_rows = tail_rows[0].reshape(-1)
    send_live = (jnp.arange(slot_total, dtype=jnp.int32)[None, :] < tail_count[0][:, None]).reshape(
        -1
    )
    recv_rows = tail_target[0].reshape(-1)
    every_slot = jnp.ones(recv_rows.shape, dtype=bool)
    outgoing = pick_columns((features,), send_rows, send_live, node_total)[0].astype(jnp.bfloat16)
    arrived = lax.all_to_all(outgoing, "dom", split_axis=1, concat_axis=1, tiled=True)
    fold_fn = partial(fold_hubs, tiles=tiles, hub_rows=hub_rows, hub_live=hub_live)
    hub_sum = fold_fn(
        jnp.zeros((own_width, node_total), jnp.float32),
        lax.all_gather(hub_part, "dom", axis=1, tiled=True),
        jnp.int32(0),
    )
    tail_sum = spread_columns(arrived, recv_rows, node_total, every_slot, False)
    degree_float = degree.astype(jnp.float32)
    mixed = (hub_sum + tail_sum / degree_float[None, :]).astype(jnp.bfloat16)
    full_feat, full_mixed = (
        lax.all_gather(features, "rep", axis=0, tiled=True),
        lax.all_gather(mixed, "rep", axis=0, tiled=True),
    )
    pre = (
        jnp.dot(w_self.T, full_feat, preferred_element_type=jnp.float32)
        + jnp.dot(w_neigh.T, full_mixed, preferred_element_type=jnp.float32)
        + out_bias[:, None]
    )
    output = jax.nn.silu(pre).astype(jnp.bfloat16)
    d_pre = (cotangent.astype(jnp.float32) * silu_slope(pre)).astype(jnp.bfloat16)
    contract_nodes = (((1,), (1,)), ((), ()))
    local_self = lax.dot_general(
        full_feat, d_pre, contract_nodes, preferred_element_type=jnp.float32
    )
    local_neigh = lax.dot_general(
        full_mixed, d_pre, contract_nodes, preferred_element_type=jnp.float32
    )
    local_bias = jnp.sum(d_pre.astype(jnp.float32), axis=1)
    grad_w_self, grad_w_neigh, grad_bias = lax.psum((local_self, local_neigh, local_bias), "dom")
    both_grads = lax.psum_scatter(
        jnp.concatenate(
            [
                jnp.dot(w_self, d_pre, preferred_element_type=jnp.float32),
                jnp.dot(w_neigh, d_pre, preferred_element_type=jnp.float32),
            ],
            axis=1,
        ),
        "rep",
        scatter_dimension=0,
        tiled=True,
    )
    direct = both_grads[:, :node_total]
    back_mixed = both_grads[:, node_total:]
    mixed_grad = back_mixed.astype(jnp.bfloat16)
    gathered, slot_degree = pick_columns(
        (mixed_grad, degree.astype(jnp.bfloat16)[None, :]), recv_rows, every_slot, node_total
    )
    slot_grads = gathered / slot_degree
    returned = lax.all_to_all(
        slot_grads.astype(jnp.bfloat16), "dom", split_axis=1, concat_axis=1, tiled=True
    ).astype(slot_grads.dtype)
    hub_grad = lax.psum_scatter(
        hub_terms(mixed_grad, tiles, hub_rows, hub_live, "fqt,qjt->qfj").reshape(
            1 * lax.axis_size("dom"), own_width * hub_total
        ),
        "dom",
        scatter_dimension=0,
        tiled=True,
    ).reshape(own_width, hub_total)
    tail_grad = spread_columns(returned, send_rows, node_total, send_live, True)
    grad_features = direct + tail_grad + jnp.pad(hub_grad, ((0, 0), (0, node_total - hub_total)))
    return (output, grad_features, grad_w_self, grad_w_neigh, grad_bias)


def solution(mesh):
    in_specs = (
        P("rep", "dom"),
        P("dom", None, None, None),
        P("dom", None),
        P("dom", None),
        P("dom", None, None),
        P("dom", None),
        P("dom", None, None),
        P("dom"),
        P(None, "rep"),
        P(None, "rep"),
        P("rep"),
        P("rep", "dom"),
    )
    out_specs = (P("rep", "dom"), P("rep", "dom"), P(None, "rep"), P(None, "rep"), P("rep"))
    return jax.shard_map(local, mesh=mesh, in_specs=in_specs, out_specs=out_specs, check_vma=False)
```

profile of v0, /device:TPU:32, one launch (start us, length us, event | category | flops | bytes accessed | tf_op | source)
XLA Modules:
  0.0 2230.6 jit_solution(11008930729087312402)
XLA Ops:
  19.3 19.8 all-to-all-start
  39.8 14.5 all_gather.9
  54.6 2.7 all-to-all-done
  61.3 82.2 %all-gather.2.cloned.1.call-done = bf16[64,8192]{0,1:T(8,128)(2,1)} async-done(((bf16[64,64]{0,1:T(8,128)(2,1)}), bf16[64,8192]{0,1:T(8,128)(2,1)}) %all-gather.2.cloned.1.call-update) | async-done | bytes 1048592 | tf_op jit(solution)/shard_map/all_gather | solution.py:124
  145.5 563.4 %while.15 = (s32[]{:T(128)}, f32[64,1024]{1,0:T(8,128)S(1)}, s32[128]{0:T(128)S(1)}, s32[128]{0:T(128)S(1)}, s32[128]{0:T(128)S(1)}, /*index=5*/bf16[64,8192]{1,...) while((s32[]{:T(128)}, f32[64,1024]{1,0:T(8,128)S(1)}, ...), condition=%wide.region_3.4_spmd, body=%wide.region_0.3_spmd.sunk | while | flops 1056797 | bytes 100370 | solution.py:79
  155.5 2.1 conditional.2
  165.0 2.1 conditional.2
  179.8 2.1 conditional.2
  189.3 2.1 conditional.2
  201.4 2.1 conditional.2
  206.2 2.1 conditional.2
  210.9 2.1 conditional.2
  215.7 2.1 conditional.2
  225.2 2.1 conditional.2
  234.6 2.1 conditional.2
  239.4 2.1 conditional.2
  244.1 2.1 conditional.2
  248.9 2.1 conditional.2
  261.0 2.1 conditional.2
  270.5 2.1 conditional.2
  280.0 2.1 conditional.2
  284.7 2.1 conditional.2
  289.5 2.1 conditional.2
  294.2 2.1 conditional.2
  303.7 2.1 conditional.2
  308.4 2.1 conditional.2
  313.2 2.1 conditional.2
  320.6 2.1 conditional.2
  325.3 2.1 conditional.2
  330.1 2.1 conditional.2
  339.6 2.1 conditional.2
  354.4 2.1 conditional.2
  363.9 2.1 conditional.2
  373.3 2.1 conditional.2
  378.1 2.1 conditional.2
  385.5 2.1 conditional.2
  390.2 2.1 conditional.2
  395.0 2.1 conditional.2
  402.4 2.1 conditional.2
  407.1 2.1 conditional.2
  710.7 6.5 all_gather.11
  726.2 68.3 %reduce-scatter.5.cloned.1.call-done = f32[64,2048]{1,0:T(8,128)} async-done(((f32[256,2048]{1,0:T(8,128)}), f32[64,2048]{1,0:T(8,128)}) %reduce-scatter.5.cloned.1.call-update) | async-done | bytes 524304 | tf_op jit(solution)/shard_map/reduce_scatter | solution.py:150
  802.1 4.8 fusion.41
  807.0 4.9 copy.87
  815.3 17.0 all-to-all-start.1
  833.6 379.2 %psum.23 = f32[64]{0:T(128)} all-reduce(f32[64]{0:T(128)S(1)} %get-tuple-element.228), channel_id=1, replica_groups=mesh['dom'=128,'rep'=4] {'dom'}, use_global_device_ids=true, to_apply=%region_9.10 | all-reduce | flops 64 | bytes 512 | tf_op jit(solution)/shard_map/psum | solution.py:149
  1217.0 1000.4 %all-reduce.5.cloned.1.call-done = (f32[128,4096]{0,1:T(8,128)}, f32[256,64]{0,1:T(8,128)}, f32[256,64]{0,1:T(8,128)}) async-done(((f32[128,4096]{0,1:T(8,128)}, f32[256,64]{0,1:T(8,128)}, f32[256,64]{0,1:T(8,128)}), (f32[128,4096]{0,1:T(8,128)}, f32[256,64]{0,1:T(8,128)}, f32[256,64]{0,1:T(8,128)})) %all-reduce.5.cloned.1.call-update) | async-done | bytes 2228240
  2217.4 3.4 dynamic-slice_reduce_fusion
  (681 shorter events, 524.9 us)
Async XLA Ops:
  7.2 710.1 %copy-start = (bf16[256,64]{0,1:T(8,128)(2,1)S(1)}, bf16[256,64]{0,1:T(8,128)(2,1)}, u32[]{:S(2)}) copy-start(bf16[256,64]{0,1:T(8,128)(2,1)} %param.25) | copy-start | bytes 98308
  7.2 8.2 copy-start.4
  7.2 136.3 %all-gather.2.cloned.1.call-start = ((), (), s32[]{:S(2)}) async-start(), calls=%async_computation.3 | async-start | bytes 2113536 | tf_op jit(solution)/shard_map/all_gather | solution.py:124
  16.3 22.8 %copy-start.3 = (s32[1,128,32]{1,2,0:T(8,128)S(1)}, s32[1,128,32]{1,2,0:T(8,128)}, u32[]{:S(2)}) copy-start(s32[1,128,32]{1,2,0:T(8,128)} %param.22) | copy-start | bytes 49156
  16.5 37.8 %copy-start.9 = (s32[1024]{0:T(1024)S(1)}, s32[1024]{0:T(1024)}, u32[]{:S(2)}) copy-start(s32[1024]{0:T(1024)} %param.23) | copy-start | bytes 12292
  16.5 37.8 %copy-start.5 = (bf16[256,64]{0,1:T(8,128)(2,1)S(1)}, bf16[256,64]{0,1:T(8,128)(2,1)}, u32[]{:S(2)}) copy-start(bf16[256,64]{0,1:T(8,128)(2,1)} %param.24) | copy-start | bytes 98308
  19.3 38.0 %all-to-all-start = ((bf16[128,2,1024]{2,1,0:T(2,128)(2,1)}), bf16[128,2,1024]{2,1,0:T(2,128)(2,1)S(1)}, u32[]{:S(2)}, u32[]{:S(2)}) async-start(bf16[128,2,1024]{2,1,0:T(2,128)(2,1)} %reshape.196), calls=%async_computation | async-start | bytes 1048576 | tf_op jit(solution)/shard_map/all_to_all | solution.py:120
  39.1 755.4 %reduce-scatter.5.cloned.1.call-start = ((), (), s32[]{:S(2)}) async-start(), calls=%async_computation.4 | async-start | bytes 2621440 | tf_op jit(solution)/shard_map/reduce_scatter | solution.py:150
  57.9 87.6 %copy-start.12 = (s32[1,128]{1,0:T(1,128)S(1)}, s32[1,128]{1,0:T(1,128)}, u32[]{:S(2)}) copy-start(s32[1,128]{1,0:T(1,128)} %param.19) | copy-start | bytes 1540
  57.9 87.6 %copy-start.13 = (s32[1,128]{1,0:T(1,128)S(1)}, s32[1,128]{1,0:T(1,128)}, u32[]{:S(2)}) copy-start(s32[1,128]{1,0:T(1,128)} %param.18) | copy-start | bytes 1540
  61.3 655.9 %copy-start.10 = (bf16[64,1024]{1,0:T(8,128)(2,1)S(1)}, bf16[64,1024]{1,0:T(8,128)(2,1)}, u32[]{:S(2)}) copy-start(bf16[64,1024]{1,0:T(8,128)(2,1)} %param.27) | copy-start | bytes 393220
  61.3 655.9 %copy-start.11 = (f32[64]{0:T(128)S(1)}, f32[64]{0:T(128)}, u32[]{:S(2)}) copy-start(f32[64]{0:T(128)} %param.26) | copy-start | bytes 772
  721.0 1496.4 %all-reduce.5.cloned.1.call-start = ((), (), s32[]{:S(2)}) async-start(), calls=%async_computation.5 | async-start | bytes 4456448
  807.0 6.2 copy-start.1
  807.0 6.2 copy-start.2
  815.3 397.5 %all-to-all-start.1 = ((bf16[128,2,1024]{2,1,0:T(2,128)(2,1)}), bf16[128,2,1024]{2,1,0:T(2,128)(2,1)S(1)}, u32[]{:S(2)}, u32[]{:S(2)}) async-start(bf16[128,2,1024]{2,1,0:T(2,128)(2,1)} %reshape.198), calls=%async_computation.1 | async-start | bytes 1048576 | tf_op jit(solution)/shard_map/all_to_all | solution.py:169
  1213.5 1007.5 %copy-start.8 = (f32[64,2048]{1,0:T(8,128)S(1)}, f32[64,2048]{1,0:T(8,128)}, u32[]{:S(2)}) copy-start(f32[64,2048]{1,0:T(8,128)} %reduce-scatter.5.cloned.1.call-done) | copy-start | bytes 1572868
  2217.4 5.4 copy-start.7
  2217.4 6.1 copy-start.6
Sparse Core Ops, SparseCore 0:
  13.1 130.3 all-gather.1
  721.1 73.3 reduce-scatter.4
  812.0 1405.3 all-reduce.4
where the time goes:
time: 2240 us; the launch traced here: 2230 us
  waiting for transfers between devices  1150 us (51%)
  blocking collectives  400 us (18%)
  local copies, waits for them, and re-layouts  248 us (11%)
  loops' own time  241 us (11%)
  matrix products  135 us (6%)
  starting transfers between devices  37.1 us (2%)
    unnamed x4, waiting for transfers between devices  1000 us
    psum x1, blocking collectives, local(): lax.psum((local_self, local_neigh, local_bias), 'dom')  379 us
    another operation x1, loops' own time, fold_hubs(): lax.scan(one_step, carry, jnp.arange(piece_len // step_len, dtype=jnp.int...  177 us
    dot_general x107, matrix products, add_tile(): product = jnp.dot(columns, weights, preferred_element_type=jnp.float32)  100 us
    dynamic_slice x128, local copies, waits for them, and re-layouts, one_step(): return (lax.cond(hub_live[owner] > 0, add_tile, keep_tile, summed), None)  85 us
    all_gather x1, waiting for transfers between devices, local(): lax.all_gather(hub_part, 'dom', axis=1, tiled=True)  82.2 us
    dynamic_slice x128, local copies, waits for them, and re-layouts, fold_hubs(): lax.scan(one_step, carry, jnp.arange(piece_len // step_len, dtype=jnp.int...  74.6 us
    reduce_scatter x1, waiting for transfers between devices, local(): lax.psum_scatter(jnp.concatenate([jnp.dot(w_self, d_pre, preferred_elemen...  68.3 us
  transfers between devices with their start and end apart: 5, of which 4 were waited for; matrix products, arithmetic and copies ran while one was open for 1% of the time, Pallas kernels for 0%

commit v1 on v0

v1 whole, which is shorter than its diff:
```python
import jax
import jax.numpy as jnp
from jax import lax
from jax.sharding import PartitionSpec as P

BF = jnp.bfloat16
F32 = jnp.float32
BOTH_ROWS = (((0,), (0,)), ((), ()))
BOTH_COLS = (((1,), (1,)), ((), ()))


def mm(a, b, dims):
    return lax.dot_general(a, b, dims, preferred_element_type=F32)


def swap(pieces, axis):
    return lax.all_to_all(pieces, axis, split_axis=0, concat_axis=0, tiled=True)


def high_low(values):
    high = lax.reduce_precision(values, 8, 7)
    return jnp.concatenate([high.astype(BF), (values - high).astype(BF)], axis=1)


def one_hot_rows(index, total):
    return (index[:, None] == lax.broadcasted_iota(jnp.int32, (1, total), 1)).astype(BF)


def slot_groups(index, groups):
    parts, slots = index.shape
    part_len = slots // groups
    return [index[:, g * part_len : (g + 1) * part_len].reshape(-1) for g in range(groups)]


def gather_slots(source, index_groups, parts):
    pieces = [
        mm(one_hot_rows(index, source.shape[1]), source, BOTH_COLS).astype(BF)
        for index in index_groups
    ]
    return jnp.concatenate(pieces, axis=1).reshape(parts, -1, 128)


def spread_slots(arrived, index_groups, width, nodes):
    flat = arrived.reshape(-1, 128)
    total = 0.0
    for g, index in enumerate(index_groups):
        total = total + mm(flat[:, g * width : (g + 1) * width], one_hot_rows(index, nodes), BOTH_ROWS)
    return total


def local(
    features,
    hub_weight,
    hub_block,
    hub_mask,
    tail_rows,
    tail_count,
    tail_target,
    degree,
    w_self,
    w_neigh,
    out_bias,
    cotangent,
):
    width, nodes = features.shape
    tiles = hub_weight[0]
    parts, hubs, tile_len = tiles.shape
    slots = tail_rows.shape[2]
    groups = 128 // width
    hub_len = hubs // groups
    blocks = nodes // tile_len
    full_width = w_self.shape[0]
    my_rep = lax.axis_index("rep")

    hub_t = features[:, :hubs].T
    hub_piece = jnp.concatenate(
        [hub_t[g * hub_len : (g + 1) * hub_len] for g in range(groups)], axis=1
    )
    hub_all = swap(jnp.broadcast_to(hub_piece[None], (parts, hub_len, 128)), "dom")

    slot_live = jnp.arange(slots, dtype=jnp.int32)[None, :] < tail_count[0][:, None]
    send_groups = slot_groups(jnp.where(slot_live, tail_rows[0], -1), groups)
    recv_groups = slot_groups(tail_target[0], groups)
    arrived = swap(gather_slots(features, send_groups, parts), "dom")

    early = lax.all_gather(
        jnp.concatenate([features, w_self.T, w_neigh.T], axis=1), "rep", axis=0, tiled=True
    )
    full_feat = early[:, :nodes]
    own_rows = my_rep * width
    w_self_rows = lax.dynamic_slice_in_dim(early[:, nodes : nodes + full_width], own_rows, width, 1)
    w_neigh_rows = lax.dynamic_slice_in_dim(early[:, nodes + full_width :], own_rows, width, 1)
    pre_self = mm(w_self, full_feat, BOTH_ROWS) + out_bias[:, None]

    live = hub_mask[0] > 0
    in_block = (hub_block[0][:, None] == jnp.arange(blocks, dtype=jnp.int32)[None, :]) & live[:, None]
    hub_out = 0.0
    for g in range(groups):
        rows = hub_all[:, :, g * width : (g + 1) * width]
        placed = jnp.where(in_block[:, None, :, None], rows[:, :, None, :], jnp.zeros((), BF))
        hub_out = hub_out + mm(
            placed.reshape(parts * hub_len, blocks * width),
            tiles[:, g * hub_len : (g + 1) * hub_len, :].reshape(parts * hub_len, tile_len),
            BOTH_ROWS,
        )
    hub_sum = jnp.concatenate([hub_out[b * width : (b + 1) * width] for b in range(blocks)], axis=1)
    tail_sum = spread_slots(arrived, recv_groups, width, nodes)
    degree_float = degree.astype(F32)[None, :]
    mixed = (hub_sum + tail_sum / degree_float).astype(BF)

    full_mixed = lax.all_gather(mixed, "rep", axis=0, tiled=True)
    pre = pre_self + mm(w_neigh, full_mixed, BOTH_ROWS)
    sigma = jax.nn.sigmoid(pre)
    output = (pre * sigma).astype(BF)
    d_pre = (cotangent.astype(F32) * (sigma * (1.0 + pre * (1.0 - sigma)))).astype(BF)

    full_d = lax.all_gather(d_pre, "rep", axis=0, tiled=True)
    mixed_grad = mm(w_neigh_rows, full_d, BOTH_ROWS).astype(BF)
    direct = mm(w_self_rows, full_d, BOTH_ROWS)

    half = full_width // groups
    grads = []
    for source in (full_feat, full_mixed):
        grad = mm(source, d_pre, BOTH_COLS)
        grads += [
            jnp.concatenate([grad[g * half : (g + 1) * half] for g in range(groups)], axis=1)
        ]
    bias_part = jnp.sum(d_pre.astype(F32), axis=1)
    bias_rows = jnp.broadcast_to(jnp.tile(bias_part, groups)[None, None], (parts, 2, 128))
    grad_rows = jnp.concatenate([g.reshape(parts, -1, 128) for g in grads] + [bias_rows], axis=1)
    kinds = grad_rows.shape[1]

    scaled = (mixed_grad.astype(F32) / degree_float).astype(BF)
    tail_send = gather_slots(scaled, recv_groups, parts)
    tail_len = tail_send.shape[1]
    first = swap(jnp.concatenate([tail_send, high_low(grad_rows)], axis=1), "dom")

    by_block = mixed_grad.reshape(width, blocks, tile_len).transpose(1, 0, 2)
    chosen = jnp.take(by_block, hub_block[0], axis=0) * live.astype(BF)[:, None, None]
    hub_terms = jnp.einsum("qjt,qft->qjf", tiles, chosen, preferred_element_type=F32).astype(BF)
    hub_send = jnp.concatenate(
        [hub_terms[:, g * hub_len : (g + 1) * hub_len] for g in range(groups)], axis=2
    )
    sums = jnp.sum(first[:, tail_len:].astype(F32), axis=0)
    sums = sums[:kinds] + sums[kinds:]
    grad_bias = sums[kinds - 1, :width]
    sum_rows = jnp.broadcast_to(high_low(sums[None]), (parts, 2 * kinds, 128))
    second = swap(jnp.concatenate([hub_send, sum_rows], axis=1), "dom")

    tail_grad = spread_slots(first[:, :tail_len], send_groups, width, nodes)
    all_sums = second[:, hub_len:].astype(F32)
    all_sums = all_sums[:, : kinds - 2] + all_sums[:, kinds : 2 * kinds - 2]
    grad_w_self, grad_w_neigh = [
        jnp.concatenate([rows[:, g * width : (g + 1) * width] for g in range(groups)], axis=0)
        for rows in jnp.split(all_sums, 2, axis=1)
        for rows in [rows.reshape(half, 128)]
    ]
    hub_back = jnp.sum(second[:, :hub_len].astype(F32), axis=0)
    hub_grad = jnp.concatenate(
        [hub_back[:, g * width : (g + 1) * width] for g in range(groups)], axis=0
    ).T
    grad_features = direct + tail_grad + jnp.pad(hub_grad, ((0, 0), (0, nodes - hubs)))
    return (output, grad_features, grad_w_self, grad_w_neigh, grad_bias)


def solution(mesh):
    in_specs = (
        P("rep", "dom"),
        P("dom", None, None, None),
        P("dom", None),
        P("dom", None),
        P("dom", None, None),
        P("dom", None),
        P("dom", None, None),
        P("dom"),
        P(None, "rep"),
        P(None, "rep"),
        P("rep"),
        P("rep", "dom"),
    )
    out_specs = (P("rep", "dom"), P("rep", "dom"), P(None, "rep"), P(None, "rep"), P("rep"))
    return jax.shard_map(local, mesh=mesh, in_specs=in_specs, out_specs=out_specs, check_vma=False)
```

time: 2240 us -> 255 us (0.11)
  the two profiles are of different devices: /device:TPU:32 before, /device:TPU:1 now
where the time goes in v1:
time: 255 us; the launch traced here: 254 us
  waiting for transfers between devices  81.2 us (32%)
  starting transfers between devices  52.7 us (21%)
  blocking collectives  42 us (16%)
  local copies, waits for them, and re-layouts  35.9 us (14%)
  matrix products  28.6 us (11%)
  other arithmetic  12.2 us (5%)
    all_to_all x4, waiting for transfers between devices, swap(): return lax.all_to_all(pieces, axis, split_axis=0, concat_axis=0, tiled=True)  81.2 us
    all_to_all x4, starting transfers between devices, swap(): return lax.all_to_all(pieces, axis, split_axis=0, concat_axis=0, tiled=True)  52.7 us
    all_gather x1, blocking collectives, local(): lax.all_gather(jnp.concatenate([features, w_self.T, w_neigh.T], axis=1),...  27.1 us
    dot_general x16, matrix products, mm(): return lax.dot_general(a, b, dims, preferred_element_type=F32)  25.8 us
    select_n x2, local copies, waits for them, and re-layouts, local(): jnp.where(in_block[:, None, :, None], rows[:, :, None, :], jnp.zeros((),...  23.6 us
    all_gather x1, blocking collectives, local(): full_d = lax.all_gather(d_pre, 'rep', axis=0, tiled=True)  7.51 us
    all_gather x1, blocking collectives, local(): full_mixed = lax.all_gather(mixed, 'rep', axis=0, tiled=True)  7.35 us
    select_n x1, other arithmetic, local(): jnp.where(in_block[:, None, :, None], rows[:, :, None, :], jnp.zeros((),...  6.48 us
  transfers between devices with their start and end apart: 4, of which 4 were waited for; matrix products, arithmetic and copies ran while one was open for 6% of the time, Pallas kernels for 0%

profile of v1, /device:TPU:1, one launch (start us, length us, event | category | flops | bytes accessed | tf_op | source)
XLA Modules:
  0.0 253.9 jit_solution(6884991157162137504)
XLA Ops:
  0.6 0.8 bitcast_select_fusion
  1.8 2.9 %fusion.16 = bf16[2048,64]{0,1:T(8,128)(2,1)S(1)} fusion(bf16[64,1024]{1,0:T(8,128)(2,1)} %param.12, s32[2048]{0:T(1024)S(1)} %eq.48), kind=kOutput, calls=%fused_computation.23 | convolution fusion | flops 270663680 | bytes 401408 | tf_op jit(solution)/shard_map/dot_general | solution.py:13
  4.7 2.0 fusion.17
  6.8 1.0 copy.37
  7.9 21.0 %all-to-all-start.1 = ((bf16[128,16,128]{2,1,0:T(8,128)(2,1)}), bf16[128,16,128]{2,1,0:T(8,128)(2,1)S(1)}, u32[]{:S(2)}, u32[]{:S(2)}) async-start(bf16[128,16,128]{2,1,0:T(8,128)(2,1)} %bitcast.10), calls=%async_computation.1 | async-start | bytes 1048576 | tf_op jit(solution)/shard_map/all_to_all | solution.py:17
  29.0 20.4 %all-to-all-done.1 = bf16[128,16,128]{2,1,0:T(8,128)(2,1)S(1)} async-done(((bf16[128,16,128]{2,1,0:T(8,128)(2,1)}), bf16[128,16,128]{2,1,0:T(8,128)(2,1)S(1)}, u32[]{:S(2)}, u32[]{:S(2)}) %all-to-all-start.1) | async-done | bytes 524320 | tf_op jit(solution)/shard_map/all_to_all | solution.py:17
  49.4 1.2 broadcast_in_dim.75
  50.6 8.1 %all-to-all-start = ((bf16[128,32,128]{2,1,0:T(8,128)(2,1)}), bf16[128,32,128]{2,1,0:T(8,128)(2,1)S(1)}, u32[]{:S(2)}, u32[]{:S(2)}) async-start(bf16[128,32,128]{2,1,0:T(8,128)(2,1)} %broadcast_in_dim.75), calls=%async_computation | async-start | bytes 2097152 | tf_op jit(solution)/shard_map/all_to_all | solution.py:17
  59.3 27.1 %all_gather.9 = bf16[256,1536]{1,0:T(8,128)(2,1)S(1)} all-gather(bf16[64,1536]{1,0:T(8,128)(2,1)S(1)} %pad_maximum_fusion.5), channel_id=1, replica_groups=mesh['dom'=128,'rep'=4] {'rep'}, dimensions={0}, use_global_device_ids=true | all-gather | bytes 983040 | tf_op jit(solution)/shard_map/all_gather | solution.py:86
  86.5 0.9 convolution_add_fusion.1
  87.4 2.0 fusion.58
  89.4 2.7 %fusion.1 = f32[64,1024]{1,0:T(8,128)} fusion(s32[2048]{0:T(1024)S(1)} %eq.60, bf16[2048,128]{1,0:T(8,128)(2,1)S(1)} %bitcast.77), kind=kOutput, calls=%fused_computation.3 | convolution fusion | flops 270532608 | bytes 794624 | tf_op jit(solution)/shard_map/dot_general | solution.py:13
  92.1 0.7 all-to-all-done
  92.8 0.4 fusion.59
  93.2 6.5 %broadcast_select_fusion = (bf16[128,32,8,64]{3,2,1,0:T(8,128)(2,1)}, bf16[128,32,8,64]{3,2,1,0:T(8,128)(2,1)}) fusion(pred[128,8]{1,0:T(8,128)(4,1)S(1)} %fusion.47, bf16[128,32,64]{2,1,0:T(8,128)(2,1)S(1)} %get-tuple-element.28, bf16[128,32,64]{2,1,0:T(8,128)(2,1)S(1)} %get-tuple-element.29), kind=kLoop, calls=%fused_computation.13 | loop fusion | flops 4194304 | bytes 9438208 | tf_op jit(solution)/shard_map/jit(_where)/select_n | solution.py:100
  99.6 11.8 %select_n.56 = bf16[4096,512]{1,0:T(8,128)(2,1)} reshape(bf16[128,32,8,64]{3,2,1,0:T(8,128)(2,1)} %get-tuple-element.52) | data formatting | bytes 8388608 | tf_op jit(solution)/shard_map/jit(_where)/select_n | solution.py:100
  111.4 11.9 %select_n.58 = bf16[4096,512]{1,0:T(8,128)(2,1)} reshape(bf16[128,32,8,64]{3,2,1,0:T(8,128)(2,1)} %get-tuple-element.51) | data formatting | bytes 8388608 | tf_op jit(solution)/shard_map/jit(_where)/select_n | solution.py:100
  123.3 3.6 %fusion.70 = f32[512,128]{1,0:T(8,128)S(1)} fusion(bf16[4096,512]{1,0:T(8,128)(2,1)} %select_n.56, bf16[4096,128]{1,0:T(8,128)(2,1)S(1)} %bitcast.72), kind=kOutput, calls=%fused_computation.125 | convolution fusion | flops 536870912 | bytes 5505024 | tf_op jit(solution)/shard_map/dot_general | solution.py:13
  126.9 1.3 convolution_add_fusion.2
  128.4 1.6 fusion.33
  130.0 7.4 %all_gather.10 = bf16[256,1024]{1,0:T(8,128)(2,1)S(1)} all-gather(bf16[64,1024]{1,0:T(8,128)(2,1)S(1)} %fusion.33), channel_id=1, replica_groups=mesh['dom'=128,'rep'=4] {'rep'}, dimensions={0}, use_global_device_ids=true | all-gather | bytes 655360 | tf_op jit(solution)/shard_map/all_gather | solution.py:111
  137.3 1.0 convert_reduce_fusion.2
  138.4 7.5 %all_gather.11 = bf16[256,1024]{1,0:T(8,128)(2,1)S(1)} all-gather(bf16[64,1024]{1,0:T(8,128)(2,1)S(1)} %get-tuple-element.23), channel_id=1, replica_groups=mesh['dom'=128,'rep'=4] {'rep'}, dimensions={0}, use_global_device_ids=true | all-gather | bytes 655360 | tf_op jit(solution)/shard_map/all_gather | solution.py:117
  145.9 0.3 convolution_convert_fusion
  146.2 2.1 fusion.18
  148.3 2.1 fusion.19
  150.4 0.3 fusion.40
  150.7 0.3 fusion.71
  151.0 0.3 copy.40
  151.7 0.2 reduce-precision_convert_fusion
  151.9 1.2 pad_maximum_fusion.1
  153.1 15.5 %all-to-all-start.2 = ((bf16[128,24,128]{2,1,0:T(8,128)(2,1)}), bf16[128,24,128]{2,1,0:T(8,128)(2,1)}, u32[]{:S(2)}, u32[]{:S(2)}) async-start(bf16[128,24,128]{2,1,0:T(8,128)(2,1)} %pad_maximum_fusion.1), calls=%async_computation.2 | async-start | bytes 1572864 | tf_op jit(solution)/shard_map/all_to_all | solution.py:17
  168.7 2.2 gather_fusion
  170.9 2.9 %convert_bitcast_fusion = bf16[128,64,64]{2,1,0:T(8,128)(2,1)S(1)} fusion(bf16[128,64,128]{2,1,0:T(8,128)(2,1)} %gather_fusion, pred[128]{0:T(512)(128)(4,1)S(1)} %compare_and_fusion, bf16[128]{0:T(256)(128)(2,1)S(1)} %get-tuple-element.55, bf16[1,128,64,128]{3,2,1,0:T(8,128)(2,1)S(1)} %copy-done.3), kind=kOutput, calls=%fused_computation.28 | convolution fusion | flops 136839168 | bytes 5243264 | tf_op jit(solution)/shard_map/qjt,qft->qjf/dot_general | solution.py:140
  173.8 0.4 fusion.57
  174.1 21.7 %all-to-all-done.2 = bf16[128,24,128]{2,1,0:T(8,128)(2,1)} async-done(((bf16[128,24,128]{2,1,0:T(8,128)(2,1)}), bf16[128,24,128]{2,1,0:T(8,128)(2,1)}, u32[]{:S(2)}, u32[]{:S(2)}) %all-to-all-start.2) | async-done | bytes 786464 | tf_op jit(solution)/shard_map/all_to_all | solution.py:17
  195.8 1.1 convert_reduce_fusion.1
  197.0 1.7 pad_maximum_fusion
  198.7 8.1 %all-to-all-start.3 = ((bf16[128,40,128]{2,1,0:T(8,128)(2,1)}), bf16[128,40,128]{2,1,0:T(8,128)(2,1)S(1)}, u32[]{:S(2)}, u32[]{:S(2)}) async-start(bf16[128,40,128]{2,1,0:T(8,128)(2,1)} %pad_maximum_fusion), calls=%async_computation.3 | async-start | bytes 2621440 | tf_op jit(solution)/shard_map/all_to_all | solution.py:17
  206.8 0.3 fusion.45
  207.1 1.1 slice.217
  208.2 0.5 slice_bitcast_fusion
  208.7 2.0 fusion.4
  210.7 38.5 %all-to-all-done.3 = bf16[128,40,128]{2,1,0:T(8,128)(2,1)S(1)} async-done(((bf16[128,40,128]{2,1,0:T(8,128)(2,1)}), bf16[128,40,128]{2,1,0:T(8,128)(2,1)S(1)}, u32[]{:S(2)}, u32[]{:S(2)}) %all-to-all-start.3) | async-done | bytes 1310752 | tf_op jit(solution)/shard_map/all_to_all | solution.py:17
  249.5 0.7 copy.47
  250.3 0.7 copy.46
  251.0 0.2 convert_reduce_fusion
  251.5 2.3 fusion.32
  (94 shorter events, 2.4 us)
Async XLA Ops:
  0.6 4.1 %copy-start.8 = (bf16[64,1024]{1,0:T(8,128)(2,1)S(1)}, bf16[64,1024]{1,0:T(8,128)(2,1)}, u32[]{:S(2)}) copy-start(bf16[64,1024]{1,0:T(8,128)(2,1)} %param.12) | copy-start | bytes 393220
  6.8 22.1 %slice-start = ((bf16[64,1024]{1,0:T(8,128)(2,1)}), bf16[64,64]{1,0:T(8,128)(2,1)S(1)}, s32[]{:S(2)}) async-start(bf16[64,1024]{1,0:T(8,128)(2,1)} %param.12), calls=%async_computation.4 | async-start | bytes 32768 | tf_op jit(solution)/shard_map/slice | solution.py:75
  7.8 50.9 %copy-start.11 = (s32[1,128,32]{1,2,0:T(8,128)S(1)}, s32[1,128,32]{1,2,0:T(8,128)}, u32[]{:S(2)}) copy-start(s32[1,128,32]{1,2,0:T(8,128)} %param.18) | copy-start | bytes 49156
  7.8 51.3 %copy-start.12 = (s32[1024]{0:T(1024)S(1)}, s32[1024]{0:T(1024)}, u32[]{:S(2)}) copy-start(s32[1024]{0:T(1024)} %param.19) | copy-start | bytes 12292
  7.8 51.3 %copy-start.16 = (s32[1,128]{1,0:T(1,128)S(1)}, s32[1,128]{1,0:T(1,128)}, u32[]{:S(2)}) copy-start(s32[1,128]{1,0:T(1,128)} %param.15) | copy-start | bytes 1540
  7.8 51.3 %copy-start.13 = (s32[1,128]{1,0:T(1,128)S(1)}, s32[1,128]{1,0:T(1,128)}, u32[]{:S(2)}) copy-start(s32[1,128]{1,0:T(1,128)} %param.14) | copy-start | bytes 1540
  7.8 51.4 %copy-start.9 = (bf16[256,64]{0,1:T(8,128)(2,1)S(1)}, bf16[256,64]{0,1:T(8,128)(2,1)}, u32[]{:S(2)}) copy-start(bf16[256,64]{0,1:T(8,128)(2,1)} %param.20) | copy-start | bytes 98308
  7.8 51.4 %copy-start.10 = (bf16[256,64]{0,1:T(8,128)(2,1)S(1)}, bf16[256,64]{0,1:T(8,128)(2,1)}, u32[]{:S(2)}) copy-start(bf16[256,64]{0,1:T(8,128)(2,1)} %param.21) | copy-start | bytes 98308
  7.9 41.5 %all-to-all-start.1 = ((bf16[128,16,128]{2,1,0:T(8,128)(2,1)}), bf16[128,16,128]{2,1,0:T(8,128)(2,1)S(1)}, u32[]{:S(2)}, u32[]{:S(2)}) async-start(bf16[128,16,128]{2,1,0:T(8,128)(2,1)} %bitcast.10), calls=%async_computation.1 | async-start | bytes 1048576 | tf_op jit(solution)/shard_map/all_to_all | solution.py:17
  49.4 1.2 copy-start.4
  50.6 35.9 %copy-start.14 = (f32[64]{0:T(128)S(1)}, f32[64]{0:T(128)}, u32[]{:S(2)}) copy-start(f32[64]{0:T(128)} %param.22) | copy-start | bytes 772
  50.6 42.2 %all-to-all-start = ((bf16[128,32,128]{2,1,0:T(8,128)(2,1)}), bf16[128,32,128]{2,1,0:T(8,128)(2,1)S(1)}, u32[]{:S(2)}, u32[]{:S(2)}) async-start(bf16[128,32,128]{2,1,0:T(8,128)(2,1)} %broadcast_in_dim.75), calls=%async_computation | async-start | bytes 2097152 | tf_op jit(solution)/shard_map/all_to_all | solution.py:17
  86.4 1.0 copy-start.1
  87.4 2.0 copy-start.5
  123.3 3.6 %copy-start = (bf16[4096,512]{1,0:T(8,128)(2,1)S(1)}, bf16[4096,512]{1,0:T(8,128)(2,1)}, u32[]{:S(2)}) copy-start(bf16[4096,512]{1,0:T(8,128)(2,1)} %select_n.58) | copy-start | bytes 12582916
  126.9 1.4 copy-start.6
  126.9 1.4 copy-start.17
  128.4 9.0 %copy-start.7 = (f32[1024,64]{0,1:T(8,128)S(1)}, f32[1024,64]{0,1:T(8,128)}, u32[]{:S(2)}) copy-start(f32[1024,64]{0,1:T(8,128)} %convolution_add_fusion.1) | copy-start | bytes 786436
  128.4 9.0 %copy-start.15 = (bf16[64,1024]{1,0:T(8,128)(2,1)S(1)}, bf16[64,1024]{1,0:T(8,128)(2,1)}, u32[]{:S(2)}) copy-start(bf16[64,1024]{1,0:T(8,128)(2,1)} %param.23) | copy-start | bytes 393220
  148.3 2.1 copy-start.2
  153.1 42.7 %all-to-all-start.2 = ((bf16[128,24,128]{2,1,0:T(8,128)(2,1)}), bf16[128,24,128]{2,1,0:T(8,128)(2,1)}, u32[]{:S(2)}, u32[]{:S(2)}) async-start(bf16[128,24,128]{2,1,0:T(8,128)(2,1)} %pad_maximum_fusion.1), calls=%async_computation.2 | async-start | bytes 1572864 | tf_op jit(solution)/shard_map/all_to_all | solution.py:17
  168.7 2.2 copy-start.3
  198.7 50.5 %all-to-all-start.3 = ((bf16[128,40,128]{2,1,0:T(8,128)(2,1)}), bf16[128,40,128]{2,1,0:T(8,128)(2,1)S(1)}, u32[]{:S(2)}, u32[]{:S(2)}) async-start(bf16[128,40,128]{2,1,0:T(8,128)(2,1)} %pad_maximum_fusion), calls=%async_computation.3 | async-start | bytes 2621440 | tf_op jit(solution)/shard_map/all_to_all | solution.py:17

commit v2 on v1

v2 whole, which is shorter than its diff:
```python
from functools import partial

import jax
import jax.numpy as jnp
from jax import lax
from jax.experimental import pallas as pl
from jax.experimental.pallas import tpu as pltpu
from jax.sharding import Mesh
from jax.sharding import PartitionSpec as P

BF = jnp.bfloat16
F32 = jnp.float32
BOTH_ROWS = (((0,), (0,)), ((), ()))
BOTH_COLS = (((1,), (1,)), ((), ()))
DOM = ("yh", "x", "z")
PLANE = ("yh", "z")
REP = ("yl", "core")


def mm(a, b, dims):
    return lax.dot_general(a, b, dims, preferred_element_type=F32)


def swap(pieces, axis):
    return lax.all_to_all(pieces, axis, split_axis=0, concat_axis=0, tiled=True)


def high_low(values):
    high = lax.reduce_precision(values, 8, 7)
    return jnp.concatenate([high.astype(BF), (values - high).astype(BF)], axis=1)


def shift(values, axis, step):
    size = lax.axis_size(axis)
    return lax.ppermute(values, axis, [(i, (i + step) % size) for i in range(size)])


def gather_rep(values):
    first = lax.axis_index("yl") == 0
    other = shift(values, "yl", 1)
    mine = jnp.stack([jnp.where(first, values, other), jnp.where(first, other, values)])
    theirs = shift(mine, "core", 1)
    first = lax.axis_index("core") == 0
    both = jnp.stack([jnp.where(first, mine, theirs), jnp.where(first, theirs, mine)], axis=1)
    return both.reshape(-1, values.shape[1])


def tile_index(x_ref, k, sizes, yh, z, sign):
    x_size, z_size = sizes
    x = lax.rem(x_ref[0] + (sign * k) % x_size, x_size)
    return (yh * x_size + x) * z_size + z


def fold_kernel(sizes, x_ref, dest_ref, *refs):
    *hub_refs, tile_ref, out_ref, total = refs
    half = hub_refs[0].shape[1]
    lanes = lax.broadcasted_iota(jnp.int32, (half, 128), 1)
    first = (lanes < 64).astype(F32).astype(BF)
    second = (lanes >= 64).astype(F32).astype(BF)
    total[...] = jnp.zeros_like(total)
    x_size, z_size = sizes
    for k, hub_ref in enumerate(hub_refs):

        @pl.loop(0, hub_ref.shape[0] // z_size)
        def _(yh):
            for z in range(z_size):
                tile = tile_index(x_ref, k, sizes, yh, z, -1)
                rows = hub_ref[yh * z_size + z]
                weights = tile_ref[tile]
                product = jnp.dot(
                    jnp.concatenate([rows * first, rows * second], axis=0),
                    jnp.concatenate([weights, weights], axis=0),
                    preferred_element_type=F32,
                )
                dest = dest_ref[tile]
                total[dest] = total[dest] + product

    for b in range(total.shape[0] - 1):
        out_ref[:, b * 128 : (b + 1) * 128] = total[b]


def fold_hubs(x_index, dest, hubs, tiles, sizes, blocks):
    width = 2 * hubs[0].shape[1]
    smem = pl.BlockSpec(memory_space=pltpu.SMEM)
    vmem = pl.BlockSpec(memory_space=pltpu.VMEM)
    return pl.pallas_call(
        partial(fold_kernel, sizes),
        out_shape=jax.ShapeDtypeStruct((width, blocks * 128), F32),
        in_specs=[smem, smem] + [vmem] * (len(hubs) + 1),
        out_specs=vmem,
        scratch_shapes=[pltpu.VMEM((blocks + 1, width, 128), F32)],
        compiler_params=pltpu.CompilerParams(vmem_limit_bytes=24 * 1024 * 1024),
        cost_estimate=pl.CostEstimate(
            flops=4 * tiles.size * width, bytes_accessed=8 * 1024 * 1024, transcendentals=0
        ),
        name="hub_sums",
    )(x_index, dest, *hubs, tiles)


def hub_grad_kernel(sizes, x_ref, dest_ref, grad_ref, tile_ref, out_ref, blocked):
    blocks = blocked.shape[0] - 1
    for b in range(blocks):
        blocked[b] = grad_ref[:, b * 128 : (b + 1) * 128]
    blocked[blocks] = jnp.zeros_like(blocked[blocks])
    half = out_ref.shape[2]
    first = lax.broadcasted_iota(jnp.int32, (half, 128), 1) < 64
    x_size, z_size = sizes
    for k in range(x_size):

        @pl.loop(0, out_ref.shape[1] // z_size)
        def _(yh):
            for z in range(z_size):
                tile = tile_index(x_ref, k, sizes, yh, z, 1)
                weights = tile_ref[tile]
                product = mm(
                    blocked[dest_ref[tile]],
                    jnp.concatenate([weights, weights], axis=0),
                    BOTH_COLS,
                )
                out_ref[k, yh * z_size + z] = jnp.where(
                    first, product[:half], product[half:]
                ).astype(BF)


def hub_grad_terms(x_index, dest, grad, tiles, sizes, blocks):
    width = grad.shape[0]
    parts = tiles.shape[0]
    smem = pl.BlockSpec(memory_space=pltpu.SMEM)
    vmem = pl.BlockSpec(memory_space=pltpu.VMEM)
    return pl.pallas_call(
        partial(hub_grad_kernel, sizes),
        out_shape=jax.ShapeDtypeStruct((sizes[0], parts // sizes[0], width // 2, 128), BF),
        in_specs=[smem, smem, vmem, vmem],
        out_specs=vmem,
        scratch_shapes=[pltpu.VMEM((blocks + 1, width, 128), BF)],
        compiler_params=pltpu.CompilerParams(vmem_limit_bytes=24 * 1024 * 1024),
        cost_estimate=pl.CostEstimate(
            flops=4 * tiles.size * width, bytes_accessed=8 * 1024 * 1024, transcendentals=0
        ),
        name="hub_grad_terms",
    )(x_index, dest, grad, tiles)


def one_hot_rows(index, total):
    return (index[:, None] == lax.broadcasted_iota(jnp.int32, (1, total), 1)).astype(BF)


def slot_groups(index, groups):
    parts, slots = index.shape
    part_len = slots // groups
    return [index[:, g * part_len : (g + 1) * part_len].reshape(-1) for g in range(groups)]


def gather_slots(source, index_groups, parts):
    pieces = [
        mm(one_hot_rows(index, source.shape[1]), source, BOTH_COLS).astype(BF)
        for index in index_groups
    ]
    return jnp.concatenate(pieces, axis=1).reshape(parts, -1, 128)


def spread_slots(arrived, index_groups, width, nodes):
    flat = arrived.reshape(-1, 128)
    total = 0.0
    for g, index in enumerate(index_groups):
        total = total + mm(flat[:, g * width : (g + 1) * width], one_hot_rows(index, nodes), BOTH_ROWS)
    return total


def local(
    features,
    hub_weight,
    hub_block,
    hub_mask,
    tail_rows,
    tail_count,
    tail_target,
    degree,
    w_self,
    w_neigh,
    out_bias,
    cotangent,
):
    width, nodes = features.shape
    tiles = hub_weight[0]
    parts, hubs, tile_len = tiles.shape
    slots = tail_rows.shape[2]
    groups = 128 // width
    half_width = width // 2
    blocks = nodes // tile_len
    full_width = w_self.shape[0]
    x_size, z_size = lax.axis_size("x"), lax.axis_size("z")
    sizes = (x_size, z_size)
    plane = parts // x_size
    x_index = lax.axis_index("x")[None]
    hub_dest = jnp.where(hub_mask[0] > 0, hub_block[0], blocks)

    hub_piece = jnp.concatenate([features[:half_width, :hubs], features[half_width:, :hubs]], axis=1)
    hub_plane = swap(jnp.broadcast_to(hub_piece[None], (plane, half_width, 128)), PLANE)
    hub_all = [hub_plane] + [shift(hub_plane, "x", k) for k in range(1, x_size)]

    slot_live = jnp.arange(slots, dtype=jnp.int32)[None, :] < tail_count[0][:, None]
    send_groups = slot_groups(jnp.where(slot_live, tail_rows[0], -1), groups)
    recv_groups = slot_groups(tail_target[0], groups)
    arrived = swap(gather_slots(features, send_groups, parts), DOM)

    early = gather_rep(jnp.concatenate([features, w_self.T, w_neigh.T], axis=1))
    full_feat = early[:, :nodes]
    own_rows = lax.axis_index(REP) * width
    w_self_rows = lax.dynamic_slice_in_dim(early[:, nodes : nodes + full_width], own_rows, width, 1)
    w_neigh_rows = lax.dynamic_slice_in_dim(early[:, nodes + full_width :], own_rows, width, 1)
    pre_self = mm(w_self, full_feat, BOTH_ROWS) + out_bias[:, None]

    hub_sum = fold_hubs(x_index, hub_dest, hub_all, tiles, sizes, blocks)
    tail_sum = spread_slots(arrived, recv_groups, width, nodes)
    degree_float = degree.astype(F32)[None, :]
    mixed = (hub_sum + tail_sum / degree_float).astype(BF)

    full_mixed = lax.all_gather(mixed, REP, axis=0, tiled=True)
    pre = pre_self + mm(w_neigh, full_mixed, BOTH_ROWS)
    sigma = jax.nn.sigmoid(pre)
    output = (pre * sigma).astype(BF)
    d_pre = (cotangent.astype(F32) * (sigma * (1.0 + pre * (1.0 - sigma)))).astype(BF)

    full_d = lax.all_gather(d_pre, REP, axis=0, tiled=True)
    mixed_grad = mm(w_neigh_rows, full_d, BOTH_ROWS).astype(BF)
    direct = mm(w_self_rows, full_d, BOTH_ROWS)

    half = full_width // groups
    grads = []
    for source in (full_feat, full_mixed):
        grad = mm(source, d_pre, BOTH_COLS)
        grads += [
            jnp.concatenate([grad[g * half : (g + 1) * half] for g in range(groups)], axis=1)
        ]
    bias_part = jnp.sum(d_pre.astype(F32), axis=1)
    bias_rows = jnp.broadcast_to(jnp.tile(bias_part, groups)[None, None], (parts, 2, 128))
    grad_rows = jnp.concatenate([g.reshape(parts, -1, 128) for g in grads] + [bias_rows], axis=1)
    kinds = grad_rows.shape[1]

    scaled = (mixed_grad.astype(F32) / degree_float).astype(BF)
    tail_send = gather_slots(scaled, recv_groups, parts)
    tail_len = tail_send.shape[1]
    first = swap(jnp.concatenate([tail_send, high_low(grad_rows)], axis=1), DOM)

    hub_terms = hub_grad_terms(x_index, hub_dest, mixed_grad, tiles, sizes, blocks)
    hub_x = hub_terms[0].astype(F32)
    for k in range(1, x_size):
        hub_x = hub_x + shift(hub_terms[k], "x", k).astype(F32)
    sums = jnp.sum(first[:, tail_len:].astype(F32), axis=0)
    sums = sums[:kinds] + sums[kinds:]
    grad_bias = sums[kinds - 1, :width]
    sum_rows = jnp.broadcast_to(high_low(sums[None]), (plane, 2 * kinds, 128))
    second = swap(jnp.concatenate([hub_x.astype(BF), sum_rows], axis=1), PLANE)

    tail_grad = spread_slots(first[:, :tail_len], send_groups, width, nodes)
    own_sums = second[:, half_width:].astype(F32)
    own_sums = own_sums[:, : kinds - 2] + own_sums[:, kinds : 2 * kinds - 2]
    far_sums = jnp.stack([own_sums] + [shift(own_sums, "x", k) for k in range(1, x_size)])
    order = lax.rem(x_index[0] + x_size - jnp.arange(x_size, dtype=jnp.int32), x_size)
    all_sums = jnp.take(far_sums, order, axis=0).reshape(x_size, -1, z_size, kinds - 2, 128)
    all_sums = all_sums.transpose(1, 0, 2, 3, 4).reshape(parts, kinds - 2, 128)
    grad_w_self, grad_w_neigh = [
        jnp.concatenate([rows[:, g * width : (g + 1) * width] for g in range(groups)], axis=0)
        for rows in jnp.split(all_sums, 2, axis=1)
        for rows in [rows.reshape(half, 128)]
    ]
    hub_back = jnp.sum(second[:, :half_width].astype(F32), axis=0)
    hub_grad = jnp.concatenate([hub_back[:, :hubs], hub_back[:, hubs:]], axis=0)
    grad_features = direct + tail_grad + jnp.pad(hub_grad, ((0, 0), (0, nodes - hubs)))
    return (output, grad_features, grad_w_self, grad_w_neigh, grad_bias)


def solution(mesh):
    grid = (4, 4, mesh.shape["dom"] // 16, 2, 2)
    parted = Mesh(mesh.devices.reshape(grid), DOM + REP)
    in_specs = (
        P(REP, DOM),
        P(DOM, None, None, None),
        P(DOM, None),
        P(DOM, None),
        P(DOM, None, None),
        P(DOM, None),
        P(DOM, None, None),
        P(DOM),
        P(None, REP),
        P(None, REP),
        P(REP),
        P(REP, DOM),
    )
    out_specs = (P(REP, DOM), P(REP, DOM), P(None, REP), P(None, REP), P(REP))
    return jax.shard_map(local, mesh=parted, in_specs=in_specs, out_specs=out_specs, check_vma=False)
```

time: 255 us -> 200 us (0.78)
  the two profiles are of different devices: /device:TPU:1 before, /device:TPU:16 now
where the time goes in v2:
time: 200 us; the launch traced here: 199 us
  starting transfers between devices  93.2 us (47%)
  waiting for transfers between devices  36.7 us (18%)
  matrix products  22.9 us (11%)
  blocking collectives  15 us (8%)
  local copies, waits for them, and re-layouts  11.7 us (6%)
  other arithmetic  9.32 us (5%)
  Pallas kernels  9.13 us (5%)
    all_to_all x4, starting transfers between devices, swap(): return lax.all_to_all(pieces, axis, split_axis=0, concat_axis=0, tiled=True)  57.8 us
    ppermute x11, starting transfers between devices, shift(): lax.ppermute(values, axis, [(i, (i + step) % size) for i in range(size)])  35.4 us
    ppermute x11, waiting for transfers between devices, shift(): lax.ppermute(values, axis, [(i, (i + step) % size) for i in range(size)])  25 us
    dot_general x14, matrix products, mm(): return lax.dot_general(a, b, dims, preferred_element_type=F32)  22.9 us
    all_to_all x4, waiting for transfers between devices, swap(): return lax.all_to_all(pieces, axis, split_axis=0, concat_axis=0, tiled=True)  11.6 us
    all_gather x1, blocking collectives, local(): full_mixed = lax.all_gather(mixed, REP, axis=0, tiled=True)  7.54 us
    all_gather x1, blocking collectives, local(): full_d = lax.all_gather(d_pre, REP, axis=0, tiled=True)  7.47 us
    pallas_call x1, Pallas kernels, hub_grad_terms(): pl.pallas_call(partial(hub_grad_kernel, sizes), out_shape=jax.ShapeDtypeS...  5.1 us
  transfers between devices with their start and end apart: 15, of which 9 were waited for; matrix products, arithmetic and copies ran while one was open for 10% of the time, Pallas kernels for 5%

profile of v2, /device:TPU:16, one launch (start us, length us, event | category | flops | bytes accessed | tf_op | source)
XLA Modules:
  0.0 199.2 jit_solution(17055326161625207103)
XLA Ops:
  0.6 1.0 pad_maximum_fusion.7
  1.6 3.5 %collective-permute-start = (bf16[64,1536]{1,0:T(8,128)(2,1)S(1)}, bf16[64,1536]{1,0:T(8,128)(2,1)S(1)}, u32[]{:S(2)}, u32[]{:S(2)}) collective-permute-start(bf16[64,1536]{1,0:T(8,128)(2,1)S(1)} %pad_maximum_fusion.7), channel_id=1, source_target_pairs={{0,2},{2,0},{1,3},{3,1},{4,6},{6,4},{5,7},{7,5},{8,10},{10,8},{9,1... | collective-permute-start | bytes 589832 | tf_op jit(solution)/shard_map/ppermute | solution.py:35
  6.6 15.2 %all-to-all-start = ((bf16[32,32,128]{2,1,0:T(8,128)(2,1)}), bf16[32,32,128]{2,1,0:T(8,128)(2,1)S(1)}, u32[]{:S(2)}, u32[]{:S(2)}) async-start(bf16[32,32,128]{2,1,0:T(8,128)(2,1)} %broadcast_in_dim.47), calls=%async_computation | async-start | bytes 524288 | tf_op jit(solution)/shard_map/all_to_all | solution.py:25
  22.7 0.8 bitcast_select_fusion
  23.7 2.9 %fusion.17 = bf16[2048,64]{0,1:T(8,128)(2,1)S(1)} fusion(bf16[64,1024]{1,0:T(8,128)(2,1)} %param.12, s32[2048]{0:T(1024)S(1)} %eq.42), kind=kOutput, calls=%fused_computation.22 | convolution fusion | flops 270663680 | bytes 401408 | tf_op jit(solution)/shard_map/dot_general | solution.py:21
  26.8 2.0 %fusion.16 = bf16[2048,64]{0,1:T(8,128)(2,1)S(1)} fusion(bf16[64,1024]{1,0:T(8,128)(2,1)S(1)} %copy-done.3, s32[2048]{0:T(1024)S(1)} %eq.38), kind=kOutput, calls=%fused_computation.21 | convolution fusion | flops 270663680 | bytes 401408 | tf_op jit(solution)/shard_map/dot_general | solution.py:21
  29.0 0.8 pad_maximum_fusion.4
  29.8 1.9 collective-permute-start.1
  31.8 1.0 copy.23
  33.2 16.2 %all-to-all-start.1 = ((bf16[128,16,128]{2,1,0:T(8,128)(2,1)}), bf16[128,16,128]{2,1,0:T(8,128)(2,1)}, u32[]{:S(2)}, u32[]{:S(2)}) async-start(bf16[128,16,128]{2,1,0:T(8,128)(2,1)} %bitcast.13), calls=%async_computation.1 | async-start | bytes 1048576 | tf_op jit(solution)/shard_map/all_to_all | solution.py:25
  49.5 3.6 %collective-permute-start.2 = (bf16[32,32,128]{2,1,0:T(8,128)(2,1)S(1)}, bf16[32,32,128]{2,1,0:T(8,128)(2,1)S(1)}, u32[]{:S(2)}, u32[]{:S(2)}) collective-permute-start(bf16[32,32,128]{2,1,0:T(8,128)(2,1)S(1)} %all-to-all-done.refs_0_), channel_id=1, source_target_pairs={{0,32},{32,64},{64,96},{96,0},{1,33},{33,65},{65,97},{97,1},{2,34}... | collective-permute-start | bytes 786440 | tf_op jit(solution)/shard_map/ppermute | solution.py:35
  53.1 4.7 %collective-permute-start.3 = (bf16[32,32,128]{2,1,0:T(8,128)(2,1)S(1)}, bf16[32,32,128]{2,1,0:T(8,128)(2,1)S(1)}, u32[]{:S(2)}, u32[]{:S(2)}) collective-permute-start(bf16[32,32,128]{2,1,0:T(8,128)(2,1)S(1)} %all-to-all-done.refs_0_), channel_id=1, source_target_pairs={{0,64},{32,96},{64,0},{96,32},{1,65},{33,97},{65,1},{97,33},{2,66}... | collective-permute-start | bytes 786440 | tf_op jit(solution)/shard_map/ppermute | solution.py:35
  57.8 3.3 %collective-permute-start.4 = (bf16[32,32,128]{2,1,0:T(8,128)(2,1)S(1)}, bf16[32,32,128]{2,1,0:T(8,128)(2,1)S(1)}, u32[]{:S(2)}, u32[]{:S(2)}) collective-permute-start(bf16[32,32,128]{2,1,0:T(8,128)(2,1)S(1)} %all-to-all-done.refs_0_), channel_id=1, source_target_pairs={{0,96},{32,0},{64,32},{96,64},{1,97},{33,1},{65,33},{97,65},{2,98}... | collective-permute-start | bytes 786440 | tf_op jit(solution)/shard_map/ppermute | solution.py:35
  61.1 1.1 select_bitcast_fusion.1
  62.3 0.9 convolution_add_fusion.1
  63.2 2.5 %collective-permute-done.2.refs_1_ = bf16[32,32,128]{2,1,0:T(8,128)(2,1)S(1)} collective-permute-done((bf16[32,32,128]{2,1,0:T(8,128)(2,1)S(1)}, bf16[32,32,128]{2,1,0:T(8,128)(2,1)S(1)}, u32[]{:S(2)}, u32[]{:S(2)}) %collective-permute-start.2) | collective-permute-done | bytes 262176 | tf_op jit(solution)/shard_map/ppermute | solution.py:35
  65.7 6.5 %collective-permute-done.3.refs_2_ = bf16[32,32,128]{2,1,0:T(8,128)(2,1)S(1)} collective-permute-done((bf16[32,32,128]{2,1,0:T(8,128)(2,1)S(1)}, bf16[32,32,128]{2,1,0:T(8,128)(2,1)S(1)}, u32[]{:S(2)}, u32[]{:S(2)}) %collective-permute-start.3) | collective-permute-done | bytes 262176 | tf_op jit(solution)/shard_map/ppermute | solution.py:35
  72.3 4.0 %hub_sums.1 = f32[64,1024]{1,0:T(8,128)S(1)} custom-call(s32[1]{0:T(128)} %bitcast.8.x_ref, s32[128]{0:T(128)S(1)} %fusion.43.dest_ref, bf16[32,32,128]{2,1,0:T(8,128)(2,1)S(1)} %all-to-all-done.refs_0_, bf16[32,32,128]{2,1,0:T(8,128)(2,1)S(1)} %collective-permute-done.2.refs_1_, bf16[32,32,128]{2,1,0:T(8,128)(2,1)S(1)} %collective-permute-done.3.refs_2_, ...), custom_call_target="tpu_custom_call" | custom-call | flops 268435456 | bytes 8388608 | tf_op jit(solution)/shard_map/hub_sums/pallas_call | solution.py:86
  76.3 3.0 %fusion.1 = f32[64,1024]{1,0:T(8,128)S(1)} fusion(s32[2048]{0:T(1024)S(1)} %eq.50, bf16[2048,128]{1,0:T(8,128)(2,1)} %bitcast.14), kind=kOutput, calls=%fused_computation.3 | convolution fusion | flops 270532608 | bytes 794624 | tf_op jit(solution)/shard_map/dot_general | solution.py:21
  79.4 2.7 %fusion.23 = f32[64,1024]{1,0:T(8,128)S(1)} fusion(f32[64,1024]{1,0:T(8,128)S(1)} %fusion.1, s32[2048]{0:T(1024)S(1)} %eq.46, bf16[2048,128]{1,0:T(8,128)(2,1)} %bitcast.14, f32[1024]{0:T(1024)S(1)} %convert_element_type.96), kind=kOutput, calls=%fused_computation.28 | convolution fusion | flops 270663680 | bytes 1060864 | tf_op jit(solution)/shard_map/dot_general | solution.py:21
  82.1 7.5 %all_gather.6 = bf16[256,1024]{1,0:T(8,128)(2,1)S(1)} all-gather(bf16[64,1024]{1,0:T(8,128)(2,1)S(1)} %add_convert_fusion), channel_id=1, replica_groups=mesh['yh'=4,'x'=4,'z'=8,'yl'=2,'core'=2] {'yl','core'}, dimensions={0}, use_global_device_ids=true | all-gather | bytes 655360 | tf_op jit(solution)/shard_map/all_gather | solution.py:219
  89.7 1.1 convert_reduce_fusion.2
  90.7 7.5 %all_gather.7 = bf16[256,1024]{1,0:T(8,128)(2,1)S(1)} all-gather(bf16[64,1024]{1,0:T(8,128)(2,1)S(1)} %get-tuple-element.13), channel_id=1, replica_groups=mesh['yh'=4,'x'=4,'z'=8,'yl'=2,'core'=2] {'yl','core'}, dimensions={0}, use_global_device_ids=true | all-gather | bytes 655360 | tf_op jit(solution)/shard_map/all_gather | solution.py:225
  98.5 0.9 fusion.33
  99.7 2.1 %fusion.19 = bf16[2048,64]{0,1:T(8,128)(2,1)S(1)} fusion(s32[2048]{0:T(1024)S(1)} %eq.50, bf16[64,1024]{1,0:T(8,128)(2,1)S(1)} %convolution_convert_fusion.grad_ref, f32[1024]{0:T(1024)S(1)} %convert_element_type.96), kind=kOutput, calls=%fused_computation.24 | convolution fusion | flops 270860288 | bytes 405504 | tf_op jit(solution)/shard_map/dot_general | solution.py:21
  101.8 2.1 %fusion.18 = bf16[2048,64]{0,1:T(8,128)(2,1)S(1)} fusion(s32[2048]{0:T(1024)S(1)} %copy-done.10, bf16[64,1024]{1,0:T(8,128)(2,1)S(1)} %convolution_convert_fusion.grad_ref, f32[1024]{0:T(1024)S(1)} %convert_element_type.96), kind=kOutput, calls=%fused_computation.23 | convolution fusion | flops 270860288 | bytes 405504 | tf_op jit(solution)/shard_map/dot_general | solution.py:21
  104.7 0.8 fusion.53
  106.2 0.8 pad_maximum_fusion.3
  107.1 1.3 copy.26
  108.4 1.1 reduce-precision_convert_fusion
  109.5 1.2 pad_maximum_fusion.1
  110.7 15.3 %all-to-all-start.2 = ((bf16[128,24,128]{2,1,0:T(8,128)(2,1)}), bf16[128,24,128]{2,1,0:T(8,128)(2,1)}, u32[]{:S(2)}, u32[]{:S(2)}) async-start(bf16[128,24,128]{2,1,0:T(8,128)(2,1)} %pad_maximum_fusion.1), calls=%async_computation.2 | async-start | bytes 1572864 | tf_op jit(solution)/shard_map/all_to_all | solution.py:25
  126.0 5.1 %hub_grad_terms.1 = bf16[4,32,32,128]{3,2,1,0:T(8,128)(2,1)S(1)} custom-call(s32[1]{0:T(128)} %bitcast.8.x_ref, s32[128]{0:T(128)S(1)} %fusion.43.dest_ref, bf16[64,1024]{1,0:T(8,128)(2,1)S(1)} %convolution_convert_fusion.grad_ref, bf16[128,64,128]{2,1,0:T(8,128)(2,1)S(1)} %bitcast.76), custom_call_target="tpu_custom_call" | custom-call | flops 268435456 | bytes 8388608 | tf_op jit(solution)/shard_map/hub_grad_terms/pallas_call | solution.py:130
  131.2 4.7 %collective-permute-start.7 = (bf16[32,32,128]{2,1,0:T(8,128)(2,1)S(1)}, bf16[32,32,128]{2,1,0:T(8,128)(2,1)S(1)}, u32[]{:S(2)}, u32[]{:S(2)}) collective-permute-start(bf16[32,32,128]{2,1,0:T(8,128)(2,1)S(1)} %get-tuple-element.15), channel_id=1, source_target_pairs={{0,96},{32,0},{64,32},{96,64},{1,97},{33,1},{65,33},{97,65},{2,98}... | collective-permute-start | bytes 786440 | tf_op jit(solution)/shard_map/ppermute | solution.py:35
  136.0 2.7 %collective-permute-start.6 = (bf16[32,32,128]{2,1,0:T(8,128)(2,1)S(1)}, bf16[32,32,128]{2,1,0:T(8,128)(2,1)S(1)}, u32[]{:S(2)}, u32[]{:S(2)}) collective-permute-start(bf16[32,32,128]{2,1,0:T(8,128)(2,1)S(1)} %get-tuple-element.16), channel_id=1, source_target_pairs={{0,64},{32,96},{64,0},{96,32},{1,65},{33,97},{65,1},{97,33},{2,66}... | collective-permute-start | bytes 786440 | tf_op jit(solution)/shard_map/ppermute | solution.py:35
  138.7 2.8 %collective-permute-start.5 = (bf16[32,32,128]{2,1,0:T(8,128)(2,1)S(1)}, bf16[32,32,128]{2,1,0:T(8,128)(2,1)S(1)}, u32[]{:S(2)}, u32[]{:S(2)}) collective-permute-start(bf16[32,32,128]{2,1,0:T(8,128)(2,1)S(1)} %get-tuple-element.14), channel_id=1, source_target_pairs={{0,32},{32,64},{64,96},{96,0},{1,33},{33,65},{65,97},{97,1},{2,34}... | collective-permute-start | bytes 786440 | tf_op jit(solution)/shard_map/ppermute | solution.py:35
  141.5 9.5 %collective-permute-done.7 = bf16[32,32,128]{2,1,0:T(8,128)(2,1)S(1)} collective-permute-done((bf16[32,32,128]{2,1,0:T(8,128)(2,1)S(1)}, bf16[32,32,128]{2,1,0:T(8,128)(2,1)S(1)}, u32[]{:S(2)}, u32[]{:S(2)}) %collective-permute-start.7) | collective-permute-done | bytes 262176 | tf_op jit(solution)/shard_map/ppermute | solution.py:35
  151.4 4.5 %collective-permute-done.5 = bf16[32,32,128]{2,1,0:T(8,128)(2,1)S(1)} collective-permute-done((bf16[32,32,128]{2,1,0:T(8,128)(2,1)S(1)}, bf16[32,32,128]{2,1,0:T(8,128)(2,1)S(1)}, u32[]{:S(2)}, u32[]{:S(2)}) %collective-permute-start.5) | collective-permute-done | bytes 262176 | tf_op jit(solution)/shard_map/ppermute | solution.py:35
  156.0 1.1 convert_reduce_fusion.1
  157.9 11.1 %all-to-all-start.3 = ((bf16[32,40,128]{2,1,0:T(8,128)(2,1)}), bf16[32,40,128]{2,1,0:T(8,128)(2,1)S(1)}, u32[]{:S(2)}, u32[]{:S(2)}) async-start(bf16[32,40,128]{2,1,0:T(8,128)(2,1)} %pad_maximum_fusion.5), calls=%async_computation.3 | async-start | bytes 655360 | tf_op jit(solution)/shard_map/all_to_all | solution.py:25
  169.3 1.1 slice.159
  170.9 2.0 fusion.4
  172.9 11.4 %all-to-all-done.3 = bf16[32,40,128]{2,1,0:T(8,128)(2,1)S(1)} async-done(((bf16[32,40,128]{2,1,0:T(8,128)(2,1)}), bf16[32,40,128]{2,1,0:T(8,128)(2,1)S(1)}, u32[]{:S(2)}, u32[]{:S(2)}) %all-to-all-start.3) | async-done | bytes 327712 | tf_op jit(solution)/shard_map/all_to_all | solution.py:25
  184.4 1.9 collective-permute-start.10
  186.4 3.0 %collective-permute-start.9 = (f32[32,2,128]{2,1,0:T(2,128)S(1)}, f32[32,2,128]{2,1,0:T(2,128)S(1)}, u32[]{:S(2)}, u32[]{:S(2)}) collective-permute-start(f32[32,2,128]{2,1,0:T(2,128)S(1)} %slice_add_fusion), channel_id=1, source_target_pairs={{0,64},{32,96},{64,0},{96,32},{1,65},{33,97},{65,1},{97,33},{2,66}... | collective-permute-start | bytes 98312 | tf_op jit(solution)/shard_map/ppermute | solution.py:35
  189.3 3.3 %collective-permute-start.8 = (f32[32,2,128]{2,1,0:T(2,128)S(1)}, f32[32,2,128]{2,1,0:T(2,128)S(1)}, u32[]{:S(2)}, u32[]{:S(2)}) collective-permute-start(f32[32,2,128]{2,1,0:T(2,128)S(1)} %slice_add_fusion), channel_id=1, source_target_pairs={{0,32},{32,64},{64,96},{96,0},{1,33},{33,65},{65,97},{97,1},{2,34}... | collective-permute-start | bytes 98312 | tf_op jit(solution)/shard_map/ppermute | solution.py:35
  192.8 2.3 %fusion.25 = f32[64,1024]{1,0:T(8,128)} fusion(f32[64,1024]{1,0:T(8,128)S(1)} %fusion.38, f32[64,1024]{1,0:T(8,128)S(1)} %fusion.4, s32[2048]{0:T(1024)S(1)} %eq.38, bf16[2048,128]{1,0:T(8,128)(2,1)S(1)} %bitcast.82, f32[32,64]{1,0:T(8,128)S(1)} %get-tuple-element.39, f32[32,64]{1,0:T(8,128)S(1)} %get-tuple-element.38), kind=kOutput, calls=%fused_computation.32 | convolution fusion | flops 270991360 | bytes 1335296 | tf_op jit(solution)/shard_map/dot_general | solution.py:21
  195.1 1.6 collective-permute-done.8
  (97 shorter events, 10.6 us)
Async XLA Ops:
  1.6 27.3 %collective-permute-start = (bf16[64,1536]{1,0:T(8,128)(2,1)S(1)}, bf16[64,1536]{1,0:T(8,128)(2,1)S(1)}, u32[]{:S(2)}, u32[]{:S(2)}) collective-permute-start(bf16[64,1536]{1,0:T(8,128)(2,1)S(1)} %pad_maximum_fusion.7), channel_id=1, source_target_pairs={{0,2},{2,0},{1,3},{3,1},{4,6},{6,4},{5,7},{7,5},{8,10},{10,8},{9,1... | collective-permute-start | bytes 589832 | tf_op jit(solution)/shard_map/ppermute | solution.py:35
  6.6 26.6 %all-to-all-start = ((bf16[32,32,128]{2,1,0:T(8,128)(2,1)}), bf16[32,32,128]{2,1,0:T(8,128)(2,1)S(1)}, u32[]{:S(2)}, u32[]{:S(2)}) async-start(bf16[32,32,128]{2,1,0:T(8,128)(2,1)} %broadcast_in_dim.47), calls=%async_computation | async-start | bytes 524288 | tf_op jit(solution)/shard_map/all_to_all | solution.py:25
  22.7 4.1 %copy-start.3 = (bf16[64,1024]{1,0:T(8,128)(2,1)S(1)}, bf16[64,1024]{1,0:T(8,128)(2,1)}, u32[]{:S(2)}) copy-start(bf16[64,1024]{1,0:T(8,128)(2,1)} %param.12) | copy-start | bytes 393220
  23.7 3.0 %copy-start.7 = (s32[2048]{0:T(1024)}, s32[2048]{0:T(1024)S(1)}, u32[]{:S(2)}) copy-start(s32[2048]{0:T(1024)S(1)} %eq.42) | copy-start | bytes 24580
  26.6 2.3 %copy-start.4 = (bf16[256,64]{0,1:T(8,128)(2,1)S(1)}, bf16[256,64]{0,1:T(8,128)(2,1)}, u32[]{:S(2)}) copy-start(bf16[256,64]{0,1:T(8,128)(2,1)} %param.20) | copy-start | bytes 98308
  26.6 2.3 %copy-start.6 = (bf16[256,64]{0,1:T(8,128)(2,1)S(1)}, bf16[256,64]{0,1:T(8,128)(2,1)}, u32[]{:S(2)}) copy-start(bf16[256,64]{0,1:T(8,128)(2,1)} %param.21) | copy-start | bytes 98308
  28.9 4.1 %copy-start.11 = (s32[1024]{0:T(1024)S(1)}, s32[1024]{0:T(1024)}, u32[]{:S(2)}) copy-start(s32[1024]{0:T(1024)} %param.19) | copy-start | bytes 12292
  28.9 4.1 %copy-start.14 = (s32[1,128]{1,0:T(1,128)S(1)}, s32[1,128]{1,0:T(1,128)}, u32[]{:S(2)}) copy-start(s32[1,128]{1,0:T(1,128)} %param.14) | copy-start | bytes 1540
  28.9 4.1 %copy-start.15 = (s32[1,128]{1,0:T(1,128)S(1)}, s32[1,128]{1,0:T(1,128)}, u32[]{:S(2)}) copy-start(s32[1,128]{1,0:T(1,128)} %param.15) | copy-start | bytes 1540
  29.8 31.3 %collective-permute-start.1 = (bf16[2,64,1536]{2,1,0:T(8,128)(2,1)}, bf16[2,64,1536]{2,1,0:T(8,128)(2,1)}, u32[]{:S(2)}, u32[]{:S(2)}) collective-permute-start(bf16[2,64,1536]{2,1,0:T(8,128)(2,1)} %pad_maximum_fusion.4), channel_id=1, source_target_pairs={{0,1},{1,0},{2,3},{3,2},{4,5},{5,4},{6,7},{7,6},{8,9},{9,8},{10,11... | collective-permute-start | bytes 1179656 | tf_op jit(solution)/shard_map/ppermute | solution.py:35
  33.0 46.4 %copy-start.9 = (s32[2048]{0:T(1024)}, s32[2048]{0:T(1024)S(1)}, u32[]{:S(2)}) copy-start(s32[2048]{0:T(1024)S(1)} %eq.46) | copy-start | bytes 24580
  33.2 43.1 %all-to-all-start.1 = ((bf16[128,16,128]{2,1,0:T(8,128)(2,1)}), bf16[128,16,128]{2,1,0:T(8,128)(2,1)}, u32[]{:S(2)}, u32[]{:S(2)}) async-start(bf16[128,16,128]{2,1,0:T(8,128)(2,1)} %bitcast.13), calls=%async_computation.1 | async-start | bytes 1048576 | tf_op jit(solution)/shard_map/all_to_all | solution.py:25
  49.5 12.8 %copy-start.12 = (f32[64]{0:T(128)S(1)}, f32[64]{0:T(128)}, u32[]{:S(2)}) copy-start(f32[64]{0:T(128)} %param.22) | copy-start | bytes 772
  49.5 22.8 %copy-start = (bf16[1,128,64,128]{3,2,1,0:T(8,128)(2,1)S(1)}, bf16[1,128,64,128]{3,2,1,0:T(8,128)(2,1)}, u32[]{:S(2)}) copy-start(bf16[1,128,64,128]{3,2,1,0:T(8,128)(2,1)} %param.13) | copy-start | bytes 6291460
  49.5 16.2 %collective-permute-start.2 = (bf16[32,32,128]{2,1,0:T(8,128)(2,1)S(1)}, bf16[32,32,128]{2,1,0:T(8,128)(2,1)S(1)}, u32[]{:S(2)}, u32[]{:S(2)}) collective-permute-start(bf16[32,32,128]{2,1,0:T(8,128)(2,1)S(1)} %all-to-all-done.refs_0_), channel_id=1, source_target_pairs={{0,32},{32,64},{64,96},{96,0},{1,33},{33,65},{65,97},{97,1},{2,34}... | collective-permute-start | bytes 786440 | tf_op jit(solution)/shard_map/ppermute | solution.py:35
  53.1 19.2 %collective-permute-start.3 = (bf16[32,32,128]{2,1,0:T(8,128)(2,1)S(1)}, bf16[32,32,128]{2,1,0:T(8,128)(2,1)S(1)}, u32[]{:S(2)}, u32[]{:S(2)}) collective-permute-start(bf16[32,32,128]{2,1,0:T(8,128)(2,1)S(1)} %all-to-all-done.refs_0_), channel_id=1, source_target_pairs={{0,64},{32,96},{64,0},{96,32},{1,65},{33,97},{65,1},{97,33},{2,66}... | collective-permute-start | bytes 786440 | tf_op jit(solution)/shard_map/ppermute | solution.py:35
  57.8 14.5 %collective-permute-start.4 = (bf16[32,32,128]{2,1,0:T(8,128)(2,1)S(1)}, bf16[32,32,128]{2,1,0:T(8,128)(2,1)S(1)}, u32[]{:S(2)}, u32[]{:S(2)}) collective-permute-start(bf16[32,32,128]{2,1,0:T(8,128)(2,1)S(1)} %all-to-all-done.refs_0_), channel_id=1, source_target_pairs={{0,96},{32,0},{64,32},{96,64},{1,97},{33,1},{65,33},{97,65},{2,98}... | collective-permute-start | bytes 786440 | tf_op jit(solution)/shard_map/ppermute | solution.py:35
  62.2 10.0 %copy-start.1 = (bf16[2,2,64,1536]{3,2,1,0:T(8,128)(2,1)}, bf16[2,2,64,1536]{3,2,1,0:T(8,128)(2,1)S(1)}, u32[]{:S(2)}) copy-start(bf16[2,2,64,1536]{3,2,1,0:T(8,128)(2,1)S(1)} %pad_maximum_fusion) | copy-start | bytes 2359300
  79.4 10.3 %copy-start.5 = (f32[1024,64]{0,1:T(8,128)S(1)}, f32[1024,64]{0,1:T(8,128)}, u32[]{:S(2)}) copy-start(f32[1024,64]{0,1:T(8,128)} %convolution_add_fusion.1) | copy-start | bytes 786436
  79.4 10.3 %copy-start.13 = (bf16[64,1024]{1,0:T(8,128)(2,1)S(1)}, bf16[64,1024]{1,0:T(8,128)(2,1)}, u32[]{:S(2)}) copy-start(bf16[64,1024]{1,0:T(8,128)(2,1)} %param.23) | copy-start | bytes 393220
  82.1 16.4 %copy-start.2 = (bf16[2,2,64,1536]{3,2,1,0:T(8,128)(2,1)S(1)}, bf16[2,2,64,1536]{3,2,1,0:T(8,128)(2,1)}, u32[]{:S(2)}) copy-start(bf16[2,2,64,1536]{3,2,1,0:T(8,128)(2,1)} %copy-done.1) | copy-start | bytes 2359300
  99.7 2.1 %copy-start.10 = (s32[2048]{0:T(1024)S(1)}, s32[2048]{0:T(1024)}, u32[]{:S(2)}) copy-start(s32[2048]{0:T(1024)} %copy-done.9) | copy-start | bytes 24580
  110.7 45.3 %all-to-all-start.2 = ((bf16[128,24,128]{2,1,0:T(8,128)(2,1)}), bf16[128,24,128]{2,1,0:T(8,128)(2,1)}, u32[]{:S(2)}, u32[]{:S(2)}) async-start(bf16[128,24,128]{2,1,0:T(8,128)(2,1)} %pad_maximum_fusion.1), calls=%async_computation.2 | async-start | bytes 1572864 | tf_op jit(solution)/shard_map/all_to_all | solution.py:25
  131.2 19.8 %collective-permute-start.7 = (bf16[32,32,128]{2,1,0:T(8,128)(2,1)S(1)}, bf16[32,32,128]{2,1,0:T(8,128)(2,1)S(1)}, u32[]{:S(2)}, u32[]{:S(2)}) collective-permute-start(bf16[32,32,128]{2,1,0:T(8,128)(2,1)S(1)} %get-tuple-element.15), channel_id=1, source_target_pairs={{0,96},{32,0},{64,32},{96,64},{1,97},{33,1},{65,33},{97,65},{2,98}... | collective-permute-start | bytes 786440 | tf_op jit(solution)/shard_map/ppermute | solution.py:35
  136.0 15.4 %collective-permute-start.6 = (bf16[32,32,128]{2,1,0:T(8,128)(2,1)S(1)}, bf16[32,32,128]{2,1,0:T(8,128)(2,1)S(1)}, u32[]{:S(2)}, u32[]{:S(2)}) collective-permute-start(bf16[32,32,128]{2,1,0:T(8,128)(2,1)S(1)} %get-tuple-element.16), channel_id=1, source_target_pairs={{0,64},{32,96},{64,0},{96,32},{1,65},{33,97},{65,1},{97,33},{2,66}... | collective-permute-start | bytes 786440 | tf_op jit(solution)/shard_map/ppermute | solution.py:35
  138.7 17.2 %collective-permute-start.5 = (bf16[32,32,128]{2,1,0:T(8,128)(2,1)S(1)}, bf16[32,32,128]{2,1,0:T(8,128)(2,1)S(1)}, u32[]{:S(2)}, u32[]{:S(2)}) collective-permute-start(bf16[32,32,128]{2,1,0:T(8,128)(2,1)S(1)} %get-tuple-element.14), channel_id=1, source_target_pairs={{0,32},{32,64},{64,96},{96,0},{1,33},{33,65},{65,97},{97,1},{2,34}... | collective-permute-start | bytes 786440 | tf_op jit(solution)/shard_map/ppermute | solution.py:35
  156.0 15.0 %copy-start.8 = (s32[2048]{0:T(1024)S(1)}, s32[2048]{0:T(1024)}, u32[]{:S(2)}) copy-start(s32[2048]{0:T(1024)} %copy-done.7) | copy-start | bytes 24580
  157.9 26.5 %all-to-all-start.3 = ((bf16[32,40,128]{2,1,0:T(8,128)(2,1)}), bf16[32,40,128]{2,1,0:T(8,128)(2,1)S(1)}, u32[]{:S(2)}, u32[]{:S(2)}) async-start(bf16[32,40,128]{2,1,0:T(8,128)(2,1)} %pad_maximum_fusion.5), calls=%async_computation.3 | async-start | bytes 655360 | tf_op jit(solution)/shard_map/all_to_all | solution.py:25
  184.4 10.7 %collective-permute-start.10 = (f32[32,2,128]{2,1,0:T(2,128)S(1)}, f32[32,2,128]{2,1,0:T(2,128)S(1)}, u32[]{:S(2)}, u32[]{:S(2)}) collective-permute-start(f32[32,2,128]{2,1,0:T(2,128)S(1)} %slice_add_fusion), channel_id=1, source_target_pairs={{0,96},{32,0},{64,32},{96,64},{1,97},{33,1},{65,33},{97,65},{2,98}... | collective-permute-start | bytes 98312 | tf_op jit(solution)/shard_map/ppermute | solution.py:35
  186.4 8.8 %collective-permute-start.9 = (f32[32,2,128]{2,1,0:T(2,128)S(1)}, f32[32,2,128]{2,1,0:T(2,128)S(1)}, u32[]{:S(2)}, u32[]{:S(2)}) collective-permute-start(f32[32,2,128]{2,1,0:T(2,128)S(1)} %slice_add_fusion), channel_id=1, source_target_pairs={{0,64},{32,96},{64,0},{96,32},{1,65},{33,97},{65,1},{97,33},{2,66}... | collective-permute-start | bytes 98312 | tf_op jit(solution)/shard_map/ppermute | solution.py:35
  189.3 7.4 %collective-permute-start.8 = (f32[32,2,128]{2,1,0:T(2,128)S(1)}, f32[32,2,128]{2,1,0:T(2,128)S(1)}, u32[]{:S(2)}, u32[]{:S(2)}) collective-permute-start(f32[32,2,128]{2,1,0:T(2,128)S(1)} %slice_add_fusion), channel_id=1, source_target_pairs={{0,32},{32,64},{64,96},{96,0},{1,33},{33,65},{65,97},{97,1},{2,34}... | collective-permute-start | bytes 98312 | tf_op jit(solution)/shard_map/ppermute | solution.py:35

commit v3 on v2

v3 whole, which is shorter than its diff:
```python
from functools import partial

import jax
import jax.numpy as jnp
from jax import lax
from jax.experimental import pallas as pl
from jax.experimental.pallas import tpu as pltpu
from jax.sharding import Mesh
from jax.sharding import PartitionSpec as P

BF = jnp.bfloat16
F32 = jnp.float32
BOTH_ROWS = (((0,), (0,)), ((), ()))
BOTH_COLS = (((1,), (1,)), ((), ()))
DOM = ("yh", "x", "z")
PLANE = ("yh", "z")
REP = ("yl", "core")
SMEM = pl.BlockSpec(memory_space=pltpu.SMEM)
VMEM = pl.BlockSpec(memory_space=pltpu.VMEM)
MIB = 1024 * 1024


def mm(a, b, dims):
    return lax.dot_general(a, b, dims, preferred_element_type=F32)


def swap(pieces, axis):
    return lax.all_to_all(pieces, axis, split_axis=0, concat_axis=0, tiled=True)


def shift(values, axis, step):
    size = lax.axis_size(axis)
    return lax.ppermute(values, axis, [(i, (i + step) % size) for i in range(size)])


def gather_rep(values):
    first = lax.axis_index("yl") == 0
    other = shift(values, "yl", 1)
    mine = jnp.stack([jnp.where(first, values, other), jnp.where(first, other, values)])
    theirs = shift(mine, "core", 1)
    first = lax.axis_index("core") == 0
    both = jnp.stack([jnp.where(first, mine, theirs), jnp.where(first, theirs, mine)], axis=1)
    return both.reshape(-1, values.shape[1])


def call(kernel, out_shape, in_specs, scratch, name, flops, mib):
    outs = VMEM if isinstance(out_shape, jax.ShapeDtypeStruct) else [VMEM] * len(out_shape)
    return pl.pallas_call(
        kernel,
        out_shape=out_shape,
        in_specs=in_specs,
        out_specs=outs,
        scratch_shapes=scratch,
        compiler_params=pltpu.CompilerParams(vmem_limit_bytes=32 * MIB),
        cost_estimate=pl.CostEstimate(flops=flops, bytes_accessed=mib * MIB, transcendentals=0),
        name=name,
    )


def high_low(values, axis):
    high = lax.reduce_precision(values, 8, 7)
    return jnp.concatenate([high.astype(BF), (values - high).astype(BF)], axis=axis)


def slot_rows(index):
    parts, slots = index.shape
    return index.reshape(parts, 2, slots // 2).transpose(1, 0, 2).reshape(2, -1)


def pick_slots(index_ref, source, out_ref):
    width, nodes = source.shape
    low_size = 256
    high_size = nodes // low_size
    split = jnp.concatenate(
        [source[:, i * low_size : (i + 1) * low_size] for i in range(high_size)], axis=0
    )
    step = 256
    rows = out_ref.shape[1]
    low_ids = lax.broadcasted_iota(jnp.int32, (low_size, step), 0)
    for start in range(0, index_ref.shape[1], step):
        halves = []
        for h in range(2):
            index = index_ref[h : h + 1, start : start + step]
            hits = jnp.where(low_ids == (index & (low_size - 1)), 1.0, 0.0).astype(BF)
            found = jnp.dot(split, hits, preferred_element_type=F32)
            high = jnp.broadcast_to(index >> 8, (width, step))
            kept = jnp.zeros((width, step), F32)
            for i in range(high_size):
                kept = jnp.where(high == i, found[i * width : (i + 1) * width], kept)
            halves.append(kept)
        block = jnp.concatenate(halves, axis=0).T
        first = start // rows
        out_ref[first : first + step // rows] = block.reshape(step // rows, rows, 128).astype(BF)


def gather_kernel(index_ref, source_ref, out_ref):
    pick_slots(index_ref, source_ref[...], out_ref)


def gather_slots(index, source, parts, slots):
    return call(
        gather_kernel,
        jax.ShapeDtypeStruct((parts, slots // 2, 128), BF),
        [VMEM, VMEM],
        [],
        "tail_rows_out",
        2 * parts * slots * 256 * 256,
        2,
    )(index, source)


def back_kernel(index_ref, weight_ref, d_ref, degree_ref, grad_ref, out_ref):
    grad = jnp.dot(weight_ref[...], d_ref[...], preferred_element_type=F32).astype(BF)
    grad_ref[...] = grad
    scaled = (grad.astype(F32) / degree_ref[...].astype(F32)).astype(BF)
    pick_slots(index_ref, scaled, out_ref)


def back_gather(index, weight, d_full, degree, parts, slots):
    width, nodes = weight.shape[0], d_full.shape[1]
    return call(
        back_kernel,
        [
            jax.ShapeDtypeStruct((width, nodes), BF),
            jax.ShapeDtypeStruct((parts, slots // 2, 128), BF),
        ],
        [VMEM] * 4,
        [],
        "mixed_grad_rows_out",
        2 * parts * slots * 256 * 256,
        2,
    )(index, weight, d_full, degree)


def sum_slots(index_ref, arrived_ref, rows, start, size):
    parts = arrived_ref.shape[0]
    flat = arrived_ref[:, :rows, :].reshape(parts * rows, 128)
    ids = lax.broadcasted_iota(jnp.int32, (size, parts * rows), 0) + start
    sums = []
    for h in range(2):
        hits = jnp.where(ids == index_ref[h : h + 1, :], 1.0, 0.0).astype(BF)
        sums.append(jnp.dot(hits, flat, preferred_element_type=F32))
    return sums[0].T[:64] + sums[1].T[64:]


def mixed_kernel(rows, index_ref, arrived_ref, hub_ref, degree_ref, out_ref):
    size = 256
    for start in range(0, out_ref.shape[1], size):
        at = slice(start, start + size)
        tail = sum_slots(index_ref, arrived_ref, rows, start, size)
        out_ref[:, at] = (hub_ref[:, at] + tail / degree_ref[:, at].astype(F32)).astype(BF)


def mixed_sums(index, arrived, hub_sum, degree):
    parts, rows, _ = arrived.shape
    width, nodes = hub_sum.shape
    return call(
        partial(mixed_kernel, rows),
        jax.ShapeDtypeStruct((width, nodes), BF),
        [VMEM] * 4,
        [],
        "mixed",
        4 * parts * rows * nodes * 128,
        2,
    )(index, arrived, hub_sum, degree)


def tail_grad_kernel(rows, index_ref, arrived_ref, direct_ref, out_ref):
    size = 256
    for start in range(0, out_ref.shape[1], size):
        at = slice(start, start + size)
        tail = sum_slots(index_ref, arrived_ref, rows, start, size)
        out_ref[:, at] = direct_ref[:, at] + tail


def tail_grads(index, arrived, direct, rows):
    parts = arrived.shape[0]
    width, nodes = direct.shape
    return call(
        partial(tail_grad_kernel, rows),
        jax.ShapeDtypeStruct((width, nodes), F32),
        [VMEM] * 3,
        [],
        "tail_grads",
        4 * parts * rows * nodes * 128,
        2,
    )(index, arrived, direct)


def weight_kernel(feat_ref, mixed_ref, d_ref, out_ref):
    d_pre = d_ref[...]
    full = feat_ref.shape[0]
    half = full // 2
    grads = []
    for ref in (feat_ref, mixed_ref):
        grad = mm(ref[...], d_pre, BOTH_COLS)
        grads.append(jnp.concatenate([grad[:half], grad[half:]], axis=1))
    grads = jnp.concatenate(grads, axis=0)
    ones = jnp.ones((8, d_pre.shape[1]), BF)
    bias = mm(ones, d_pre, BOTH_COLS)
    bias = jnp.concatenate([bias, bias], axis=1)
    high = grads.astype(BF).astype(F32)
    low = (grads - high).reshape(-1, 8, 128)
    high = high.reshape(-1, 8, 128)
    bias_high = bias.astype(BF).astype(F32)
    place = lax.broadcasted_iota(jnp.int32, low.shape, 1)
    rest = jnp.where(place == 4, bias_high[None], (bias - bias_high)[None])
    made = []
    for j in range(4):
        up = high if j == 0 else pltpu.roll(high, 8 - 2 * j, 1)
        down = low if j == 1 else pltpu.roll(low, (10 - 2 * j) % 8, 1)
        made.append(jnp.where(place < 2, up, jnp.where(place < 4, down, rest)))
    out_ref[:, 0] = jnp.concatenate(made[:2], axis=1).astype(BF)
    out_ref[:, 1] = jnp.concatenate(made[2:], axis=1).astype(BF)


def weight_rows(full_feat, full_mixed, d_pre, parts):
    full = full_feat.shape[0]
    made = call(
        weight_kernel,
        jax.ShapeDtypeStruct((full // 8, 2, 16, 128), BF),
        [VMEM] * 3,
        [],
        "weight_grad_rows",
        4 * full_feat.size * d_pre.shape[0],
        2,
    )(full_feat, full_mixed, d_pre)
    return made.reshape(full // 2, 8, 128)


def tile_index(x_ref, k, sizes, yh, z, sign):
    x_size, z_size = sizes
    x = lax.rem(x_ref[0] + (sign * k) % x_size, x_size)
    return (yh * x_size + x) * z_size + z


def fold_kernel(steps, sizes, has_base, x_ref, dest_ref, *refs):
    hub_refs, (tile_ref, *base_ref, out_ref, total) = refs[: len(steps)], refs[len(steps) :]
    blocks = total.shape[0] - 1
    half = hub_refs[0].shape[1]
    lanes = lax.broadcasted_iota(jnp.int32, (half, 128), 1)
    first = (lanes < 64).astype(F32).astype(BF)
    second = (lanes >= 64).astype(F32).astype(BF)
    for b in range(blocks):
        at = slice(b * 128, (b + 1) * 128)
        total[b] = base_ref[0][:, at] if has_base else jnp.zeros_like(total[b])
    total[blocks] = jnp.zeros_like(total[blocks])
    z_size = sizes[1]
    for k, hub_ref in zip(steps, hub_refs):

        @pl.loop(0, hub_ref.shape[0] // z_size)
        def _(yh):
            for z in range(z_size):
                tile = tile_index(x_ref, k, sizes, yh, z, -1)
                rows = hub_ref[yh * z_size + z]
                weights = tile_ref[tile]
                product = jnp.dot(
                    jnp.concatenate([rows * first, rows * second], axis=0),
                    jnp.concatenate([weights, weights], axis=0),
                    preferred_element_type=F32,
                )
                dest = dest_ref[tile]
                total[dest] = total[dest] + product

    for b in range(blocks):
        out_ref[:, b * 128 : (b + 1) * 128] = total[b]


def fold_hubs(x_index, dest, hubs, steps, tiles, sizes, blocks, base):
    width = 2 * hubs[0].shape[1]
    bases = [] if base is None else [base]
    return call(
        partial(fold_kernel, steps, sizes, base is not None),
        jax.ShapeDtypeStruct((width, blocks * 128), F32),
        [SMEM, SMEM] + [VMEM] * (len(hubs) + 1 + len(bases)),
        [pltpu.VMEM((blocks + 1, width, 128), F32)],
        "hub_sums",
        tiles.size * width * len(hubs),
        4,
    )(x_index, dest, *hubs, tiles, *bases)


def hub_grad_kernel(k, sizes, x_ref, dest_ref, grad_ref, tile_ref, out_ref, blocked):
    blocks = blocked.shape[0] - 1
    for b in range(blocks):
        blocked[b] = grad_ref[:, b * 128 : (b + 1) * 128]
    blocked[blocks] = jnp.zeros_like(blocked[blocks])
    half = out_ref.shape[1]
    first = lax.broadcasted_iota(jnp.int32, (half, 128), 1) < 64
    z_size = sizes[1]

    @pl.loop(0, out_ref.shape[0] // z_size)
    def _(yh):
        for z in range(z_size):
            tile = tile_index(x_ref, k, sizes, yh, z, 1)
            weights = tile_ref[tile]
            product = mm(
                blocked[dest_ref[tile]],
                jnp.concatenate([weights, weights], axis=0),
                BOTH_COLS,
            )
            out_ref[yh * z_size + z] = jnp.where(first, product[:half], product[half:]).astype(BF)


def hub_grad_terms(x_index, dest, grad, tiles, k, sizes, blocks):
    width = grad.shape[0]
    return call(
        partial(hub_grad_kernel, k, sizes),
        jax.ShapeDtypeStruct((tiles.shape[0] // sizes[0], width // 2, 128), BF),
        [SMEM, SMEM, VMEM, VMEM],
        [pltpu.VMEM((blocks + 1, width, 128), BF)],
        "hub_grad_terms",
        tiles.size * width,
        4,
    )(x_index, dest, grad, tiles)


def local(
    features,
    hub_weight,
    hub_block,
    hub_mask,
    tail_rows,
    tail_count,
    tail_target,
    degree,
    w_self,
    w_neigh,
    out_bias,
    cotangent,
):
    width, nodes = features.shape
    tiles = hub_weight[0]
    parts, hubs, tile_len = tiles.shape
    slots = tail_rows.shape[2]
    half_width = width // 2
    blocks = nodes // tile_len
    full_width = w_self.shape[0]
    half_full = full_width // 2
    x_size, z_size = lax.axis_size("x"), lax.axis_size("z")
    sizes = (x_size, z_size)
    plane = parts // x_size
    x_index = lax.axis_index("x")[None]
    hub_dest = jnp.where(hub_mask[0] > 0, hub_block[0], blocks)
    degree = degree[None, :]

    hub_piece = jnp.concatenate([features[:half_width, :hubs], features[half_width:, :hubs]], axis=1)
    hub_plane = swap(jnp.broadcast_to(hub_piece[None], (plane, half_width, 128)), PLANE)

    slot_live = jnp.arange(slots, dtype=jnp.int32)[None, :] < tail_count[0][:, None]
    send_index = slot_rows(jnp.where(slot_live, tail_rows[0], -1))
    recv_index = slot_rows(tail_target[0])
    arrived = swap(gather_slots(send_index, features, parts, slots), DOM)

    own = jnp.concatenate([features, w_self.T, w_neigh.T], axis=1)
    hub_plane, own = lax.optimization_barrier((hub_plane, own))
    hub_all = [hub_plane] + [shift(hub_plane, "x", k) for k in range(1, x_size)]
    early = gather_rep(own)
    full_feat = early[:, :nodes]
    own_rows = lax.axis_index(REP) * width
    w_self_rows = lax.dynamic_slice_in_dim(early[:, nodes : nodes + full_width], own_rows, width, 1)
    w_neigh_rows = lax.dynamic_slice_in_dim(early[:, nodes + full_width :], own_rows, width, 1)
    pre_self = mm(w_self, full_feat, BOTH_ROWS) + out_bias[:, None]

    hub_sum = fold_hubs(x_index, hub_dest, hub_all[:2], (0, 1), tiles, sizes, blocks, None)
    hub_sum = fold_hubs(x_index, hub_dest, hub_all[2:], (2, 3), tiles, sizes, blocks, hub_sum)
    mixed = mixed_sums(recv_index, arrived, hub_sum, degree)

    full_mixed = lax.all_gather(mixed, REP, axis=0, tiled=True)
    pre = pre_self + mm(w_neigh, full_mixed, BOTH_ROWS)
    sigma = jax.nn.sigmoid(pre)
    output = (pre * sigma).astype(BF)
    d_pre = (cotangent.astype(F32) * (sigma * (1.0 + pre * (1.0 - sigma)))).astype(BF)

    full_d = lax.all_gather(d_pre, REP, axis=0, tiled=True)
    grad_rows = weight_rows(full_feat, full_mixed, d_pre, parts)
    mixed_grad, tail_send = back_gather(recv_index, w_neigh_rows.T, full_d, degree, parts, slots)
    tail_len = tail_send.shape[1]
    first = swap(jnp.concatenate([tail_send, grad_rows], axis=1), DOM)
    direct = mm(w_self_rows, full_d, BOTH_ROWS)

    hub_terms = [
        hub_grad_terms(x_index, hub_dest, mixed_grad, tiles, k, sizes, blocks)
        for k in range(x_size)
    ]
    hub_x = hub_terms[0].astype(F32)
    for k in range(1, x_size):
        hub_x = hub_x + shift(hub_terms[k], "x", k).astype(F32)

    sums = jnp.sum(first[:, tail_len:].astype(F32), axis=0)
    grad_bias = (sums[4] + sums[5])[:width]
    sums = sums[:2] + sums[2:4]
    far_sums = jnp.stack([sums] + [shift(sums, "x", k) for k in range(1, x_size)])
    order = lax.rem(x_index[0] + x_size - jnp.arange(x_size, dtype=jnp.int32), x_size)
    x_sums = jnp.take(far_sums, order, axis=0).reshape(2 * x_size, 128)
    sum_rows = jnp.broadcast_to(high_low(x_sums, 0)[None], (plane, 4 * x_size, 128))
    second = swap(jnp.concatenate([hub_x.astype(BF), sum_rows], axis=1), PLANE)

    tail_grad = tail_grads(send_index, first, direct, tail_len)
    all_sums = second[:, half_width:].astype(F32)
    all_sums = all_sums[:, : 2 * x_size] + all_sums[:, 2 * x_size :]
    all_sums = all_sums.reshape(-1, z_size, x_size, 2, 128).transpose(0, 2, 1, 3, 4)
    all_sums = all_sums.reshape(full_width, 128)
    grad_w_self, grad_w_neigh = [
        jnp.concatenate([rows[:, :width], rows[:, width:]], axis=0)
        for rows in (all_sums[:half_full], all_sums[half_full:])
    ]
    hub_back = jnp.sum(second[:, :half_width].astype(F32), axis=0)
    hub_grad = jnp.concatenate([hub_back[:, :hubs], hub_back[:, hubs:]], axis=0)
    grad_features = tail_grad.at[:, :hubs].add(hub_grad)
    return (output, grad_features, grad_w_self, grad_w_neigh, grad_bias)


def solution(mesh):
    grid = (4, 4, mesh.shape["dom"] // 16, 2, 2)
    parted = Mesh(mesh.devices.reshape(grid), DOM + REP)
    in_specs = (
        P(REP, DOM),
        P(DOM, None, None, None),
        P(DOM, None),
        P(DOM, None),
        P(DOM, None, None),
        P(DOM, None),
        P(DOM, None, None),
        P(DOM),
        P(None, REP),
        P(None, REP),
        P(REP),
        P(REP, DOM),
    )
    out_specs = (P(REP, DOM), P(REP, DOM), P(None, REP), P(None, REP), P(REP))
    return jax.shard_map(local, mesh=parted, in_specs=in_specs, out_specs=out_specs, check_vma=False)
```

time: 200 us -> 188 us (0.940)
  the two profiles are of different devices: /device:TPU:16 before, /device:TPU:8 now
where the time goes in v3:
time: 188 us; the launch traced here: 186 us
  starting transfers between devices  89.2 us (47%)
  waiting for transfers between devices  34.5 us (18%)
  Pallas kernels  23 us (12%)
  blocking collectives  13.8 us (7%)
  local copies, waits for them, and re-layouts  12.2 us (6%)
  other arithmetic  11 us (6%)
    all_to_all x4, starting transfers between devices, swap(): return lax.all_to_all(pieces, axis, split_axis=0, concat_axis=0, tiled=True)  50.9 us
    ppermute x11, starting transfers between devices, shift(): lax.ppermute(values, axis, [(i, (i + step) % size) for i in range(size)])  38.3 us
    all_to_all x4, waiting for transfers between devices, swap(): return lax.all_to_all(pieces, axis, split_axis=0, concat_axis=0, tiled=True)  23.5 us
    ppermute x11, waiting for transfers between devices, shift(): lax.ppermute(values, axis, [(i, (i + step) % size) for i in range(size)])  11.1 us
    pallas_call x4, Pallas kernels, hub_grad_terms(): call(partial(hub_grad_kernel, k, sizes), jax.ShapeDtypeStruct((tiles.shap...  8.89 us
    all_gather x1, blocking collectives, local(): full_d = lax.all_gather(d_pre, REP, axis=0, tiled=True)  7.28 us
    all_gather x1, blocking collectives, local(): full_mixed = lax.all_gather(mixed, REP, axis=0, tiled=True)  6.51 us
    pallas_call x2, Pallas kernels, fold_hubs(): call(partial(fold_kernel, steps, sizes, base is not None), jax.ShapeDtype...  5.03 us
  transfers between devices with their start and end apart: 15, of which 7 were waited for; matrix products, arithmetic and copies ran while one was open for 5% of the time, Pallas kernels for 11%

profile of v3, /device:TPU:8, one launch (start us, length us, event | category | flops | bytes accessed | tf_op | source)
XLA Modules:
  0.0 186.4 jit_solution(15605411187541249613)
XLA Ops:
  0.6 0.8 fusion.12
  2.2 15.1 %all-to-all-start = ((bf16[32,32,128]{2,1,0:T(8,128)(2,1)}), bf16[32,32,128]{2,1,0:T(8,128)(2,1)S(1)}, u32[]{:S(2)}, u32[]{:S(2)}) async-start(bf16[32,32,128]{2,1,0:T(8,128)(2,1)} %broadcast_in_dim.42), calls=%async_computation | async-start | bytes 524288 | tf_op jit(solution)/shard_map/all_to_all | solution.py:28
  17.3 0.8 copy.25
  18.1 1.6 pad_maximum_fusion.4
  19.8 11.5 %all-to-all-done.refs_0_ = bf16[32,32,128]{2,1,0:T(8,128)(2,1)S(1)} async-done(((bf16[32,32,128]{2,1,0:T(8,128)(2,1)}), bf16[32,32,128]{2,1,0:T(8,128)(2,1)S(1)}, u32[]{:S(2)}, u32[]{:S(2)}) %all-to-all-start) | async-done | bytes 262176 | tf_op jit(solution)/shard_map/all_to_all | solution.py:28
  31.3 3.5 %collective-permute-start = (bf16[64,1536]{1,0:T(8,128)(2,1)}, bf16[64,1536]{1,0:T(8,128)(2,1)}, u32[]{:S(2)}, u32[]{:S(2)}) collective-permute-start(bf16[64,1536]{1,0:T(8,128)(2,1)} %pad_maximum_fusion.4), channel_id=1, source_target_pairs={{0,2},{2,0},{1,3},{3,1},{4,6},{6,4},{5,7},{7,5},{8,10},{10,8},{9,1... | collective-permute-start | bytes 589832 | tf_op jit(solution)/shard_map/ppermute | solution.py:33
  35.7 1.8 tail_rows_out.1
  38.1 9.2 %all-to-all-start.1 = ((bf16[128,16,128]{2,1,0:T(8,128)(2,1)}), bf16[128,16,128]{2,1,0:T(8,128)(2,1)S(1)}, u32[]{:S(2)}, u32[]{:S(2)}) async-start(bf16[128,16,128]{2,1,0:T(8,128)(2,1)} %tail_rows_out.1), calls=%async_computation.1 | async-start | bytes 1048576 | tf_op jit(solution)/shard_map/all_to_all | solution.py:28
  47.3 3.0 %collective-permute-start.4 = (bf16[32,32,128]{2,1,0:T(8,128)(2,1)S(1)}, bf16[32,32,128]{2,1,0:T(8,128)(2,1)}, u32[]{:S(2)}, u32[]{:S(2)}) collective-permute-start(bf16[32,32,128]{2,1,0:T(8,128)(2,1)S(1)} %all-to-all-done.refs_0_), channel_id=1, source_target_pairs={{0,32},{32,64},{64,96},{96,0},{1,33},{33,65},{65,97},{97,1},{2,34}... | collective-permute-start | bytes 786440 | tf_op jit(solution)/shard_map/ppermute | solution.py:33
  50.4 4.0 %collective-permute-start.3 = (bf16[32,32,128]{2,1,0:T(8,128)(2,1)S(1)}, bf16[32,32,128]{2,1,0:T(8,128)(2,1)S(1)}, u32[]{:S(2)}, u32[]{:S(2)}) collective-permute-start(bf16[32,32,128]{2,1,0:T(8,128)(2,1)S(1)} %all-to-all-done.refs_0_), channel_id=1, source_target_pairs={{0,96},{32,0},{64,32},{96,64},{1,97},{33,1},{65,33},{97,65},{2,98}... | collective-permute-start | bytes 786440 | tf_op jit(solution)/shard_map/ppermute | solution.py:33
  54.4 3.3 %collective-permute-start.2 = (bf16[32,32,128]{2,1,0:T(8,128)(2,1)S(1)}, bf16[32,32,128]{2,1,0:T(8,128)(2,1)S(1)}, u32[]{:S(2)}, u32[]{:S(2)}) collective-permute-start(bf16[32,32,128]{2,1,0:T(8,128)(2,1)S(1)} %all-to-all-done.refs_0_), channel_id=1, source_target_pairs={{0,64},{32,96},{64,0},{96,32},{1,65},{33,97},{65,1},{97,33},{2,66}... | collective-permute-start | bytes 786440 | tf_op jit(solution)/shard_map/ppermute | solution.py:33
  57.7 1.1 select_bitcast_fusion.3
  58.8 0.9 pad_maximum_fusion.2
  59.7 1.9 %collective-permute-start.1 = (bf16[2,64,1536]{2,1,0:T(8,128)(2,1)}, bf16[2,64,1536]{2,1,0:T(8,128)(2,1)}, u32[]{:S(2)}, u32[]{:S(2)}) collective-permute-start(bf16[2,64,1536]{2,1,0:T(8,128)(2,1)} %pad_maximum_fusion.2), channel_id=1, source_target_pairs={{0,1},{1,0},{2,3},{3,2},{4,5},{5,4},{6,7},{7,6},{8,9},{9,8},{10,11... | collective-permute-start | bytes 1179656 | tf_op jit(solution)/shard_map/ppermute | solution.py:33
  62.4 1.0 reshape.123.index_ref
  63.5 2.7 %hub_sums.2.refs_3_ = f32[64,1024]{1,0:T(8,128)S(1)} custom-call(s32[1]{0:T(128)} %bitcast.12.x_ref, s32[128]{0:T(128)S(1)} %fusion.4.dest_ref, bf16[32,32,128]{2,1,0:T(8,128)(2,1)S(1)} %all-to-all-done.refs_0_, bf16[32,32,128]{2,1,0:T(8,128)(2,1)} %collective-permute-done.4.refs_1_, bf16[128,64,128]{2,1,0:T(8,128)(2,1)S(1)} %bitcast.47), custom_call_target="tpu_custom_call" | custom-call | flops 134217728 | bytes 4194304 | tf_op jit(solution)/shard_map/hub_sums/pallas_call | solution.py:272
  66.2 1.9 %collective-permute-done.3.refs_1_ = bf16[32,32,128]{2,1,0:T(8,128)(2,1)S(1)} collective-permute-done((bf16[32,32,128]{2,1,0:T(8,128)(2,1)S(1)}, bf16[32,32,128]{2,1,0:T(8,128)(2,1)S(1)}, u32[]{:S(2)}, u32[]{:S(2)}) %collective-permute-start.3) | collective-permute-done | bytes 262176 | tf_op jit(solution)/shard_map/ppermute | solution.py:33
  68.7 2.3 %hub_sums.3.hub_ref = f32[64,1024]{1,0:T(8,128)S(1)} custom-call(s32[1]{0:T(128)} %bitcast.12.x_ref, s32[128]{0:T(128)S(1)} %fusion.4.dest_ref, bf16[32,32,128]{2,1,0:T(8,128)(2,1)S(1)} %collective-permute-done.2.refs_0_, bf16[32,32,128]{2,1,0:T(8,128)(2,1)S(1)} %collective-permute-done.3.refs_1_, bf16[128,64,128]{2,1,0:T(8,128)(2,1)S(1)} %bitcast.48, ...), custom_call_target="tpu_custom_call" | custom-call | flops 134217728 | bytes 4194304 | tf_op jit(solution)/shard_map/hub_sums/pallas_call | solution.py:272
  71.0 2.4 %mixed.1 = bf16[64,1024]{1,0:T(8,128)(2,1)S(1)} custom-call(s32[2,2048]{1,0:T(2,128)S(1)} %reshape.123.index_ref, bf16[128,16,128]{2,1,0:T(8,128)(2,1)S(1)} %all-to-all-done.1.arrived_ref, f32[64,1024]{1,0:T(8,128)S(1)} %hub_sums.3.hub_ref, s32[1,1024]{1,0:T(1,128)S(1)} %bitcast.54), custom_call_target="tpu_custom_call" | custom-call | flops 1073741824 | bytes 2097152 | tf_op jit(solution)/shard_map/mixed/pallas_call | solution.py:157
  73.4 6.5 %all_gather.6.mixed_ref = bf16[256,1024]{1,0:T(8,128)(2,1)S(1)} all-gather(bf16[64,1024]{1,0:T(8,128)(2,1)S(1)} %mixed.1), channel_id=1, replica_groups=mesh['yh'=4,'x'=4,'z'=8,'yl'=2,'core'=2] {'yl','core'}, dimensions={0}, use_global_device_ids=true | all-gather | bytes 655360 | tf_op jit(solution)/shard_map/all_gather | solution.py:369
  80.0 1.1 select_bitcast_fusion.1
  81.9 0.9 slice.126.feat_ref
  83.2 0.9 multiply_convert_fusion
  84.1 7.3 %all_gather.7.d_ref = bf16[256,1024]{1,0:T(8,128)(2,1)S(1)} all-gather(bf16[64,1024]{1,0:T(8,128)(2,1)S(1)} %get-tuple-element.36.d_ref), channel_id=1, replica_groups=mesh['yh'=4,'x'=4,'z'=8,'yl'=2,'core'=2] {'yl','core'}, dimensions={0}, use_global_device_ids=true | all-gather | bytes 655360 | tf_op jit(solution)/shard_map/all_gather | solution.py:375
  91.4 1.0 copy-done.1
  93.1 1.2 mixed_grad_rows_out.1
  94.2 1.0 pad_maximum_fusion.1
  95.3 15.7 %all-to-all-start.2 = ((bf16[128,24,128]{2,1,0:T(8,128)(2,1)}), bf16[128,24,128]{2,1,0:T(8,128)(2,1)S(1)}, u32[]{:S(2)}, u32[]{:S(2)}) async-start(bf16[128,24,128]{2,1,0:T(8,128)(2,1)} %pad_maximum_fusion.1), calls=%async_computation.2 | async-start | bytes 1572864 | tf_op jit(solution)/shard_map/all_to_all | solution.py:28
  111.0 2.4 %hub_grad_terms.5 = bf16[32,32,128]{2,1,0:T(8,128)(2,1)} custom-call(s32[1]{0:T(128)} %bitcast.12.x_ref, s32[128]{0:T(128)S(1)} %fusion.4.dest_ref, bf16[64,1024]{1,0:T(8,128)(2,1)S(1)} %get-tuple-element.24.grad_ref, bf16[128,64,128]{2,1,0:T(8,128)(2,1)S(1)} %bitcast.49), custom_call_target="tpu_custom_call" | custom-call | flops 67108864 | bytes 4194304 | tf_op jit(solution)/shard_map/hub_grad_terms/pallas_call | solution.py:307
  113.4 3.0 %collective-permute-start.5 = (bf16[32,32,128]{2,1,0:T(8,128)(2,1)}, bf16[32,32,128]{2,1,0:T(8,128)(2,1)}, u32[]{:S(2)}, u32[]{:S(2)}) collective-permute-start(bf16[32,32,128]{2,1,0:T(8,128)(2,1)} %hub_grad_terms.5), channel_id=1, source_target_pairs={{0,32},{32,64},{64,96},{96,0},{1,33},{33,65},{65,97},{97,1},{2,34}... | collective-permute-start | bytes 786440 | tf_op jit(solution)/shard_map/ppermute | solution.py:33
  116.4 2.4 %hub_grad_terms.6 = bf16[32,32,128]{2,1,0:T(8,128)(2,1)} custom-call(s32[1]{0:T(128)} %bitcast.12.x_ref, s32[128]{0:T(128)S(1)} %fusion.4.dest_ref, bf16[64,1024]{1,0:T(8,128)(2,1)S(1)} %get-tuple-element.24.grad_ref, bf16[128,64,128]{2,1,0:T(8,128)(2,1)S(1)} %bitcast.50), custom_call_target="tpu_custom_call" | custom-call | flops 67108864 | bytes 4194304 | tf_op jit(solution)/shard_map/hub_grad_terms/pallas_call | solution.py:307
  118.8 4.6 %collective-permute-start.6 = (bf16[32,32,128]{2,1,0:T(8,128)(2,1)}, bf16[32,32,128]{2,1,0:T(8,128)(2,1)}, u32[]{:S(2)}, u32[]{:S(2)}) collective-permute-start(bf16[32,32,128]{2,1,0:T(8,128)(2,1)} %hub_grad_terms.6), channel_id=1, source_target_pairs={{0,64},{32,96},{64,0},{96,32},{1,65},{33,97},{65,1},{97,33},{2,66}... | collective-permute-start | bytes 786440 | tf_op jit(solution)/shard_map/ppermute | solution.py:33
  123.5 2.4 %hub_grad_terms.7 = bf16[32,32,128]{2,1,0:T(8,128)(2,1)} custom-call(s32[1]{0:T(128)} %bitcast.12.x_ref, s32[128]{0:T(128)S(1)} %fusion.4.dest_ref, bf16[64,1024]{1,0:T(8,128)(2,1)S(1)} %get-tuple-element.24.grad_ref, bf16[128,64,128]{2,1,0:T(8,128)(2,1)S(1)} %bitcast.51), custom_call_target="tpu_custom_call" | custom-call | flops 67108864 | bytes 4194304 | tf_op jit(solution)/shard_map/hub_grad_terms/pallas_call | solution.py:307
  125.9 3.3 %collective-permute-start.7 = (bf16[32,32,128]{2,1,0:T(8,128)(2,1)}, bf16[32,32,128]{2,1,0:T(8,128)(2,1)}, u32[]{:S(2)}, u32[]{:S(2)}) collective-permute-start(bf16[32,32,128]{2,1,0:T(8,128)(2,1)} %hub_grad_terms.7), channel_id=1, source_target_pairs={{0,96},{32,0},{64,32},{96,64},{1,97},{33,1},{65,33},{97,65},{2,98}... | collective-permute-start | bytes 786440 | tf_op jit(solution)/shard_map/ppermute | solution.py:33
  130.0 1.7 hub_grad_terms.4
  131.8 5.9 %collective-permute-done.6 = bf16[32,32,128]{2,1,0:T(8,128)(2,1)} collective-permute-done((bf16[32,32,128]{2,1,0:T(8,128)(2,1)}, bf16[32,32,128]{2,1,0:T(8,128)(2,1)}, u32[]{:S(2)}, u32[]{:S(2)}) %collective-permute-start.6) | collective-permute-done | bytes 262176 | tf_op jit(solution)/shard_map/ppermute | solution.py:33
  137.7 1.5 collective-permute-done.7
  139.1 1.2 add_convert_fusion
  140.5 4.5 %collective-permute-start.9 = (f32[2,128]{1,0:T(2,128)S(1)}, f32[2,128]{1,0:T(2,128)S(1)}, u32[]{:S(2)}, u32[]{:S(2)}) collective-permute-start(f32[2,128]{1,0:T(2,128)S(1)} %slice_add_fusion.1), channel_id=1, source_target_pairs={{0,64},{32,96},{64,0},{96,32},{1,65},{33,97},{65,1},{97,33},{2,66}... | collective-permute-start | bytes 3080 | tf_op jit(solution)/shard_map/ppermute | solution.py:33
  145.0 2.6 %collective-permute-start.8 = (f32[2,128]{1,0:T(2,128)S(1)}, f32[2,128]{1,0:T(2,128)S(1)}, u32[]{:S(2)}, u32[]{:S(2)}) collective-permute-start(f32[2,128]{1,0:T(2,128)S(1)} %slice_add_fusion.1), channel_id=1, source_target_pairs={{0,32},{32,64},{64,96},{96,0},{1,33},{33,65},{65,97},{97,1},{2,34}... | collective-permute-start | bytes 3080 | tf_op jit(solution)/shard_map/ppermute | solution.py:33
  147.7 4.4 %collective-permute-start.10 = (f32[2,128]{1,0:T(2,128)S(1)}, f32[2,128]{1,0:T(2,128)S(1)}, u32[]{:S(2)}, u32[]{:S(2)}) collective-permute-start(f32[2,128]{1,0:T(2,128)S(1)} %slice_add_fusion.1), channel_id=1, source_target_pairs={{0,96},{32,0},{64,32},{96,64},{1,97},{33,1},{65,33},{97,65},{2,98}... | collective-permute-start | bytes 3080 | tf_op jit(solution)/shard_map/ppermute | solution.py:33
  152.1 1.2 collective-permute-done.10
  154.1 0.8 pad_maximum_fusion.3
  154.9 10.9 %all-to-all-start.3 = ((bf16[32,48,128]{2,1,0:T(8,128)(2,1)}), bf16[32,48,128]{2,1,0:T(8,128)(2,1)S(1)}, u32[]{:S(2)}, u32[]{:S(2)}) async-start(bf16[32,48,128]{2,1,0:T(8,128)(2,1)} %pad_maximum_fusion.3), calls=%async_computation.3 | async-start | bytes 786432 | tf_op jit(solution)/shard_map/all_to_all | solution.py:28
  166.1 3.1 %tail_grads.1 = f32[64,1024]{1,0:T(8,128)} custom-call(s32[2,2048]{1,0:T(2,128)S(1)} %copy-done.4, bf16[128,24,128]{2,1,0:T(8,128)(2,1)S(1)} %all-to-all-done.2.arrived_ref, f32[64,1024]{1,0:T(8,128)S(1)} %fusion.1.direct_ref), custom_call_target="tpu_custom_call" | custom-call | flops 1073741824 | bytes 2097152 | tf_op jit(solution)/shard_map/tail_grads/pallas_call | solution.py:179
  169.7 11.9 %all-to-all-done.3 = bf16[32,48,128]{2,1,0:T(8,128)(2,1)S(1)} async-done(((bf16[32,48,128]{2,1,0:T(8,128)(2,1)}), bf16[32,48,128]{2,1,0:T(8,128)(2,1)S(1)}, u32[]{:S(2)}, u32[]{:S(2)}) %all-to-all-start.3) | async-done | bytes 393248 | tf_op jit(solution)/shard_map/all_to_all | solution.py:28
  181.9 1.4 add_select_fusion
  183.3 1.5 scatter-add.4
  (87 shorter events, 9.8 us)
Async XLA Ops:
  0.6 35.0 %copy-start.2 = (bf16[64,1024]{1,0:T(8,128)(2,1)S(1)}, bf16[64,1024]{1,0:T(8,128)(2,1)}, u32[]{:S(2)}) copy-start(bf16[64,1024]{1,0:T(8,128)(2,1)} %source_ref.1) | copy-start | bytes 393220
  2.2 29.1 %all-to-all-start = ((bf16[32,32,128]{2,1,0:T(8,128)(2,1)}), bf16[32,32,128]{2,1,0:T(8,128)(2,1)S(1)}, u32[]{:S(2)}, u32[]{:S(2)}) async-start(bf16[32,32,128]{2,1,0:T(8,128)(2,1)} %broadcast_in_dim.42), calls=%async_computation | async-start | bytes 524288 | tf_op jit(solution)/shard_map/all_to_all | solution.py:28
  31.3 26.4 %collective-permute-start = (bf16[64,1536]{1,0:T(8,128)(2,1)}, bf16[64,1536]{1,0:T(8,128)(2,1)}, u32[]{:S(2)}, u32[]{:S(2)}) collective-permute-start(bf16[64,1536]{1,0:T(8,128)(2,1)} %pad_maximum_fusion.4), channel_id=1, source_target_pairs={{0,2},{2,0},{1,3},{3,1},{4,6},{6,4},{5,7},{7,5},{8,10},{10,8},{9,1... | collective-permute-start | bytes 589832 | tf_op jit(solution)/shard_map/ppermute | solution.py:33
  37.5 0.6 copy-start.3
  38.1 23.5 %copy-start.16 = (s32[1,128]{1,0:T(1,128)S(1)}, s32[1,128]{1,0:T(1,128)}, u32[]{:S(2)}) copy-start(s32[1,128]{1,0:T(1,128)} %param.16) | copy-start | bytes 1540
  38.1 23.5 %copy-start.17 = (s32[1,128]{1,0:T(1,128)S(1)}, s32[1,128]{1,0:T(1,128)}, u32[]{:S(2)}) copy-start(s32[1,128]{1,0:T(1,128)} %param.17) | copy-start | bytes 1540
  38.1 23.6 %copy-start.13 = (s32[1,128,32]{1,2,0:T(8,128)S(1)}, s32[1,128,32]{1,2,0:T(8,128)}, u32[]{:S(2)}) copy-start(s32[1,128,32]{1,2,0:T(8,128)} %param.20) | copy-start | bytes 49156
  38.1 25.4 %copy-start = (bf16[1,128,64,128]{3,2,1,0:T(8,128)(2,1)S(1)}, bf16[1,128,64,128]{3,2,1,0:T(8,128)(2,1)}, u32[]{:S(2)}) copy-start(bf16[1,128,64,128]{3,2,1,0:T(8,128)(2,1)} %param.15) | copy-start | bytes 6291460
  38.1 32.9 %all-to-all-start.1 = ((bf16[128,16,128]{2,1,0:T(8,128)(2,1)}), bf16[128,16,128]{2,1,0:T(8,128)(2,1)S(1)}, u32[]{:S(2)}, u32[]{:S(2)}) async-start(bf16[128,16,128]{2,1,0:T(8,128)(2,1)} %tail_rows_out.1), calls=%async_computation.1 | async-start | bytes 1048576 | tf_op jit(solution)/shard_map/all_to_all | solution.py:28
  47.3 16.1 %collective-permute-start.4 = (bf16[32,32,128]{2,1,0:T(8,128)(2,1)S(1)}, bf16[32,32,128]{2,1,0:T(8,128)(2,1)}, u32[]{:S(2)}, u32[]{:S(2)}) collective-permute-start(bf16[32,32,128]{2,1,0:T(8,128)(2,1)S(1)} %all-to-all-done.refs_0_), channel_id=1, source_target_pairs={{0,32},{32,64},{64,96},{96,0},{1,33},{33,65},{65,97},{97,1},{2,34}... | collective-permute-start | bytes 786440 | tf_op jit(solution)/shard_map/ppermute | solution.py:33
  50.4 17.8 %collective-permute-start.3 = (bf16[32,32,128]{2,1,0:T(8,128)(2,1)S(1)}, bf16[32,32,128]{2,1,0:T(8,128)(2,1)S(1)}, u32[]{:S(2)}, u32[]{:S(2)}) collective-permute-start(bf16[32,32,128]{2,1,0:T(8,128)(2,1)S(1)} %all-to-all-done.refs_0_), channel_id=1, source_target_pairs={{0,96},{32,0},{64,32},{96,64},{1,97},{33,1},{65,33},{97,65},{2,98}... | collective-permute-start | bytes 786440 | tf_op jit(solution)/shard_map/ppermute | solution.py:33
  54.4 14.3 %collective-permute-start.2 = (bf16[32,32,128]{2,1,0:T(8,128)(2,1)S(1)}, bf16[32,32,128]{2,1,0:T(8,128)(2,1)S(1)}, u32[]{:S(2)}, u32[]{:S(2)}) collective-permute-start(bf16[32,32,128]{2,1,0:T(8,128)(2,1)S(1)} %all-to-all-done.refs_0_), channel_id=1, source_target_pairs={{0,64},{32,96},{64,0},{96,32},{1,65},{33,97},{65,1},{97,33},{2,66}... | collective-permute-start | bytes 786440 | tf_op jit(solution)/shard_map/ppermute | solution.py:33
  58.8 0.9 copy-start.6
  58.8 2.8 %copy-start.8 = (bf16[1,64,1536]{2,1,0:T(8,128)(2,1)}, bf16[1,64,1536]{2,1,0:T(8,128)(2,1)S(1)}, u32[]{:S(2)}) copy-start(bf16[1,64,1536]{2,1,0:T(8,128)(2,1)S(1)} %get-tuple-element.35) | copy-start | bytes 589828
  59.7 20.3 %collective-permute-start.1 = (bf16[2,64,1536]{2,1,0:T(8,128)(2,1)}, bf16[2,64,1536]{2,1,0:T(8,128)(2,1)}, u32[]{:S(2)}, u32[]{:S(2)}) collective-permute-start(bf16[2,64,1536]{2,1,0:T(8,128)(2,1)} %pad_maximum_fusion.2), channel_id=1, source_target_pairs={{0,1},{1,0},{2,3},{3,2},{4,5},{5,4},{6,7},{7,6},{8,9},{9,8},{10,11... | collective-permute-start | bytes 1179656 | tf_op jit(solution)/shard_map/ppermute | solution.py:33
  66.2 4.8 %copy-start.5 = (s32[1024]{0:T(1024)S(1)}, s32[1024]{0:T(1024)}, u32[]{:S(2)}) copy-start(s32[1024]{0:T(1024)} %param.21) | copy-start | bytes 12292
  71.0 8.9 %copy-start.7 = (bf16[1,64,1536]{2,1,0:T(8,128)(2,1)S(1)}, bf16[1,64,1536]{2,1,0:T(8,128)(2,1)}, u32[]{:S(2)}) copy-start(bf16[1,64,1536]{2,1,0:T(8,128)(2,1)} %copy-done.6) | copy-start | bytes 589828
  71.0 8.9 %copy-start.9 = (bf16[1,64,1536]{2,1,0:T(8,128)(2,1)S(1)}, bf16[1,64,1536]{2,1,0:T(8,128)(2,1)}, u32[]{:S(2)}) copy-start(bf16[1,64,1536]{2,1,0:T(8,128)(2,1)} %copy-done.8) | copy-start | bytes 589828
  81.1 1.6 copy-start.11
  81.1 1.6 copy-start.14
  81.2 2.0 %copy-start.12 = (bf16[256,64]{0,1:T(8,128)(2,1)S(1)}, bf16[256,64]{0,1:T(8,128)(2,1)}, u32[]{:S(2)}) copy-start(bf16[256,64]{0,1:T(8,128)(2,1)} %param.23) | copy-start | bytes 98308
  81.2 2.0 %copy-start.15 = (bf16[64,1024]{1,0:T(8,128)(2,1)S(1)}, bf16[64,1024]{1,0:T(8,128)(2,1)}, u32[]{:S(2)}) copy-start(bf16[64,1024]{1,0:T(8,128)(2,1)} %param.25) | copy-start | bytes 393220
  91.4 1.0 copy-start.1
  95.3 45.1 %all-to-all-start.2 = ((bf16[128,24,128]{2,1,0:T(8,128)(2,1)}), bf16[128,24,128]{2,1,0:T(8,128)(2,1)S(1)}, u32[]{:S(2)}, u32[]{:S(2)}) async-start(bf16[128,24,128]{2,1,0:T(8,128)(2,1)} %pad_maximum_fusion.1), calls=%async_computation.2 | async-start | bytes 1572864 | tf_op jit(solution)/shard_map/all_to_all | solution.py:28
  113.4 18.4 %collective-permute-start.5 = (bf16[32,32,128]{2,1,0:T(8,128)(2,1)}, bf16[32,32,128]{2,1,0:T(8,128)(2,1)}, u32[]{:S(2)}, u32[]{:S(2)}) collective-permute-start(bf16[32,32,128]{2,1,0:T(8,128)(2,1)} %hub_grad_terms.5), channel_id=1, source_target_pairs={{0,32},{32,64},{64,96},{96,0},{1,33},{33,65},{65,97},{97,1},{2,34}... | collective-permute-start | bytes 786440 | tf_op jit(solution)/shard_map/ppermute | solution.py:33
  118.8 18.8 %collective-permute-start.6 = (bf16[32,32,128]{2,1,0:T(8,128)(2,1)}, bf16[32,32,128]{2,1,0:T(8,128)(2,1)}, u32[]{:S(2)}, u32[]{:S(2)}) collective-permute-start(bf16[32,32,128]{2,1,0:T(8,128)(2,1)} %hub_grad_terms.6), channel_id=1, source_target_pairs={{0,64},{32,96},{64,0},{96,32},{1,65},{33,97},{65,1},{97,33},{2,66}... | collective-permute-start | bytes 786440 | tf_op jit(solution)/shard_map/ppermute | solution.py:33
  125.9 13.2 %collective-permute-start.7 = (bf16[32,32,128]{2,1,0:T(8,128)(2,1)}, bf16[32,32,128]{2,1,0:T(8,128)(2,1)}, u32[]{:S(2)}, u32[]{:S(2)}) collective-permute-start(bf16[32,32,128]{2,1,0:T(8,128)(2,1)} %hub_grad_terms.7), channel_id=1, source_target_pairs={{0,96},{32,0},{64,32},{96,64},{1,97},{33,1},{65,33},{97,65},{2,98}... | collective-permute-start | bytes 786440 | tf_op jit(solution)/shard_map/ppermute | solution.py:33
  131.7 34.0 %copy-start.10 = (bf16[256,256]{1,0:T(8,128)(2,1)S(1)}, bf16[256,256]{1,0:T(8,128)(2,1)}, u32[]{:S(2)}) copy-start(bf16[256,256]{1,0:T(8,128)(2,1)} %get-tuple-element.30) | copy-start | bytes 393220
  140.4 25.7 %copy-start.4 = (s32[2,2048]{1,0:T(2,128)S(1)}, s32[2,2048]{1,0:T(2,128)}, u32[]{:S(2)}) copy-start(s32[2,2048]{1,0:T(2,128)} %copy-done.3) | copy-start | bytes 49156
  140.5 11.6 %collective-permute-start.9 = (f32[2,128]{1,0:T(2,128)S(1)}, f32[2,128]{1,0:T(2,128)S(1)}, u32[]{:S(2)}, u32[]{:S(2)}) collective-permute-start(f32[2,128]{1,0:T(2,128)S(1)} %slice_add_fusion.1), channel_id=1, source_target_pairs={{0,64},{32,96},{64,0},{96,32},{1,65},{33,97},{65,1},{97,33},{2,66}... | collective-permute-start | bytes 3080 | tf_op jit(solution)/shard_map/ppermute | solution.py:33
  145.0 7.1 %collective-permute-start.8 = (f32[2,128]{1,0:T(2,128)S(1)}, f32[2,128]{1,0:T(2,128)S(1)}, u32[]{:S(2)}, u32[]{:S(2)}) collective-permute-start(f32[2,128]{1,0:T(2,128)S(1)} %slice_add_fusion.1), channel_id=1, source_target_pairs={{0,32},{32,64},{64,96},{96,0},{1,33},{33,65},{65,97},{97,1},{2,34}... | collective-permute-start | bytes 3080 | tf_op jit(solution)/shard_map/ppermute | solution.py:33
  147.7 5.7 %collective-permute-start.10 = (f32[2,128]{1,0:T(2,128)S(1)}, f32[2,128]{1,0:T(2,128)S(1)}, u32[]{:S(2)}, u32[]{:S(2)}) collective-permute-start(f32[2,128]{1,0:T(2,128)S(1)} %slice_add_fusion.1), channel_id=1, source_target_pairs={{0,96},{32,0},{64,32},{96,64},{1,97},{33,1},{65,33},{97,65},{2,98}... | collective-permute-start | bytes 3080 | tf_op jit(solution)/shard_map/ppermute | solution.py:33
  154.9 26.8 %all-to-all-start.3 = ((bf16[32,48,128]{2,1,0:T(8,128)(2,1)}), bf16[32,48,128]{2,1,0:T(8,128)(2,1)S(1)}, u32[]{:S(2)}, u32[]{:S(2)}) async-start(bf16[32,48,128]{2,1,0:T(8,128)(2,1)} %pad_maximum_fusion.3), calls=%async_computation.3 | async-start | bytes 786432 | tf_op jit(solution)/shard_map/all_to_all | solution.py:28

commit v4 on v3

v4 whole, which is shorter than its diff:
```python
from functools import partial

import jax
import jax.numpy as jnp
from jax import lax
from jax.experimental import pallas as pl
from jax.experimental.pallas import tpu as pltpu
from jax.sharding import Mesh
from jax.sharding import PartitionSpec as P

BF = jnp.bfloat16
F32 = jnp.float32
BOTH_ROWS = (((0,), (0,)), ((), ()))
BOTH_COLS = (((1,), (1,)), ((), ()))
DOM = ("yh", "x", "z")
PLANE = ("yh", "z")
REP = ("yl", "core")
SMEM = pl.BlockSpec(memory_space=pltpu.SMEM)
VMEM = pl.BlockSpec(memory_space=pltpu.VMEM)
MIB = 1024 * 1024


def mm(a, b, dims):
    return lax.dot_general(a, b, dims, preferred_element_type=F32)


def swap(pieces, axis):
    return lax.all_to_all(pieces, axis, split_axis=0, concat_axis=0, tiled=True)


def shift(values, axis, step):
    size = lax.axis_size(axis)
    return lax.ppermute(values, axis, [(i, (i + step) % size) for i in range(size)])


def call(kernel, out_shape, in_specs, scratch, name, flops, mib):
    outs = VMEM if isinstance(out_shape, jax.ShapeDtypeStruct) else [VMEM] * len(out_shape)
    return pl.pallas_call(
        kernel,
        out_shape=out_shape,
        in_specs=in_specs,
        out_specs=outs,
        scratch_shapes=scratch,
        compiler_params=pltpu.CompilerParams(vmem_limit_bytes=32 * MIB),
        cost_estimate=pl.CostEstimate(flops=flops, bytes_accessed=mib * MIB, transcendentals=0),
        name=name,
    )


def slot_rows(index):
    parts, slots = index.shape
    return index.reshape(parts, 2, slots // 2).transpose(1, 0, 2).reshape(2, -1)


def pick_slots(index_ref, source, out_ref):
    width, nodes = source.shape
    low_size = 256
    high_size = nodes // low_size
    split = jnp.concatenate(
        [source[:, i * low_size : (i + 1) * low_size] for i in range(high_size)], axis=0
    )
    step = 256
    rows = out_ref.shape[1]
    low_ids = lax.broadcasted_iota(jnp.int32, (low_size, step), 0)
    for start in range(0, index_ref.shape[1], step):
        halves = []
        for h in range(2):
            index = index_ref[h : h + 1, start : start + step]
            hits = jnp.where(low_ids == (index & (low_size - 1)), 1.0, 0.0).astype(BF)
            found = jnp.dot(split, hits, preferred_element_type=F32)
            high = jnp.broadcast_to(index >> 8, (width, step))
            kept = jnp.zeros((width, step), F32)
            for i in range(high_size):
                kept = jnp.where(high == i, found[i * width : (i + 1) * width], kept)
            halves.append(kept)
        block = jnp.concatenate(halves, axis=0).T
        first = start // rows
        out_ref[first : first + step // rows] = block.reshape(step // rows, rows, 128).astype(BF)


def gather_kernel(index_ref, source_ref, out_ref):
    pick_slots(index_ref, source_ref[...], out_ref)


def gather_slots(index, source, parts, slots):
    return call(
        gather_kernel,
        jax.ShapeDtypeStruct((parts, slots // 2, 128), BF),
        [VMEM, VMEM],
        [],
        "tail_rows_out",
        2 * parts * slots * 256 * 256,
        2,
    )(index, source)


def back_kernel(index_ref, weight_ref, d_ref, degree_ref, grad_ref, out_ref):
    grad = jnp.dot(weight_ref[...], d_ref[...], preferred_element_type=F32).astype(BF)
    grad_ref[...] = grad
    scaled = (grad.astype(F32) / degree_ref[...].astype(F32)).astype(BF)
    pick_slots(index_ref, scaled, out_ref)


def back_gather(index, weight, d_full, degree, parts, slots):
    width, nodes = weight.shape[0], d_full.shape[1]
    return call(
        back_kernel,
        [
            jax.ShapeDtypeStruct((width, nodes), BF),
            jax.ShapeDtypeStruct((parts, slots // 2, 128), BF),
        ],
        [VMEM] * 4,
        [],
        "mixed_grad_rows_out",
        2 * parts * slots * 256 * 256,
        2,
    )(index, weight, d_full, degree)


def sum_slots(index_ref, arrived_ref, rows, start, size):
    parts = arrived_ref.shape[0]
    flat = arrived_ref[:, :rows, :].reshape(parts * rows, 128)
    ids = lax.broadcasted_iota(jnp.int32, (size, parts * rows), 0) + start
    sums = []
    for h in range(2):
        hits = jnp.where(ids == index_ref[h : h + 1, :], 1.0, 0.0).astype(BF)
        sums.append(jnp.dot(hits, flat, preferred_element_type=F32))
    return sums[0].T[:64] + sums[1].T[64:]


def mixed_kernel(rows, index_ref, arrived_ref, hub_ref, degree_ref, out_ref):
    size = 256
    for start in range(0, out_ref.shape[1], size):
        at = slice(start, start + size)
        tail = sum_slots(index_ref, arrived_ref, rows, start, size)
        out_ref[:, at] = (hub_ref[:, at] + tail / degree_ref[:, at].astype(F32)).astype(BF)


def mixed_sums(index, arrived, hub_sum, degree):
    parts, rows, _ = arrived.shape
    width, nodes = hub_sum.shape
    return call(
        partial(mixed_kernel, rows),
        jax.ShapeDtypeStruct((width, nodes), BF),
        [VMEM] * 4,
        [],
        "mixed",
        4 * parts * rows * nodes * 128,
        2,
    )(index, arrived, hub_sum, degree)


def tail_grad_kernel(rows, index_ref, arrived_ref, direct_ref, out_ref):
    size = 256
    for start in range(0, out_ref.shape[1], size):
        at = slice(start, start + size)
        tail = sum_slots(index_ref, arrived_ref, rows, start, size)
        out_ref[:, at] = direct_ref[:, at] + tail


def tail_grads(index, arrived, direct, rows):
    parts = arrived.shape[0]
    width, nodes = direct.shape
    return call(
        partial(tail_grad_kernel, rows),
        jax.ShapeDtypeStruct((width, nodes), F32),
        [VMEM] * 3,
        [],
        "tail_grads",
        4 * parts * rows * nodes * 128,
        2,
    )(index, arrived, direct)


def arrange_kernel(place_ref, near_ref, far_ref, w_ref, bias_ref, *refs):
    feat_ref, pre_ref, self_ref, neigh_ref, wide = refs
    width, nodes = pre_ref.shape
    full = feat_ref.shape[0]
    for i in range(4):
        block = (near_ref, far_ref)[i // 2].at[i % 2]
        at = pl.ds(pl.multiple_of(place_ref[i] * width, width), width)
        feat_ref[at, :] = block[:, :nodes]
        wide[at, :] = block[:, nodes:].astype(F32)
    pre_ref[...] = (
        jnp.dot(w_ref[...], feat_ref[...], preferred_element_type=F32) + bias_ref[...]
    )
    own = place_ref[0]
    for first, out_ref in ((0, self_ref), (full, neigh_ref)):
        rows = wide[:, first : first + width]
        for k in range(1, 4):
            at = first + k * width
            rows = jnp.where(own == k, wide[:, at : at + width], rows)
        out_ref[...] = rows.T.astype(BF)


def arrange(place, near, far, w_self, bias):
    width, full = w_self.shape
    nodes = near.shape[2] - 2 * full
    return call(
        arrange_kernel,
        [
            jax.ShapeDtypeStruct((full, nodes), BF),
            jax.ShapeDtypeStruct((width, nodes), F32),
            jax.ShapeDtypeStruct((width, full), BF),
            jax.ShapeDtypeStruct((width, full), BF),
        ],
        [SMEM] + [VMEM] * 4,
        [pltpu.VMEM((full, 2 * full), F32)],
        "own_columns",
        2 * width * full * nodes,
        2,
    )(place, near, far, w_self, bias)


def weight_kernel(feat_ref, mixed_ref, d_ref, out_ref, bias_ref):
    d_pre = d_ref[...]
    half = feat_ref.shape[0] // 2
    y_size, x_size, pairs = out_ref.shape[:3]
    for place, ref in enumerate((feat_ref, mixed_ref)):
        grad = mm(ref[...], d_pre, BOTH_COLS)
        grad = jnp.concatenate([grad[:half], grad[half:]], axis=1)
        grad = grad.reshape(y_size // 2, pairs, 16, 128).astype(BF)
        at = slice(place * (y_size // 2), (place + 1) * (y_size // 2))
        for x in range(x_size):
            out_ref[at, x] = grad
    rows = bias_ref.shape[0]
    bias = mm(jnp.ones((rows, d_pre.shape[1]), BF), d_pre, BOTH_COLS)
    bias = jnp.concatenate([bias, bias], axis=1)
    high = bias.astype(BF).astype(F32)
    row = lax.broadcasted_iota(jnp.int32, bias.shape, 0)
    kept = jnp.where(row == 0, high, jnp.where(row == 1, bias - high, 0.0))
    bias_ref[...] = kept.astype(BF)


def weight_rows(full_feat, full_mixed, d_pre, sizes, plane):
    x_size, z_size = sizes
    width = d_pre.shape[0]
    made, bias = call(
        weight_kernel,
        [
            jax.ShapeDtypeStruct((plane // z_size, x_size, z_size // 2, 16, 128), BF),
            jax.ShapeDtypeStruct((width // 2, 128), BF),
        ],
        [VMEM] * 3,
        [],
        "weight_grad_rows",
        4 * full_feat.size * width,
        2,
    )(full_feat, full_mixed, d_pre)
    return made.reshape(plane * x_size, 8, 128), bias


def quarter_call(kernel, out_shape, scalars, blocks, specs, out_spec, scratch, name, flops, steps):
    return pl.pallas_call(
        kernel,
        out_shape=out_shape,
        grid_spec=pltpu.PrefetchScalarGridSpec(
            num_scalar_prefetch=len(scalars),
            grid=(steps,),
            in_specs=specs,
            out_specs=out_spec,
            scratch_shapes=scratch,
        ),
        compiler_params=pltpu.CompilerParams(vmem_limit_bytes=32 * MIB),
        cost_estimate=pl.CostEstimate(flops=flops, bytes_accessed=2 * MIB, transcendentals=0),
        name=name,
    )(*scalars, *blocks)


def x_at(x_ref, step, x_size):
    return lax.rem(x_ref[0] + step % x_size, x_size)


def quarter_spec(tiles, step):
    _, x_size, z_size, hubs, tile_len = tiles.shape
    return pl.BlockSpec(
        (1, 1, z_size, hubs, tile_len),
        lambda y, x_ref, dest_ref: (y, x_at(x_ref, step, x_size), 0, 0, 0),
    )


def whole_spec(shape):
    return pl.BlockSpec(shape, lambda y, x_ref, dest_ref: (0,) * len(shape))


def fold_kernel(steps, sizes, has_base, x_ref, dest_ref, *refs):
    count = len(steps)
    hub_refs, tile_refs = refs[:count], refs[count : 2 * count]
    *base_ref, out_ref, total = refs[2 * count :]
    blocks = total.shape[0] - 1
    half = hub_refs[0].shape[1]
    x_size, z_size = sizes
    y = pl.program_id(0)

    @pl.when(y == 0)
    def _():
        for b in range(blocks):
            at = slice(b * 128, (b + 1) * 128)
            total[b] = base_ref[0][:, at] if has_base else jnp.zeros_like(total[b])
        total[blocks] = jnp.zeros_like(total[blocks])

    lanes = lax.broadcasted_iota(jnp.int32, (half, 128), 1)
    first = (lanes < 64).astype(F32).astype(BF)
    second = (lanes >= 64).astype(F32).astype(BF)
    for k, hub_ref, tile_ref in zip(steps, hub_refs, tile_refs):
        tile = (y * x_size + x_at(x_ref, -k, x_size)) * z_size
        for z in range(z_size):
            rows = hub_ref[z]
            weights = tile_ref[0, 0, z]
            product = jnp.dot(
                jnp.concatenate([rows * first, rows * second], axis=0),
                jnp.concatenate([weights, weights], axis=0),
                preferred_element_type=F32,
            )
            dest = dest_ref[tile + z]
            total[dest] = total[dest] + product

    @pl.when(y == pl.num_programs(0) - 1)
    def _():
        for b in range(blocks):
            out_ref[:, b * 128 : (b + 1) * 128] = total[b]


def fold_hubs(x_index, dest, hubs, steps, tiles, blocks, base):
    y_size, x_size, z_size = tiles.shape[:3]
    half = hubs[0].shape[1]
    shape = (2 * half, blocks * 128)
    bases = [] if base is None else [base]
    hub_spec = pl.BlockSpec((z_size, half, 128), lambda y, x_ref, dest_ref: (y, 0, 0))
    return quarter_call(
        partial(fold_kernel, steps, (x_size, z_size), base is not None),
        jax.ShapeDtypeStruct(shape, F32),
        (x_index, dest),
        (*hubs, *[tiles for _ in steps], *bases),
        [hub_spec for _ in hubs]
        + [quarter_spec(tiles, -k) for k in steps]
        + [whole_spec(shape) for _ in bases],
        whole_spec(shape),
        [pltpu.VMEM((blocks + 1, 2 * half, 128), F32)],
        "hub_sums",
        tiles.size * half * len(hubs),
        y_size,
    )


def hub_grad_kernel(k, sizes, x_ref, dest_ref, grad_ref, bias_ref, tile_ref, out_ref, blocked):
    blocks = blocked.shape[0] - 1
    x_size, z_size = sizes
    y = pl.program_id(0)

    @pl.when(y == 0)
    def _():
        for b in range(blocks):
            blocked[b] = grad_ref[:, b * 128 : (b + 1) * 128]
        blocked[blocks] = jnp.zeros_like(blocked[blocks])
        out_ref[out_ref.shape[0] - 1] = bias_ref[...]

    half = out_ref.shape[1]
    first = lax.broadcasted_iota(jnp.int32, (half, 128), 1) < 64
    tile = (y * x_size + x_at(x_ref, k, x_size)) * z_size
    for z in range(z_size):
        weights = tile_ref[0, 0, z]
        product = mm(
            blocked[dest_ref[tile + z]],
            jnp.concatenate([weights, weights], axis=0),
            BOTH_COLS,
        )
        out_ref[y * z_size + z] = jnp.where(first, product[:half], product[half:]).astype(BF)


def hub_grad_terms(x_index, dest, grad, bias, tiles, k, blocks):
    y_size, x_size, z_size = tiles.shape[:3]
    width = grad.shape[0]
    out = (y_size * z_size + 1, width // 2, 128)
    return quarter_call(
        partial(hub_grad_kernel, k, (x_size, z_size)),
        jax.ShapeDtypeStruct(out, BF),
        (x_index, dest),
        (grad, bias, tiles),
        [whole_spec(grad.shape), whole_spec(bias.shape), quarter_spec(tiles, k)],
        whole_spec(out),
        [pltpu.VMEM((blocks + 1, width, 128), BF)],
        "hub_grad_terms",
        tiles.size * width // 2,
        y_size,
    )


def pack_kernel(*refs):
    *term_refs, sum_ref, out_ref = refs
    count, half = out_ref.shape[0], term_refs[0].shape[1]
    total = term_refs[0][...].astype(F32)
    for ref in term_refs[1:]:
        total = total + ref[...].astype(F32)
    out_ref[:, :half] = total[:count].astype(BF)
    bias = total[count]
    bias = jnp.broadcast_to(bias[0:1] + bias[1:2], (8, 128))
    high = bias.astype(BF).astype(F32)
    row = lax.broadcasted_iota(jnp.int32, (8, 128), 0)
    bias = jnp.where(row == 0, high, jnp.where(row == 1, bias - high, 0.0))
    extra = jnp.concatenate([sum_ref[...], bias], axis=0).astype(BF)
    out_ref[:, half:] = jnp.broadcast_to(extra[None], (count, 16, 128))


def pack_rows(terms, sums):
    count, half, _ = terms[0].shape
    return call(
        pack_kernel,
        jax.ShapeDtypeStruct((count - 1, half + 16, 128), BF),
        [VMEM] * (len(terms) + 1),
        [],
        "hub_grads_over_x",
        MIB,
        2,
    )(*terms, sums)


def final_kernel(second_ref, base_ref, out_ref, self_ref, neigh_ref, bias_ref):
    half = out_ref.shape[0] // 2
    hub = jnp.sum(second_ref[:, :half].astype(F32), axis=0)
    hub = jnp.concatenate([hub, pltpu.roll(hub, 64, 1)], axis=0)
    lane = lax.broadcasted_iota(jnp.int32, hub.shape, 1)
    out_ref[...] = base_ref[...] + jnp.where(lane < 64, hub, 0.0)
    extra = second_ref[:, half:].astype(F32)
    grads = extra[:, :8].reshape(-1, 128)
    rows = grads.shape[0] // 2
    for place, ref in enumerate((self_ref, neigh_ref)):
        turned = grads[place * rows : (place + 1) * rows].T
        ref[...] = jnp.concatenate([turned[:64], turned[64:]], axis=1)
    bias = jnp.sum(extra[:, 8:], axis=0)
    bias_ref[...] = jnp.broadcast_to(bias[0:1] + bias[1:2], bias_ref.shape)


def finish(second, base, full):
    width, nodes = base.shape
    hub_part = pl.BlockSpec((width, 128), lambda i: (0, 0))
    return pl.pallas_call(
        final_kernel,
        out_shape=[
            jax.ShapeDtypeStruct((width, nodes), F32),
            jax.ShapeDtypeStruct((width, full), F32),
            jax.ShapeDtypeStruct((width, full), F32),
            jax.ShapeDtypeStruct((8, 128), F32),
        ],
        grid=(1,),
        in_specs=[pl.BlockSpec(second.shape, lambda i: (0, 0, 0)), hub_part],
        out_specs=[hub_part]
        + [pl.BlockSpec((width, full), lambda i: (0, 0))] * 2
        + [pl.BlockSpec((8, 128), lambda i: (0, 0))],
        input_output_aliases={1: 0},
        compiler_params=pltpu.CompilerParams(vmem_limit_bytes=32 * MIB),
        cost_estimate=pl.CostEstimate(flops=MIB, bytes_accessed=MIB, transcendentals=0),
        name="gradients",
    )(second, base)


def local(
    features,
    hub_weight,
    hub_block,
    hub_mask,
    tail_rows,
    tail_count,
    tail_target,
    degree,
    w_self,
    w_neigh,
    out_bias,
    cotangent,
):
    width, nodes = features.shape
    parts, hubs, tile_len = hub_weight.shape[1:]
    slots = tail_rows.shape[2]
    half_width = width // 2
    blocks = nodes // tile_len
    full_width = w_self.shape[0]
    x_size, z_size = lax.axis_size("x"), lax.axis_size("z")
    sizes = (x_size, z_size)
    plane = parts // x_size
    x_index = lax.axis_index("x")[None]
    tiles = hub_weight.reshape(-1, x_size, z_size, hubs, tile_len)
    hub_dest = jnp.where(hub_mask[0] > 0, hub_block[0], blocks)
    degree = degree[None, :]

    hub_piece = jnp.concatenate([features[:half_width, :hubs], features[half_width:, :hubs]], axis=1)
    hub_send = jnp.broadcast_to(hub_piece[None], (plane, half_width, 128))
    hub_plane = swap(hub_send, PLANE)

    slot_live = jnp.arange(slots, dtype=jnp.int32)[None, :] < tail_count[0][:, None]
    send_index = slot_rows(jnp.where(slot_live, tail_rows[0], -1))
    recv_index = slot_rows(tail_target[0])
    own = jnp.concatenate([features, w_self.T, w_neigh.T], axis=1)
    own, send_index, _ = lax.optimization_barrier((own, send_index, hub_send))
    near = jnp.stack([own, shift(own, "yl", 1)])
    tail_send = gather_slots(send_index, features, parts, slots)
    hub_plane, tail_send, recv_index, near = lax.optimization_barrier(
        (hub_plane, tail_send, recv_index, near)
    )
    arrived = swap(tail_send, DOM)
    hub_all = [hub_plane] + [shift(hub_plane, "x", k) for k in range(1, x_size)]
    far = shift(near, "core", 1)
    place = lax.axis_index(REP) ^ jnp.array([0, 2, 1, 3], jnp.int32)
    full_feat, pre_self, w_self_rows, w_neigh_rows = arrange(
        place, near, far, w_self.T, out_bias[:, None]
    )

    hub_sum = fold_hubs(x_index, hub_dest, hub_all[:2], (0, 1), tiles, blocks, None)
    hub_sum = fold_hubs(x_index, hub_dest, hub_all[2:], (2, 3), tiles, blocks, hub_sum)
    mixed = mixed_sums(recv_index, arrived, hub_sum, degree)

    full_mixed = lax.all_gather(mixed, REP, axis=0, tiled=True)
    pre = pre_self + mm(w_neigh, full_mixed, BOTH_ROWS)
    sigma = jax.nn.sigmoid(pre)
    output = (pre * sigma).astype(BF)
    d_pre = (cotangent.astype(F32) * (sigma * (1.0 + pre * (1.0 - sigma)))).astype(BF)

    full_d = lax.all_gather(d_pre, REP, axis=0, tiled=True)
    grad_rows, bias_rows = weight_rows(full_feat, full_mixed, d_pre, sizes, plane)
    mixed_grad, tail_back = back_gather(recv_index, w_neigh_rows, full_d, degree, parts, slots)
    tail_len = tail_back.shape[1]
    first = swap(jnp.concatenate([tail_back, grad_rows], axis=1), DOM)
    direct = jnp.dot(w_self_rows, full_d, preferred_element_type=F32)

    terms = [
        hub_grad_terms(x_index, hub_dest, mixed_grad, bias_rows, tiles, k, blocks)
        for k in range(x_size)
    ]
    terms = terms[:1] + [shift(terms[k], "x", k) for k in range(1, x_size)]
    sums = jnp.sum(first[:, tail_len:].astype(F32), axis=0)
    second = swap(pack_rows(terms, sums), PLANE)

    base = tail_grads(send_index, first, direct, tail_len)
    grad_features, grad_w_self, grad_w_neigh, grad_bias = finish(second, base, full_width)
    return (output, grad_features, grad_w_self.T, grad_w_neigh.T, grad_bias[0, :width])


def solution(mesh):
    grid = (4, 4, mesh.shape["dom"] // 16, 2, 2)
    parted = Mesh(mesh.devices.reshape(grid), DOM + REP)
    in_specs = (
        P(REP, DOM),
        P(DOM, None, None, None),
        P(DOM, None),
        P(DOM, None),
        P(DOM, None, None),
        P(DOM, None),
        P(DOM, None, None),
        P(DOM),
        P(None, REP),
        P(None, REP),
        P(REP),
        P(REP, DOM),
    )
    out_specs = (P(REP, DOM), P(REP, DOM), P(None, REP), P(None, REP), P(REP))
    return jax.shard_map(local, mesh=parted, in_specs=in_specs, out_specs=out_specs, check_vma=False)
```

time: 188 us -> 174 us (0.926)
  the two profiles are of different devices: /device:TPU:8 before, /device:TPU:74 now
where the time goes in v4:
time: 174 us; the launch traced here: 172 us
  starting transfers between devices  79.3 us (46%)
  waiting for transfers between devices  34 us (20%)
  Pallas kernels  29.4 us (17%)
  blocking collectives  14.8 us (9%)
  local copies, waits for them, and re-layouts  8.96 us (5%)
  other arithmetic  4.42 us (3%)
    all_to_all x4, starting transfers between devices, swap(): return lax.all_to_all(pieces, axis, split_axis=0, concat_axis=0, tiled=True)  53.8 us
    ppermute x8, starting transfers between devices, shift(): lax.ppermute(values, axis, [(i, (i + step) % size) for i in range(size)])  25.5 us
    all_to_all x4, waiting for transfers between devices, swap(): return lax.all_to_all(pieces, axis, split_axis=0, concat_axis=0, tiled=True)  22 us
    pallas_call x6, Pallas kernels, quarter_call(): pl.pallas_call(kernel, out_shape=out_shape, grid_spec=pltpu.PrefetchScala...  15.3 us
    ppermute x8, waiting for transfers between devices, shift(): lax.ppermute(values, axis, [(i, (i + step) % size) for i in range(size)])  12 us
    all_gather x1, blocking collectives, local(): full_mixed = lax.all_gather(mixed, REP, axis=0, tiled=True)  7.53 us
    all_gather x1, blocking collectives, local(): full_d = lax.all_gather(d_pre, REP, axis=0, tiled=True)  7.28 us
    unnamed x46, local copies, waits for them, and re-layouts  4.49 us
  transfers between devices with their start and end apart: 12, of which 7 were waited for; matrix products, arithmetic and copies ran while one was open for 3% of the time, Pallas kernels for 13%

profile of v4, /device:TPU:74, one launch (start us, length us, event | category | flops | bytes accessed | tf_op | source)
XLA Modules:
  0.0 172.3 jit_solution(16089051211028053367)
XLA Ops:
  0.7 0.8 fusion.1
  1.5 0.7 broadcast_in_dim.24
  2.2 14.5 %all-to-all-start = ((bf16[32,32,128]{2,1,0:T(8,128)(2,1)}), bf16[32,32,128]{2,1,0:T(8,128)(2,1)S(1)}, u32[]{:S(2)}, u32[]{:S(2)}) async-start(bf16[32,32,128]{2,1,0:T(8,128)(2,1)} %broadcast_in_dim.24), calls=%async_computation | async-start | bytes 524288 | tf_op jit(solution)/shard_map/all_to_all | solution.py:28
  16.7 0.8 copy.22
  17.6 0.7 select_bitcast_fusion
  18.3 1.0 pad_maximum_fusion.2
  19.4 3.3 %collective-permute-start = (bf16[64,1536]{1,0:T(8,128)(2,1)S(1)}, bf16[64,1536]{1,0:T(8,128)(2,1)S(1)}, u32[]{:S(2)}, u32[]{:S(2)}) collective-permute-start(bf16[64,1536]{1,0:T(8,128)(2,1)S(1)} %pad_maximum_fusion.2), channel_id=1, source_target_pairs={{0,2},{2,0},{1,3},{3,1},{4,6},{6,4},{5,7},{7,5},{8,10},{10,8},{9,1... | collective-permute-start | bytes 589832 | tf_op jit(solution)/shard_map/ppermute | solution.py:33
  22.8 0.7 reshape.45.index_ref
  23.5 1.8 %tail_rows_out.1 = bf16[128,16,128]{2,1,0:T(8,128)(2,1)} custom-call(s32[2,2048]{1,0:T(2,128)S(1)} %reshape.44.index_ref, bf16[64,1024]{1,0:T(8,128)(2,1)S(1)} %copy-done.5), custom_call_target="tpu_custom_call" | custom-call | flops 536870912 | bytes 2097152 | tf_op jit(solution)/shard_map/tail_rows_out/pallas_call | solution.py:86
  25.3 2.9 %collective-permute-done = bf16[64,1536]{1,0:T(8,128)(2,1)S(1)} collective-permute-done((bf16[64,1536]{1,0:T(8,128)(2,1)S(1)}, bf16[64,1536]{1,0:T(8,128)(2,1)S(1)}, u32[]{:S(2)}, u32[]{:S(2)}) %collective-permute-start) | collective-permute-done | bytes 196640 | tf_op jit(solution)/shard_map/ppermute | solution.py:33
  28.3 2.0 %all-to-all-done.refs_0_ = bf16[32,32,128]{2,1,0:T(8,128)(2,1)S(1)} async-done(((bf16[32,32,128]{2,1,0:T(8,128)(2,1)}), bf16[32,32,128]{2,1,0:T(8,128)(2,1)S(1)}, u32[]{:S(2)}, u32[]{:S(2)}) %all-to-all-start) | async-done | bytes 262176 | tf_op jit(solution)/shard_map/all_to_all | solution.py:28
  30.3 13.0 %all-to-all-start.1 = ((bf16[128,16,128]{2,1,0:T(8,128)(2,1)}), bf16[128,16,128]{2,1,0:T(8,128)(2,1)S(1)}, u32[]{:S(2)}, u32[]{:S(2)}) async-start(bf16[128,16,128]{2,1,0:T(8,128)(2,1)} %tail_rows_out.1), calls=%async_computation.1 | async-start | bytes 1048576 | tf_op jit(solution)/shard_map/all_to_all | solution.py:28
  43.3 3.4 %collective-permute-start.4 = (bf16[32,32,128]{2,1,0:T(8,128)(2,1)S(1)}, bf16[32,32,128]{2,1,0:T(8,128)(2,1)}, u32[]{:S(2)}, u32[]{:S(2)}) collective-permute-start(bf16[32,32,128]{2,1,0:T(8,128)(2,1)S(1)} %all-to-all-done.refs_0_), channel_id=1, source_target_pairs={{0,32},{32,64},{64,96},{96,0},{1,33},{33,65},{65,97},{97,1},{2,34}... | collective-permute-start | bytes 786440 | tf_op jit(solution)/shard_map/ppermute | solution.py:33
  46.7 2.5 %collective-permute-start.3 = (bf16[32,32,128]{2,1,0:T(8,128)(2,1)S(1)}, bf16[32,32,128]{2,1,0:T(8,128)(2,1)S(1)}, u32[]{:S(2)}, u32[]{:S(2)}) collective-permute-start(bf16[32,32,128]{2,1,0:T(8,128)(2,1)S(1)} %all-to-all-done.refs_0_), channel_id=1, source_target_pairs={{0,96},{32,0},{64,32},{96,64},{1,97},{33,1},{65,33},{97,65},{2,98}... | collective-permute-start | bytes 786440 | tf_op jit(solution)/shard_map/ppermute | solution.py:33
  49.2 4.0 %collective-permute-start.2 = (bf16[32,32,128]{2,1,0:T(8,128)(2,1)S(1)}, bf16[32,32,128]{2,1,0:T(8,128)(2,1)}, u32[]{:S(2)}, u32[]{:S(2)}) collective-permute-start(bf16[32,32,128]{2,1,0:T(8,128)(2,1)S(1)} %all-to-all-done.refs_0_), channel_id=1, source_target_pairs={{0,64},{32,96},{64,0},{96,32},{1,65},{33,97},{65,1},{97,33},{2,66}... | collective-permute-start | bytes 786440 | tf_op jit(solution)/shard_map/ppermute | solution.py:33
  53.2 1.9 %collective-permute-start.1 = (bf16[2,64,1536]{2,1,0:T(8,128)(2,1)S(1)}, bf16[2,64,1536]{2,1,0:T(8,128)(2,1)}, u32[]{:S(2)}, u32[]{:S(2)}) collective-permute-start(bf16[2,64,1536]{2,1,0:T(8,128)(2,1)S(1)} %pad_maximum_fusion.1.near_ref), channel_id=1, source_target_pairs={{0,1},{1,0},{2,3},{3,2},{4,5},{5,4},{6,7},{7,6},{8,9},{9,8},{10,11... | collective-permute-start | bytes 1179656 | tf_op jit(solution)/shard_map/ppermute | solution.py:33
  55.2 0.7 copy.24.bias_ref
  55.9 0.7 fusion.dest_ref
  56.5 1.3 collective-permute-done.4.refs_1_
  57.8 3.2 %hub_sums.2.refs_4_ = f32[64,1024]{1,0:T(8,128)S(1)} custom-call(s32[1]{0:T(128)} %bitcast.10.x_ref, s32[128]{0:T(128)S(1)} %fusion.dest_ref, bf16[32,32,128]{2,1,0:T(8,128)(2,1)S(1)} %all-to-all-done.refs_0_, bf16[32,32,128]{2,1,0:T(8,128)(2,1)} %collective-permute-done.4.refs_1_, bf16[4,4,8,64,128]{4,3,2,1,0:T(8,128)(2,1)S(1)} %bitcast.27, ...), custom_call_target="tpu_custom_call" | custom-call | flops 67108864 | bytes 2097152 | tf_op jit(solution)/shard_map/hub_sums/pallas_call | solution.py:254
  61.0 3.5 %collective-permute-done.2.refs_0_ = bf16[32,32,128]{2,1,0:T(8,128)(2,1)} collective-permute-done((bf16[32,32,128]{2,1,0:T(8,128)(2,1)S(1)}, bf16[32,32,128]{2,1,0:T(8,128)(2,1)}, u32[]{:S(2)}, u32[]{:S(2)}) %collective-permute-start.2) | collective-permute-done | bytes 262176 | tf_op jit(solution)/shard_map/ppermute | solution.py:33
  64.5 3.1 %hub_sums.3.hub_ref = f32[64,1024]{1,0:T(8,128)S(1)} custom-call(s32[1]{0:T(128)} %bitcast.10.x_ref, s32[128]{0:T(128)S(1)} %fusion.dest_ref, bf16[32,32,128]{2,1,0:T(8,128)(2,1)} %collective-permute-done.2.refs_0_, bf16[32,32,128]{2,1,0:T(8,128)(2,1)S(1)} %collective-permute-done.3.refs_1_, bf16[4,4,8,64,128]{4,3,2,1,0:T(8,128)(2,1)S(1)} %bitcast.29, ...), custom_call_target="tpu_custom_call" | custom-call | flops 67108864 | bytes 2097152 | tf_op jit(solution)/shard_map/hub_sums/pallas_call | solution.py:254
  67.7 1.5 own_columns.1
  69.3 0.8 copy-done.3
  71.3 0.7 copy-done.12
  72.0 2.4 %mixed.1 = bf16[64,1024]{1,0:T(8,128)(2,1)S(1)} custom-call(s32[2,2048]{1,0:T(2,128)S(1)} %copy-done.12, bf16[128,16,128]{2,1,0:T(8,128)(2,1)S(1)} %all-to-all-done.1.arrived_ref, f32[64,1024]{1,0:T(8,128)S(1)} %hub_sums.3.hub_ref, s32[1,1024]{1,0:T(1,128)S(1)} %bitcast.38), custom_call_target="tpu_custom_call" | custom-call | flops 1073741824 | bytes 2097152 | tf_op jit(solution)/shard_map/mixed/pallas_call | solution.py:142
  74.4 7.5 %all_gather.6.mixed_ref = bf16[256,1024]{1,0:T(8,128)(2,1)S(1)} all-gather(bf16[64,1024]{1,0:T(8,128)(2,1)S(1)} %mixed.1), channel_id=1, replica_groups=mesh['yh'=4,'x'=4,'z'=8,'yl'=2,'core'=2] {'yl','core'}, dimensions={0}, use_global_device_ids=true | all-gather | bytes 655360 | tf_op jit(solution)/shard_map/all_gather | solution.py:511
  82.2 0.8 multiply_convert_fusion
  83.0 7.3 %all_gather.7.d_ref = bf16[256,1024]{1,0:T(8,128)(2,1)S(1)} all-gather(bf16[64,1024]{1,0:T(8,128)(2,1)S(1)} %get-tuple-element.41.d_ref), channel_id=1, replica_groups=mesh['yh'=4,'x'=4,'z'=8,'yl'=2,'core'=2] {'yl','core'}, dimensions={0}, use_global_device_ids=true | all-gather | bytes 655360 | tf_op jit(solution)/shard_map/all_gather | solution.py:517
  90.8 1.2 mixed_grad_rows_out.1
  92.0 1.0 pad_maximum_fusion
  93.0 15.0 %all-to-all-start.2 = ((bf16[128,24,128]{2,1,0:T(8,128)(2,1)}), bf16[128,24,128]{2,1,0:T(8,128)(2,1)S(1)}, u32[]{:S(2)}, u32[]{:S(2)}) async-start(bf16[128,24,128]{2,1,0:T(8,128)(2,1)} %pad_maximum_fusion), calls=%async_computation.2 | async-start | bytes 1572864 | tf_op jit(solution)/shard_map/all_to_all | solution.py:28
  108.0 2.4 %hub_grad_terms.7 = bf16[33,32,128]{2,1,0:T(8,128)(2,1)} custom-call(s32[1]{0:T(128)} %bitcast.10.x_ref, s32[128]{0:T(128)S(1)} %fusion.dest_ref, bf16[64,1024]{1,0:T(8,128)(2,1)S(1)} %get-tuple-element.31.grad_ref, bf16[32,128]{1,0:T(8,128)(2,1)S(1)} %get-tuple-element.33.bias_ref, bf16[4,4,8,64,128]{4,3,2,1,0:T(8,128)(2,1)S(1)} %bitcast.31), custom_call_target="tpu_custom_call" | custom-call | flops 33554432 | bytes 2097152 | tf_op jit(solution)/shard_map/hub_grad_terms/pallas_call | solution.py:254
  110.5 2.4 %hub_grad_terms.6 = bf16[33,32,128]{2,1,0:T(8,128)(2,1)} custom-call(s32[1]{0:T(128)} %bitcast.10.x_ref, s32[128]{0:T(128)S(1)} %fusion.dest_ref, bf16[64,1024]{1,0:T(8,128)(2,1)S(1)} %get-tuple-element.31.grad_ref, bf16[32,128]{1,0:T(8,128)(2,1)S(1)} %get-tuple-element.33.bias_ref, bf16[4,4,8,64,128]{4,3,2,1,0:T(8,128)(2,1)S(1)} %bitcast.32), custom_call_target="tpu_custom_call" | custom-call | flops 33554432 | bytes 2097152 | tf_op jit(solution)/shard_map/hub_grad_terms/pallas_call | solution.py:254
  112.9 2.4 %hub_grad_terms.5 = bf16[33,32,128]{2,1,0:T(8,128)(2,1)} custom-call(s32[1]{0:T(128)} %bitcast.10.x_ref, s32[128]{0:T(128)S(1)} %fusion.dest_ref, bf16[64,1024]{1,0:T(8,128)(2,1)S(1)} %get-tuple-element.31.grad_ref, bf16[32,128]{1,0:T(8,128)(2,1)S(1)} %get-tuple-element.33.bias_ref, bf16[4,4,8,64,128]{4,3,2,1,0:T(8,128)(2,1)S(1)} %bitcast.33), custom_call_target="tpu_custom_call" | custom-call | flops 33554432 | bytes 2097152 | tf_op jit(solution)/shard_map/hub_grad_terms/pallas_call | solution.py:254
  115.3 3.4 %collective-permute-start.5 = (bf16[33,32,128]{2,1,0:T(8,128)(2,1)}, bf16[33,32,128]{2,1,0:T(8,128)(2,1)}, u32[]{:S(2)}, u32[]{:S(2)}) collective-permute-start(bf16[33,32,128]{2,1,0:T(8,128)(2,1)} %hub_grad_terms.5), channel_id=1, source_target_pairs={{0,32},{32,64},{64,96},{96,0},{1,33},{33,65},{65,97},{97,1},{2,34}... | collective-permute-start | bytes 811016 | tf_op jit(solution)/shard_map/ppermute | solution.py:33
  118.7 3.1 %collective-permute-start.6 = (bf16[33,32,128]{2,1,0:T(8,128)(2,1)}, bf16[33,32,128]{2,1,0:T(8,128)(2,1)}, u32[]{:S(2)}, u32[]{:S(2)}) collective-permute-start(bf16[33,32,128]{2,1,0:T(8,128)(2,1)} %hub_grad_terms.6), channel_id=1, source_target_pairs={{0,64},{32,96},{64,0},{96,32},{1,65},{33,97},{65,1},{97,33},{2,66}... | collective-permute-start | bytes 811016 | tf_op jit(solution)/shard_map/ppermute | solution.py:33
  121.8 4.0 %collective-permute-start.7 = (bf16[33,32,128]{2,1,0:T(8,128)(2,1)}, bf16[33,32,128]{2,1,0:T(8,128)(2,1)}, u32[]{:S(2)}, u32[]{:S(2)}) collective-permute-start(bf16[33,32,128]{2,1,0:T(8,128)(2,1)} %hub_grad_terms.7), channel_id=1, source_target_pairs={{0,96},{32,0},{64,32},{96,64},{1,97},{33,1},{65,33},{97,65},{2,98}... | collective-permute-start | bytes 811016 | tf_op jit(solution)/shard_map/ppermute | solution.py:33
  125.8 1.7 hub_grad_terms.4.refs_0_
  127.5 0.7 copy-done.1
  128.2 6.6 %all-to-all-done.2.arrived_ref = bf16[128,24,128]{2,1,0:T(8,128)(2,1)S(1)} async-done(((bf16[128,24,128]{2,1,0:T(8,128)(2,1)}), bf16[128,24,128]{2,1,0:T(8,128)(2,1)S(1)}, u32[]{:S(2)}, u32[]{:S(2)}) %all-to-all-start.2) | async-done | bytes 786464 | tf_op jit(solution)/shard_map/all_to_all | solution.py:28
  135.0 4.3 %collective-permute-done.7.refs_3_ = bf16[33,32,128]{2,1,0:T(8,128)(2,1)} collective-permute-done((bf16[33,32,128]{2,1,0:T(8,128)(2,1)}, bf16[33,32,128]{2,1,0:T(8,128)(2,1)}, u32[]{:S(2)}, u32[]{:S(2)}) %collective-permute-start.7) | collective-permute-done | bytes 270368 | tf_op jit(solution)/shard_map/ppermute | solution.py:33
  139.3 1.0 copy-done.2
  140.2 2.0 %hub_grads_over_x.1 = bf16[32,48,128]{2,1,0:T(8,128)(2,1)} custom-call(bf16[33,32,128]{2,1,0:T(8,128)(2,1)S(1)} %copy-done.2, bf16[33,32,128]{2,1,0:T(8,128)(2,1)} %collective-permute-done.5.refs_1_, bf16[33,32,128]{2,1,0:T(8,128)(2,1)} %collective-permute-done.6.refs_2_, bf16[33,32,128]{2,1,0:T(8,128)(2,1)} %collective-permute-done.7.refs_3_, ...), custom_call_target="tpu_custom_call" | custom-call | flops 1048576 | bytes 2097152 | tf_op jit(solution)/shard_map/hub_grads_over_x/pallas_call | solution.py:407
  142.2 11.3 %all-to-all-start.3 = ((bf16[32,48,128]{2,1,0:T(8,128)(2,1)}), bf16[32,48,128]{2,1,0:T(8,128)(2,1)S(1)}, u32[]{:S(2)}, u32[]{:S(2)}) async-start(bf16[32,48,128]{2,1,0:T(8,128)(2,1)} %hub_grads_over_x.1), calls=%async_computation.3 | async-start | bytes 786432 | tf_op jit(solution)/shard_map/all_to_all | solution.py:28
  153.7 3.1 %tail_grads.1.base_ref = f32[64,1024]{1,0:T(8,128)} custom-call(s32[2,2048]{1,0:T(2,128)S(1)} %copy-done.11, bf16[128,24,128]{2,1,0:T(8,128)(2,1)S(1)} %all-to-all-done.2.arrived_ref, f32[64,1024]{1,0:T(8,128)S(1)} %fusion.2.direct_ref), custom_call_target="tpu_custom_call" | custom-call | flops 1073741824 | bytes 2097152 | tf_op jit(solution)/shard_map/tail_grads/pallas_call | solution.py:164
  156.8 13.4 %all-to-all-done.3.second_ref = bf16[32,48,128]{2,1,0:T(8,128)(2,1)S(1)} async-done(((bf16[32,48,128]{2,1,0:T(8,128)(2,1)}), bf16[32,48,128]{2,1,0:T(8,128)(2,1)S(1)}, u32[]{:S(2)}, u32[]{:S(2)}) %all-to-all-start.3) | async-done | bytes 393248 | tf_op jit(solution)/shard_map/all_to_all | solution.py:28
  170.3 1.6 gradients.1
  (58 shorter events, 3.2 us)
Async XLA Ops:
  0.6 22.9 %copy-start.5 = (bf16[64,1024]{1,0:T(8,128)(2,1)S(1)}, bf16[64,1024]{1,0:T(8,128)(2,1)}, u32[]{:S(2)}) copy-start(bf16[64,1024]{1,0:T(8,128)(2,1)} %source_ref.1) | copy-start | bytes 393220
  0.6 22.0 %copy-start.19 = (s32[1,128,32]{1,2,0:T(8,128)S(1)}, s32[1,128,32]{1,2,0:T(8,128)}, u32[]{:S(2)}) copy-start(s32[1,128,32]{1,2,0:T(8,128)} %param.19) | copy-start | bytes 49156
  2.2 28.0 %all-to-all-start = ((bf16[32,32,128]{2,1,0:T(8,128)(2,1)}), bf16[32,32,128]{2,1,0:T(8,128)(2,1)S(1)}, u32[]{:S(2)}, u32[]{:S(2)}) async-start(bf16[32,32,128]{2,1,0:T(8,128)(2,1)} %broadcast_in_dim.24), calls=%async_computation | async-start | bytes 524288 | tf_op jit(solution)/shard_map/all_to_all | solution.py:28
  19.4 8.9 %copy-start.10 = (s32[2,2048]{1,0:T(2,128)}, s32[2,2048]{1,0:T(2,128)S(1)}, u32[]{:S(2)}) copy-start(s32[2,2048]{1,0:T(2,128)S(1)} %reshape.44.index_ref) | copy-start | bytes 49156
  19.4 8.9 %collective-permute-start = (bf16[64,1536]{1,0:T(8,128)(2,1)S(1)}, bf16[64,1536]{1,0:T(8,128)(2,1)S(1)}, u32[]{:S(2)}, u32[]{:S(2)}) collective-permute-start(bf16[64,1536]{1,0:T(8,128)(2,1)S(1)} %pad_maximum_fusion.2), channel_id=1, source_target_pairs={{0,2},{2,0},{1,3},{3,1},{4,6},{6,4},{5,7},{7,5},{8,10},{10,8},{9,1... | collective-permute-start | bytes 589832 | tf_op jit(solution)/shard_map/ppermute | solution.py:33
  23.5 31.7 %copy-start.22 = (s32[4]{0:T(128)S(1)}, s32[4]{0:T(128)}, u32[]{:S(2)}) copy-start(s32[4]{0:T(128)} %constant.28.clone) | copy-start | bytes 52
  23.5 31.7 %copy-start.20 = (f32[64]{0:T(128)S(1)}, f32[64]{0:T(128)}, u32[]{:S(2)}) copy-start(f32[64]{0:T(128)} %param.23) | copy-start | bytes 772
  23.5 32.4 %copy-start.21 = (s32[1,128]{1,0:T(1,128)S(1)}, s32[1,128]{1,0:T(1,128)}, u32[]{:S(2)}) copy-start(s32[1,128]{1,0:T(1,128)} %param.15) | copy-start | bytes 1540
  23.5 34.3 %copy-start = (bf16[1,128,64,128]{3,2,1,0:T(8,128)(2,1)S(1)}, bf16[1,128,64,128]{3,2,1,0:T(8,128)(2,1)}, u32[]{:S(2)}) copy-start(bf16[1,128,64,128]{3,2,1,0:T(8,128)(2,1)} %param.14) | copy-start | bytes 6291460
  30.3 41.0 %all-to-all-start.1 = ((bf16[128,16,128]{2,1,0:T(8,128)(2,1)}), bf16[128,16,128]{2,1,0:T(8,128)(2,1)S(1)}, u32[]{:S(2)}, u32[]{:S(2)}) async-start(bf16[128,16,128]{2,1,0:T(8,128)(2,1)} %tail_rows_out.1), calls=%async_computation.1 | async-start | bytes 1048576 | tf_op jit(solution)/shard_map/all_to_all | solution.py:28
  43.3 14.5 %collective-permute-start.4 = (bf16[32,32,128]{2,1,0:T(8,128)(2,1)S(1)}, bf16[32,32,128]{2,1,0:T(8,128)(2,1)}, u32[]{:S(2)}, u32[]{:S(2)}) collective-permute-start(bf16[32,32,128]{2,1,0:T(8,128)(2,1)S(1)} %all-to-all-done.refs_0_), channel_id=1, source_target_pairs={{0,32},{32,64},{64,96},{96,0},{1,33},{33,65},{65,97},{97,1},{2,34}... | collective-permute-start | bytes 786440 | tf_op jit(solution)/shard_map/ppermute | solution.py:33
  46.7 14.3 %collective-permute-start.3 = (bf16[32,32,128]{2,1,0:T(8,128)(2,1)S(1)}, bf16[32,32,128]{2,1,0:T(8,128)(2,1)S(1)}, u32[]{:S(2)}, u32[]{:S(2)}) collective-permute-start(bf16[32,32,128]{2,1,0:T(8,128)(2,1)S(1)} %all-to-all-done.refs_0_), channel_id=1, source_target_pairs={{0,96},{32,0},{64,32},{96,64},{1,97},{33,1},{65,33},{97,65},{2,98}... | collective-permute-start | bytes 786440 | tf_op jit(solution)/shard_map/ppermute | solution.py:33
  49.2 15.4 %collective-permute-start.2 = (bf16[32,32,128]{2,1,0:T(8,128)(2,1)S(1)}, bf16[32,32,128]{2,1,0:T(8,128)(2,1)}, u32[]{:S(2)}, u32[]{:S(2)}) collective-permute-start(bf16[32,32,128]{2,1,0:T(8,128)(2,1)S(1)} %all-to-all-done.refs_0_), channel_id=1, source_target_pairs={{0,64},{32,96},{64,0},{96,32},{1,65},{33,97},{65,1},{97,33},{2,66}... | collective-permute-start | bytes 786440 | tf_op jit(solution)/shard_map/ppermute | solution.py:33
  53.2 14.5 %collective-permute-start.1 = (bf16[2,64,1536]{2,1,0:T(8,128)(2,1)S(1)}, bf16[2,64,1536]{2,1,0:T(8,128)(2,1)}, u32[]{:S(2)}, u32[]{:S(2)}) collective-permute-start(bf16[2,64,1536]{2,1,0:T(8,128)(2,1)S(1)} %pad_maximum_fusion.1.near_ref), channel_id=1, source_target_pairs={{0,1},{1,0},{2,3},{3,2},{4,5},{5,4},{6,7},{7,6},{8,9},{9,8},{10,11... | collective-permute-start | bytes 1179656 | tf_op jit(solution)/shard_map/ppermute | solution.py:33
  61.0 6.7 %copy-start.6 = (bf16[256,64]{0,1:T(8,128)(2,1)S(1)}, bf16[256,64]{0,1:T(8,128)(2,1)}, u32[]{:S(2)}) copy-start(bf16[256,64]{0,1:T(8,128)(2,1)} %param.21) | copy-start | bytes 98308
  61.0 6.7 %copy-start.7 = (f32[64,1]{1,0:T(8,128)S(1)}, f32[64,1]{1,0:T(8,128)}, u32[]{:S(2)}) copy-start(f32[64,1]{1,0:T(8,128)} %copy.24.bias_ref) | copy-start | bytes 772
  61.0 10.3 %copy-start.16 = (s32[1024]{0:T(1024)S(1)}, s32[1024]{0:T(1024)}, u32[]{:S(2)}) copy-start(s32[1024]{0:T(1024)} %param.20) | copy-start | bytes 12292
  69.3 0.8 copy-start.3
  70.1 0.6 copy-start.8
  70.7 0.6 copy-start.14
  71.3 0.7 copy-start.12
  72.0 10.0 %copy-start.18 = (bf16[256,64]{0,1:T(8,128)(2,1)S(1)}, bf16[256,64]{0,1:T(8,128)(2,1)}, u32[]{:S(2)}) copy-start(bf16[256,64]{0,1:T(8,128)(2,1)} %param.22) | copy-start | bytes 98308
  72.0 10.2 %copy-start.17 = (bf16[64,1024]{1,0:T(8,128)(2,1)S(1)}, bf16[64,1024]{1,0:T(8,128)(2,1)}, u32[]{:S(2)}) copy-start(bf16[64,1024]{1,0:T(8,128)(2,1)} %param.24) | copy-start | bytes 393220
  74.4 15.8 %copy-start.4 = (bf16[256,1024]{1,0:T(8,128)(2,1)S(1)}, bf16[256,1024]{1,0:T(8,128)(2,1)}, u32[]{:S(2)}) copy-start(bf16[256,1024]{1,0:T(8,128)(2,1)} %copy-done.3) | copy-start | bytes 1572868
  82.2 8.6 %copy-start.13 = (s32[2,2048]{1,0:T(2,128)S(1)}, s32[2,2048]{1,0:T(2,128)}, u32[]{:S(2)}) copy-start(s32[2,2048]{1,0:T(2,128)} %reshape.45.index_ref) | copy-start | bytes 49156
  82.2 8.6 %copy-start.15 = (bf16[64,256]{1,0:T(8,128)(2,1)S(1)}, bf16[64,256]{1,0:T(8,128)(2,1)}, u32[]{:S(2)}) copy-start(bf16[64,256]{1,0:T(8,128)(2,1)} %copy-done.14) | copy-start | bytes 98308
  93.0 41.8 %all-to-all-start.2 = ((bf16[128,24,128]{2,1,0:T(8,128)(2,1)}), bf16[128,24,128]{2,1,0:T(8,128)(2,1)S(1)}, u32[]{:S(2)}, u32[]{:S(2)}) async-start(bf16[128,24,128]{2,1,0:T(8,128)(2,1)} %pad_maximum_fusion), calls=%async_computation.2 | async-start | bytes 1572864 | tf_op jit(solution)/shard_map/all_to_all | solution.py:28
  115.3 19.6 %collective-permute-start.5 = (bf16[33,32,128]{2,1,0:T(8,128)(2,1)}, bf16[33,32,128]{2,1,0:T(8,128)(2,1)}, u32[]{:S(2)}, u32[]{:S(2)}) collective-permute-start(bf16[33,32,128]{2,1,0:T(8,128)(2,1)} %hub_grad_terms.5), channel_id=1, source_target_pairs={{0,32},{32,64},{64,96},{96,0},{1,33},{33,65},{65,97},{97,1},{2,34}... | collective-permute-start | bytes 811016 | tf_op jit(solution)/shard_map/ppermute | solution.py:33
  118.7 16.3 %collective-permute-start.6 = (bf16[33,32,128]{2,1,0:T(8,128)(2,1)}, bf16[33,32,128]{2,1,0:T(8,128)(2,1)}, u32[]{:S(2)}, u32[]{:S(2)}) collective-permute-start(bf16[33,32,128]{2,1,0:T(8,128)(2,1)} %hub_grad_terms.6), channel_id=1, source_target_pairs={{0,64},{32,96},{64,0},{96,32},{1,65},{33,97},{65,1},{97,33},{2,66}... | collective-permute-start | bytes 811016 | tf_op jit(solution)/shard_map/ppermute | solution.py:33
  121.8 17.5 %collective-permute-start.7 = (bf16[33,32,128]{2,1,0:T(8,128)(2,1)}, bf16[33,32,128]{2,1,0:T(8,128)(2,1)}, u32[]{:S(2)}, u32[]{:S(2)}) collective-permute-start(bf16[33,32,128]{2,1,0:T(8,128)(2,1)} %hub_grad_terms.7), channel_id=1, source_target_pairs={{0,96},{32,0},{64,32},{96,64},{1,97},{33,1},{65,33},{97,65},{2,98}... | collective-permute-start | bytes 811016 | tf_op jit(solution)/shard_map/ppermute | solution.py:33
  127.5 0.7 copy-start.1
  128.2 25.3 %copy-start.9 = (bf16[64,256]{1,0:T(8,128)(2,1)S(1)}, bf16[64,256]{1,0:T(8,128)(2,1)}, u32[]{:S(2)}) copy-start(bf16[64,256]{1,0:T(8,128)(2,1)} %copy-done.8) | copy-start | bytes 98308
  134.8 18.9 %copy-start.11 = (s32[2,2048]{1,0:T(2,128)S(1)}, s32[2,2048]{1,0:T(2,128)}, u32[]{:S(2)}) copy-start(s32[2,2048]{1,0:T(2,128)} %copy-done.10) | copy-start | bytes 49156
  139.3 1.0 copy-start.2
  142.2 28.0 %all-to-all-start.3 = ((bf16[32,48,128]{2,1,0:T(8,128)(2,1)}), bf16[32,48,128]{2,1,0:T(8,128)(2,1)S(1)}, u32[]{:S(2)}, u32[]{:S(2)}) async-start(bf16[32,48,128]{2,1,0:T(8,128)(2,1)} %hub_grads_over_x.1), calls=%async_computation.3 | async-start | bytes 786432 | tf_op jit(solution)/shard_map/all_to_all | solution.py:28

commit v5 on v3

v5 whole, which is shorter than its diff:
```python
from functools import partial

import jax
import jax.numpy as jnp
from jax import lax
from jax.experimental import pallas as pl
from jax.experimental.pallas import tpu as pltpu
from jax.sharding import Mesh
from jax.sharding import PartitionSpec as P

BF = jnp.bfloat16
F32 = jnp.float32
BOTH_ROWS = (((0,), (0,)), ((), ()))
BOTH_COLS = (((1,), (1,)), ((), ()))
DOM = ("yh", "x", "z")
PLANE = ("yh", "z")
REP = ("yl", "core")
SMEM = pl.BlockSpec(memory_space=pltpu.SMEM)
VMEM = pl.BlockSpec(memory_space=pltpu.VMEM)
MIB = 1024 * 1024
VMEM_LIMIT = 16 * MIB


def mm(a, b, dims):
    return lax.dot_general(a, b, dims, preferred_element_type=F32)


def swap(pieces, axis):
    return lax.all_to_all(pieces, axis, split_axis=0, concat_axis=0, tiled=True)


def shift(values, axis, step):
    size = lax.axis_size(axis)
    return lax.ppermute(values, axis, [(i, (i + step) % size) for i in range(size)])


def call(kernel, out_shape, in_specs, scratch, name, flops, mib):
    outs = VMEM if isinstance(out_shape, jax.ShapeDtypeStruct) else [VMEM] * len(out_shape)
    return pl.pallas_call(
        kernel,
        out_shape=out_shape,
        in_specs=in_specs,
        out_specs=outs,
        scratch_shapes=scratch,
        compiler_params=pltpu.CompilerParams(vmem_limit_bytes=VMEM_LIMIT),
        cost_estimate=pl.CostEstimate(flops=flops, bytes_accessed=mib * MIB, transcendentals=0),
        name=name,
    )


def slot_rows(index):
    parts, slots = index.shape
    return index.reshape(parts, 2, slots // 2).transpose(1, 0, 2).reshape(2, -1)


def pick_slots(index_ref, source, step):
    width, nodes = source.shape
    low_size = 256
    high_size = nodes // low_size
    split = jnp.concatenate(
        [source[:, i * low_size : (i + 1) * low_size] for i in range(high_size)], axis=0
    )
    low_ids = lax.broadcasted_iota(jnp.int32, (low_size, step), 0)
    for start in range(0, index_ref.shape[1], step):
        halves = []
        for h in range(2):
            index = index_ref[h : h + 1, start : start + step]
            hits = jnp.where(low_ids == (index & (low_size - 1)), 1.0, 0.0).astype(BF)
            found = jnp.dot(split, hits, preferred_element_type=F32)
            high = jnp.broadcast_to(index >> 8, (width, step))
            kept = jnp.zeros((width, step), F32)
            for i in range(high_size):
                kept = jnp.where(high == i, found[i * width : (i + 1) * width], kept)
            halves.append(kept)
        yield start, jnp.concatenate(halves, axis=0).T


def gather_kernel(index_ref, source_ref, out_ref):
    rows, step = out_ref.shape[1], 256
    for start, block in pick_slots(index_ref, source_ref[...], step):
        first = start // rows
        out_ref[first : first + step // rows] = block.reshape(-1, rows, 128).astype(BF)


def gather_slots(index, source, parts, slots):
    return call(
        gather_kernel,
        jax.ShapeDtypeStruct((parts, slots // 2, 128), BF),
        [VMEM, VMEM],
        [],
        "tail_rows_out",
        2 * parts * slots * 256 * 256,
        2,
    )(index, source)


def layer_kernel(sizes, place_ref, index_ref, degree_ref, *refs):
    mixed_ref, feat_ref, pre_ref, cot_ref, w_ref, neigh_ref, *out_refs = refs
    output_ref, d_ref, grad_ref, send_ref, bias_ref, pre_full = out_refs
    x_size, z_size = sizes
    width = output_ref.shape[0]
    full = mixed_ref.shape[0]
    half = full // 2
    mixed = mixed_ref[...]
    for first in range(0, full, width):
        at = slice(first, first + width)
        pre = pre_ref[at] + jnp.dot(w_ref[at], mixed, preferred_element_type=F32)
        sigma = jax.nn.sigmoid(pre)
        pre_full[at] = pre * sigma
        slope = sigma * (1.0 + pre * (1.0 - sigma))
        d_ref[at] = (cot_ref[at].astype(F32) * slope).astype(BF)
    own = pl.ds(pl.multiple_of(place_ref[0] * width, width), width)
    output_ref[...] = pre_full[own].astype(BF)
    d_pre = d_ref[own]

    made = []
    for source in (feat_ref[...], mixed):
        grad = mm(source, d_pre, BOTH_COLS)
        grad = jnp.concatenate([grad[:half], grad[half:]], axis=1)
        made.append(grad.reshape(-1, z_size // 2, 16, 128))
    made = jnp.concatenate(made, axis=0)
    bias = mm(jnp.ones((bias_ref.shape[0], d_pre.shape[1]), BF), d_pre, BOTH_COLS)
    bias = jnp.concatenate([bias, bias], axis=1)
    high = bias.astype(BF).astype(F32)
    row = lax.broadcasted_iota(jnp.int32, bias.shape, 0)
    bias_ref[...] = jnp.where(row == 0, high, jnp.where(row == 1, bias - high, 0.0)).astype(BF)

    grad = jnp.dot(neigh_ref[...], d_ref[...], preferred_element_type=F32).astype(BF)
    grad_ref[...] = grad
    scaled = (grad.astype(F32) / degree_ref[...].astype(F32)).astype(BF)
    rows = (send_ref.shape[1] - 16) // 2
    step = 256
    for start, block in pick_slots(index_ref, scaled, step):
        block = block.reshape(-1, 2, rows, 128)
        count = block.shape[0]
        first = start // (2 * rows)
        weight = made[first // (x_size * z_size // 2)]
        weight = jnp.concatenate([weight] * (count // weight.shape[0]), axis=0)
        block = jnp.concatenate([block[:, 0], weight[:, :8], block[:, 1], weight[:, 8:]], axis=1)
        send_ref[first : first + count] = block.astype(BF)


def layer(place, index, degree, mixed, feat, pre, cot, w_all, neigh_rows, sizes, parts, slots):
    full, nodes = mixed.shape
    width = neigh_rows.shape[0]
    return call(
        partial(layer_kernel, sizes),
        [
            jax.ShapeDtypeStruct((width, nodes), BF),
            jax.ShapeDtypeStruct((full, nodes), BF),
            jax.ShapeDtypeStruct((width, nodes), BF),
            jax.ShapeDtypeStruct((parts // 2, slots + 16, 128), BF),
            jax.ShapeDtypeStruct((width // 2, 128), BF),
        ],
        [SMEM] + [VMEM] * 8,
        [pltpu.VMEM((full, nodes), F32)],
        "layer",
        2 * parts * slots * 256 * 256,
        4,
    )(place, index, degree, mixed, feat, pre, cot, w_all, neigh_rows)


def sum_slots(index_ref, arrived_ref, rows, start, size):
    parts = arrived_ref.shape[0]
    flat = arrived_ref[:, :rows, :].reshape(parts * rows, 128)
    ids = lax.broadcasted_iota(jnp.int32, (size, parts * rows), 0) + start
    sums = []
    for h in range(2):
        hits = jnp.where(ids == index_ref[h : h + 1, :], 1.0, 0.0).astype(BF)
        sums.append(jnp.dot(hits, flat, preferred_element_type=F32))
    return sums[0].T[:64] + sums[1].T[64:]


def mixed_kernel(rows, index_ref, arrived_ref, hub_ref, degree_ref, out_ref):
    size = 256
    for start in range(0, out_ref.shape[1], size):
        at = slice(start, start + size)
        tail = sum_slots(index_ref, arrived_ref, rows, start, size)
        out_ref[:, at] = (hub_ref[:, at] + tail / degree_ref[:, at].astype(F32)).astype(BF)


def mixed_sums(index, arrived, hub_sum, degree):
    parts, rows, _ = arrived.shape
    width, nodes = hub_sum.shape
    return call(
        partial(mixed_kernel, rows),
        jax.ShapeDtypeStruct((width, nodes), BF),
        [VMEM] * 4,
        [],
        "mixed",
        4 * parts * rows * nodes * 128,
        2,
    )(index, arrived, hub_sum, degree)


def tail_grad_kernel(rows, index_ref, arrived_ref, weight_ref, d_ref, out_ref):
    size = 256
    for start in range(0, out_ref.shape[1], size):
        at = slice(start, start + size)
        tail = sum_slots(index_ref, arrived_ref, rows, start, size)
        direct = jnp.dot(weight_ref[...], d_ref[:, at], preferred_element_type=F32)
        out_ref[:, at] = direct + tail


def tail_grads(index, arrived, weight, d_full, rows):
    parts = arrived.shape[0]
    width, nodes = weight.shape[0], d_full.shape[1]
    return call(
        partial(tail_grad_kernel, rows),
        jax.ShapeDtypeStruct((width, nodes), F32),
        [VMEM] * 4,
        [],
        "tail_grads",
        4 * parts * rows * nodes * 128,
        2,
    )(index, arrived, weight, d_full)


def arrange_kernel(place_ref, near_ref, far_ref, *refs):
    feat_ref, cot_ref, pre_ref, w_ref, self_ref, neigh_ref, wide = refs
    full, nodes = pre_ref.shape
    width = self_ref.shape[0]
    for i in range(4):
        block = (near_ref, far_ref)[i // 2].at[i % 2]
        at = pl.ds(pl.multiple_of(place_ref[i] * width, width), width)
        feat_ref[at, :] = block[:, :nodes]
        cot_ref[at, :] = block[:, nodes : 2 * nodes]
        wide[at, :] = block[:, 2 * nodes :].astype(F32)
    bias = jnp.sum(wide[:, 2 * full : 2 * full + 128], axis=1, keepdims=True)
    w_self = wide[:, :full].astype(BF)
    w_ref[...] = wide[:, full : 2 * full].astype(BF)
    pre_ref[...] = jnp.dot(w_self, feat_ref[...], preferred_element_type=F32) + bias
    own = place_ref[0]
    for first, out_ref in ((0, self_ref), (full, neigh_ref)):
        rows = wide[:, first : first + width]
        for k in range(1, 4):
            at = first + k * width
            rows = jnp.where(own == k, wide[:, at : at + width], rows)
        out_ref[...] = rows.T.astype(BF)


def arrange(place, near, far, nodes, full):
    width = near.shape[1]
    return call(
        arrange_kernel,
        [
            jax.ShapeDtypeStruct((full, nodes), BF),
            jax.ShapeDtypeStruct((full, nodes), BF),
            jax.ShapeDtypeStruct((full, nodes), F32),
            jax.ShapeDtypeStruct((full, full), BF),
            jax.ShapeDtypeStruct((width, full), BF),
            jax.ShapeDtypeStruct((width, full), BF),
        ],
        [SMEM] + [VMEM] * 2,
        [pltpu.VMEM((full, 2 * full + 128), F32)],
        "own_columns",
        2 * full * full * nodes,
        4,
    )(place, near, far)


def three_terms(values):
    high = lax.reduce_precision(values, 8, 7)
    rest = values - high
    middle = lax.reduce_precision(rest, 8, 7)
    return [high.astype(BF), middle.astype(BF), (rest - middle).astype(BF)]


def tile_index(x_ref, k, sizes, yh, z, sign):
    x_size, z_size = sizes
    x = lax.rem(x_ref[0] + (sign * k) % x_size, x_size)
    return (yh * x_size + x) * z_size + z


def fold_kernel(steps, sizes, has_base, x_ref, dest_ref, *refs):
    hub_refs, (tile_ref, *base_ref, out_ref, total) = refs[: len(steps)], refs[len(steps) :]
    blocks = total.shape[0] - 1
    half = hub_refs[0].shape[1]
    lanes = lax.broadcasted_iota(jnp.int32, (half, 128), 1)
    first = (lanes < 64).astype(F32).astype(BF)
    second = (lanes >= 64).astype(F32).astype(BF)
    for b in range(blocks):
        at = slice(b * 128, (b + 1) * 128)
        total[b] = base_ref[0][:, at] if has_base else jnp.zeros_like(total[b])
    total[blocks] = jnp.zeros_like(total[blocks])
    z_size = sizes[1]
    for k, hub_ref in zip(steps, hub_refs):

        @pl.loop(0, hub_ref.shape[0] // z_size)
        def _(yh):
            for z in range(z_size):
                tile = tile_index(x_ref, k, sizes, yh, z, -1)
                rows = hub_ref[yh * z_size + z]
                weights = tile_ref[tile]
                product = jnp.dot(
                    jnp.concatenate([rows * first, rows * second], axis=0),
                    jnp.concatenate([weights, weights], axis=0),
                    preferred_element_type=F32,
                )
                dest = dest_ref[tile]
                total[dest] = total[dest] + product

    for b in range(blocks):
        out_ref[:, b * 128 : (b + 1) * 128] = total[b]


def fold_hubs(x_index, dest, hubs, steps, tiles, sizes, blocks, base):
    width = 2 * hubs[0].shape[1]
    bases = [] if base is None else [base]
    return call(
        partial(fold_kernel, steps, sizes, base is not None),
        jax.ShapeDtypeStruct((width, blocks * 128), F32),
        [SMEM, SMEM] + [VMEM] * (len(hubs) + 1 + len(bases)),
        [pltpu.VMEM((blocks + 1, width, 128), F32)],
        "hub_sums",
        tiles.size * width * len(hubs),
        4,
    )(x_index, dest, *hubs, tiles, *bases)


def hub_grad_kernel(steps, sizes, x_ref, dest_ref, grad_ref, bias_ref, tile_ref, *refs):
    *out_refs, blocked = refs
    blocks = blocked.shape[0] - 1
    for b in range(blocks):
        blocked[b] = grad_ref[:, b * 128 : (b + 1) * 128]
    blocked[blocks] = jnp.zeros_like(blocked[blocks])
    count, half, _ = out_refs[0].shape
    first = lax.broadcasted_iota(jnp.int32, (half, 128), 1) < 64
    z_size = sizes[1]
    for k, out_ref in zip(steps, out_refs):
        out_ref[count - 1] = bias_ref[...]

        @pl.loop(0, count // z_size)
        def _(yh):
            for z in range(z_size):
                tile = tile_index(x_ref, k, sizes, yh, z, 1)
                weights = tile_ref[tile]
                product = mm(
                    blocked[dest_ref[tile]],
                    jnp.concatenate([weights, weights], axis=0),
                    BOTH_COLS,
                )
                out_ref[yh * z_size + z] = jnp.where(
                    first, product[:half], product[half:]
                ).astype(BF)


def hub_grad_terms(x_index, dest, grad, bias, tiles, steps, sizes, blocks):
    width = grad.shape[0]
    shape = (tiles.shape[0] // sizes[0] + 1, width // 2, 128)
    return call(
        partial(hub_grad_kernel, steps, sizes),
        [jax.ShapeDtypeStruct(shape, BF) for _ in steps],
        [SMEM, SMEM, VMEM, VMEM, VMEM],
        [pltpu.VMEM((blocks + 1, width, 128), BF)],
        "hub_grad_terms",
        tiles.size * width * len(steps),
        4,
    )(x_index, dest, grad, bias, tiles)


def pack_kernel(*refs):
    *term_refs, sum_ref, out_ref = refs
    count, half = out_ref.shape[0], term_refs[0].shape[1]
    total = term_refs[0][...].astype(F32)
    for ref in term_refs[1:]:
        total = total + ref[...].astype(F32)
    out_ref[:, :half] = total[:count].astype(BF)
    bias = total[count]
    bias = jnp.broadcast_to(bias[0:1] + bias[1:2], (8, 128))
    high = bias.astype(BF).astype(F32)
    row = lax.broadcasted_iota(jnp.int32, (8, 128), 0)
    bias = jnp.where(row == 0, high, jnp.where(row == 1, bias - high, 0.0))
    extra = jnp.concatenate([sum_ref[...], bias], axis=0).astype(BF)
    out_ref[:, half:] = jnp.broadcast_to(extra[None], (count, 16, 128))


def pack_rows(terms, sums):
    count, half, _ = terms[0].shape
    return call(
        pack_kernel,
        jax.ShapeDtypeStruct((count - 1, half + 16, 128), BF),
        [VMEM] * (len(terms) + 1),
        [],
        "hub_grads_over_x",
        MIB,
        2,
    )(*terms, sums)


def final_kernel(second_ref, base_ref, out_ref, self_ref, neigh_ref, bias_ref):
    half = out_ref.shape[0] // 2
    hub = jnp.sum(second_ref[:, :half].astype(F32), axis=0)
    hub = jnp.concatenate([hub, pltpu.roll(hub, 64, 1)], axis=0)
    lane = lax.broadcasted_iota(jnp.int32, hub.shape, 1)
    out_ref[...] = base_ref[...] + jnp.where(lane < 64, hub, 0.0)
    extra = second_ref[:, half:].astype(F32)
    grads = extra[:, :8].reshape(-1, 128)
    rows = grads.shape[0] // 2
    for place, ref in enumerate((self_ref, neigh_ref)):
        turned = grads[place * rows : (place + 1) * rows].T
        ref[...] = jnp.concatenate([turned[:64], turned[64:]], axis=1)
    bias = jnp.sum(extra[:, 8:], axis=0)
    bias_ref[...] = (bias[0:1] + bias[1:2])[:, : bias_ref.shape[1]]


def finish(second, base, full):
    width, nodes = base.shape
    hub_part = pl.BlockSpec((width, 128), lambda i: (0, 0))
    return pl.pallas_call(
        final_kernel,
        out_shape=[
            jax.ShapeDtypeStruct((width, nodes), F32),
            jax.ShapeDtypeStruct((width, full), F32),
            jax.ShapeDtypeStruct((width, full), F32),
            jax.ShapeDtypeStruct((1, width), F32),
        ],
        grid=(1,),
        in_specs=[pl.BlockSpec(second.shape, lambda i: (0, 0, 0)), hub_part],
        out_specs=[hub_part]
        + [pl.BlockSpec((width, full), lambda i: (0, 0))] * 2
        + [pl.BlockSpec((1, width), lambda i: (0, 0))],
        input_output_aliases={1: 0},
        compiler_params=pltpu.CompilerParams(vmem_limit_bytes=VMEM_LIMIT),
        cost_estimate=pl.CostEstimate(flops=MIB, bytes_accessed=MIB, transcendentals=0),
        name="gradients",
    )(second, base)


def local(
    features,
    hub_weight,
    hub_block,
    hub_mask,
    tail_rows,
    tail_count,
    tail_target,
    degree,
    w_self,
    w_neigh,
    out_bias,
    cotangent,
):
    width, nodes = features.shape
    parts, hubs, tile_len = hub_weight.shape[1:]
    slots = tail_rows.shape[2]
    half_width = width // 2
    blocks = nodes // tile_len
    full_width = w_self.shape[0]
    x_size, z_size = lax.axis_size("x"), lax.axis_size("z")
    sizes = (x_size, z_size)
    plane = parts // x_size
    x_index = lax.axis_index("x")[None]
    tiles = hub_weight[0]
    hub_dest = jnp.where(hub_mask[0] > 0, hub_block[0], blocks)
    degree = degree[None, :]

    hub_piece = jnp.concatenate([features[:half_width, :hubs], features[half_width:, :hubs]], axis=1)
    hub_send = jnp.broadcast_to(hub_piece[None], (plane, half_width, 128))
    hub_plane = swap(hub_send, PLANE)

    slot_live = jnp.arange(slots, dtype=jnp.int32)[None, :] < tail_count[0][:, None]
    send_index = slot_rows(jnp.where(slot_live, tail_rows[0], -1))
    recv_index = slot_rows(tail_target[0])
    bias_terms = jnp.stack(three_terms(out_bias), axis=1)
    bias_terms = jnp.pad(bias_terms, ((0, 0), (0, 128 - bias_terms.shape[1])))
    own = jnp.concatenate([features, cotangent, w_self.T, w_neigh.T, bias_terms], axis=1)
    own, send_index, _ = lax.optimization_barrier((own, send_index, hub_send))
    near = jnp.stack([own, shift(own, "yl", 1)])
    tail_send = gather_slots(send_index, features, parts, slots)
    hub_plane, tail_send, recv_index, near = lax.optimization_barrier(
        (hub_plane, tail_send, recv_index, near)
    )
    arrived = swap(tail_send, DOM)
    hub_all = [hub_plane] + [shift(hub_plane, "x", k) for k in range(1, x_size)]
    far = shift(near, "core", 1)
    place = lax.axis_index(REP) ^ jnp.array([0, 2, 1, 3], jnp.int32)
    own_columns = arrange(place, near, far, nodes, full_width)

    fold = partial(fold_hubs, x_index, hub_dest, tiles=tiles, sizes=sizes, blocks=blocks)
    hub_sum = fold(hub_all[:2], (0, 1), base=None)
    hub_sum, own_columns = lax.optimization_barrier((hub_sum, own_columns))
    full_feat, full_cot, pre_self, w_neigh_all, w_self_rows, w_neigh_rows = own_columns
    hub_sum = fold(hub_all[2:], (2, 3), base=hub_sum)
    mixed = mixed_sums(recv_index, arrived, hub_sum, degree)
    full_mixed = lax.all_gather(mixed, REP, axis=0, tiled=True)

    output, d_full, mixed_grad, tail_back, bias_rows = layer(
        place,
        recv_index,
        degree,
        full_mixed,
        full_feat,
        pre_self,
        full_cot,
        w_neigh_all,
        w_neigh_rows,
        sizes,
        parts,
        slots,
    )
    tail_len = slots // 2
    first = swap(tail_back.reshape(parts, tail_len + 8, 128), DOM)

    hub_terms = partial(
        hub_grad_terms, x_index, hub_dest, mixed_grad, bias_rows, tiles, sizes=sizes, blocks=blocks
    )
    far_steps = (2, 1, 3)
    terms = [shift(term, "x", k) for term, k in zip(hub_terms(far_steps), far_steps)]
    terms = list(hub_terms((0,))) + terms
    sums = jnp.sum(first[:, tail_len:].astype(F32), axis=0)
    second = swap(pack_rows(terms, sums), PLANE)

    base = tail_grads(send_index, first, w_self_rows, d_full, tail_len)
    grad_features, grad_w_self, grad_w_neigh, grad_bias = finish(second, base, full_width)
    return (output, grad_features, grad_w_self.T, grad_w_neigh.T, grad_bias[0])


def solution(mesh):
    grid = (4, 4, mesh.shape["dom"] // 16, 2, 2)
    parted = Mesh(mesh.devices.reshape(grid), DOM + REP)
    in_specs = (
        P(REP, DOM),
        P(DOM, None, None, None),
        P(DOM, None),
        P(DOM, None),
        P(DOM, None, None),
        P(DOM, None),
        P(DOM, None, None),
        P(DOM),
        P(None, REP),
        P(None, REP),
        P(REP),
        P(REP, DOM),
    )
    out_specs = (P(REP, DOM), P(REP, DOM), P(None, REP), P(None, REP), P(REP))
    return jax.shard_map(local, mesh=parted, in_specs=in_specs, out_specs=out_specs, check_vma=False)
```

time: 188 us -> 172 us (0.915)
  the two profiles are of different devices: /device:TPU:8 before, /device:TPU:16 now
where the time goes in v5:
time: 172 us; the launch traced here: 171 us
  starting transfers between devices  84.9 us (49%)
  waiting for transfers between devices  31.9 us (19%)
  Pallas kernels  27.5 us (16%)
  local copies, waits for them, and re-layouts  15.8 us (9%)
  blocking collectives  7.07 us (4%)
  other arithmetic  2.69 us (2%)
    all_to_all x4, starting transfers between devices, swap(): return lax.all_to_all(pieces, axis, split_axis=0, concat_axis=0, tiled=True)  56.1 us
    ppermute x8, starting transfers between devices, shift(): lax.ppermute(values, axis, [(i, (i + step) % size) for i in range(size)])  28.9 us
    all_to_all x4, waiting for transfers between devices, swap(): return lax.all_to_all(pieces, axis, split_axis=0, concat_axis=0, tiled=True)  26.3 us
    unnamed x54, local copies, waits for them, and re-layouts  13.1 us
    all_gather x1, blocking collectives, local(): full_mixed = lax.all_gather(mixed, REP, axis=0, tiled=True)  7.07 us
    pallas_call x2, Pallas kernels, hub_grad_terms(): call(partial(hub_grad_kernel, steps, sizes), [jax.ShapeDtypeStruct(shape,...  6.35 us
    ppermute x8, waiting for transfers between devices, shift(): lax.ppermute(values, axis, [(i, (i + step) % size) for i in range(size)])  5.57 us
    pallas_call x2, Pallas kernels, fold_hubs(): call(partial(fold_kernel, steps, sizes, base is not None), jax.ShapeDtype...  5.47 us
  transfers between devices with their start and end apart: 12, of which 5 were waited for; matrix products, arithmetic and copies ran while one was open for 1% of the time, Pallas kernels for 10%

profile of v5, /device:TPU:16, one launch (start us, length us, event | category | flops | bytes accessed | tf_op | source)
XLA Modules:
  0.0 171.0 jit_solution(2416905379207670848)
XLA Ops:
  0.7 1.0 constant_dynamic-update-slice_fusion.1
  1.6 0.7 fusion.5
  3.1 0.8 copy.30
  4.0 0.7 select_bitcast_fusion
  4.8 0.9 constant_dynamic-update-slice_fusion
  5.7 0.8 bitcast_dynamic-update-slice_fusion.1
  6.5 0.8 bitcast_dynamic-update-slice_fusion
  7.4 0.7 broadcast_in_dim.21
  8.1 3.5 %collective-permute-start = (bf16[64,2688]{1,0:T(8,128)(2,1)S(1)}, bf16[64,2688]{1,0:T(8,128)(2,1)}, u32[]{:S(2)}, u32[]{:S(2)}) collective-permute-start(bf16[64,2688]{1,0:T(8,128)(2,1)S(1)} %pad_dynamic-update-slice_fusion), channel_id=1, source_target_pairs={{0,2},{2,0},{1,3},{3,1},{4,6},{6,4},{5,7},{7,5},{8,10},{10,8},{9,1... | collective-permute-start | bytes 1032200 | tf_op jit(solution)/shard_map/ppermute | solution.py:34
  11.6 15.2 %all-to-all-start = ((bf16[32,32,128]{2,1,0:T(8,128)(2,1)}), bf16[32,32,128]{2,1,0:T(8,128)(2,1)S(1)}, u32[]{:S(2)}, u32[]{:S(2)}) async-start(bf16[32,32,128]{2,1,0:T(8,128)(2,1)} %broadcast_in_dim.21), calls=%async_computation | async-start | bytes 524288 | tf_op jit(solution)/shard_map/all_to_all | solution.py:29
  27.1 1.0 tail_rows_out.1
  28.1 0.8 copy-done.4
  28.9 1.1 pad_maximum_fusion.near_ref
  30.0 8.3 %all-to-all-done.refs_0_ = bf16[32,32,128]{2,1,0:T(8,128)(2,1)S(1)} async-done(((bf16[32,32,128]{2,1,0:T(8,128)(2,1)}), bf16[32,32,128]{2,1,0:T(8,128)(2,1)S(1)}, u32[]{:S(2)}, u32[]{:S(2)}) %all-to-all-start) | async-done | bytes 262176 | tf_op jit(solution)/shard_map/all_to_all | solution.py:29
  38.2 11.1 %all-to-all-start.1 = ((bf16[128,16,128]{2,1,0:T(8,128)(2,1)}), bf16[128,16,128]{2,1,0:T(8,128)(2,1)}, u32[]{:S(2)}, u32[]{:S(2)}) async-start(bf16[128,16,128]{2,1,0:T(8,128)(2,1)} %copy-done.4), calls=%async_computation.1 | async-start | bytes 1048576 | tf_op jit(solution)/shard_map/all_to_all | solution.py:29
  49.3 1.9 %collective-permute-start.4 = (bf16[2,64,2688]{2,1,0:T(8,128)(2,1)S(1)}, bf16[2,64,2688]{2,1,0:T(8,128)(2,1)}, u32[]{:S(2)}, u32[]{:S(2)}) collective-permute-start(bf16[2,64,2688]{2,1,0:T(8,128)(2,1)S(1)} %pad_maximum_fusion.near_ref), channel_id=1, source_target_pairs={{0,1},{1,0},{2,3},{3,2},{4,5},{5,4},{6,7},{7,6},{8,9},{9,8},{10,11... | collective-permute-start | bytes 2064392 | tf_op jit(solution)/shard_map/ppermute | solution.py:34
  51.2 3.4 %collective-permute-start.3 = (bf16[32,32,128]{2,1,0:T(8,128)(2,1)S(1)}, bf16[32,32,128]{2,1,0:T(8,128)(2,1)}, u32[]{:S(2)}, u32[]{:S(2)}) collective-permute-start(bf16[32,32,128]{2,1,0:T(8,128)(2,1)S(1)} %all-to-all-done.refs_0_), channel_id=1, source_target_pairs={{0,32},{32,64},{64,96},{96,0},{1,33},{33,65},{65,97},{97,1},{2,34}... | collective-permute-start | bytes 786440 | tf_op jit(solution)/shard_map/ppermute | solution.py:34
  54.7 4.7 %collective-permute-start.1 = (bf16[32,32,128]{2,1,0:T(8,128)(2,1)S(1)}, bf16[32,32,128]{2,1,0:T(8,128)(2,1)S(1)}, u32[]{:S(2)}, u32[]{:S(2)}) collective-permute-start(bf16[32,32,128]{2,1,0:T(8,128)(2,1)S(1)} %all-to-all-done.refs_0_), channel_id=1, source_target_pairs={{0,64},{32,96},{64,0},{96,32},{1,65},{33,97},{65,1},{97,33},{2,66}... | collective-permute-start | bytes 786440 | tf_op jit(solution)/shard_map/ppermute | solution.py:34
  59.4 3.3 %collective-permute-start.2 = (bf16[32,32,128]{2,1,0:T(8,128)(2,1)S(1)}, bf16[32,32,128]{2,1,0:T(8,128)(2,1)}, u32[]{:S(2)}, u32[]{:S(2)}) collective-permute-start(bf16[32,32,128]{2,1,0:T(8,128)(2,1)S(1)} %all-to-all-done.refs_0_), channel_id=1, source_target_pairs={{0,96},{32,0},{64,32},{96,64},{1,97},{33,1},{65,33},{97,65},{2,98}... | collective-permute-start | bytes 786440 | tf_op jit(solution)/shard_map/ppermute | solution.py:34
  62.8 3.8 %collective-permute-done.3.refs_1_ = bf16[32,32,128]{2,1,0:T(8,128)(2,1)} collective-permute-done((bf16[32,32,128]{2,1,0:T(8,128)(2,1)S(1)}, bf16[32,32,128]{2,1,0:T(8,128)(2,1)}, u32[]{:S(2)}, u32[]{:S(2)}) %collective-permute-start.3) | collective-permute-done | bytes 262176 | tf_op jit(solution)/shard_map/ppermute | solution.py:34
  66.5 2.7 %hub_sums.2.refs_3_ = f32[64,1024]{1,0:T(8,128)S(1)} custom-call(s32[1]{0:T(128)} %bitcast.13.x_ref, s32[128]{0:T(128)S(1)} %fusion.4.dest_ref, bf16[32,32,128]{2,1,0:T(8,128)(2,1)S(1)} %all-to-all-done.refs_0_, bf16[32,32,128]{2,1,0:T(8,128)(2,1)} %collective-permute-done.3.refs_1_, bf16[128,64,128]{2,1,0:T(8,128)(2,1)S(1)} %bitcast.27), custom_call_target="tpu_custom_call" | custom-call | flops 134217728 | bytes 4194304 | tf_op jit(solution)/shard_map/hub_sums/pallas_call | solution.py:310
  69.3 1.8 %own_columns.1 = (bf16[256,1024]{1,0:T(8,128)(2,1)S(1)}, bf16[256,1024]{1,0:T(8,128)(2,1)S(1)}, f32[256,1024]{1,0:T(8,128)S(1)}, bf16[256,256]{1,0:T(8,128)(2,1)...) custom-call(s32[4]{0:T(128)S(1)} %broadcast_xor_fusion.place_ref, ...), custom_call_target="tpu_custom_call" | custom-call | flops 134217728 | bytes 4194304 | tf_op jit(solution)/shard_map/own_columns/pallas_call | solution.py:244
  71.1 1.0 copy-done.1
  72.1 0.8 copy-done.5
  72.9 0.8 copy-done.7
  74.4 2.7 %hub_sums.3.hub_ref = f32[64,1024]{1,0:T(8,128)S(1)} custom-call(s32[1]{0:T(128)} %bitcast.13.x_ref, s32[128]{0:T(128)S(1)} %fusion.4.dest_ref, bf16[32,32,128]{2,1,0:T(8,128)(2,1)S(1)} %collective-permute-done.1.refs_0_, bf16[32,32,128]{2,1,0:T(8,128)(2,1)} %collective-permute-done.2.refs_1_, bf16[128,64,128]{2,1,0:T(8,128)(2,1)S(1)} %bitcast.28, ...), custom_call_target="tpu_custom_call" | custom-call | flops 134217728 | bytes 4194304 | tf_op jit(solution)/shard_map/hub_sums/pallas_call | solution.py:310
  77.1 3.6 %mixed.1 = bf16[64,1024]{1,0:T(8,128)(2,1)S(1)} custom-call(s32[2,2048]{1,0:T(2,128)S(1)} %reshape.42.index_ref, bf16[128,16,128]{2,1,0:T(8,128)(2,1)} %all-to-all-done.1.arrived_ref, f32[64,1024]{1,0:T(8,128)S(1)} %hub_sums.3.hub_ref, s32[1,1024]{1,0:T(1,128)S(1)} %bitcast.32), custom_call_target="tpu_custom_call" | custom-call | flops 1073741824 | bytes 2097152 | tf_op jit(solution)/shard_map/mixed/pallas_call | solution.py:185
  80.7 7.1 %all_gather.3.refs_0_ = bf16[256,1024]{1,0:T(8,128)(2,1)S(1)} all-gather(bf16[64,1024]{1,0:T(8,128)(2,1)S(1)} %mixed.1), channel_id=1, replica_groups=mesh['yh'=4,'x'=4,'z'=8,'yl'=2,'core'=2] {'yl','core'}, dimensions={0}, use_global_device_ids=true | all-gather | bytes 655360 | tf_op jit(solution)/shard_map/all_gather | solution.py:486
  87.8 2.7 %layer.1 = (bf16[64,1024]{1,0:T(8,128)(2,1)}, bf16[256,1024]{1,0:T(8,128)(2,1)S(1)}, bf16[64,1024]{1,0:T(8,128)(2,1)S(1)}, bf16[64,48,128]{2,1,0:T(8,128)(2,1)S(1)}, bf16[32,128]{1,0:T(8,128)(2,1)S(1)}) custom-call(s32[4]{0:T(128)S(1)} %broadcast_xor_fusion.place_ref, s32[2,2048]{1,0:T(2,128)S(1)} %reshape.42.index_ref, s32[1,1024]{1,0:T(1,128)S(1)} %bitcast.33, ...), custom_call_target="tpu_custom_call" | custom-call | flops 536870912 | bytes 4194304 | tf_op jit(solution)/shard_map/layer/pallas_call | solution.py:146
  90.5 0.9 copy-done.3
  91.4 0.8 copy-done.17
  92.2 19.1 %all-to-all-start.2 = ((bf16[128,24,128]{2,1,0:T(8,128)(2,1)}), bf16[128,24,128]{2,1,0:T(8,128)(2,1)S(1)}, u32[]{:S(2)}, u32[]{:S(2)}) async-start(bf16[128,24,128]{2,1,0:T(8,128)(2,1)} %bitcast.31), calls=%async_computation.2 | async-start | bytes 1572864 | tf_op jit(solution)/shard_map/all_to_all | solution.py:29
  111.3 4.7 %hub_grad_terms.3 = (bf16[33,32,128]{2,1,0:T(8,128)(2,1)}, bf16[33,32,128]{2,1,0:T(8,128)(2,1)}, bf16[33,32,128]{2,1,0:T(8,128)(2,1)}) custom-call(s32[1]{0:T(128)} %bitcast.13.x_ref, s32[128]{0:T(128)S(1)} %fusion.4.dest_ref, bf16[64,1024]{1,0:T(8,128)(2,1)S(1)} %get-tuple-element.55.grad_ref, bf16[32,128]{1,0:T(8,128)(2,1)S(1)} %get-tuple-element.56.bias_ref, ...), custom_call_target="tpu_custom_call" | custom-call | flops 201326592 | bytes 4194304 | tf_op jit(solution)/shard_map/hub_grad_terms/pallas_call | solution.py:351
  116.0 5.0 %collective-permute-start.5 = (bf16[33,32,128]{2,1,0:T(8,128)(2,1)}, bf16[33,32,128]{2,1,0:T(8,128)(2,1)S(1)}, u32[]{:S(2)}, u32[]{:S(2)}) collective-permute-start(bf16[33,32,128]{2,1,0:T(8,128)(2,1)} %get-tuple-element.57), channel_id=1, source_target_pairs={{0,64},{32,96},{64,0},{96,32},{1,65},{33,97},{65,1},{97,33},{2,66}... | collective-permute-start | bytes 811016 | tf_op jit(solution)/shard_map/ppermute | solution.py:34
  121.0 2.5 %collective-permute-start.6 = (bf16[33,32,128]{2,1,0:T(8,128)(2,1)}, bf16[33,32,128]{2,1,0:T(8,128)(2,1)}, u32[]{:S(2)}, u32[]{:S(2)}) collective-permute-start(bf16[33,32,128]{2,1,0:T(8,128)(2,1)} %get-tuple-element.58), channel_id=1, source_target_pairs={{0,32},{32,64},{64,96},{96,0},{1,33},{33,65},{65,97},{97,1},{2,34}... | collective-permute-start | bytes 811016 | tf_op jit(solution)/shard_map/ppermute | solution.py:34
  123.5 4.5 %collective-permute-start.7 = (bf16[33,32,128]{2,1,0:T(8,128)(2,1)}, bf16[33,32,128]{2,1,0:T(8,128)(2,1)}, u32[]{:S(2)}, u32[]{:S(2)}) collective-permute-start(bf16[33,32,128]{2,1,0:T(8,128)(2,1)} %get-tuple-element.59), channel_id=1, source_target_pairs={{0,96},{32,0},{64,32},{96,64},{1,97},{33,1},{65,33},{97,65},{2,98}... | collective-permute-start | bytes 811016 | tf_op jit(solution)/shard_map/ppermute | solution.py:34
  128.1 0.7 copy-done.11
  129.4 1.7 hub_grad_terms.2.refs_0_
  131.1 6.8 %all-to-all-done.2.arrived_ref = bf16[128,24,128]{2,1,0:T(8,128)(2,1)S(1)} async-done(((bf16[128,24,128]{2,1,0:T(8,128)(2,1)}), bf16[128,24,128]{2,1,0:T(8,128)(2,1)S(1)}, u32[]{:S(2)}, u32[]{:S(2)}) %all-to-all-start.2) | async-done | bytes 786464 | tf_op jit(solution)/shard_map/all_to_all | solution.py:29
  138.0 1.8 %collective-permute-done.6.refs_2_ = bf16[33,32,128]{2,1,0:T(8,128)(2,1)} collective-permute-done((bf16[33,32,128]{2,1,0:T(8,128)(2,1)}, bf16[33,32,128]{2,1,0:T(8,128)(2,1)}, u32[]{:S(2)}, u32[]{:S(2)}) %collective-permute-start.6) | collective-permute-done | bytes 270368 | tf_op jit(solution)/shard_map/ppermute | solution.py:34
  139.8 1.9 %hub_grads_over_x.1 = bf16[32,48,128]{2,1,0:T(8,128)(2,1)} custom-call(bf16[33,32,128]{2,1,0:T(8,128)(2,1)S(1)} %hub_grad_terms.2.refs_0_, bf16[33,32,128]{2,1,0:T(8,128)(2,1)S(1)} %collective-permute-done.5.refs_1_, bf16[33,32,128]{2,1,0:T(8,128)(2,1)} %collective-permute-done.6.refs_2_, bf16[33,32,128]{2,1,0:T(8,128)(2,1)} %collective-permute-done.7.refs_3_, ...), custom_call_target="tpu_custom_call" | custom-call | flops 1048576 | bytes 2097152 | tf_op jit(solution)/shard_map/hub_grads_over_x/pallas_call | solution.py:380
  141.7 10.7 %all-to-all-start.3 = ((bf16[32,48,128]{2,1,0:T(8,128)(2,1)}), bf16[32,48,128]{2,1,0:T(8,128)(2,1)S(1)}, u32[]{:S(2)}, u32[]{:S(2)}) async-start(bf16[32,48,128]{2,1,0:T(8,128)(2,1)} %hub_grads_over_x.1), calls=%async_computation.3 | async-start | bytes 786432 | tf_op jit(solution)/shard_map/all_to_all | solution.py:29
  152.4 0.7 copy-done.13
  153.1 1.0 copy-done.18
  154.2 0.8 copy-done.20
  154.9 3.1 %tail_grads.1.base_ref = f32[64,1024]{1,0:T(8,128)} custom-call(s32[2,2048]{1,0:T(2,128)S(1)} %copy-done.13, bf16[128,24,128]{2,1,0:T(8,128)(2,1)S(1)} %all-to-all-done.2.arrived_ref, bf16[64,256]{1,0:T(8,128)(2,1)S(1)} %copy-done.20, bf16[256,1024]{1,0:T(8,128)(2,1)S(1)} %copy-done.18), custom_call_target="tpu_custom_call" | custom-call | flops 1073741824 | bytes 2097152 | tf_op jit(solution)/shard_map/tail_grads/pallas_call | solution.py:208
  158.1 11.3 %all-to-all-done.3.second_ref = bf16[32,48,128]{2,1,0:T(8,128)(2,1)S(1)} async-done(((bf16[32,48,128]{2,1,0:T(8,128)(2,1)}), bf16[32,48,128]{2,1,0:T(8,128)(2,1)S(1)}, u32[]{:S(2)}, u32[]{:S(2)}) %all-to-all-start.3) | async-done | bytes 393248 | tf_op jit(solution)/shard_map/all_to_all | solution.py:29
  169.4 1.6 gradients.1
  (59 shorter events, 2.8 us)
Async XLA Ops:
  0.6 26.4 %copy-start.9 = (bf16[64,1024]{1,0:T(8,128)(2,1)S(1)}, bf16[64,1024]{1,0:T(8,128)(2,1)}, u32[]{:S(2)}) copy-start(bf16[64,1024]{1,0:T(8,128)(2,1)} %source_ref.1) | copy-start | bytes 393220
  0.6 26.1 %copy-start.21 = (s32[1,128,32]{1,2,0:T(8,128)S(1)}, s32[1,128,32]{1,2,0:T(8,128)}, u32[]{:S(2)}) copy-start(s32[1,128,32]{1,2,0:T(8,128)} %param.19) | copy-start | bytes 49156
  4.8 24.1 %copy-start.12 = (s32[2,2048]{1,0:T(2,128)}, s32[2,2048]{1,0:T(2,128)S(1)}, u32[]{:S(2)}) copy-start(s32[2,2048]{1,0:T(2,128)S(1)} %reshape.41.index_ref) | copy-start | bytes 49156
  8.1 20.8 %collective-permute-start = (bf16[64,2688]{1,0:T(8,128)(2,1)S(1)}, bf16[64,2688]{1,0:T(8,128)(2,1)}, u32[]{:S(2)}, u32[]{:S(2)}) collective-permute-start(bf16[64,2688]{1,0:T(8,128)(2,1)S(1)} %pad_dynamic-update-slice_fusion), channel_id=1, source_target_pairs={{0,2},{2,0},{1,3},{3,1},{4,6},{6,4},{5,7},{7,5},{8,10},{10,8},{9,1... | collective-permute-start | bytes 1032200 | tf_op jit(solution)/shard_map/ppermute | solution.py:34
  11.6 26.6 %all-to-all-start = ((bf16[32,32,128]{2,1,0:T(8,128)(2,1)}), bf16[32,32,128]{2,1,0:T(8,128)(2,1)S(1)}, u32[]{:S(2)}, u32[]{:S(2)}) async-start(bf16[32,32,128]{2,1,0:T(8,128)(2,1)} %broadcast_in_dim.21), calls=%async_computation | async-start | bytes 524288 | tf_op jit(solution)/shard_map/all_to_all | solution.py:29
  27.0 35.7 %copy-start.24 = (s32[4]{0:T(128)S(1)}, s32[4]{0:T(128)}, u32[]{:S(2)}) copy-start(s32[4]{0:T(128)} %constant.29.clone) | copy-start | bytes 52
  27.0 35.7 %copy-start.22 = (s32[1,128]{1,0:T(1,128)S(1)}, s32[1,128]{1,0:T(1,128)}, u32[]{:S(2)}) copy-start(s32[1,128]{1,0:T(1,128)} %param.15) | copy-start | bytes 1540
  27.0 35.7 %copy-start.23 = (s32[1,128]{1,0:T(1,128)S(1)}, s32[1,128]{1,0:T(1,128)}, u32[]{:S(2)}) copy-start(s32[1,128]{1,0:T(1,128)} %param.16) | copy-start | bytes 1540
  27.1 39.5 %copy-start = (bf16[1,128,64,128]{3,2,1,0:T(8,128)(2,1)S(1)}, bf16[1,128,64,128]{3,2,1,0:T(8,128)(2,1)}, u32[]{:S(2)}) copy-start(bf16[1,128,64,128]{3,2,1,0:T(8,128)(2,1)} %param.14) | copy-start | bytes 6291460
  28.1 0.8 copy-start.4
  38.2 38.9 %all-to-all-start.1 = ((bf16[128,16,128]{2,1,0:T(8,128)(2,1)}), bf16[128,16,128]{2,1,0:T(8,128)(2,1)}, u32[]{:S(2)}, u32[]{:S(2)}) async-start(bf16[128,16,128]{2,1,0:T(8,128)(2,1)} %copy-done.4), calls=%async_computation.1 | async-start | bytes 1048576 | tf_op jit(solution)/shard_map/all_to_all | solution.py:29
  49.3 20.0 %collective-permute-start.4 = (bf16[2,64,2688]{2,1,0:T(8,128)(2,1)S(1)}, bf16[2,64,2688]{2,1,0:T(8,128)(2,1)}, u32[]{:S(2)}, u32[]{:S(2)}) collective-permute-start(bf16[2,64,2688]{2,1,0:T(8,128)(2,1)S(1)} %pad_maximum_fusion.near_ref), channel_id=1, source_target_pairs={{0,1},{1,0},{2,3},{3,2},{4,5},{5,4},{6,7},{7,6},{8,9},{9,8},{10,11... | collective-permute-start | bytes 2064392 | tf_op jit(solution)/shard_map/ppermute | solution.py:34
  51.2 15.3 %collective-permute-start.3 = (bf16[32,32,128]{2,1,0:T(8,128)(2,1)S(1)}, bf16[32,32,128]{2,1,0:T(8,128)(2,1)}, u32[]{:S(2)}, u32[]{:S(2)}) collective-permute-start(bf16[32,32,128]{2,1,0:T(8,128)(2,1)S(1)} %all-to-all-done.refs_0_), channel_id=1, source_target_pairs={{0,32},{32,64},{64,96},{96,0},{1,33},{33,65},{65,97},{97,1},{2,34}... | collective-permute-start | bytes 786440 | tf_op jit(solution)/shard_map/ppermute | solution.py:34
  54.7 19.7 %collective-permute-start.1 = (bf16[32,32,128]{2,1,0:T(8,128)(2,1)S(1)}, bf16[32,32,128]{2,1,0:T(8,128)(2,1)S(1)}, u32[]{:S(2)}, u32[]{:S(2)}) collective-permute-start(bf16[32,32,128]{2,1,0:T(8,128)(2,1)S(1)} %all-to-all-done.refs_0_), channel_id=1, source_target_pairs={{0,64},{32,96},{64,0},{96,32},{1,65},{33,97},{65,1},{97,33},{2,66}... | collective-permute-start | bytes 786440 | tf_op jit(solution)/shard_map/ppermute | solution.py:34
  59.4 15.0 %collective-permute-start.2 = (bf16[32,32,128]{2,1,0:T(8,128)(2,1)S(1)}, bf16[32,32,128]{2,1,0:T(8,128)(2,1)}, u32[]{:S(2)}, u32[]{:S(2)}) collective-permute-start(bf16[32,32,128]{2,1,0:T(8,128)(2,1)S(1)} %all-to-all-done.refs_0_), channel_id=1, source_target_pairs={{0,96},{32,0},{64,32},{96,64},{1,97},{33,1},{65,33},{97,65},{2,98}... | collective-permute-start | bytes 786440 | tf_op jit(solution)/shard_map/ppermute | solution.py:34
  62.8 48.5 %copy-start.14 = (s32[128]{0:T(128)}, s32[128]{0:T(128)S(1)}, u32[]{:S(2)}) copy-start(s32[128]{0:T(128)S(1)} %fusion.4.dest_ref) | copy-start | bytes 1540
  69.3 7.8 %copy-start.16 = (s32[1024]{0:T(1024)S(1)}, s32[1024]{0:T(1024)}, u32[]{:S(2)}) copy-start(s32[1024]{0:T(1024)} %param.20) | copy-start | bytes 12292
  71.1 1.0 copy-start.1
  72.1 0.8 copy-start.5
  72.9 0.8 copy-start.7
  73.7 0.6 copy-start.19
  77.1 10.7 %copy-start.2 = (f32[256,1024]{1,0:T(8,128)S(1)}, f32[256,1024]{1,0:T(8,128)}, u32[]{:S(2)}) copy-start(f32[256,1024]{1,0:T(8,128)} %copy-done.1) | copy-start | bytes 3145732
  77.1 10.7 %copy-start.6 = (bf16[256,1024]{1,0:T(8,128)(2,1)S(1)}, bf16[256,1024]{1,0:T(8,128)(2,1)}, u32[]{:S(2)}) copy-start(bf16[256,1024]{1,0:T(8,128)(2,1)} %copy-done.5) | copy-start | bytes 1572868
  77.1 10.7 %copy-start.8 = (bf16[256,1024]{1,0:T(8,128)(2,1)S(1)}, bf16[256,1024]{1,0:T(8,128)(2,1)}, u32[]{:S(2)}) copy-start(bf16[256,1024]{1,0:T(8,128)(2,1)} %copy-done.7) | copy-start | bytes 1572868
  90.5 0.9 copy-start.3
  91.4 0.8 copy-start.17
  92.2 31.3 %copy-start.10 = (bf16[32,128]{1,0:T(8,128)(2,1)}, bf16[32,128]{1,0:T(8,128)(2,1)S(1)}, u32[]{:S(2)}) copy-start(bf16[32,128]{1,0:T(8,128)(2,1)S(1)} %get-tuple-element.56.bias_ref) | copy-start | bytes 24580
  92.2 45.7 %all-to-all-start.2 = ((bf16[128,24,128]{2,1,0:T(8,128)(2,1)}), bf16[128,24,128]{2,1,0:T(8,128)(2,1)S(1)}, u32[]{:S(2)}, u32[]{:S(2)}) async-start(bf16[128,24,128]{2,1,0:T(8,128)(2,1)} %bitcast.31), calls=%async_computation.2 | async-start | bytes 1572864 | tf_op jit(solution)/shard_map/all_to_all | solution.py:29
  116.0 22.0 %collective-permute-start.5 = (bf16[33,32,128]{2,1,0:T(8,128)(2,1)}, bf16[33,32,128]{2,1,0:T(8,128)(2,1)S(1)}, u32[]{:S(2)}, u32[]{:S(2)}) collective-permute-start(bf16[33,32,128]{2,1,0:T(8,128)(2,1)} %get-tuple-element.57), channel_id=1, source_target_pairs={{0,64},{32,96},{64,0},{96,32},{1,65},{33,97},{65,1},{97,33},{2,66}... | collective-permute-start | bytes 811016 | tf_op jit(solution)/shard_map/ppermute | solution.py:34
  121.0 18.8 %collective-permute-start.6 = (bf16[33,32,128]{2,1,0:T(8,128)(2,1)}, bf16[33,32,128]{2,1,0:T(8,128)(2,1)}, u32[]{:S(2)}, u32[]{:S(2)}) collective-permute-start(bf16[33,32,128]{2,1,0:T(8,128)(2,1)} %get-tuple-element.58), channel_id=1, source_target_pairs={{0,32},{32,64},{64,96},{96,0},{1,33},{33,65},{65,97},{97,1},{2,34}... | collective-permute-start | bytes 811016 | tf_op jit(solution)/shard_map/ppermute | solution.py:34
  123.5 16.3 %collective-permute-start.7 = (bf16[33,32,128]{2,1,0:T(8,128)(2,1)}, bf16[33,32,128]{2,1,0:T(8,128)(2,1)}, u32[]{:S(2)}, u32[]{:S(2)}) collective-permute-start(bf16[33,32,128]{2,1,0:T(8,128)(2,1)} %get-tuple-element.59), channel_id=1, source_target_pairs={{0,96},{32,0},{64,32},{96,64},{1,97},{33,1},{65,33},{97,65},{2,98}... | collective-permute-start | bytes 811016 | tf_op jit(solution)/shard_map/ppermute | solution.py:34
  128.1 0.7 copy-start.11
  128.8 0.7 copy-start.15
  141.7 27.7 %all-to-all-start.3 = ((bf16[32,48,128]{2,1,0:T(8,128)(2,1)}), bf16[32,48,128]{2,1,0:T(8,128)(2,1)S(1)}, u32[]{:S(2)}, u32[]{:S(2)}) async-start(bf16[32,48,128]{2,1,0:T(8,128)(2,1)} %hub_grads_over_x.1), calls=%async_computation.3 | async-start | bytes 786432 | tf_op jit(solution)/shard_map/all_to_all | solution.py:29
  152.4 0.7 copy-start.13
  153.1 1.0 copy-start.18
  154.2 0.8 copy-start.20

commit v6 on v5

--- a/solution.py
+++ b/solution.py
@@ -94,40 +94,67 @@
     )(index, source)
 
 
-def layer_kernel(sizes, place_ref, index_ref, degree_ref, *refs):
-    mixed_ref, feat_ref, pre_ref, cot_ref, w_ref, neigh_ref, *out_refs = refs
-    output_ref, d_ref, grad_ref, send_ref, bias_ref, pre_full = out_refs
+def layer_kernel(sizes, place_ref, index_ref, degree_ref, mixed_ref, *refs):
+    block_refs, refs = refs[:4], refs[4:]
+    outs, (bias_ref, *held), (feat, low_rows, sems) = refs[:5], refs[5:11], refs[11:]
+    output_ref, d_ref, grad_ref, send_ref, self_ref = held
     x_size, z_size = sizes
-    width = output_ref.shape[0]
+    width, nodes = output_ref.shape
     full = mixed_ref.shape[0]
     half = full // 2
-    mixed = mixed_ref[...]
-    for first in range(0, full, width):
-        at = slice(first, first + width)
-        pre = pre_ref[at] + jnp.dot(w_ref[at], mixed, preferred_element_type=F32)
+    copies = [pltpu.make_async_copy(h, o, sems.at[i]) for i, (h, o) in enumerate(zip(held, outs))]
+    own = place_ref[0]
+    rows_of = [pl.ds(pl.multiple_of(place_ref[i] * width, width), width) for i in range(4)]
+    for at, ref in zip(rows_of, block_refs):
+        feat[at, :] = ref[:, :nodes]
+        low_rows[at, :] = ref[:, 2 * nodes : 2 * nodes + 2 * full].astype(F32)
+
+    own_weights = []
+    for first in (0, full):
+        rows = low_rows[:, first : first + width]
+        for k in range(1, 4):
+            start = first + k * width
+            rows = jnp.where(own == k, low_rows[:, start : start + width], rows)
+        own_weights.append(rows.T.astype(BF))
+    self_ref[...] = own_weights[0]
+    copies[4].start()
+
+    mixed, full_feat = mixed_ref[...], feat[...]
+    for i, (at, ref) in enumerate(zip(rows_of, block_refs)):
+        first = 2 * nodes
+        bias = ref[:, first + 2 * full :].astype(F32)
+        pre = jnp.dot(ref[:, first : first + full], full_feat, preferred_element_type=F32)
+        pre = pre + jnp.dot(
+            ref[:, first + full : first + 2 * full], mixed, preferred_element_type=F32
+        )
+        pre = pre + jnp.sum(bias, axis=1, keepdims=True)
         sigma = jax.nn.sigmoid(pre)
-        pre_full[at] = pre * sigma
         slope = sigma * (1.0 + pre * (1.0 - sigma))
-        d_ref[at] = (cot_ref[at].astype(F32) * slope).astype(BF)
-    own = pl.ds(pl.multiple_of(place_ref[0] * width, width), width)
-    output_ref[...] = pre_full[own].astype(BF)
-    d_pre = d_ref[own]
+        d_part = (ref[:, nodes : 2 * nodes].astype(F32) * slope).astype(BF)
+        d_ref[at, :] = d_part
+        if i == 0:
+            d_pre = d_part
+            output_ref[...] = (pre * sigma).astype(BF)
+            copies[0].start()
+    copies[1].start()
+
+    grad = jnp.dot(own_weights[1], d_ref[...], preferred_element_type=F32).astype(BF)
+    grad_ref[...] = grad
+    copies[2].start()
+    scaled = (grad.astype(F32) / degree_ref[...].astype(F32)).astype(BF)
 
     made = []
-    for source in (feat_ref[...], mixed):
-        grad = mm(source, d_pre, BOTH_COLS)
-        grad = jnp.concatenate([grad[:half], grad[half:]], axis=1)
-        made.append(grad.reshape(-1, z_size // 2, 16, 128))
+    for source in (full_feat, mixed):
+        total = mm(source, d_pre, BOTH_COLS)
+        total = jnp.concatenate([total[:half], total[half:]], axis=1)
+        made.append(total.reshape(-1, z_size // 2, 16, 128))
     made = jnp.concatenate(made, axis=0)
-    bias = mm(jnp.ones((bias_ref.shape[0], d_pre.shape[1]), BF), d_pre, BOTH_COLS)
+    bias = mm(jnp.ones((bias_ref.shape[0], nodes), BF), d_pre, BOTH_COLS)
     bias = jnp.concatenate([bias, bias], axis=1)
     high = bias.astype(BF).astype(F32)
     row = lax.broadcasted_iota(jnp.int32, bias.shape, 0)
     bias_ref[...] = jnp.where(row == 0, high, jnp.where(row == 1, bias - high, 0.0)).astype(BF)
 
-    grad = jnp.dot(neigh_ref[...], d_ref[...], preferred_element_type=F32).astype(BF)
-    grad_ref[...] = grad
-    scaled = (grad.astype(F32) / degree_ref[...].astype(F32)).astype(BF)
     rows = (send_ref.shape[1] - 16) // 2
     step = 256
     for start, block in pick_slots(index_ref, scaled, step):
@@ -138,26 +165,37 @@
         weight = jnp.concatenate([weight] * (count // weight.shape[0]), axis=0)
         block = jnp.concatenate([block[:, 0], weight[:, :8], block[:, 1], weight[:, 8:]], axis=1)
         send_ref[first : first + count] = block.astype(BF)
-
-
-def layer(place, index, degree, mixed, feat, pre, cot, w_all, neigh_rows, sizes, parts, slots):
+    copies[3].start()
+    for copy in copies:
+        copy.wait()
+
+
+def layer(place, index, degree, mixed, own_blocks, sizes, parts, slots):
     full, nodes = mixed.shape
-    width = neigh_rows.shape[0]
-    return call(
+    width = own_blocks[0].shape[0]
+    held = [
+        (width, nodes),
+        (full, nodes),
+        (width, nodes),
+        (parts // 2, slots + 16, 128),
+        (width, full),
+    ]
+    bias_shape = (width // 2, 128)
+    return pl.pallas_call(
         partial(layer_kernel, sizes),
-        [
-            jax.ShapeDtypeStruct((width, nodes), BF),
-            jax.ShapeDtypeStruct((full, nodes), BF),
-            jax.ShapeDtypeStruct((width, nodes), BF),
-            jax.ShapeDtypeStruct((parts // 2, slots + 16, 128), BF),
-            jax.ShapeDtypeStruct((width // 2, 128), BF),
+        out_shape=[jax.ShapeDtypeStruct(shape, BF) for shape in [*held, bias_shape]],
+        in_specs=[SMEM] + [VMEM] * 7,
+        out_specs=[pl.BlockSpec(memory_space=pl.ANY)] * len(held) + [VMEM],
+        scratch_shapes=[pltpu.VMEM(shape, BF) for shape in held]
+        + [
+            pltpu.VMEM((full, nodes), BF),
+            pltpu.VMEM((full, 2 * full), F32),
+            pltpu.SemaphoreType.DMA((len(held),)),
         ],
-        [SMEM] + [VMEM] * 8,
-        [pltpu.VMEM((full, nodes), F32)],
-        "layer",
-        2 * parts * slots * 256 * 256,
-        4,
-    )(place, index, degree, mixed, feat, pre, cot, w_all, neigh_rows)
+        compiler_params=pltpu.CompilerParams(vmem_limit_bytes=VMEM_LIMIT),
+        cost_estimate=pl.CostEstimate(flops=1000 * MIB, bytes_accessed=4 * MIB, transcendentals=0),
+        name="layer",
+    )(place, index, degree, mixed, *own_blocks)
 
 
 def sum_slots(index_ref, arrived_ref, rows, start, size):
@@ -216,47 +254,24 @@
     )(index, arrived, weight, d_full)
 
 
-def arrange_kernel(place_ref, near_ref, far_ref, *refs):
-    feat_ref, cot_ref, pre_ref, w_ref, self_ref, neigh_ref, wide = refs
-    full, nodes = pre_ref.shape
-    width = self_ref.shape[0]
-    for i in range(4):
-        block = (near_ref, far_ref)[i // 2].at[i % 2]
-        at = pl.ds(pl.multiple_of(place_ref[i] * width, width), width)
-        feat_ref[at, :] = block[:, :nodes]
-        cot_ref[at, :] = block[:, nodes : 2 * nodes]
-        wide[at, :] = block[:, 2 * nodes :].astype(F32)
-    bias = jnp.sum(wide[:, 2 * full : 2 * full + 128], axis=1, keepdims=True)
-    w_self = wide[:, :full].astype(BF)
-    w_ref[...] = wide[:, full : 2 * full].astype(BF)
-    pre_ref[...] = jnp.dot(w_self, feat_ref[...], preferred_element_type=F32) + bias
-    own = place_ref[0]
-    for first, out_ref in ((0, self_ref), (full, neigh_ref)):
-        rows = wide[:, first : first + width]
-        for k in range(1, 4):
-            at = first + k * width
-            rows = jnp.where(own == k, wide[:, at : at + width], rows)
-        out_ref[...] = rows.T.astype(BF)
-
-
-def arrange(place, near, far, nodes, full):
-    width = near.shape[1]
-    return call(
-        arrange_kernel,
-        [
-            jax.ShapeDtypeStruct((full, nodes), BF),
-            jax.ShapeDtypeStruct((full, nodes), BF),
-            jax.ShapeDtypeStruct((full, nodes), F32),
-            jax.ShapeDtypeStruct((full, full), BF),
-            jax.ShapeDtypeStruct((width, full), BF),
-            jax.ShapeDtypeStruct((width, full), BF),
-        ],
-        [SMEM] + [VMEM] * 2,
-        [pltpu.VMEM((full, 2 * full + 128), F32)],
-        "own_columns",
-        2 * full * full * nodes,
-        4,
-    )(place, near, far)
+def own_kernel(feat_ref, cot_ref, self_ref, neigh_ref, bias_ref, out_ref):
+    first = 0
+    for ref in (feat_ref, cot_ref, self_ref, neigh_ref, bias_ref):
+        out_ref[:, first : first + ref.shape[1]] = ref[...].astype(BF)
+        first += ref.shape[1]
+
+
+def own_block(*pieces):
+    columns = sum(piece.shape[1] for piece in pieces)
+    return call(
+        own_kernel,
+        jax.ShapeDtypeStruct((pieces[0].shape[0], columns), BF),
+        [VMEM] * len(pieces),
+        [],
+        "own_block",
+        0,
+        0,
+    )(*pieces)
 
 
 def three_terms(values):
@@ -272,7 +287,7 @@
     return (yh * x_size + x) * z_size + z
 
 
-def fold_kernel(steps, sizes, has_base, x_ref, dest_ref, *refs):
+def fold_kernel(steps, sizes, has_base, x_ref, block_ref, mask_ref, *refs):
     hub_refs, (tile_ref, *base_ref, out_ref, total) = refs[: len(steps)], refs[len(steps) :]
     blocks = total.shape[0] - 1
     half = hub_refs[0].shape[1]
@@ -297,28 +312,28 @@
                     jnp.concatenate([weights, weights], axis=0),
                     preferred_element_type=F32,
                 )
-                dest = dest_ref[tile]
+                dest = jnp.where(mask_ref[tile] > 0, block_ref[tile], blocks)
                 total[dest] = total[dest] + product
 
     for b in range(blocks):
         out_ref[:, b * 128 : (b + 1) * 128] = total[b]
 
 
-def fold_hubs(x_index, dest, hubs, steps, tiles, sizes, blocks, base):
+def fold_hubs(x_index, block, mask, hubs, steps, tiles, sizes, blocks, base):
     width = 2 * hubs[0].shape[1]
     bases = [] if base is None else [base]
     return call(
         partial(fold_kernel, steps, sizes, base is not None),
         jax.ShapeDtypeStruct((width, blocks * 128), F32),
-        [SMEM, SMEM] + [VMEM] * (len(hubs) + 1 + len(bases)),
+        [SMEM, SMEM, SMEM] + [VMEM] * (len(hubs) + 1 + len(bases)),
         [pltpu.VMEM((blocks + 1, width, 128), F32)],
         "hub_sums",
         tiles.size * width * len(hubs),
         4,
-    )(x_index, dest, *hubs, tiles, *bases)
-
-
-def hub_grad_kernel(steps, sizes, x_ref, dest_ref, grad_ref, bias_ref, tile_ref, *refs):
+    )(x_index, block, mask, *hubs, tiles, *bases)
+
+
+def hub_grad_kernel(steps, sizes, x_ref, block_ref, mask_ref, grad_ref, bias_ref, tile_ref, *refs):
     *out_refs, blocked = refs
     blocks = blocked.shape[0] - 1
     for b in range(blocks):
@@ -335,8 +350,9 @@
             for z in range(z_size):
                 tile = tile_index(x_ref, k, sizes, yh, z, 1)
                 weights = tile_ref[tile]
+                dest = jnp.where(mask_ref[tile] > 0, block_ref[tile], blocks)
                 product = mm(
-                    blocked[dest_ref[tile]],
+                    blocked[dest],
                     jnp.concatenate([weights, weights], axis=0),
                     BOTH_COLS,
                 )
@@ -345,18 +361,18 @@
                 ).astype(BF)
 
 
-def hub_grad_terms(x_index, dest, grad, bias, tiles, steps, sizes, blocks):
+def hub_grad_terms(x_index, block, mask, grad, bias, tiles, steps, sizes, blocks):
     width = grad.shape[0]
     shape = (tiles.shape[0] // sizes[0] + 1, width // 2, 128)
     return call(
         partial(hub_grad_kernel, steps, sizes),
         [jax.ShapeDtypeStruct(shape, BF) for _ in steps],
-        [SMEM, SMEM, VMEM, VMEM, VMEM],
+        [SMEM, SMEM, SMEM, VMEM, VMEM, VMEM],
         [pltpu.VMEM((blocks + 1, width, 128), BF)],
         "hub_grad_terms",
         tiles.size * width * len(steps),
         4,
-    )(x_index, dest, grad, bias, tiles)
+    )(x_index, block, mask, grad, bias, tiles)
 
 
 def pack_kernel(*refs):
@@ -452,7 +468,7 @@
     plane = parts // x_size
     x_index = lax.axis_index("x")[None]
     tiles = hub_weight[0]
-    hub_dest = jnp.where(hub_mask[0] > 0, hub_block[0], blocks)
+    hub_at = (x_index, hub_block[0], hub_mask[0])
     degree = degree[None, :]
 
     hub_piece = jnp.concatenate([features[:half_width, :hubs], features[half_width:, :hubs]], axis=1)
@@ -464,46 +480,32 @@
     recv_index = slot_rows(tail_target[0])
     bias_terms = jnp.stack(three_terms(out_bias), axis=1)
     bias_terms = jnp.pad(bias_terms, ((0, 0), (0, 128 - bias_terms.shape[1])))
-    own = jnp.concatenate([features, cotangent, w_self.T, w_neigh.T, bias_terms], axis=1)
-    own, send_index, _ = lax.optimization_barrier((own, send_index, hub_send))
-    near = jnp.stack([own, shift(own, "yl", 1)])
+    feat_own, send_index, _ = lax.optimization_barrier((features, send_index, hub_send))
+    own = own_block(feat_own, cotangent, w_self.T, w_neigh.T, bias_terms)
+    near = (own, shift(own, "yl", 1), shift(own, "core", 1))
     tail_send = gather_slots(send_index, features, parts, slots)
     hub_plane, tail_send, recv_index, near = lax.optimization_barrier(
         (hub_plane, tail_send, recv_index, near)
     )
     arrived = swap(tail_send, DOM)
     hub_all = [hub_plane] + [shift(hub_plane, "x", k) for k in range(1, x_size)]
-    far = shift(near, "core", 1)
+    own_blocks = [*near, shift(near[1], "core", 1)]
     place = lax.axis_index(REP) ^ jnp.array([0, 2, 1, 3], jnp.int32)
-    own_columns = arrange(place, near, far, nodes, full_width)
-
-    fold = partial(fold_hubs, x_index, hub_dest, tiles=tiles, sizes=sizes, blocks=blocks)
+
+    fold = partial(fold_hubs, *hub_at, tiles=tiles, sizes=sizes, blocks=blocks)
     hub_sum = fold(hub_all[:2], (0, 1), base=None)
-    hub_sum, own_columns = lax.optimization_barrier((hub_sum, own_columns))
-    full_feat, full_cot, pre_self, w_neigh_all, w_self_rows, w_neigh_rows = own_columns
     hub_sum = fold(hub_all[2:], (2, 3), base=hub_sum)
     mixed = mixed_sums(recv_index, arrived, hub_sum, degree)
     full_mixed = lax.all_gather(mixed, REP, axis=0, tiled=True)
 
-    output, d_full, mixed_grad, tail_back, bias_rows = layer(
-        place,
-        recv_index,
-        degree,
-        full_mixed,
-        full_feat,
-        pre_self,
-        full_cot,
-        w_neigh_all,
-        w_neigh_rows,
-        sizes,
-        parts,
-        slots,
+    output, d_full, mixed_grad, tail_back, w_self_rows, bias_rows = layer(
+        place, recv_index, degree, full_mixed, own_blocks, sizes, parts, slots
     )
     tail_len = slots // 2
     first = swap(tail_back.reshape(parts, tail_len + 8, 128), DOM)
 
     hub_terms = partial(
-        hub_grad_terms, x_index, hub_dest, mixed_grad, bias_rows, tiles, sizes=sizes, blocks=blocks
+        hub_grad_terms, *hub_at, mixed_grad, bias_rows, tiles, sizes=sizes, blocks=blocks
     )
     far_steps = (2, 1, 3)
     terms = [shift(term, "x", k) for term, k in zip(hub_terms(far_steps), far_steps)]

time: 172 us -> 173 us (level)
  the two profiles are of different devices: /device:TPU:16 before, /device:TPU:8 now
where the time goes in v6:
time: 173 us; the launch traced here: 171 us
  starting transfers between devices  86.3 us (50%)
  waiting for transfers between devices  36 us (21%)
  Pallas kernels  27.3 us (16%)
  local copies, waits for them, and re-layouts  11.4 us (7%)
  blocking collectives  7.26 us (4%)
  other arithmetic  2.16 us (1%)
    all_to_all x4, starting transfers between devices, swap(): return lax.all_to_all(pieces, axis, split_axis=0, concat_axis=0, tiled=True)  57.2 us
    ppermute x9, starting transfers between devices, shift(): lax.ppermute(values, axis, [(i, (i + step) % size) for i in range(size)])  29.1 us
    all_to_all x4, waiting for transfers between devices, swap(): return lax.all_to_all(pieces, axis, split_axis=0, concat_axis=0, tiled=True)  22.6 us
    ppermute x9, waiting for transfers between devices, shift(): lax.ppermute(values, axis, [(i, (i + step) % size) for i in range(size)])  13.5 us
    unnamed x44, local copies, waits for them, and re-layouts  8.58 us
    all_gather x1, blocking collectives, local(): full_mixed = lax.all_gather(mixed, REP, axis=0, tiled=True)  7.26 us
    pallas_call x2, Pallas kernels, hub_grad_terms(): call(partial(hub_grad_kernel, steps, sizes), [jax.ShapeDtypeStruct(shape,...  6.34 us
    pallas_call x2, Pallas kernels, fold_hubs(): call(partial(fold_kernel, steps, sizes, base is not None), jax.ShapeDtype...  5.44 us
  transfers between devices with their start and end apart: 13, of which 7 were waited for; matrix products, arithmetic and copies ran while one was open for 2% of the time, Pallas kernels for 11%

profile of v6, /device:TPU:8, one launch (start us, length us, event | category | flops | bytes accessed | tf_op | source)
XLA Modules:
  0.0 171.4 jit_solution(3945690053766987587)
XLA Ops:
  0.7 0.8 fusion.4
  1.5 0.7 broadcast_in_dim.17
  2.2 15.1 %all-to-all-start = ((bf16[32,32,128]{2,1,0:T(8,128)(2,1)}), bf16[32,32,128]{2,1,0:T(8,128)(2,1)S(1)}, u32[]{:S(2)}, u32[]{:S(2)}) async-start(bf16[32,32,128]{2,1,0:T(8,128)(2,1)} %broadcast_in_dim.17), calls=%async_computation | async-start | bytes 524288 | tf_op jit(solution)/shard_map/all_to_all | solution.py:29
  17.3 0.7 fusion
  18.1 0.8 copy.29
  19.0 0.8 select_bitcast_fusion
  19.9 1.0 copy-done.4
  20.9 0.9 copy-done.6
  21.8 0.8 copy-done.7
  22.6 0.8 copy-done.8
  23.4 1.9 %collective-permute-start.1 = (bf16[64,2688]{1,0:T(8,128)(2,1)S(1)}, bf16[64,2688]{1,0:T(8,128)(2,1)}, u32[]{:S(2)}, u32[]{:S(2)}) collective-permute-start(bf16[64,2688]{1,0:T(8,128)(2,1)S(1)} %own_block.1.refs_0_), channel_id=1, source_target_pairs={{0,1},{1,0},{2,3},{3,2},{4,5},{5,4},{6,7},{7,6},{8,9},{9,8},{10,11... | collective-permute-start | bytes 1032200 | tf_op jit(solution)/shard_map/ppermute | solution.py:34
  25.3 3.3 %collective-permute-start = (bf16[64,2688]{1,0:T(8,128)(2,1)S(1)}, bf16[64,2688]{1,0:T(8,128)(2,1)}, u32[]{:S(2)}, u32[]{:S(2)}) collective-permute-start(bf16[64,2688]{1,0:T(8,128)(2,1)S(1)} %own_block.1.refs_0_), channel_id=1, source_target_pairs={{0,2},{2,0},{1,3},{3,1},{4,6},{6,4},{5,7},{7,5},{8,10},{10,8},{9,1... | collective-permute-start | bytes 1032200 | tf_op jit(solution)/shard_map/ppermute | solution.py:34
  28.8 1.8 %tail_rows_out.1 = bf16[128,16,128]{2,1,0:T(8,128)(2,1)} custom-call(s32[2,2048]{1,0:T(2,128)S(1)} %reshape.37.index_ref, bf16[64,1024]{1,0:T(8,128)(2,1)S(1)} %copy-done.5), custom_call_target="tpu_custom_call" | custom-call | flops 536870912 | bytes 2097152 | tf_op jit(solution)/shard_map/tail_rows_out/pallas_call | solution.py:86
  30.6 7.1 %collective-permute-done.refs_1_ = bf16[64,2688]{1,0:T(8,128)(2,1)} collective-permute-done((bf16[64,2688]{1,0:T(8,128)(2,1)S(1)}, bf16[64,2688]{1,0:T(8,128)(2,1)}, u32[]{:S(2)}, u32[]{:S(2)}) %collective-permute-start) | collective-permute-done | bytes 344096 | tf_op jit(solution)/shard_map/ppermute | solution.py:34
  37.8 16.5 %all-to-all-start.1 = ((bf16[128,16,128]{2,1,0:T(8,128)(2,1)}), bf16[128,16,128]{2,1,0:T(8,128)(2,1)S(1)}, u32[]{:S(2)}, u32[]{:S(2)}) async-start(bf16[128,16,128]{2,1,0:T(8,128)(2,1)} %tail_rows_out.1), calls=%async_computation.1 | async-start | bytes 1048576 | tf_op jit(solution)/shard_map/all_to_all | solution.py:29
  54.3 3.0 %collective-permute-start.4 = (bf16[32,32,128]{2,1,0:T(8,128)(2,1)S(1)}, bf16[32,32,128]{2,1,0:T(8,128)(2,1)}, u32[]{:S(2)}, u32[]{:S(2)}) collective-permute-start(bf16[32,32,128]{2,1,0:T(8,128)(2,1)S(1)} %all-to-all-done.refs_0_), channel_id=1, source_target_pairs={{0,32},{32,64},{64,96},{96,0},{1,33},{33,65},{65,97},{97,1},{2,34}... | collective-permute-start | bytes 786440 | tf_op jit(solution)/shard_map/ppermute | solution.py:34
  57.3 4.0 %collective-permute-start.3 = (bf16[32,32,128]{2,1,0:T(8,128)(2,1)S(1)}, bf16[32,32,128]{2,1,0:T(8,128)(2,1)S(1)}, u32[]{:S(2)}, u32[]{:S(2)}) collective-permute-start(bf16[32,32,128]{2,1,0:T(8,128)(2,1)S(1)} %all-to-all-done.refs_0_), channel_id=1, source_target_pairs={{0,96},{32,0},{64,32},{96,64},{1,97},{33,1},{65,33},{97,65},{2,98}... | collective-permute-start | bytes 786440 | tf_op jit(solution)/shard_map/ppermute | solution.py:34
  61.3 3.3 %collective-permute-start.2 = (bf16[32,32,128]{2,1,0:T(8,128)(2,1)S(1)}, bf16[32,32,128]{2,1,0:T(8,128)(2,1)}, u32[]{:S(2)}, u32[]{:S(2)}) collective-permute-start(bf16[32,32,128]{2,1,0:T(8,128)(2,1)S(1)} %all-to-all-done.refs_0_), channel_id=1, source_target_pairs={{0,64},{32,96},{64,0},{96,32},{1,65},{33,97},{65,1},{97,33},{2,66}... | collective-permute-start | bytes 786440 | tf_op jit(solution)/shard_map/ppermute | solution.py:34
  64.7 1.9 %collective-permute-start.5 = (bf16[64,2688]{1,0:T(8,128)(2,1)}, bf16[64,2688]{1,0:T(8,128)(2,1)}, u32[]{:S(2)}, u32[]{:S(2)}) collective-permute-start(bf16[64,2688]{1,0:T(8,128)(2,1)} %collective-permute-done.refs_1_), channel_id=1, source_target_pairs={{0,1},{1,0},{2,3},{3,2},{4,5},{5,4},{6,7},{7,6},{8,9},{9,8},{10,11... | collective-permute-start | bytes 1032200 | tf_op jit(solution)/shard_map/ppermute | solution.py:34
  66.6 0.5 broadcast_xor_fusion.place_ref
  67.1 3.5 %collective-permute-done.4.refs_1_ = bf16[32,32,128]{2,1,0:T(8,128)(2,1)} collective-permute-done((bf16[32,32,128]{2,1,0:T(8,128)(2,1)S(1)}, bf16[32,32,128]{2,1,0:T(8,128)(2,1)}, u32[]{:S(2)}, u32[]{:S(2)}) %collective-permute-start.4) | collective-permute-done | bytes 262176 | tf_op jit(solution)/shard_map/ppermute | solution.py:34
  70.7 2.7 %hub_sums.2.refs_3_ = f32[64,1024]{1,0:T(8,128)S(1)} custom-call(s32[1]{0:T(128)} %bitcast.11.x_ref, s32[128]{0:T(128)S(1)} %bitcast.30, s32[128]{0:T(128)S(1)} %bitcast.34, bf16[32,32,128]{2,1,0:T(8,128)(2,1)S(1)} %all-to-all-done.refs_0_, bf16[32,32,128]{2,1,0:T(8,128)(2,1)} %collective-permute-done.4.refs_1_, bf16[128,64,128]{2,1,0:T(8,128)(2,1)S(1)} %bitcast.23), custom_call_target="tpu_custom_call" | custom-call | flops 134217728 | bytes 4194304 | tf_op jit(solution)/shard_map/hub_sums/pallas_call | solution.py:325
  73.4 1.7 %collective-permute-done.3.refs_1_ = bf16[32,32,128]{2,1,0:T(8,128)(2,1)S(1)} collective-permute-done((bf16[32,32,128]{2,1,0:T(8,128)(2,1)S(1)}, bf16[32,32,128]{2,1,0:T(8,128)(2,1)S(1)}, u32[]{:S(2)}, u32[]{:S(2)}) %collective-permute-start.3) | collective-permute-done | bytes 262176 | tf_op jit(solution)/shard_map/ppermute | solution.py:34
  75.1 0.8 collective-permute-done.2.refs_0_
  76.0 2.7 %hub_sums.3.hub_ref = f32[64,1024]{1,0:T(8,128)S(1)} custom-call(s32[1]{0:T(128)} %bitcast.11.x_ref, s32[128]{0:T(128)S(1)} %bitcast.31, s32[128]{0:T(128)S(1)} %bitcast.35, bf16[32,32,128]{2,1,0:T(8,128)(2,1)} %collective-permute-done.2.refs_0_, bf16[32,32,128]{2,1,0:T(8,128)(2,1)S(1)} %collective-permute-done.3.refs_1_, ...), custom_call_target="tpu_custom_call" | custom-call | flops 134217728 | bytes 4194304 | tf_op jit(solution)/shard_map/hub_sums/pallas_call | solution.py:325
  78.7 0.7 copy-done.2
  79.4 0.9 copy-done.3
  80.4 2.4 %mixed.1 = bf16[64,1024]{1,0:T(8,128)(2,1)S(1)} custom-call(s32[2,2048]{1,0:T(2,128)S(1)} %reshape.38.index_ref, bf16[128,16,128]{2,1,0:T(8,128)(2,1)S(1)} %all-to-all-done.1.arrived_ref, f32[64,1024]{1,0:T(8,128)S(1)} %copy-done.3, s32[1,1024]{1,0:T(1,128)S(1)} %bitcast.38), custom_call_target="tpu_custom_call" | custom-call | flops 1073741824 | bytes 2097152 | tf_op jit(solution)/shard_map/mixed/pallas_call | solution.py:223
  82.8 7.3 %all_gather.3.mixed_ref = bf16[256,1024]{1,0:T(8,128)(2,1)S(1)} all-gather(bf16[64,1024]{1,0:T(8,128)(2,1)S(1)} %mixed.1), channel_id=1, replica_groups=mesh['yh'=4,'x'=4,'z'=8,'yl'=2,'core'=2] {'yl','core'}, dimensions={0}, use_global_device_ids=true | all-gather | bytes 655360 | tf_op jit(solution)/shard_map/all_gather | solution.py:499
  90.1 0.7 copy-done.12
  90.8 4.5 %layer.1 = (bf16[64,1024]{1,0:T(8,128)(2,1)}, bf16[256,1024]{1,0:T(8,128)(2,1)S(1)}, bf16[64,1024]{1,0:T(8,128)(2,1)S(1)}, bf16[64,48,128]{2,1,0:T(8,128)(2,1)S(...) custom-call(s32[4]{0:T(128)S(1)} %copy-done.17, s32[2,2048]{1,0:T(2,128)S(1)} %copy-done.12, ...), custom_call_target="tpu_custom_call" | custom-call | flops 1048576000 | bytes 4194304 | tf_op jit(solution)/shard_map/layer/pallas_call | solution.py:184
  95.3 0.9 copy-done.1
  96.2 0.8 copy-done.18
  97.0 15.6 %all-to-all-start.2 = ((bf16[128,24,128]{2,1,0:T(8,128)(2,1)}), bf16[128,24,128]{2,1,0:T(8,128)(2,1)S(1)}, u32[]{:S(2)}, u32[]{:S(2)}) async-start(bf16[128,24,128]{2,1,0:T(8,128)(2,1)} %bitcast.27), calls=%async_computation.2 | async-start | bytes 1572864 | tf_op jit(solution)/shard_map/all_to_all | solution.py:29
  112.6 4.7 %hub_grad_terms.3 = (bf16[33,32,128]{2,1,0:T(8,128)(2,1)}, bf16[33,32,128]{2,1,0:T(8,128)(2,1)}, bf16[33,32,128]{2,1,0:T(8,128)(2,1)}) custom-call(s32[1]{0:T(128)} %bitcast.11.x_ref, s32[128]{0:T(128)S(1)} %bitcast.32, s32[128]{0:T(128)S(1)} %bitcast.36, bf16[64,1024]{1,0:T(8,128)(2,1)S(1)} %get-tuple-element.35.grad_ref, ...), custom_call_target="tpu_custom_call" | custom-call | flops 201326592 | bytes 4194304 | tf_op jit(solution)/shard_map/hub_grad_terms/pallas_call | solution.py:367
  117.3 4.5 %collective-permute-start.6 = (bf16[33,32,128]{2,1,0:T(8,128)(2,1)}, bf16[33,32,128]{2,1,0:T(8,128)(2,1)}, u32[]{:S(2)}, u32[]{:S(2)}) collective-permute-start(bf16[33,32,128]{2,1,0:T(8,128)(2,1)} %get-tuple-element.37), channel_id=1, source_target_pairs={{0,64},{32,96},{64,0},{96,32},{1,65},{33,97},{65,1},{97,33},{2,66}... | collective-permute-start | bytes 811016 | tf_op jit(solution)/shard_map/ppermute | solution.py:34
  121.8 2.5 %collective-permute-start.7 = (bf16[33,32,128]{2,1,0:T(8,128)(2,1)}, bf16[33,32,128]{2,1,0:T(8,128)(2,1)}, u32[]{:S(2)}, u32[]{:S(2)}) collective-permute-start(bf16[33,32,128]{2,1,0:T(8,128)(2,1)} %get-tuple-element.38), channel_id=1, source_target_pairs={{0,32},{32,64},{64,96},{96,0},{1,33},{33,65},{65,97},{97,1},{2,34}... | collective-permute-start | bytes 811016 | tf_op jit(solution)/shard_map/ppermute | solution.py:34
  124.3 4.5 %collective-permute-start.8 = (bf16[33,32,128]{2,1,0:T(8,128)(2,1)}, bf16[33,32,128]{2,1,0:T(8,128)(2,1)}, u32[]{:S(2)}, u32[]{:S(2)}) collective-permute-start(bf16[33,32,128]{2,1,0:T(8,128)(2,1)} %get-tuple-element.39), channel_id=1, source_target_pairs={{0,96},{32,0},{64,32},{96,64},{1,97},{33,1},{65,33},{97,65},{2,98}... | collective-permute-start | bytes 811016 | tf_op jit(solution)/shard_map/ppermute | solution.py:34
  128.9 1.7 hub_grad_terms.2.refs_0_
  130.6 10.3 %all-to-all-done.2.arrived_ref = bf16[128,24,128]{2,1,0:T(8,128)(2,1)S(1)} async-done(((bf16[128,24,128]{2,1,0:T(8,128)(2,1)}), bf16[128,24,128]{2,1,0:T(8,128)(2,1)S(1)}, u32[]{:S(2)}, u32[]{:S(2)}) %all-to-all-start.2) | async-done | bytes 786464 | tf_op jit(solution)/shard_map/all_to_all | solution.py:29
  140.9 0.1 convert_reduce_fusion.refs_4_
  141.1 0.3 collective-permute-done.7.refs_2_
  141.3 2.0 %hub_grads_over_x.1 = bf16[32,48,128]{2,1,0:T(8,128)(2,1)} custom-call(bf16[33,32,128]{2,1,0:T(8,128)(2,1)S(1)} %hub_grad_terms.2.refs_0_, bf16[33,32,128]{2,1,0:T(8,128)(2,1)} %collective-permute-done.6.refs_1_, bf16[33,32,128]{2,1,0:T(8,128)(2,1)} %collective-permute-done.7.refs_2_, bf16[33,32,128]{2,1,0:T(8,128)(2,1)} %collective-permute-done.8.refs_3_, ...), custom_call_target="tpu_custom_call" | custom-call | flops 1048576 | bytes 2097152 | tf_op jit(solution)/shard_map/hub_grads_over_x/pallas_call | solution.py:396
  143.3 10.1 %all-to-all-start.3 = ((bf16[32,48,128]{2,1,0:T(8,128)(2,1)}), bf16[32,48,128]{2,1,0:T(8,128)(2,1)S(1)}, u32[]{:S(2)}, u32[]{:S(2)}) async-start(bf16[32,48,128]{2,1,0:T(8,128)(2,1)} %hub_grads_over_x.1), calls=%async_computation.3 | async-start | bytes 786432 | tf_op jit(solution)/shard_map/all_to_all | solution.py:29
  153.5 1.0 copy-done.19
  154.5 3.1 %tail_grads.1.base_ref = f32[64,1024]{1,0:T(8,128)} custom-call(s32[2,2048]{1,0:T(2,128)S(1)} %copy-done.10, bf16[128,24,128]{2,1,0:T(8,128)(2,1)S(1)} %all-to-all-done.2.arrived_ref, bf16[64,256]{1,0:T(8,128)(2,1)S(1)} %get-tuple-element.41.weight_ref, bf16[256,1024]{1,0:T(8,128)(2,1)S(1)} %copy-done.19), custom_call_target="tpu_custom_call" | custom-call | flops 1073741824 | bytes 2097152 | tf_op jit(solution)/shard_map/tail_grads/pallas_call | solution.py:246
  157.6 12.2 %all-to-all-done.3.second_ref = bf16[32,48,128]{2,1,0:T(8,128)(2,1)S(1)} async-done(((bf16[32,48,128]{2,1,0:T(8,128)(2,1)}), bf16[32,48,128]{2,1,0:T(8,128)(2,1)S(1)}, u32[]{:S(2)}, u32[]{:S(2)}) %all-to-all-start.3) | async-done | bytes 393248 | tf_op jit(solution)/shard_map/all_to_all | solution.py:29
  169.8 1.6 gradients.1
  (49 shorter events, 0.7 us)
Async XLA Ops:
  0.6 28.2 %copy-start.5 = (bf16[64,1024]{1,0:T(8,128)(2,1)S(1)}, bf16[64,1024]{1,0:T(8,128)(2,1)}, u32[]{:S(2)}) copy-start(bf16[64,1024]{1,0:T(8,128)(2,1)} %feat_ref) | copy-start | bytes 393220
  0.6 27.9 %copy-start.20 = (s32[1,128,32]{1,2,0:T(8,128)S(1)}, s32[1,128,32]{1,2,0:T(8,128)}, u32[]{:S(2)}) copy-start(s32[1,128,32]{1,2,0:T(8,128)} %param.19) | copy-start | bytes 49156
  2.2 35.5 %all-to-all-start = ((bf16[32,32,128]{2,1,0:T(8,128)(2,1)}), bf16[32,32,128]{2,1,0:T(8,128)(2,1)S(1)}, u32[]{:S(2)}, u32[]{:S(2)}) async-start(bf16[32,32,128]{2,1,0:T(8,128)(2,1)} %broadcast_in_dim.17), calls=%async_computation | async-start | bytes 524288 | tf_op jit(solution)/shard_map/all_to_all | solution.py:29
  18.9 47.7 %copy-start.21 = (s32[4]{0:T(128)S(1)}, s32[4]{0:T(128)}, u32[]{:S(2)}) copy-start(s32[4]{0:T(128)} %constant.25.clone) | copy-start | bytes 52
  18.9 51.7 %copy-start.13 = (s32[1,128]{1,0:T(1,128)S(1)}, s32[1,128]{1,0:T(1,128)}, u32[]{:S(2)}) copy-start(s32[1,128]{1,0:T(1,128)} %param.15) | copy-start | bytes 1540
  18.9 51.7 %copy-start.14 = (s32[1,128]{1,0:T(1,128)S(1)}, s32[1,128]{1,0:T(1,128)}, u32[]{:S(2)}) copy-start(s32[1,128]{1,0:T(1,128)} %param.16) | copy-start | bytes 1540
  19.7 51.0 %copy-start = (bf16[1,128,64,128]{3,2,1,0:T(8,128)(2,1)S(1)}, bf16[1,128,64,128]{3,2,1,0:T(8,128)(2,1)}, u32[]{:S(2)}) copy-start(bf16[1,128,64,128]{3,2,1,0:T(8,128)(2,1)} %param.14) | copy-start | bytes 6291460
  19.9 17.9 %copy-start.9 = (s32[2,2048]{1,0:T(2,128)}, s32[2,2048]{1,0:T(2,128)S(1)}, u32[]{:S(2)}) copy-start(s32[2,2048]{1,0:T(2,128)S(1)} %reshape.37.index_ref) | copy-start | bytes 49156
  19.9 1.0 copy-start.4
  20.9 0.9 copy-start.6
  21.8 0.8 copy-start.7
  22.6 0.8 copy-start.8
  23.4 7.3 %collective-permute-start.1 = (bf16[64,2688]{1,0:T(8,128)(2,1)S(1)}, bf16[64,2688]{1,0:T(8,128)(2,1)}, u32[]{:S(2)}, u32[]{:S(2)}) collective-permute-start(bf16[64,2688]{1,0:T(8,128)(2,1)S(1)} %own_block.1.refs_0_), channel_id=1, source_target_pairs={{0,1},{1,0},{2,3},{3,2},{4,5},{5,4},{6,7},{7,6},{8,9},{9,8},{10,11... | collective-permute-start | bytes 1032200 | tf_op jit(solution)/shard_map/ppermute | solution.py:34
  25.3 12.5 %collective-permute-start = (bf16[64,2688]{1,0:T(8,128)(2,1)S(1)}, bf16[64,2688]{1,0:T(8,128)(2,1)}, u32[]{:S(2)}, u32[]{:S(2)}) collective-permute-start(bf16[64,2688]{1,0:T(8,128)(2,1)S(1)} %own_block.1.refs_0_), channel_id=1, source_target_pairs={{0,2},{2,0},{1,3},{3,1},{4,6},{6,4},{5,7},{7,5},{8,10},{10,8},{9,1... | collective-permute-start | bytes 1032200 | tf_op jit(solution)/shard_map/ppermute | solution.py:34
  28.8 50.6 %copy-start.11 = (s32[2,2048]{1,0:T(2,128)}, s32[2,2048]{1,0:T(2,128)S(1)}, u32[]{:S(2)}) copy-start(s32[2,2048]{1,0:T(2,128)S(1)} %reshape.38.index_ref) | copy-start | bytes 49156
  37.8 41.6 %all-to-all-start.1 = ((bf16[128,16,128]{2,1,0:T(8,128)(2,1)}), bf16[128,16,128]{2,1,0:T(8,128)(2,1)S(1)}, u32[]{:S(2)}, u32[]{:S(2)}) async-start(bf16[128,16,128]{2,1,0:T(8,128)(2,1)} %tail_rows_out.1), calls=%async_computation.1 | async-start | bytes 1048576 | tf_op jit(solution)/shard_map/all_to_all | solution.py:29
  54.3 16.4 %collective-permute-start.4 = (bf16[32,32,128]{2,1,0:T(8,128)(2,1)S(1)}, bf16[32,32,128]{2,1,0:T(8,128)(2,1)}, u32[]{:S(2)}, u32[]{:S(2)}) collective-permute-start(bf16[32,32,128]{2,1,0:T(8,128)(2,1)S(1)} %all-to-all-done.refs_0_), channel_id=1, source_target_pairs={{0,32},{32,64},{64,96},{96,0},{1,33},{33,65},{65,97},{97,1},{2,34}... | collective-permute-start | bytes 786440 | tf_op jit(solution)/shard_map/ppermute | solution.py:34
  57.3 17.8 %collective-permute-start.3 = (bf16[32,32,128]{2,1,0:T(8,128)(2,1)S(1)}, bf16[32,32,128]{2,1,0:T(8,128)(2,1)S(1)}, u32[]{:S(2)}, u32[]{:S(2)}) collective-permute-start(bf16[32,32,128]{2,1,0:T(8,128)(2,1)S(1)} %all-to-all-done.refs_0_), channel_id=1, source_target_pairs={{0,96},{32,0},{64,32},{96,64},{1,97},{33,1},{65,33},{97,65},{2,98}... | collective-permute-start | bytes 786440 | tf_op jit(solution)/shard_map/ppermute | solution.py:34
  61.3 14.6 %collective-permute-start.2 = (bf16[32,32,128]{2,1,0:T(8,128)(2,1)S(1)}, bf16[32,32,128]{2,1,0:T(8,128)(2,1)}, u32[]{:S(2)}, u32[]{:S(2)}) collective-permute-start(bf16[32,32,128]{2,1,0:T(8,128)(2,1)S(1)} %all-to-all-done.refs_0_), channel_id=1, source_target_pairs={{0,64},{32,96},{64,0},{96,32},{1,65},{33,97},{65,1},{97,33},{2,66}... | collective-permute-start | bytes 786440 | tf_op jit(solution)/shard_map/ppermute | solution.py:34
  64.7 25.4 %collective-permute-start.5 = (bf16[64,2688]{1,0:T(8,128)(2,1)}, bf16[64,2688]{1,0:T(8,128)(2,1)}, u32[]{:S(2)}, u32[]{:S(2)}) collective-permute-start(bf16[64,2688]{1,0:T(8,128)(2,1)} %collective-permute-done.refs_1_), channel_id=1, source_target_pairs={{0,1},{1,0},{2,3},{3,2},{4,5},{5,4},{6,7},{7,6},{8,9},{9,8},{10,11... | collective-permute-start | bytes 1032200 | tf_op jit(solution)/shard_map/ppermute | solution.py:34
  73.4 6.0 %copy-start.15 = (s32[1024]{0:T(1024)S(1)}, s32[1024]{0:T(1024)}, u32[]{:S(2)}) copy-start(s32[1024]{0:T(1024)} %param.20) | copy-start | bytes 12292
  78.7 0.7 copy-start.2
  79.4 1.0 copy-start.3
  80.4 9.7 %copy-start.16 = (s32[1024]{0:T(1024)S(1)}, s32[1024]{0:T(1024)}, u32[]{:S(2)}) copy-start(s32[1024]{0:T(1024)} %param.20) | copy-start | bytes 12292
  80.4 9.7 %copy-start.17 = (s32[4]{0:T(128)S(1)}, s32[4]{0:T(128)}, u32[]{:S(2)}) copy-start(s32[4]{0:T(128)} %broadcast_xor_fusion.place_ref) | copy-start | bytes 52
  90.0 0.7 copy-start.12
  95.3 0.9 copy-start.1
  96.2 0.8 copy-start.18
  97.0 43.9 %all-to-all-start.2 = ((bf16[128,24,128]{2,1,0:T(8,128)(2,1)}), bf16[128,24,128]{2,1,0:T(8,128)(2,1)S(1)}, u32[]{:S(2)}, u32[]{:S(2)}) async-start(bf16[128,24,128]{2,1,0:T(8,128)(2,1)} %bitcast.27), calls=%async_computation.2 | async-start | bytes 1572864 | tf_op jit(solution)/shard_map/all_to_all | solution.py:29
  117.3 23.8 %collective-permute-start.6 = (bf16[33,32,128]{2,1,0:T(8,128)(2,1)}, bf16[33,32,128]{2,1,0:T(8,128)(2,1)}, u32[]{:S(2)}, u32[]{:S(2)}) collective-permute-start(bf16[33,32,128]{2,1,0:T(8,128)(2,1)} %get-tuple-element.37), channel_id=1, source_target_pairs={{0,64},{32,96},{64,0},{96,32},{1,65},{33,97},{65,1},{97,33},{2,66}... | collective-permute-start | bytes 811016 | tf_op jit(solution)/shard_map/ppermute | solution.py:34
  121.8 19.5 %collective-permute-start.7 = (bf16[33,32,128]{2,1,0:T(8,128)(2,1)}, bf16[33,32,128]{2,1,0:T(8,128)(2,1)}, u32[]{:S(2)}, u32[]{:S(2)}) collective-permute-start(bf16[33,32,128]{2,1,0:T(8,128)(2,1)} %get-tuple-element.38), channel_id=1, source_target_pairs={{0,32},{32,64},{64,96},{96,0},{1,33},{33,65},{65,97},{97,1},{2,34}... | collective-permute-start | bytes 811016 | tf_op jit(solution)/shard_map/ppermute | solution.py:34
  124.3 29.1 %copy-start.10 = (s32[2,2048]{1,0:T(2,128)S(1)}, s32[2,2048]{1,0:T(2,128)}, u32[]{:S(2)}) copy-start(s32[2,2048]{1,0:T(2,128)} %copy-done.9) | copy-start | bytes 49156
  124.3 17.0 %collective-permute-start.8 = (bf16[33,32,128]{2,1,0:T(8,128)(2,1)}, bf16[33,32,128]{2,1,0:T(8,128)(2,1)}, u32[]{:S(2)}, u32[]{:S(2)}) collective-permute-start(bf16[33,32,128]{2,1,0:T(8,128)(2,1)} %get-tuple-element.39), channel_id=1, source_target_pairs={{0,96},{32,0},{64,32},{96,64},{1,97},{33,1},{65,33},{97,65},{2,98}... | collective-permute-start | bytes 811016 | tf_op jit(solution)/shard_map/ppermute | solution.py:34
  143.3 26.5 %all-to-all-start.3 = ((bf16[32,48,128]{2,1,0:T(8,128)(2,1)}), bf16[32,48,128]{2,1,0:T(8,128)(2,1)S(1)}, u32[]{:S(2)}, u32[]{:S(2)}) async-start(bf16[32,48,128]{2,1,0:T(8,128)(2,1)} %hub_grads_over_x.1), calls=%async_computation.3 | async-start | bytes 786432 | tf_op jit(solution)/shard_map/all_to_all | solution.py:29
  153.4 1.0 copy-start.19

commit v7 on v6

--- a/solution.py
+++ b/solution.py
@@ -185,14 +185,14 @@
         partial(layer_kernel, sizes),
         out_shape=[jax.ShapeDtypeStruct(shape, BF) for shape in [*held, bias_shape]],
         in_specs=[SMEM] + [VMEM] * 7,
-        out_specs=[pl.BlockSpec(memory_space=pl.ANY)] * len(held) + [VMEM],
+        out_specs=[pl.BlockSpec(memory_space=pltpu.HBM)] * len(held) + [VMEM],
         scratch_shapes=[pltpu.VMEM(shape, BF) for shape in held]
         + [
             pltpu.VMEM((full, nodes), BF),
             pltpu.VMEM((full, 2 * full), F32),
             pltpu.SemaphoreType.DMA((len(held),)),
         ],
-        compiler_params=pltpu.CompilerParams(vmem_limit_bytes=VMEM_LIMIT),
+        compiler_params=pltpu.CompilerParams(vmem_limit_bytes=60 * MIB),
         cost_estimate=pl.CostEstimate(flops=1000 * MIB, bytes_accessed=4 * MIB, transcendentals=0),
         name="layer",
     )(place, index, degree, mixed, *own_blocks)
@@ -482,14 +482,15 @@
     bias_terms = jnp.pad(bias_terms, ((0, 0), (0, 128 - bias_terms.shape[1])))
     feat_own, send_index, _ = lax.optimization_barrier((features, send_index, hub_send))
     own = own_block(feat_own, cotangent, w_self.T, w_neigh.T, bias_terms)
-    near = (own, shift(own, "yl", 1), shift(own, "core", 1))
+    across = shift(own, "core", 1)
     tail_send = gather_slots(send_index, features, parts, slots)
-    hub_plane, tail_send, recv_index, near = lax.optimization_barrier(
-        (hub_plane, tail_send, recv_index, near)
+    hub_plane, tail_send, recv_index, own, across = lax.optimization_barrier(
+        (hub_plane, tail_send, recv_index, own, across)
     )
     arrived = swap(tail_send, DOM)
     hub_all = [hub_plane] + [shift(hub_plane, "x", k) for k in range(1, x_size)]
-    own_blocks = [*near, shift(near[1], "core", 1)]
+    near = shift(own, "yl", 1)
+    own_blocks = [own, near, across, shift(near, "core", 1)]
     place = lax.axis_index(REP) ^ jnp.array([0, 2, 1, 3], jnp.int32)
 
     fold = partial(fold_hubs, *hub_at, tiles=tiles, sizes=sizes, blocks=blocks)

time: 173 us -> 166 us (0.960)
  the two profiles are of different devices: /device:TPU:8 before, /device:TPU:16 now
where the time goes in v7:
time: 166 us; the launch traced here: 164 us
  starting transfers between devices  84 us (51%)
  waiting for transfers between devices  32.2 us (19%)
  Pallas kernels  28.2 us (17%)
  local copies, waits for them, and re-layouts  8.9 us (5%)
  blocking collectives  7.89 us (5%)
  other arithmetic  2.16 us (1%)
    all_to_all x4, starting transfers between devices, swap(): return lax.all_to_all(pieces, axis, split_axis=0, concat_axis=0, tiled=True)  54.7 us
    ppermute x9, starting transfers between devices, shift(): lax.ppermute(values, axis, [(i, (i + step) % size) for i in range(size)])  29.3 us
    all_to_all x4, waiting for transfers between devices, swap(): return lax.all_to_all(pieces, axis, split_axis=0, concat_axis=0, tiled=True)  23.7 us
    ppermute x9, waiting for transfers between devices, shift(): lax.ppermute(values, axis, [(i, (i + step) % size) for i in range(size)])  8.52 us
    all_gather x1, blocking collectives, local(): full_mixed = lax.all_gather(mixed, REP, axis=0, tiled=True)  7.89 us
    pallas_call x2, Pallas kernels, hub_grad_terms(): call(partial(hub_grad_kernel, steps, sizes), [jax.ShapeDtypeStruct(shape,...  6.36 us
    unnamed x34, local copies, waits for them, and re-layouts  6.13 us
    pallas_call x1, Pallas kernels, layer(): pl.pallas_call(partial(layer_kernel, sizes), out_shape=[jax.ShapeDtypeStr...  5.46 us
  transfers between devices with their start and end apart: 13, of which 5 were waited for; matrix products, arithmetic and copies ran while one was open for 2% of the time, Pallas kernels for 12%

profile of v7, /device:TPU:16, one launch (start us, length us, event | category | flops | bytes accessed | tf_op | source)
XLA Modules:
  0.0 164.3 jit_solution(2326928950987934398)
XLA Ops:
  0.7 0.8 fusion.4
  1.4 0.1 pad_maximum_fusion
  1.5 0.7 broadcast_in_dim.17
  2.2 16.1 %all-to-all-start = ((bf16[32,32,128]{2,1,0:T(8,128)(2,1)}), bf16[32,32,128]{2,1,0:T(8,128)(2,1)S(1)}, u32[]{:S(2)}, u32[]{:S(2)}) async-start(bf16[32,32,128]{2,1,0:T(8,128)(2,1)} %broadcast_in_dim.17), calls=%async_computation | async-start | bytes 524288 | tf_op jit(solution)/shard_map/all_to_all | solution.py:29
  18.3 0.7 fusion
  19.0 0.1 copy.31
  19.1 0.8 copy.29
  20.0 0.8 select_bitcast_fusion
  20.7 0.1 reshape.37.index_ref
  20.9 1.0 copy-done.3
  21.9 0.9 copy-done.5
  22.8 0.8 copy-done.7
  23.6 0.8 copy-done.8
  24.4 1.9 %collective-permute-start = (bf16[64,2688]{1,0:T(8,128)(2,1)S(1)}, bf16[64,2688]{1,0:T(8,128)(2,1)}, u32[]{:S(2)}, u32[]{:S(2)}) collective-permute-start(bf16[64,2688]{1,0:T(8,128)(2,1)S(1)} %own_block.1.refs_0_), channel_id=1, source_target_pairs={{0,1},{1,0},{2,3},{3,2},{4,5},{5,4},{6,7},{7,6},{8,9},{9,8},{10,11... | collective-permute-start | bytes 1032200 | tf_op jit(solution)/shard_map/ppermute | solution.py:34
  26.3 0.1 copy.30
  26.4 0.1 reshape.38.index_ref
  26.5 1.8 %tail_rows_out.1 = bf16[128,16,128]{2,1,0:T(8,128)(2,1)} custom-call(s32[2,2048]{1,0:T(2,128)S(1)} %reshape.37.index_ref, bf16[64,1024]{1,0:T(8,128)(2,1)S(1)} %copy-done.4), custom_call_target="tpu_custom_call" | custom-call | flops 536870912 | bytes 2097152 | tf_op jit(solution)/shard_map/tail_rows_out/pallas_call | solution.py:86
  28.4 3.9 %all-to-all-done.refs_0_ = bf16[32,32,128]{2,1,0:T(8,128)(2,1)S(1)} async-done(((bf16[32,32,128]{2,1,0:T(8,128)(2,1)}), bf16[32,32,128]{2,1,0:T(8,128)(2,1)S(1)}, u32[]{:S(2)}, u32[]{:S(2)}) %all-to-all-start) | async-done | bytes 262176 | tf_op jit(solution)/shard_map/all_to_all | solution.py:29
  32.3 12.0 %all-to-all-start.1 = ((bf16[128,16,128]{2,1,0:T(8,128)(2,1)}), bf16[128,16,128]{2,1,0:T(8,128)(2,1)S(1)}, u32[]{:S(2)}, u32[]{:S(2)}) async-start(bf16[128,16,128]{2,1,0:T(8,128)(2,1)} %tail_rows_out.1), calls=%async_computation.1 | async-start | bytes 1048576 | tf_op jit(solution)/shard_map/all_to_all | solution.py:29
  44.3 2.6 %collective-permute-start.4 = (bf16[64,2688]{1,0:T(8,128)(2,1)S(1)}, bf16[64,2688]{1,0:T(8,128)(2,1)}, u32[]{:S(2)}, u32[]{:S(2)}) collective-permute-start(bf16[64,2688]{1,0:T(8,128)(2,1)S(1)} %own_block.1.refs_0_), channel_id=1, source_target_pairs={{0,2},{2,0},{1,3},{3,1},{4,6},{6,4},{5,7},{7,5},{8,10},{10,8},{9,1... | collective-permute-start | bytes 1032200 | tf_op jit(solution)/shard_map/ppermute | solution.py:34
  46.9 3.4 %collective-permute-start.3 = (bf16[32,32,128]{2,1,0:T(8,128)(2,1)S(1)}, bf16[32,32,128]{2,1,0:T(8,128)(2,1)}, u32[]{:S(2)}, u32[]{:S(2)}) collective-permute-start(bf16[32,32,128]{2,1,0:T(8,128)(2,1)S(1)} %all-to-all-done.refs_0_), channel_id=1, source_target_pairs={{0,32},{32,64},{64,96},{96,0},{1,33},{33,65},{65,97},{97,1},{2,34}... | collective-permute-start | bytes 786440 | tf_op jit(solution)/shard_map/ppermute | solution.py:34
  50.3 3.6 %collective-permute-start.2 = (bf16[32,32,128]{2,1,0:T(8,128)(2,1)S(1)}, bf16[32,32,128]{2,1,0:T(8,128)(2,1)S(1)}, u32[]{:S(2)}, u32[]{:S(2)}) collective-permute-start(bf16[32,32,128]{2,1,0:T(8,128)(2,1)S(1)} %all-to-all-done.refs_0_), channel_id=1, source_target_pairs={{0,96},{32,0},{64,32},{96,64},{1,97},{33,1},{65,33},{97,65},{2,98}... | collective-permute-start | bytes 786440 | tf_op jit(solution)/shard_map/ppermute | solution.py:34
  54.0 3.8 %collective-permute-start.1 = (bf16[32,32,128]{2,1,0:T(8,128)(2,1)S(1)}, bf16[32,32,128]{2,1,0:T(8,128)(2,1)}, u32[]{:S(2)}, u32[]{:S(2)}) collective-permute-start(bf16[32,32,128]{2,1,0:T(8,128)(2,1)S(1)} %all-to-all-done.refs_0_), channel_id=1, source_target_pairs={{0,64},{32,96},{64,0},{96,32},{1,65},{33,97},{65,1},{97,33},{2,66}... | collective-permute-start | bytes 786440 | tf_op jit(solution)/shard_map/ppermute | solution.py:34
  57.8 6.1 %collective-permute-done.4.refs_1_ = bf16[64,2688]{1,0:T(8,128)(2,1)} collective-permute-done((bf16[64,2688]{1,0:T(8,128)(2,1)S(1)}, bf16[64,2688]{1,0:T(8,128)(2,1)}, u32[]{:S(2)}, u32[]{:S(2)}) %collective-permute-start.4) | collective-permute-done | bytes 344096 | tf_op jit(solution)/shard_map/ppermute | solution.py:34
  63.9 1.9 %collective-permute-start.5 = (bf16[64,2688]{1,0:T(8,128)(2,1)}, bf16[64,2688]{1,0:T(8,128)(2,1)}, u32[]{:S(2)}, u32[]{:S(2)}) collective-permute-start(bf16[64,2688]{1,0:T(8,128)(2,1)} %collective-permute-done.4.refs_1_), channel_id=1, source_target_pairs={{0,1},{1,0},{2,3},{3,2},{4,5},{5,4},{6,7},{7,6},{8,9},{9,8},{10,11... | collective-permute-start | bytes 1032200 | tf_op jit(solution)/shard_map/ppermute | solution.py:34
  65.8 0.5 broadcast_xor_fusion.place_ref
  66.3 2.7 %hub_sums.2.refs_3_ = f32[64,1024]{1,0:T(8,128)S(1)} custom-call(s32[1]{0:T(128)} %bitcast.11.x_ref, s32[128]{0:T(128)S(1)} %bitcast.29, s32[128]{0:T(128)S(1)} %bitcast.33, bf16[32,32,128]{2,1,0:T(8,128)(2,1)S(1)} %all-to-all-done.refs_0_, bf16[32,32,128]{2,1,0:T(8,128)(2,1)} %collective-permute-done.3.refs_1_, bf16[128,64,128]{2,1,0:T(8,128)(2,1)S(1)} %bitcast.23), custom_call_target="tpu_custom_call" | custom-call | flops 134217728 | bytes 4194304 | tf_op jit(solution)/shard_map/hub_sums/pallas_call | solution.py:325
  69.1 2.7 %hub_sums.3.hub_ref = f32[64,1024]{1,0:T(8,128)S(1)} custom-call(s32[1]{0:T(128)} %bitcast.11.x_ref, s32[128]{0:T(128)S(1)} %bitcast.30, s32[128]{0:T(128)S(1)} %bitcast.34, bf16[32,32,128]{2,1,0:T(8,128)(2,1)} %collective-permute-done.1.refs_0_, bf16[32,32,128]{2,1,0:T(8,128)(2,1)S(1)} %collective-permute-done.2.refs_1_, ...), custom_call_target="tpu_custom_call" | custom-call | flops 134217728 | bytes 4194304 | tf_op jit(solution)/shard_map/hub_sums/pallas_call | solution.py:325
  71.9 2.4 %mixed.1 = bf16[64,1024]{1,0:T(8,128)(2,1)S(1)} custom-call(s32[2,2048]{1,0:T(2,128)S(1)} %reshape.38.index_ref, bf16[128,16,128]{2,1,0:T(8,128)(2,1)S(1)} %all-to-all-done.1.arrived_ref, f32[64,1024]{1,0:T(8,128)S(1)} %hub_sums.3.hub_ref, s32[1,1024]{1,0:T(1,128)S(1)} %bitcast.38), custom_call_target="tpu_custom_call" | custom-call | flops 1073741824 | bytes 2097152 | tf_op jit(solution)/shard_map/mixed/pallas_call | solution.py:223
  74.3 7.9 %all_gather.3.mixed_ref = bf16[256,1024]{1,0:T(8,128)(2,1)} all-gather(bf16[64,1024]{1,0:T(8,128)(2,1)S(1)} %mixed.1), channel_id=1, replica_groups=mesh['yh'=4,'x'=4,'z'=8,'yl'=2,'core'=2] {'yl','core'}, dimensions={0}, use_global_device_ids=true | all-gather | bytes 655360 | tf_op jit(solution)/shard_map/all_gather | solution.py:500
  82.2 5.5 %layer.1 = (bf16[64,1024]{1,0:T(8,128)(2,1)}, bf16[256,1024]{1,0:T(8,128)(2,1)}, bf16[64,1024]{1,0:T(8,128)(2,1)}, bf16[64,48,128]{2,1,0:T(8,128)(2,1)}, bf16[64...) custom-call(s32[4]{0:T(128)} %broadcast_xor_fusion.place_ref, s32[2,2048]{1,0:T(2,128)} %copy-done.9, s32[1,1024]{1,0:T(1,128)} %bitcast.37, ...), custom_call_target="tpu_custom_call" | custom-call | flops 1048576000 | bytes 4194304 | tf_op jit(solution)/shard_map/layer/pallas_call | solution.py:184
  87.7 16.2 %all-to-all-start.2 = ((bf16[128,24,128]{2,1,0:T(8,128)(2,1)}), bf16[128,24,128]{2,1,0:T(8,128)(2,1)S(1)}, u32[]{:S(2)}, u32[]{:S(2)}) async-start(bf16[128,24,128]{2,1,0:T(8,128)(2,1)} %bitcast.39), calls=%async_computation.2 | async-start | bytes 1572864 | tf_op jit(solution)/shard_map/all_to_all | solution.py:29
  103.9 0.9 copy-done.1
  104.8 0.7 copy-done.6
  105.5 4.7 %hub_grad_terms.3 = (bf16[33,32,128]{2,1,0:T(8,128)(2,1)}, bf16[33,32,128]{2,1,0:T(8,128)(2,1)}, bf16[33,32,128]{2,1,0:T(8,128)(2,1)}) custom-call(s32[1]{0:T(128)} %bitcast.11.x_ref, s32[128]{0:T(128)S(1)} %bitcast.31, s32[128]{0:T(128)S(1)} %bitcast.35, bf16[64,1024]{1,0:T(8,128)(2,1)S(1)} %copy-done.1, bf16[32,128]{1,0:T(8,128)(2,1)S(1)} %copy-done.6, ...), custom_call_target="tpu_custom_call" | custom-call | flops 201326592 | bytes 4194304 | tf_op jit(solution)/shard_map/hub_grad_terms/pallas_call | solution.py:367
  110.2 5.0 %collective-permute-start.6 = (bf16[33,32,128]{2,1,0:T(8,128)(2,1)}, bf16[33,32,128]{2,1,0:T(8,128)(2,1)S(1)}, u32[]{:S(2)}, u32[]{:S(2)}) collective-permute-start(bf16[33,32,128]{2,1,0:T(8,128)(2,1)} %get-tuple-element.35), channel_id=1, source_target_pairs={{0,64},{32,96},{64,0},{96,32},{1,65},{33,97},{65,1},{97,33},{2,66}... | collective-permute-start | bytes 811016 | tf_op jit(solution)/shard_map/ppermute | solution.py:34
  115.1 2.5 %collective-permute-start.7 = (bf16[33,32,128]{2,1,0:T(8,128)(2,1)}, bf16[33,32,128]{2,1,0:T(8,128)(2,1)}, u32[]{:S(2)}, u32[]{:S(2)}) collective-permute-start(bf16[33,32,128]{2,1,0:T(8,128)(2,1)} %get-tuple-element.36), channel_id=1, source_target_pairs={{0,32},{32,64},{64,96},{96,0},{1,33},{33,65},{65,97},{97,1},{2,34}... | collective-permute-start | bytes 811016 | tf_op jit(solution)/shard_map/ppermute | solution.py:34
  117.7 4.5 %collective-permute-start.8 = (bf16[33,32,128]{2,1,0:T(8,128)(2,1)}, bf16[33,32,128]{2,1,0:T(8,128)(2,1)}, u32[]{:S(2)}, u32[]{:S(2)}) collective-permute-start(bf16[33,32,128]{2,1,0:T(8,128)(2,1)} %get-tuple-element.37), channel_id=1, source_target_pairs={{0,96},{32,0},{64,32},{96,64},{1,97},{33,1},{65,33},{97,65},{2,98}... | collective-permute-start | bytes 811016 | tf_op jit(solution)/shard_map/ppermute | solution.py:34
  122.2 1.7 %hub_grad_terms.2.refs_0_ = bf16[33,32,128]{2,1,0:T(8,128)(2,1)S(1)} custom-call(s32[1]{0:T(128)} %bitcast.11.x_ref, s32[128]{0:T(128)S(1)} %bitcast.32, s32[128]{0:T(128)S(1)} %bitcast.36, bf16[64,1024]{1,0:T(8,128)(2,1)S(1)} %copy-done.1, bf16[32,128]{1,0:T(8,128)(2,1)S(1)} %copy-done.6, bf16[128,64,128]{2,1,0:T(8,128)(2,1)S(1)} %bitcast.26), custom_call_target="tpu_custom_call" | custom-call | flops 67108864 | bytes 4194304 | tf_op jit(solution)/shard_map/hub_grad_terms/pallas_call | solution.py:367
  123.9 7.4 %all-to-all-done.2.arrived_ref = bf16[128,24,128]{2,1,0:T(8,128)(2,1)S(1)} async-done(((bf16[128,24,128]{2,1,0:T(8,128)(2,1)}), bf16[128,24,128]{2,1,0:T(8,128)(2,1)S(1)}, u32[]{:S(2)}, u32[]{:S(2)}) %all-to-all-start.2) | async-done | bytes 786464 | tf_op jit(solution)/shard_map/all_to_all | solution.py:29
  131.3 0.1 convert_reduce_fusion.refs_4_
  131.4 2.4 %collective-permute-done.7.refs_2_ = bf16[33,32,128]{2,1,0:T(8,128)(2,1)} collective-permute-done((bf16[33,32,128]{2,1,0:T(8,128)(2,1)}, bf16[33,32,128]{2,1,0:T(8,128)(2,1)}, u32[]{:S(2)}, u32[]{:S(2)}) %collective-permute-start.7) | collective-permute-done | bytes 270368 | tf_op jit(solution)/shard_map/ppermute | solution.py:34
  133.8 1.9 %hub_grads_over_x.1 = bf16[32,48,128]{2,1,0:T(8,128)(2,1)} custom-call(bf16[33,32,128]{2,1,0:T(8,128)(2,1)S(1)} %hub_grad_terms.2.refs_0_, bf16[33,32,128]{2,1,0:T(8,128)(2,1)S(1)} %collective-permute-done.6.refs_1_, bf16[33,32,128]{2,1,0:T(8,128)(2,1)} %collective-permute-done.7.refs_2_, bf16[33,32,128]{2,1,0:T(8,128)(2,1)} %collective-permute-done.8.refs_3_, ...), custom_call_target="tpu_custom_call" | custom-call | flops 1048576 | bytes 2097152 | tf_op jit(solution)/shard_map/hub_grads_over_x/pallas_call | solution.py:396
  135.8 10.5 %all-to-all-start.3 = ((bf16[32,48,128]{2,1,0:T(8,128)(2,1)}), bf16[32,48,128]{2,1,0:T(8,128)(2,1)S(1)}, u32[]{:S(2)}, u32[]{:S(2)}) async-start(bf16[32,48,128]{2,1,0:T(8,128)(2,1)} %hub_grads_over_x.1), calls=%async_computation.3 | async-start | bytes 786432 | tf_op jit(solution)/shard_map/all_to_all | solution.py:29
  146.2 1.0 copy-done.13
  147.3 3.1 %tail_grads.1.base_ref = f32[64,1024]{1,0:T(8,128)} custom-call(s32[2,2048]{1,0:T(2,128)S(1)} %reshape.37.index_ref, bf16[128,24,128]{2,1,0:T(8,128)(2,1)S(1)} %all-to-all-done.2.arrived_ref, bf16[64,256]{1,0:T(8,128)(2,1)S(1)} %copy-done.14, bf16[256,1024]{1,0:T(8,128)(2,1)S(1)} %copy-done.13), custom_call_target="tpu_custom_call" | custom-call | flops 1073741824 | bytes 2097152 | tf_op jit(solution)/shard_map/tail_grads/pallas_call | solution.py:246
  150.4 12.4 %all-to-all-done.3.second_ref = bf16[32,48,128]{2,1,0:T(8,128)(2,1)S(1)} async-done(((bf16[32,48,128]{2,1,0:T(8,128)(2,1)}), bf16[32,48,128]{2,1,0:T(8,128)(2,1)S(1)}, u32[]{:S(2)}, u32[]{:S(2)}) %all-to-all-start.3) | async-done | bytes 393248 | tf_op jit(solution)/shard_map/all_to_all | solution.py:29
  162.8 1.6 gradients.1
  (39 shorter events, 0.1 us)
Async XLA Ops:
  0.6 25.9 %copy-start.4 = (bf16[64,1024]{1,0:T(8,128)(2,1)S(1)}, bf16[64,1024]{1,0:T(8,128)(2,1)}, u32[]{:S(2)}) copy-start(bf16[64,1024]{1,0:T(8,128)(2,1)} %feat_ref) | copy-start | bytes 393220
  0.6 25.6 %copy-start.15 = (s32[1,128,32]{1,2,0:T(8,128)S(1)}, s32[1,128,32]{1,2,0:T(8,128)}, u32[]{:S(2)}) copy-start(s32[1,128,32]{1,2,0:T(8,128)} %param.19) | copy-start | bytes 49156
  2.2 30.1 %all-to-all-start = ((bf16[32,32,128]{2,1,0:T(8,128)(2,1)}), bf16[32,32,128]{2,1,0:T(8,128)(2,1)S(1)}, u32[]{:S(2)}, u32[]{:S(2)}) async-start(bf16[32,32,128]{2,1,0:T(8,128)(2,1)} %broadcast_in_dim.17), calls=%async_computation | async-start | bytes 524288 | tf_op jit(solution)/shard_map/all_to_all | solution.py:29
  19.9 45.9 %copy-start.16 = (s32[4]{0:T(128)S(1)}, s32[4]{0:T(128)}, u32[]{:S(2)}) copy-start(s32[4]{0:T(128)} %constant.25.clone) | copy-start | bytes 52
  19.9 46.4 %copy-start.10 = (s32[1,128]{1,0:T(1,128)S(1)}, s32[1,128]{1,0:T(1,128)}, u32[]{:S(2)}) copy-start(s32[1,128]{1,0:T(1,128)} %param.15) | copy-start | bytes 1540
  20.0 46.4 %copy-start.11 = (s32[1,128]{1,0:T(1,128)S(1)}, s32[1,128]{1,0:T(1,128)}, u32[]{:S(2)}) copy-start(s32[1,128]{1,0:T(1,128)} %param.16) | copy-start | bytes 1540
  20.7 45.6 %copy-start = (bf16[1,128,64,128]{3,2,1,0:T(8,128)(2,1)S(1)}, bf16[1,128,64,128]{3,2,1,0:T(8,128)(2,1)}, u32[]{:S(2)}) copy-start(bf16[1,128,64,128]{3,2,1,0:T(8,128)(2,1)} %param.14) | copy-start | bytes 6291460
  20.9 1.0 copy-start.3
  21.9 0.9 copy-start.5
  22.8 0.8 copy-start.7
  23.6 0.8 copy-start.8
  24.4 44.7 %copy-start.2 = (bf16[64,2688]{1,0:T(8,128)(2,1)}, bf16[64,2688]{1,0:T(8,128)(2,1)S(1)}, u32[]{:S(2)}) copy-start(bf16[64,2688]{1,0:T(8,128)(2,1)S(1)} %own_block.1.refs_0_) | copy-start | bytes 1032196
  24.4 4.0 %collective-permute-start = (bf16[64,2688]{1,0:T(8,128)(2,1)S(1)}, bf16[64,2688]{1,0:T(8,128)(2,1)}, u32[]{:S(2)}, u32[]{:S(2)}) collective-permute-start(bf16[64,2688]{1,0:T(8,128)(2,1)S(1)} %own_block.1.refs_0_), channel_id=1, source_target_pairs={{0,1},{1,0},{2,3},{3,2},{4,5},{5,4},{6,7},{7,6},{8,9},{9,8},{10,11... | collective-permute-start | bytes 1032200 | tf_op jit(solution)/shard_map/ppermute | solution.py:34
  26.5 45.3 %copy-start.9 = (s32[2,2048]{1,0:T(2,128)}, s32[2,2048]{1,0:T(2,128)S(1)}, u32[]{:S(2)}) copy-start(s32[2,2048]{1,0:T(2,128)S(1)} %reshape.38.index_ref) | copy-start | bytes 49156
  32.3 39.5 %all-to-all-start.1 = ((bf16[128,16,128]{2,1,0:T(8,128)(2,1)}), bf16[128,16,128]{2,1,0:T(8,128)(2,1)S(1)}, u32[]{:S(2)}, u32[]{:S(2)}) async-start(bf16[128,16,128]{2,1,0:T(8,128)(2,1)} %tail_rows_out.1), calls=%async_computation.1 | async-start | bytes 1048576 | tf_op jit(solution)/shard_map/all_to_all | solution.py:29
  44.3 19.6 %collective-permute-start.4 = (bf16[64,2688]{1,0:T(8,128)(2,1)S(1)}, bf16[64,2688]{1,0:T(8,128)(2,1)}, u32[]{:S(2)}, u32[]{:S(2)}) collective-permute-start(bf16[64,2688]{1,0:T(8,128)(2,1)S(1)} %own_block.1.refs_0_), channel_id=1, source_target_pairs={{0,2},{2,0},{1,3},{3,1},{4,6},{6,4},{5,7},{7,5},{8,10},{10,8},{9,1... | collective-permute-start | bytes 1032200 | tf_op jit(solution)/shard_map/ppermute | solution.py:34
  46.9 19.4 %collective-permute-start.3 = (bf16[32,32,128]{2,1,0:T(8,128)(2,1)S(1)}, bf16[32,32,128]{2,1,0:T(8,128)(2,1)}, u32[]{:S(2)}, u32[]{:S(2)}) collective-permute-start(bf16[32,32,128]{2,1,0:T(8,128)(2,1)S(1)} %all-to-all-done.refs_0_), channel_id=1, source_target_pairs={{0,32},{32,64},{64,96},{96,0},{1,33},{33,65},{65,97},{97,1},{2,34}... | collective-permute-start | bytes 786440 | tf_op jit(solution)/shard_map/ppermute | solution.py:34
  50.3 18.7 %collective-permute-start.2 = (bf16[32,32,128]{2,1,0:T(8,128)(2,1)S(1)}, bf16[32,32,128]{2,1,0:T(8,128)(2,1)S(1)}, u32[]{:S(2)}, u32[]{:S(2)}) collective-permute-start(bf16[32,32,128]{2,1,0:T(8,128)(2,1)S(1)} %all-to-all-done.refs_0_), channel_id=1, source_target_pairs={{0,96},{32,0},{64,32},{96,64},{1,97},{33,1},{65,33},{97,65},{2,98}... | collective-permute-start | bytes 786440 | tf_op jit(solution)/shard_map/ppermute | solution.py:34
  54.0 15.1 %collective-permute-start.1 = (bf16[32,32,128]{2,1,0:T(8,128)(2,1)S(1)}, bf16[32,32,128]{2,1,0:T(8,128)(2,1)}, u32[]{:S(2)}, u32[]{:S(2)}) collective-permute-start(bf16[32,32,128]{2,1,0:T(8,128)(2,1)S(1)} %all-to-all-done.refs_0_), channel_id=1, source_target_pairs={{0,64},{32,96},{64,0},{96,32},{1,65},{33,97},{65,1},{97,33},{2,66}... | collective-permute-start | bytes 786440 | tf_op jit(solution)/shard_map/ppermute | solution.py:34
  63.9 18.3 %collective-permute-start.5 = (bf16[64,2688]{1,0:T(8,128)(2,1)}, bf16[64,2688]{1,0:T(8,128)(2,1)}, u32[]{:S(2)}, u32[]{:S(2)}) collective-permute-start(bf16[64,2688]{1,0:T(8,128)(2,1)} %collective-permute-done.4.refs_1_), channel_id=1, source_target_pairs={{0,1},{1,0},{2,3},{3,2},{4,5},{5,4},{6,7},{7,6},{8,9},{9,8},{10,11... | collective-permute-start | bytes 1032200 | tf_op jit(solution)/shard_map/ppermute | solution.py:34
  69.1 2.8 %copy-start.12 = (s32[1024]{0:T(1024)S(1)}, s32[1024]{0:T(1024)}, u32[]{:S(2)}) copy-start(s32[1024]{0:T(1024)} %param.20) | copy-start | bytes 12292
  87.7 43.6 %all-to-all-start.2 = ((bf16[128,24,128]{2,1,0:T(8,128)(2,1)}), bf16[128,24,128]{2,1,0:T(8,128)(2,1)S(1)}, u32[]{:S(2)}, u32[]{:S(2)}) async-start(bf16[128,24,128]{2,1,0:T(8,128)(2,1)} %bitcast.39), calls=%async_computation.2 | async-start | bytes 1572864 | tf_op jit(solution)/shard_map/all_to_all | solution.py:29
  103.9 0.9 copy-start.1
  104.8 0.7 copy-start.6
  110.2 21.3 %collective-permute-start.6 = (bf16[33,32,128]{2,1,0:T(8,128)(2,1)}, bf16[33,32,128]{2,1,0:T(8,128)(2,1)S(1)}, u32[]{:S(2)}, u32[]{:S(2)}) collective-permute-start(bf16[33,32,128]{2,1,0:T(8,128)(2,1)} %get-tuple-element.35), channel_id=1, source_target_pairs={{0,64},{32,96},{64,0},{96,32},{1,65},{33,97},{65,1},{97,33},{2,66}... | collective-permute-start | bytes 811016 | tf_op jit(solution)/shard_map/ppermute | solution.py:34
  115.1 18.7 %collective-permute-start.7 = (bf16[33,32,128]{2,1,0:T(8,128)(2,1)}, bf16[33,32,128]{2,1,0:T(8,128)(2,1)}, u32[]{:S(2)}, u32[]{:S(2)}) collective-permute-start(bf16[33,32,128]{2,1,0:T(8,128)(2,1)} %get-tuple-element.36), channel_id=1, source_target_pairs={{0,32},{32,64},{64,96},{96,0},{1,33},{33,65},{65,97},{97,1},{2,34}... | collective-permute-start | bytes 811016 | tf_op jit(solution)/shard_map/ppermute | solution.py:34
  117.7 28.6 %copy-start.14 = (bf16[64,256]{1,0:T(8,128)(2,1)S(1)}, bf16[64,256]{1,0:T(8,128)(2,1)}, u32[]{:S(2)}) copy-start(bf16[64,256]{1,0:T(8,128)(2,1)} %get-tuple-element.39.weight_ref) | copy-start | bytes 98308
  117.7 16.2 %collective-permute-start.8 = (bf16[33,32,128]{2,1,0:T(8,128)(2,1)}, bf16[33,32,128]{2,1,0:T(8,128)(2,1)}, u32[]{:S(2)}, u32[]{:S(2)}) collective-permute-start(bf16[33,32,128]{2,1,0:T(8,128)(2,1)} %get-tuple-element.37), channel_id=1, source_target_pairs={{0,96},{32,0},{64,32},{96,64},{1,97},{33,1},{65,33},{97,65},{2,98}... | collective-permute-start | bytes 811016 | tf_op jit(solution)/shard_map/ppermute | solution.py:34
  135.8 27.0 %all-to-all-start.3 = ((bf16[32,48,128]{2,1,0:T(8,128)(2,1)}), bf16[32,48,128]{2,1,0:T(8,128)(2,1)S(1)}, u32[]{:S(2)}, u32[]{:S(2)}) async-start(bf16[32,48,128]{2,1,0:T(8,128)(2,1)} %hub_grads_over_x.1), calls=%async_computation.3 | async-start | bytes 786432 | tf_op jit(solution)/shard_map/all_to_all | solution.py:29
  146.2 1.0 copy-start.13

commit v8 on v7

--- a/solution.py
+++ b/solution.py
@@ -34,7 +34,7 @@
     return lax.ppermute(values, axis, [(i, (i + step) % size) for i in range(size)])
 
 
-def call(kernel, out_shape, in_specs, scratch, name, flops, mib):
+def call(kernel, out_shape, in_specs, scratch, name, flops, mib, limit=VMEM_LIMIT):
     outs = VMEM if isinstance(out_shape, jax.ShapeDtypeStruct) else [VMEM] * len(out_shape)
     return pl.pallas_call(
         kernel,
@@ -42,7 +42,7 @@
         in_specs=in_specs,
         out_specs=outs,
         scratch_shapes=scratch,
-        compiler_params=pltpu.CompilerParams(vmem_limit_bytes=VMEM_LIMIT),
+        compiler_params=pltpu.CompilerParams(vmem_limit_bytes=limit),
         cost_estimate=pl.CostEstimate(flops=flops, bytes_accessed=mib * MIB, transcendentals=0),
         name=name,
     )
@@ -347,18 +347,20 @@
 
         @pl.loop(0, count // z_size)
         def _(yh):
-            for z in range(z_size):
+            for z in range(0, z_size, 2):
                 tile = tile_index(x_ref, k, sizes, yh, z, 1)
-                weights = tile_ref[tile]
-                dest = jnp.where(mask_ref[tile] > 0, block_ref[tile], blocks)
+                dests = [
+                    jnp.where(mask_ref[tile + i] > 0, block_ref[tile + i], blocks) for i in range(2)
+                ]
                 product = mm(
-                    blocked[dest],
-                    jnp.concatenate([weights, weights], axis=0),
+                    jnp.concatenate([blocked[dest] for dest in dests], axis=0),
+                    jnp.concatenate([tile_ref[tile], tile_ref[tile + 1]], axis=0),
                     BOTH_COLS,
                 )
-                out_ref[yh * z_size + z] = jnp.where(
-                    first, product[:half], product[half:]
-                ).astype(BF)
+                turned = pltpu.roll(product[half : 3 * half], 64, 1)
+                place = yh * z_size + z
+                out_ref[place] = jnp.where(first, product[:half], turned[:half]).astype(BF)
+                out_ref[place + 1] = jnp.where(first, turned[half:], product[3 * half :]).astype(BF)
 
 
 def hub_grad_terms(x_index, block, mask, grad, bias, tiles, steps, sizes, blocks):
@@ -372,6 +374,7 @@
         "hub_grad_terms",
         tiles.size * width * len(steps),
         4,
+        60 * MIB,
     )(x_index, block, mask, grad, bias, tiles)
 
 
@@ -490,11 +493,12 @@
     arrived = swap(tail_send, DOM)
     hub_all = [hub_plane] + [shift(hub_plane, "x", k) for k in range(1, x_size)]
     near = shift(own, "yl", 1)
-    own_blocks = [own, near, across, shift(near, "core", 1)]
     place = lax.axis_index(REP) ^ jnp.array([0, 2, 1, 3], jnp.int32)
 
     fold = partial(fold_hubs, *hub_at, tiles=tiles, sizes=sizes, blocks=blocks)
     hub_sum = fold(hub_all[:2], (0, 1), base=None)
+    hub_sum, near = lax.optimization_barrier((hub_sum, near))
+    own_blocks = [own, near, across, shift(near, "core", 1)]
     hub_sum = fold(hub_all[2:], (2, 3), base=hub_sum)
     mixed = mixed_sums(recv_index, arrived, hub_sum, degree)
     full_mixed = lax.all_gather(mixed, REP, axis=0, tiled=True)

time: 166 us -> 166 us (level)
  the two profiles are of different devices: /device:TPU:16 before, /device:TPU:8 now
where the time goes in v8:
time: 166 us; the launch traced here: 165 us
  starting transfers between devices  84.9 us (51%)
  waiting for transfers between devices  31.5 us (19%)
  Pallas kernels  30.1 us (18%)
  local copies, waits for them, and re-layouts  7.96 us (5%)
  blocking collectives  7.1 us (4%)
  other arithmetic  2.16 us (1%)
    all_to_all x4, starting transfers between devices, swap(): return lax.all_to_all(pieces, axis, split_axis=0, concat_axis=0, tiled=True)  55.8 us
    ppermute x9, starting transfers between devices, shift(): lax.ppermute(values, axis, [(i, (i + step) % size) for i in range(size)])  29 us
    all_to_all x4, waiting for transfers between devices, swap(): return lax.all_to_all(pieces, axis, split_axis=0, concat_axis=0, tiled=True)  24.6 us
    pallas_call x2, Pallas kernels, hub_grad_terms(): call(partial(hub_grad_kernel, steps, sizes), [jax.ShapeDtypeStruct(shape,...  9.34 us
    all_gather x1, blocking collectives, local(): full_mixed = lax.all_gather(mixed, REP, axis=0, tiled=True)  7.1 us
    ppermute x9, waiting for transfers between devices, shift(): lax.ppermute(values, axis, [(i, (i + step) % size) for i in range(size)])  6.94 us
    pallas_call x1, Pallas kernels, layer(): pl.pallas_call(partial(layer_kernel, sizes), out_shape=[jax.ShapeDtypeStr...  5.45 us
    pallas_call x2, Pallas kernels, fold_hubs(): call(partial(fold_kernel, steps, sizes, base is not None), jax.ShapeDtype...  5.44 us
  transfers between devices with their start and end apart: 13, of which 6 were waited for; matrix products, arithmetic and copies ran while one was open for 2% of the time, Pallas kernels for 13%

profile of v8, /device:TPU:8, one launch (start us, length us, event | category | flops | bytes accessed | tf_op | source)
XLA Modules:
  0.0 164.7 jit_solution(2831680758177867381)
XLA Ops:
  0.7 0.8 fusion.4
  1.4 0.1 pad_maximum_fusion
  1.5 0.7 broadcast_in_dim.17
  2.2 15.1 %all-to-all-start = ((bf16[32,32,128]{2,1,0:T(8,128)(2,1)}), bf16[32,32,128]{2,1,0:T(8,128)(2,1)S(1)}, u32[]{:S(2)}, u32[]{:S(2)}) async-start(bf16[32,32,128]{2,1,0:T(8,128)(2,1)} %broadcast_in_dim.17), calls=%async_computation | async-start | bytes 524288 | tf_op jit(solution)/shard_map/all_to_all | solution.py:29
  17.3 0.7 fusion
  18.0 0.1 copy.31
  18.1 0.8 copy.29
  19.0 0.7 select_bitcast_fusion
  19.7 0.1 reshape.37.index_ref
  19.9 1.0 copy-done.3
  20.9 0.9 copy-done.5
  21.8 0.8 copy-done.6
  22.5 0.8 copy-done.7
  23.3 1.9 %collective-permute-start = (bf16[64,2688]{1,0:T(8,128)(2,1)S(1)}, bf16[64,2688]{1,0:T(8,128)(2,1)}, u32[]{:S(2)}, u32[]{:S(2)}) collective-permute-start(bf16[64,2688]{1,0:T(8,128)(2,1)S(1)} %own_block.1.refs_0_), channel_id=1, source_target_pairs={{0,1},{1,0},{2,3},{3,2},{4,5},{5,4},{6,7},{7,6},{8,9},{9,8},{10,11... | collective-permute-start | bytes 1032200 | tf_op jit(solution)/shard_map/ppermute | solution.py:34
  25.3 0.1 copy.30
  25.4 0.1 reshape.38.index_ref
  25.5 1.8 %tail_rows_out.1 = bf16[128,16,128]{2,1,0:T(8,128)(2,1)} custom-call(s32[2,2048]{1,0:T(2,128)S(1)} %reshape.37.index_ref, bf16[64,1024]{1,0:T(8,128)(2,1)S(1)} %copy-done.4), custom_call_target="tpu_custom_call" | custom-call | flops 536870912 | bytes 2097152 | tf_op jit(solution)/shard_map/tail_rows_out/pallas_call | solution.py:86
  27.4 3.9 %all-to-all-done.refs_0_ = bf16[32,32,128]{2,1,0:T(8,128)(2,1)S(1)} async-done(((bf16[32,32,128]{2,1,0:T(8,128)(2,1)}), bf16[32,32,128]{2,1,0:T(8,128)(2,1)S(1)}, u32[]{:S(2)}, u32[]{:S(2)}) %all-to-all-start) | async-done | bytes 262176 | tf_op jit(solution)/shard_map/all_to_all | solution.py:29
  31.3 12.6 %all-to-all-start.1 = ((bf16[128,16,128]{2,1,0:T(8,128)(2,1)}), bf16[128,16,128]{2,1,0:T(8,128)(2,1)S(1)}, u32[]{:S(2)}, u32[]{:S(2)}) async-start(bf16[128,16,128]{2,1,0:T(8,128)(2,1)} %tail_rows_out.1), calls=%async_computation.1 | async-start | bytes 1048576 | tf_op jit(solution)/shard_map/all_to_all | solution.py:29
  43.9 3.3 %collective-permute-start.4 = (bf16[64,2688]{1,0:T(8,128)(2,1)S(1)}, bf16[64,2688]{1,0:T(8,128)(2,1)}, u32[]{:S(2)}, u32[]{:S(2)}) collective-permute-start(bf16[64,2688]{1,0:T(8,128)(2,1)S(1)} %own_block.1.refs_0_), channel_id=1, source_target_pairs={{0,2},{2,0},{1,3},{3,1},{4,6},{6,4},{5,7},{7,5},{8,10},{10,8},{9,1... | collective-permute-start | bytes 1032200 | tf_op jit(solution)/shard_map/ppermute | solution.py:34
  47.1 3.0 %collective-permute-start.3 = (bf16[32,32,128]{2,1,0:T(8,128)(2,1)S(1)}, bf16[32,32,128]{2,1,0:T(8,128)(2,1)}, u32[]{:S(2)}, u32[]{:S(2)}) collective-permute-start(bf16[32,32,128]{2,1,0:T(8,128)(2,1)S(1)} %all-to-all-done.refs_0_), channel_id=1, source_target_pairs={{0,32},{32,64},{64,96},{96,0},{1,33},{33,65},{65,97},{97,1},{2,34}... | collective-permute-start | bytes 786440 | tf_op jit(solution)/shard_map/ppermute | solution.py:34
  50.2 4.0 %collective-permute-start.2 = (bf16[32,32,128]{2,1,0:T(8,128)(2,1)S(1)}, bf16[32,32,128]{2,1,0:T(8,128)(2,1)S(1)}, u32[]{:S(2)}, u32[]{:S(2)}) collective-permute-start(bf16[32,32,128]{2,1,0:T(8,128)(2,1)S(1)} %all-to-all-done.refs_0_), channel_id=1, source_target_pairs={{0,96},{32,0},{64,32},{96,64},{1,97},{33,1},{65,33},{97,65},{2,98}... | collective-permute-start | bytes 786440 | tf_op jit(solution)/shard_map/ppermute | solution.py:34
  54.2 3.3 %collective-permute-start.1 = (bf16[32,32,128]{2,1,0:T(8,128)(2,1)S(1)}, bf16[32,32,128]{2,1,0:T(8,128)(2,1)}, u32[]{:S(2)}, u32[]{:S(2)}) collective-permute-start(bf16[32,32,128]{2,1,0:T(8,128)(2,1)S(1)} %all-to-all-done.refs_0_), channel_id=1, source_target_pairs={{0,64},{32,96},{64,0},{96,32},{1,65},{33,97},{65,1},{97,33},{2,66}... | collective-permute-start | bytes 786440 | tf_op jit(solution)/shard_map/ppermute | solution.py:34
  57.6 4.7 %collective-permute-done.3.refs_1_ = bf16[32,32,128]{2,1,0:T(8,128)(2,1)} collective-permute-done((bf16[32,32,128]{2,1,0:T(8,128)(2,1)S(1)}, bf16[32,32,128]{2,1,0:T(8,128)(2,1)}, u32[]{:S(2)}, u32[]{:S(2)}) %collective-permute-start.3) | collective-permute-done | bytes 262176 | tf_op jit(solution)/shard_map/ppermute | solution.py:34
  62.3 2.7 %hub_sums.2.refs_3_ = f32[64,1024]{1,0:T(8,128)S(1)} custom-call(s32[1]{0:T(128)} %bitcast.11.x_ref, s32[128]{0:T(128)S(1)} %bitcast.31, s32[128]{0:T(128)S(1)} %bitcast.35, bf16[32,32,128]{2,1,0:T(8,128)(2,1)S(1)} %all-to-all-done.refs_0_, bf16[32,32,128]{2,1,0:T(8,128)(2,1)} %collective-permute-done.3.refs_1_, bf16[128,64,128]{2,1,0:T(8,128)(2,1)S(1)} %bitcast.25), custom_call_target="tpu_custom_call" | custom-call | flops 134217728 | bytes 4194304 | tf_op jit(solution)/shard_map/hub_sums/pallas_call | solution.py:325
  65.1 1.9 %collective-permute-start.5 = (bf16[64,2688]{1,0:T(8,128)(2,1)}, bf16[64,2688]{1,0:T(8,128)(2,1)S(1)}, u32[]{:S(2)}, u32[]{:S(2)}) collective-permute-start(bf16[64,2688]{1,0:T(8,128)(2,1)} %collective-permute-done.4.refs_1_), channel_id=1, source_target_pairs={{0,1},{1,0},{2,3},{3,2},{4,5},{5,4},{6,7},{7,6},{8,9},{9,8},{10,11... | collective-permute-start | bytes 1032200 | tf_op jit(solution)/shard_map/ppermute | solution.py:34
  67.0 0.5 broadcast_xor_fusion.place_ref
  67.5 1.0 collective-permute-done.1.refs_0_
  68.6 2.7 %hub_sums.3.hub_ref = f32[64,1024]{1,0:T(8,128)S(1)} custom-call(s32[1]{0:T(128)} %bitcast.11.x_ref, s32[128]{0:T(128)S(1)} %bitcast.32, s32[128]{0:T(128)S(1)} %bitcast.36, bf16[32,32,128]{2,1,0:T(8,128)(2,1)} %collective-permute-done.1.refs_0_, bf16[32,32,128]{2,1,0:T(8,128)(2,1)S(1)} %collective-permute-done.2.refs_1_, ...), custom_call_target="tpu_custom_call" | custom-call | flops 134217728 | bytes 4194304 | tf_op jit(solution)/shard_map/hub_sums/pallas_call | solution.py:325
  71.3 2.4 %mixed.1 = bf16[64,1024]{1,0:T(8,128)(2,1)S(1)} custom-call(s32[2,2048]{1,0:T(2,128)S(1)} %reshape.38.index_ref, bf16[128,16,128]{2,1,0:T(8,128)(2,1)S(1)} %all-to-all-done.1.arrived_ref, f32[64,1024]{1,0:T(8,128)S(1)} %hub_sums.3.hub_ref, s32[1,1024]{1,0:T(1,128)S(1)} %bitcast.38), custom_call_target="tpu_custom_call" | custom-call | flops 1073741824 | bytes 2097152 | tf_op jit(solution)/shard_map/mixed/pallas_call | solution.py:223
  73.7 7.1 %all_gather.3.mixed_ref = bf16[256,1024]{1,0:T(8,128)(2,1)} all-gather(bf16[64,1024]{1,0:T(8,128)(2,1)S(1)} %mixed.1), channel_id=1, replica_groups=mesh['yh'=4,'x'=4,'z'=8,'yl'=2,'core'=2] {'yl','core'}, dimensions={0}, use_global_device_ids=true | all-gather | bytes 655360 | tf_op jit(solution)/shard_map/all_gather | solution.py:504
  80.8 0.7 copy-done.15
  81.6 5.5 %layer.1 = (bf16[64,1024]{1,0:T(8,128)(2,1)}, bf16[256,1024]{1,0:T(8,128)(2,1)}, bf16[64,1024]{1,0:T(8,128)(2,1)}, bf16[64,48,128]{2,1,0:T(8,128)(2,1)}, bf16[64...) custom-call(s32[4]{0:T(128)} %broadcast_xor_fusion.place_ref, s32[2,2048]{1,0:T(2,128)} %copy-done.8, s32[1,1024]{1,0:T(1,128)} %bitcast.37, ...), custom_call_target="tpu_custom_call" | custom-call | flops 1048576000 | bytes 4194304 | tf_op jit(solution)/shard_map/layer/pallas_call | solution.py:184
  87.0 18.6 %all-to-all-start.2 = ((bf16[128,24,128]{2,1,0:T(8,128)(2,1)}), bf16[128,24,128]{2,1,0:T(8,128)(2,1)S(1)}, u32[]{:S(2)}, u32[]{:S(2)}) async-start(bf16[128,24,128]{2,1,0:T(8,128)(2,1)} %bitcast.39), calls=%async_computation.2 | async-start | bytes 1572864 | tf_op jit(solution)/shard_map/all_to_all | solution.py:29
  105.6 5.8 %hub_grad_terms.3 = (bf16[33,32,128]{2,1,0:T(8,128)(2,1)}, bf16[33,32,128]{2,1,0:T(8,128)(2,1)}, bf16[33,32,128]{2,1,0:T(8,128)(2,1)}) custom-call(s32[1]{0:T(128)} %bitcast.11.x_ref, s32[128]{0:T(128)} %bitcast.29, s32[128]{0:T(128)} %bitcast.33, bf16[64,1024]{1,0:T(8,128)(2,1)} %get-tuple-element.37.grad_ref, bf16[32,128]{1,0:T(8,128)(2,1)} %get-tuple-element.38.bias_ref, ...), custom_call_target="tpu_custom_call" | custom-call | flops 201326592 | bytes 4194304 | tf_op jit(solution)/shard_map/hub_grad_terms/pallas_call | solution.py:369
  111.4 4.4 %collective-permute-start.6 = (bf16[33,32,128]{2,1,0:T(8,128)(2,1)}, bf16[33,32,128]{2,1,0:T(8,128)(2,1)S(1)}, u32[]{:S(2)}, u32[]{:S(2)}) collective-permute-start(bf16[33,32,128]{2,1,0:T(8,128)(2,1)} %get-tuple-element.39), channel_id=1, source_target_pairs={{0,64},{32,96},{64,0},{96,32},{1,65},{33,97},{65,1},{97,33},{2,66}... | collective-permute-start | bytes 811016 | tf_op jit(solution)/shard_map/ppermute | solution.py:34
  115.8 2.5 %collective-permute-start.7 = (bf16[33,32,128]{2,1,0:T(8,128)(2,1)}, bf16[33,32,128]{2,1,0:T(8,128)(2,1)S(1)}, u32[]{:S(2)}, u32[]{:S(2)}) collective-permute-start(bf16[33,32,128]{2,1,0:T(8,128)(2,1)} %get-tuple-element.40), channel_id=1, source_target_pairs={{0,32},{32,64},{64,96},{96,0},{1,33},{33,65},{65,97},{97,1},{2,34}... | collective-permute-start | bytes 811016 | tf_op jit(solution)/shard_map/ppermute | solution.py:34
  118.3 4.7 %collective-permute-start.8 = (bf16[33,32,128]{2,1,0:T(8,128)(2,1)}, bf16[33,32,128]{2,1,0:T(8,128)(2,1)S(1)}, u32[]{:S(2)}, u32[]{:S(2)}) collective-permute-start(bf16[33,32,128]{2,1,0:T(8,128)(2,1)} %get-tuple-element.41), channel_id=1, source_target_pairs={{0,96},{32,0},{64,32},{96,64},{1,97},{33,1},{65,33},{97,65},{2,98}... | collective-permute-start | bytes 811016 | tf_op jit(solution)/shard_map/ppermute | solution.py:34
  123.0 3.5 %hub_grad_terms.2.refs_0_ = bf16[33,32,128]{2,1,0:T(8,128)(2,1)} custom-call(s32[1]{0:T(128)} %bitcast.11.x_ref, s32[128]{0:T(128)} %bitcast.30, s32[128]{0:T(128)} %bitcast.34, bf16[64,1024]{1,0:T(8,128)(2,1)} %get-tuple-element.37.grad_ref, bf16[32,128]{1,0:T(8,128)(2,1)} %get-tuple-element.38.bias_ref, bf16[128,64,128]{2,1,0:T(8,128)(2,1)} %bitcast.24), custom_call_target="tpu_custom_call" | custom-call | flops 67108864 | bytes 4194304 | tf_op jit(solution)/shard_map/hub_grad_terms/pallas_call | solution.py:369
  126.5 7.6 %all-to-all-done.2.arrived_ref = bf16[128,24,128]{2,1,0:T(8,128)(2,1)S(1)} async-done(((bf16[128,24,128]{2,1,0:T(8,128)(2,1)}), bf16[128,24,128]{2,1,0:T(8,128)(2,1)S(1)}, u32[]{:S(2)}, u32[]{:S(2)}) %all-to-all-start.2) | async-done | bytes 786464 | tf_op jit(solution)/shard_map/all_to_all | solution.py:29
  134.2 0.1 convert_reduce_fusion.refs_4_
  134.3 1.2 collective-permute-done.7.refs_2_
  135.5 1.0 copy-done.1
  136.5 0.9 hub_grads_over_x.1
  137.3 9.6 %all-to-all-start.3 = ((bf16[32,48,128]{2,1,0:T(8,128)(2,1)}), bf16[32,48,128]{2,1,0:T(8,128)(2,1)S(1)}, u32[]{:S(2)}, u32[]{:S(2)}) async-start(bf16[32,48,128]{2,1,0:T(8,128)(2,1)} %hub_grads_over_x.1), calls=%async_computation.3 | async-start | bytes 786432 | tf_op jit(solution)/shard_map/all_to_all | solution.py:29
  147.0 3.1 %tail_grads.1.base_ref = f32[64,1024]{1,0:T(8,128)} custom-call(s32[2,2048]{1,0:T(2,128)S(1)} %reshape.37.index_ref, bf16[128,24,128]{2,1,0:T(8,128)(2,1)S(1)} %all-to-all-done.2.arrived_ref, bf16[64,256]{1,0:T(8,128)(2,1)S(1)} %copy-done.13, bf16[256,1024]{1,0:T(8,128)(2,1)S(1)} %copy-done.12), custom_call_target="tpu_custom_call" | custom-call | flops 1073741824 | bytes 2097152 | tf_op jit(solution)/shard_map/tail_grads/pallas_call | solution.py:246
  150.1 13.0 %all-to-all-done.3.second_ref = bf16[32,48,128]{2,1,0:T(8,128)(2,1)S(1)} async-done(((bf16[32,48,128]{2,1,0:T(8,128)(2,1)}), bf16[32,48,128]{2,1,0:T(8,128)(2,1)S(1)}, u32[]{:S(2)}, u32[]{:S(2)}) %all-to-all-start.3) | async-done | bytes 393248 | tf_op jit(solution)/shard_map/all_to_all | solution.py:29
  163.1 1.6 gradients.1
  (39 shorter events, 0.1 us)
Async XLA Ops:
  0.6 24.9 %copy-start.4 = (bf16[64,1024]{1,0:T(8,128)(2,1)S(1)}, bf16[64,1024]{1,0:T(8,128)(2,1)}, u32[]{:S(2)}) copy-start(bf16[64,1024]{1,0:T(8,128)(2,1)} %feat_ref) | copy-start | bytes 393220
  0.6 24.6 %copy-start.14 = (s32[1,128,32]{1,2,0:T(8,128)S(1)}, s32[1,128,32]{1,2,0:T(8,128)}, u32[]{:S(2)}) copy-start(s32[1,128,32]{1,2,0:T(8,128)} %param.19) | copy-start | bytes 49156
  2.2 29.1 %all-to-all-start = ((bf16[32,32,128]{2,1,0:T(8,128)(2,1)}), bf16[32,32,128]{2,1,0:T(8,128)(2,1)S(1)}, u32[]{:S(2)}, u32[]{:S(2)}) async-start(bf16[32,32,128]{2,1,0:T(8,128)(2,1)} %broadcast_in_dim.17), calls=%async_computation | async-start | bytes 524288 | tf_op jit(solution)/shard_map/all_to_all | solution.py:29
  18.9 43.4 %copy-start.9 = (s32[1,128]{1,0:T(1,128)S(1)}, s32[1,128]{1,0:T(1,128)}, u32[]{:S(2)}) copy-start(s32[1,128]{1,0:T(1,128)} %param.15) | copy-start | bytes 1540
  18.9 43.4 %copy-start.10 = (s32[1,128]{1,0:T(1,128)S(1)}, s32[1,128]{1,0:T(1,128)}, u32[]{:S(2)}) copy-start(s32[1,128]{1,0:T(1,128)} %param.16) | copy-start | bytes 1540
  19.7 42.6 %copy-start = (bf16[1,128,64,128]{3,2,1,0:T(8,128)(2,1)S(1)}, bf16[1,128,64,128]{3,2,1,0:T(8,128)(2,1)}, u32[]{:S(2)}) copy-start(bf16[1,128,64,128]{3,2,1,0:T(8,128)(2,1)} %param.14) | copy-start | bytes 6291460
  19.9 1.0 copy-start.3
  20.9 0.9 copy-start.5
  21.8 0.8 copy-start.6
  22.5 0.8 copy-start.7
  23.3 41.7 %copy-start.2 = (bf16[64,2688]{1,0:T(8,128)(2,1)}, bf16[64,2688]{1,0:T(8,128)(2,1)S(1)}, u32[]{:S(2)}) copy-start(bf16[64,2688]{1,0:T(8,128)(2,1)S(1)} %own_block.1.refs_0_) | copy-start | bytes 1032196
  23.3 4.0 %collective-permute-start = (bf16[64,2688]{1,0:T(8,128)(2,1)S(1)}, bf16[64,2688]{1,0:T(8,128)(2,1)}, u32[]{:S(2)}, u32[]{:S(2)}) collective-permute-start(bf16[64,2688]{1,0:T(8,128)(2,1)S(1)} %own_block.1.refs_0_), channel_id=1, source_target_pairs={{0,1},{1,0},{2,3},{3,2},{4,5},{5,4},{6,7},{7,6},{8,9},{9,8},{10,11... | collective-permute-start | bytes 1032200 | tf_op jit(solution)/shard_map/ppermute | solution.py:34
  25.5 45.8 %copy-start.8 = (s32[2,2048]{1,0:T(2,128)}, s32[2,2048]{1,0:T(2,128)S(1)}, u32[]{:S(2)}) copy-start(s32[2,2048]{1,0:T(2,128)S(1)} %reshape.38.index_ref) | copy-start | bytes 49156
  27.3 39.6 %copy-start.16 = (s32[4]{0:T(128)S(1)}, s32[4]{0:T(128)}, u32[]{:S(2)}) copy-start(s32[4]{0:T(128)} %constant.25.clone) | copy-start | bytes 52
  31.3 40.0 %all-to-all-start.1 = ((bf16[128,16,128]{2,1,0:T(8,128)(2,1)}), bf16[128,16,128]{2,1,0:T(8,128)(2,1)S(1)}, u32[]{:S(2)}, u32[]{:S(2)}) async-start(bf16[128,16,128]{2,1,0:T(8,128)(2,1)} %tail_rows_out.1), calls=%async_computation.1 | async-start | bytes 1048576 | tf_op jit(solution)/shard_map/all_to_all | solution.py:29
  43.9 21.2 %collective-permute-start.4 = (bf16[64,2688]{1,0:T(8,128)(2,1)S(1)}, bf16[64,2688]{1,0:T(8,128)(2,1)}, u32[]{:S(2)}, u32[]{:S(2)}) collective-permute-start(bf16[64,2688]{1,0:T(8,128)(2,1)S(1)} %own_block.1.refs_0_), channel_id=1, source_target_pairs={{0,2},{2,0},{1,3},{3,1},{4,6},{6,4},{5,7},{7,5},{8,10},{10,8},{9,1... | collective-permute-start | bytes 1032200 | tf_op jit(solution)/shard_map/ppermute | solution.py:34
  47.1 15.2 %collective-permute-start.3 = (bf16[32,32,128]{2,1,0:T(8,128)(2,1)S(1)}, bf16[32,32,128]{2,1,0:T(8,128)(2,1)}, u32[]{:S(2)}, u32[]{:S(2)}) collective-permute-start(bf16[32,32,128]{2,1,0:T(8,128)(2,1)S(1)} %all-to-all-done.refs_0_), channel_id=1, source_target_pairs={{0,32},{32,64},{64,96},{96,0},{1,33},{33,65},{65,97},{97,1},{2,34}... | collective-permute-start | bytes 786440 | tf_op jit(solution)/shard_map/ppermute | solution.py:34
  50.2 17.3 %collective-permute-start.2 = (bf16[32,32,128]{2,1,0:T(8,128)(2,1)S(1)}, bf16[32,32,128]{2,1,0:T(8,128)(2,1)S(1)}, u32[]{:S(2)}, u32[]{:S(2)}) collective-permute-start(bf16[32,32,128]{2,1,0:T(8,128)(2,1)S(1)} %all-to-all-done.refs_0_), channel_id=1, source_target_pairs={{0,96},{32,0},{64,32},{96,64},{1,97},{33,1},{65,33},{97,65},{2,98}... | collective-permute-start | bytes 786440 | tf_op jit(solution)/shard_map/ppermute | solution.py:34
  54.2 14.4 %collective-permute-start.1 = (bf16[32,32,128]{2,1,0:T(8,128)(2,1)S(1)}, bf16[32,32,128]{2,1,0:T(8,128)(2,1)}, u32[]{:S(2)}, u32[]{:S(2)}) collective-permute-start(bf16[32,32,128]{2,1,0:T(8,128)(2,1)S(1)} %all-to-all-done.refs_0_), channel_id=1, source_target_pairs={{0,64},{32,96},{64,0},{96,32},{1,65},{33,97},{65,1},{97,33},{2,66}... | collective-permute-start | bytes 786440 | tf_op jit(solution)/shard_map/ppermute | solution.py:34
  65.0 6.3 %copy-start.11 = (s32[1024]{0:T(1024)S(1)}, s32[1024]{0:T(1024)}, u32[]{:S(2)}) copy-start(s32[1024]{0:T(1024)} %param.20) | copy-start | bytes 12292
  65.1 15.8 %collective-permute-start.5 = (bf16[64,2688]{1,0:T(8,128)(2,1)}, bf16[64,2688]{1,0:T(8,128)(2,1)S(1)}, u32[]{:S(2)}, u32[]{:S(2)}) collective-permute-start(bf16[64,2688]{1,0:T(8,128)(2,1)} %collective-permute-done.4.refs_1_), channel_id=1, source_target_pairs={{0,1},{1,0},{2,3},{3,2},{4,5},{5,4},{6,7},{7,6},{8,9},{9,8},{10,11... | collective-permute-start | bytes 1032200 | tf_op jit(solution)/shard_map/ppermute | solution.py:34
  80.8 0.7 copy-start.15
  87.0 47.2 %all-to-all-start.2 = ((bf16[128,24,128]{2,1,0:T(8,128)(2,1)}), bf16[128,24,128]{2,1,0:T(8,128)(2,1)S(1)}, u32[]{:S(2)}, u32[]{:S(2)}) async-start(bf16[128,24,128]{2,1,0:T(8,128)(2,1)} %bitcast.39), calls=%async_computation.2 | async-start | bytes 1572864 | tf_op jit(solution)/shard_map/all_to_all | solution.py:29
  111.4 22.9 %collective-permute-start.6 = (bf16[33,32,128]{2,1,0:T(8,128)(2,1)}, bf16[33,32,128]{2,1,0:T(8,128)(2,1)S(1)}, u32[]{:S(2)}, u32[]{:S(2)}) collective-permute-start(bf16[33,32,128]{2,1,0:T(8,128)(2,1)} %get-tuple-element.39), channel_id=1, source_target_pairs={{0,64},{32,96},{64,0},{96,32},{1,65},{33,97},{65,1},{97,33},{2,66}... | collective-permute-start | bytes 811016 | tf_op jit(solution)/shard_map/ppermute | solution.py:34
  115.8 19.7 %collective-permute-start.7 = (bf16[33,32,128]{2,1,0:T(8,128)(2,1)}, bf16[33,32,128]{2,1,0:T(8,128)(2,1)S(1)}, u32[]{:S(2)}, u32[]{:S(2)}) collective-permute-start(bf16[33,32,128]{2,1,0:T(8,128)(2,1)} %get-tuple-element.40), channel_id=1, source_target_pairs={{0,32},{32,64},{64,96},{96,0},{1,33},{33,65},{65,97},{97,1},{2,34}... | collective-permute-start | bytes 811016 | tf_op jit(solution)/shard_map/ppermute | solution.py:34
  118.3 28.7 %copy-start.12 = (bf16[256,1024]{1,0:T(8,128)(2,1)S(1)}, bf16[256,1024]{1,0:T(8,128)(2,1)}, u32[]{:S(2)}) copy-start(bf16[256,1024]{1,0:T(8,128)(2,1)} %get-tuple-element.44.d_ref) | copy-start | bytes 1572868
  118.3 28.7 %copy-start.13 = (bf16[64,256]{1,0:T(8,128)(2,1)S(1)}, bf16[64,256]{1,0:T(8,128)(2,1)}, u32[]{:S(2)}) copy-start(bf16[64,256]{1,0:T(8,128)(2,1)} %get-tuple-element.43.weight_ref) | copy-start | bytes 98308
  118.3 17.2 %collective-permute-start.8 = (bf16[33,32,128]{2,1,0:T(8,128)(2,1)}, bf16[33,32,128]{2,1,0:T(8,128)(2,1)S(1)}, u32[]{:S(2)}, u32[]{:S(2)}) collective-permute-start(bf16[33,32,128]{2,1,0:T(8,128)(2,1)} %get-tuple-element.41), channel_id=1, source_target_pairs={{0,96},{32,0},{64,32},{96,64},{1,97},{33,1},{65,33},{97,65},{2,98}... | collective-permute-start | bytes 811016 | tf_op jit(solution)/shard_map/ppermute | solution.py:34
  135.5 1.0 copy-start.1
  137.3 25.8 %all-to-all-start.3 = ((bf16[32,48,128]{2,1,0:T(8,128)(2,1)}), bf16[32,48,128]{2,1,0:T(8,128)(2,1)S(1)}, u32[]{:S(2)}, u32[]{:S(2)}) async-start(bf16[32,48,128]{2,1,0:T(8,128)(2,1)} %hub_grads_over_x.1), calls=%async_computation.3 | async-start | bytes 786432 | tf_op jit(solution)/shard_map/all_to_all | solution.py:29

commit v9 on v7

--- a/solution.py
+++ b/solution.py
@@ -75,23 +75,25 @@
         yield start, jnp.concatenate(halves, axis=0).T
 
 
-def gather_kernel(index_ref, source_ref, out_ref):
-    rows, step = out_ref.shape[1], 256
+def forward_kernel(index_ref, source_ref, hub_ref, out_ref):
+    rows, step = out_ref.shape[1] - hub_ref.shape[0], 256
+    hub = jnp.broadcast_to(hub_ref[...].astype(F32)[None], (step // rows, *hub_ref.shape))
     for start, block in pick_slots(index_ref, source_ref[...], step):
         first = start // rows
-        out_ref[first : first + step // rows] = block.reshape(-1, rows, 128).astype(BF)
-
-
-def gather_slots(index, source, parts, slots):
+        block = jnp.concatenate([block.reshape(-1, rows, 128), hub], axis=1)
+        out_ref[first : first + step // rows] = block.astype(BF)
+
+
+def forward_rows(index, source, hub, parts, slots):
     return call(
-        gather_kernel,
-        jax.ShapeDtypeStruct((parts, slots // 2, 128), BF),
-        [VMEM, VMEM],
+        forward_kernel,
+        jax.ShapeDtypeStruct((parts, slots // 2 + hub.shape[0], 128), BF),
+        [VMEM, VMEM, VMEM],
         [],
-        "tail_rows_out",
+        "forward_rows",
         2 * parts * slots * 256 * 256,
         2,
-    )(index, source)
+    )(index, source, hub)
 
 
 def layer_kernel(sizes, place_ref, index_ref, degree_ref, mixed_ref, *refs):
@@ -209,26 +211,51 @@
     return sums[0].T[:64] + sums[1].T[64:]
 
 
-def mixed_kernel(rows, index_ref, arrived_ref, hub_ref, degree_ref, out_ref):
+def mixed_kernel(
+    rows, block_ref, mask_ref, index_ref, arrived_ref, degree_ref, tile_ref, out_ref, total
+):
+    blocks = total.shape[0] - 1
+    half = arrived_ref.shape[1] - rows
+    lanes = lax.broadcasted_iota(jnp.int32, (half, 128), 1)
+    first = (lanes < 64).astype(F32).astype(BF)
+    second = (lanes >= 64).astype(F32).astype(BF)
+    total[...] = jnp.zeros_like(total)
+    group = 8
+
+    @pl.loop(0, arrived_ref.shape[0] // group)
+    def _(g):
+        for i in range(group):
+            tile = g * group + i
+            hub = arrived_ref[tile, rows:, :]
+            weights = tile_ref[tile]
+            product = jnp.dot(
+                jnp.concatenate([hub * first, hub * second], axis=0),
+                jnp.concatenate([weights, weights], axis=0),
+                preferred_element_type=F32,
+            )
+            dest = jnp.where(mask_ref[tile] > 0, block_ref[tile], blocks)
+            total[dest] = total[dest] + product
+
     size = 256
     for start in range(0, out_ref.shape[1], size):
         at = slice(start, start + size)
         tail = sum_slots(index_ref, arrived_ref, rows, start, size)
-        out_ref[:, at] = (hub_ref[:, at] + tail / degree_ref[:, at].astype(F32)).astype(BF)
-
-
-def mixed_sums(index, arrived, hub_sum, degree):
-    parts, rows, _ = arrived.shape
-    width, nodes = hub_sum.shape
+        hub = jnp.concatenate([total[start // 128], total[start // 128 + 1]], axis=1)
+        out_ref[:, at] = (hub + tail / degree_ref[:, at].astype(F32)).astype(BF)
+
+
+def mixed_sums(block, mask, index, arrived, degree, tiles, rows, width):
+    parts = arrived.shape[0]
+    nodes = degree.shape[1]
     return call(
         partial(mixed_kernel, rows),
         jax.ShapeDtypeStruct((width, nodes), BF),
-        [VMEM] * 4,
-        [],
+        [SMEM, SMEM] + [VMEM] * 4,
+        [pltpu.VMEM((nodes // 128 + 1, width, 128), F32)],
         "mixed",
         4 * parts * rows * nodes * 128,
         2,
-    )(index, arrived, hub_sum, degree)
+    )(block, mask, index, arrived, degree, tiles)
 
 
 def tail_grad_kernel(rows, index_ref, arrived_ref, weight_ref, d_ref, out_ref):
@@ -285,52 +312,6 @@
     x_size, z_size = sizes
     x = lax.rem(x_ref[0] + (sign * k) % x_size, x_size)
     return (yh * x_size + x) * z_size + z
-
-
-def fold_kernel(steps, sizes, has_base, x_ref, block_ref, mask_ref, *refs):
-    hub_refs, (tile_ref, *base_ref, out_ref, total) = refs[: len(steps)], refs[len(steps) :]
-    blocks = total.shape[0] - 1
-    half = hub_refs[0].shape[1]
-    lanes = lax.broadcasted_iota(jnp.int32, (half, 128), 1)
-    first = (lanes < 64).astype(F32).astype(BF)
-    second = (lanes >= 64).astype(F32).astype(BF)
-    for b in range(blocks):
-        at = slice(b * 128, (b + 1) * 128)
-        total[b] = base_ref[0][:, at] if has_base else jnp.zeros_like(total[b])
-    total[blocks] = jnp.zeros_like(total[blocks])
-    z_size = sizes[1]
-    for k, hub_ref in zip(steps, hub_refs):
-
-        @pl.loop(0, hub_ref.shape[0] // z_size)
-        def _(yh):
-            for z in range(z_size):
-                tile = tile_index(x_ref, k, sizes, yh, z, -1)
-                rows = hub_ref[yh * z_size + z]
-                weights = tile_ref[tile]
-                product = jnp.dot(
-                    jnp.concatenate([rows * first, rows * second], axis=0),
-                    jnp.concatenate([weights, weights], axis=0),
-                    preferred_element_type=F32,
-                )
-                dest = jnp.where(mask_ref[tile] > 0, block_ref[tile], blocks)
-                total[dest] = total[dest] + product
-
-    for b in range(blocks):
-        out_ref[:, b * 128 : (b + 1) * 128] = total[b]
-
-
-def fold_hubs(x_index, block, mask, hubs, steps, tiles, sizes, blocks, base):
-    width = 2 * hubs[0].shape[1]
-    bases = [] if base is None else [base]
-    return call(
-        partial(fold_kernel, steps, sizes, base is not None),
-        jax.ShapeDtypeStruct((width, blocks * 128), F32),
-        [SMEM, SMEM, SMEM] + [VMEM] * (len(hubs) + 1 + len(bases)),
-        [pltpu.VMEM((blocks + 1, width, 128), F32)],
-        "hub_sums",
-        tiles.size * width * len(hubs),
-        4,
-    )(x_index, block, mask, *hubs, tiles, *bases)
 
 
 def hub_grad_kernel(steps, sizes, x_ref, block_ref, mask_ref, grad_ref, bias_ref, tile_ref, *refs):
@@ -472,31 +453,21 @@
     degree = degree[None, :]
 
     hub_piece = jnp.concatenate([features[:half_width, :hubs], features[half_width:, :hubs]], axis=1)
-    hub_send = jnp.broadcast_to(hub_piece[None], (plane, half_width, 128))
-    hub_plane = swap(hub_send, PLANE)
-
     slot_live = jnp.arange(slots, dtype=jnp.int32)[None, :] < tail_count[0][:, None]
     send_index = slot_rows(jnp.where(slot_live, tail_rows[0], -1))
-    recv_index = slot_rows(tail_target[0])
+    send = forward_rows(send_index, features, hub_piece, parts, slots)
+    arrived = swap(send, DOM)
+
+    feat_own, targets, _ = lax.optimization_barrier((features, tail_target[0], send))
+    recv_index = slot_rows(targets)
     bias_terms = jnp.stack(three_terms(out_bias), axis=1)
     bias_terms = jnp.pad(bias_terms, ((0, 0), (0, 128 - bias_terms.shape[1])))
-    feat_own, send_index, _ = lax.optimization_barrier((features, send_index, hub_send))
     own = own_block(feat_own, cotangent, w_self.T, w_neigh.T, bias_terms)
-    across = shift(own, "core", 1)
-    tail_send = gather_slots(send_index, features, parts, slots)
-    hub_plane, tail_send, recv_index, own, across = lax.optimization_barrier(
-        (hub_plane, tail_send, recv_index, own, across)
-    )
-    arrived = swap(tail_send, DOM)
-    hub_all = [hub_plane] + [shift(hub_plane, "x", k) for k in range(1, x_size)]
     near = shift(own, "yl", 1)
-    own_blocks = [own, near, across, shift(near, "core", 1)]
+    own_blocks = [own, near, shift(own, "core", 1), shift(near, "core", 1)]
     place = lax.axis_index(REP) ^ jnp.array([0, 2, 1, 3], jnp.int32)
 
-    fold = partial(fold_hubs, *hub_at, tiles=tiles, sizes=sizes, blocks=blocks)
-    hub_sum = fold(hub_all[:2], (0, 1), base=None)
-    hub_sum = fold(hub_all[2:], (2, 3), base=hub_sum)
-    mixed = mixed_sums(recv_index, arrived, hub_sum, degree)
+    mixed = mixed_sums(*hub_at[1:], recv_index, arrived, degree, tiles, slots // 2, width)
     full_mixed = lax.all_gather(mixed, REP, axis=0, tiled=True)
 
     output, d_full, mixed_grad, tail_back, w_self_rows, bias_rows = layer(

time: 166 us -> 168 us (1.012)
  waiting for transfers between devices: 32.2 us -> 59.2 us
  starting transfers between devices: 84 us -> 65 us
  local copies, waits for them, and re-layouts: 8.9 us -> 6.66 us
    ppermute x9 -> x6, waiting for transfers between devices: 8.52 us -> 37.6 us  [shift(): lax.ppermute(values, axis, [(i, (i + step) % size) for i in range(size)])]
    ppermute x9 -> x6, starting transfers between devices: 29.3 us -> 18.4 us  [shift(): lax.ppermute(values, axis, [(i, (i + step) % size) for i in range(size)])]
    all_to_all x4 -> x3, starting transfers between devices: 54.7 us -> 46.5 us  [swap(): return lax.all_to_all(pieces, axis, split_axis=0, concat_axis=0, tiled=True)]
    pallas_call x3 -> x1, Pallas kernels: 7.28 us -> 1.18 us  [forward_rows(): call(forward_kernel, jax.ShapeDtypeStruct((parts, slots // 2 + hub.shape[...]
    pallas_call x1, Pallas kernels: 2.41 us -> 7.19 us  [mixed_sums(): call(partial(mixed_kernel, rows), jax.ShapeDtypeStruct((width, nodes), BF...]
    all_to_all x4 -> x3, waiting for transfers between devices: 23.7 us -> 21.5 us  [swap(): return lax.all_to_all(pieces, axis, split_axis=0, concat_axis=0, tiled=True)]
    unnamed x34 -> x50, local copies, waits for them, and re-layouts: 6.13 us -> 4.68 us
  transfers between devices with their start and end apart: 13 -> 9, of which waited for: 5 -> 5; matrix products, arithmetic and copies ran while one was open for 2% -> 1% of each run, Pallas kernels for 12% -> 10%
where the time goes in v9:
time: 168 us; the launch traced here: 167 us
  starting transfers between devices  65 us (39%)
  waiting for transfers between devices  59.2 us (35%)
  Pallas kernels  26.9 us (16%)
  blocking collectives  6.96 us (4%)
  local copies, waits for them, and re-layouts  6.66 us (4%)
    all_to_all x3, starting transfers between devices, swap(): return lax.all_to_all(pieces, axis, split_axis=0, concat_axis=0, tiled=True)  46.5 us
    ppermute x6, waiting for transfers between devices, shift(): lax.ppermute(values, axis, [(i, (i + step) % size) for i in range(size)])  37.6 us
    all_to_all x3, waiting for transfers between devices, swap(): return lax.all_to_all(pieces, axis, split_axis=0, concat_axis=0, tiled=True)  21.5 us
    ppermute x6, starting transfers between devices, shift(): lax.ppermute(values, axis, [(i, (i + step) % size) for i in range(size)])  18.4 us
    pallas_call x1, Pallas kernels, mixed_sums(): call(partial(mixed_kernel, rows), jax.ShapeDtypeStruct((width, nodes), BF...  7.19 us
    all_gather x1, blocking collectives, local(): full_mixed = lax.all_gather(mixed, REP, axis=0, tiled=True)  6.96 us
    pallas_call x2, Pallas kernels, hub_grad_terms(): call(partial(hub_grad_kernel, steps, sizes), [jax.ShapeDtypeStruct(shape,...  6.36 us
    pallas_call x1, Pallas kernels, layer(): pl.pallas_call(partial(layer_kernel, sizes), out_shape=[jax.ShapeDtypeStr...  5.46 us
  transfers between devices with their start and end apart: 9, of which 5 were waited for; matrix products, arithmetic and copies ran while one was open for 1% of the time, Pallas kernels for 10%

profile of v9, /device:TPU:16, one launch (start us, length us, event | category | flops | bytes accessed | tf_op | source)
XLA Modules:
  0.0 167.2 jit_solution(14921318032161429431)
XLA Ops:
  0.6 0.7 fusion.4
  1.4 0.8 copy.29
  2.2 0.7 select_bitcast_fusion
  2.9 0.1 reshape.39.index_ref
  3.0 0.1 pad_maximum_fusion.hub_ref
  3.1 0.5 copy-done.11
  3.6 0.9 copy-done.4
  4.5 1.2 forward_rows.1
  5.7 1.1 copy-done.1
  6.9 0.0 copy-start.10
  6.9 0.0 copy-start.24
  6.9 0.0 copy-start.21
  6.9 0.0 copy-start
  6.9 0.0 copy-start.14
  6.9 0.0 copy-start.16
  7.0 0.0 copy-start.18
  7.0 20.4 %all-to-all-start = ((bf16[128,48,128]{2,1,0:T(8,128)(2,1)}), bf16[128,48,128]{2,1,0:T(8,128)(2,1)}, u32[]{:S(2)}, u32[]{:S(2)}) async-start(bf16[128,48,128]{2,1,0:T(8,128)(2,1)} %copy-done.1), calls=%async_computation | async-start | bytes 3145728 | tf_op jit(solution)/shard_map/all_to_all | solution.py:29
  27.4 0.1 copy.31
  27.6 2.6 %collective-permute-start = (bf16[64,2688]{1,0:T(8,128)(2,1)S(1)}, bf16[64,2688]{1,0:T(8,128)(2,1)S(1)}, u32[]{:S(2)}, u32[]{:S(2)}) collective-permute-start(bf16[64,2688]{1,0:T(8,128)(2,1)S(1)} %own_block.1.refs_0_), channel_id=1, source_target_pairs={{0,2},{2,0},{1,3},{3,1},{4,6},{6,4},{5,7},{7,5},{8,10},{10,8},{9,1... | collective-permute-start | bytes 1032200 | tf_op jit(solution)/shard_map/ppermute | solution.py:34
  30.2 1.9 %collective-permute-start.1 = (bf16[64,2688]{1,0:T(8,128)(2,1)S(1)}, bf16[64,2688]{1,0:T(8,128)(2,1)}, u32[]{:S(2)}, u32[]{:S(2)}) collective-permute-start(bf16[64,2688]{1,0:T(8,128)(2,1)S(1)} %own_block.1.refs_0_), channel_id=1, source_target_pairs={{0,1},{1,0},{2,3},{3,2},{4,5},{5,4},{6,7},{7,6},{8,9},{9,8},{10,11... | collective-permute-start | bytes 1032200 | tf_op jit(solution)/shard_map/ppermute | solution.py:34
  32.1 36.1 %collective-permute-done.refs_1_ = bf16[64,2688]{1,0:T(8,128)(2,1)S(1)} collective-permute-done((bf16[64,2688]{1,0:T(8,128)(2,1)S(1)}, bf16[64,2688]{1,0:T(8,128)(2,1)S(1)}, u32[]{:S(2)}, u32[]{:S(2)}) %collective-permute-start) | collective-permute-done | bytes 344096 | tf_op jit(solution)/shard_map/ppermute | solution.py:34
  68.2 1.9 %collective-permute-start.2 = (bf16[64,2688]{1,0:T(8,128)(2,1)S(1)}, bf16[64,2688]{1,0:T(8,128)(2,1)}, u32[]{:S(2)}, u32[]{:S(2)}) collective-permute-start(bf16[64,2688]{1,0:T(8,128)(2,1)S(1)} %collective-permute-done.refs_1_), channel_id=1, source_target_pairs={{0,1},{1,0},{2,3},{3,2},{4,5},{5,4},{6,7},{7,6},{8,9},{9,8},{10,11... | collective-permute-start | bytes 1032200 | tf_op jit(solution)/shard_map/ppermute | solution.py:34
  70.1 0.5 broadcast_xor_fusion.place_ref
  70.6 0.1 copy.30
  70.7 0.1 reshape.41.index_ref
  70.9 1.6 all-to-all-done.arrived_ref
  72.5 7.2 %mixed.1 = bf16[64,1024]{1,0:T(8,128)(2,1)S(1)} custom-call(s32[128]{0:T(128)S(1)} %bitcast.29, s32[128]{0:T(128)S(1)} %bitcast.32, s32[2,2048]{1,0:T(2,128)S(1)} %reshape.41.index_ref, bf16[128,48,128]{2,1,0:T(8,128)(2,1)} %all-to-all-done.arrived_ref, s32[1,1024]{1,0:T(1,128)S(1)} %bitcast.36, bf16[128,64,128]{2,1,0:T(8,128)(2,1)S(1)} %bitcast.24), custom_call_target="tpu_custom_call" | custom-call | flops 1073741824 | bytes 2097152 | tf_op jit(solution)/shard_map/mixed/pallas_call | solution.py:250
  79.7 7.0 %all_gather.3.mixed_ref = bf16[256,1024]{1,0:T(8,128)(2,1)} all-gather(bf16[64,1024]{1,0:T(8,128)(2,1)S(1)} %mixed.1), channel_id=1, replica_groups=mesh['yh'=4,'x'=4,'z'=8,'yl'=2,'core'=2] {'yl','core'}, dimensions={0}, use_global_device_ids=true | all-gather | bytes 655360 | tf_op jit(solution)/shard_map/all_gather | solution.py:471
  86.7 5.5 %layer.1 = (bf16[64,1024]{1,0:T(8,128)(2,1)}, bf16[256,1024]{1,0:T(8,128)(2,1)}, bf16[64,1024]{1,0:T(8,128)(2,1)}, bf16[64,48,128]{2,1,0:T(8,128)(2,1)}, bf16[64...) custom-call(s32[4]{0:T(128)} %broadcast_xor_fusion.place_ref, s32[2,2048]{1,0:T(2,128)} %copy-done.13, s32[1,1024]{1,0:T(1,128)} %bitcast.35, ...), custom_call_target="tpu_custom_call" | custom-call | flops 1048576000 | bytes 4194304 | tf_op jit(solution)/shard_map/layer/pallas_call | solution.py:186
  92.2 0.0 copy-start.2
  92.2 15.6 %all-to-all-start.1 = ((bf16[128,24,128]{2,1,0:T(8,128)(2,1)}), bf16[128,24,128]{2,1,0:T(8,128)(2,1)S(1)}, u32[]{:S(2)}, u32[]{:S(2)}) async-start(bf16[128,24,128]{2,1,0:T(8,128)(2,1)} %bitcast.37), calls=%async_computation.1 | async-start | bytes 1572864 | tf_op jit(solution)/shard_map/all_to_all | solution.py:29
  107.9 4.7 %hub_grad_terms.3 = (bf16[33,32,128]{2,1,0:T(8,128)(2,1)}, bf16[33,32,128]{2,1,0:T(8,128)(2,1)}, bf16[33,32,128]{2,1,0:T(8,128)(2,1)}) custom-call(s32[1]{0:T(128)} %bitcast.15.x_ref, s32[128]{0:T(128)S(1)} %bitcast.30, s32[128]{0:T(128)S(1)} %bitcast.33, bf16[64,1024]{1,0:T(8,128)(2,1)S(1)} %copy-done.2, bf16[32,128]{1,0:T(8,128)(2,1)S(1)} %copy-done.7, ...), custom_call_target="tpu_custom_call" | custom-call | flops 201326592 | bytes 4194304 | tf_op jit(solution)/shard_map/hub_grad_terms/pallas_call | solution.py:348
  112.6 5.0 %collective-permute-start.3 = (bf16[33,32,128]{2,1,0:T(8,128)(2,1)}, bf16[33,32,128]{2,1,0:T(8,128)(2,1)S(1)}, u32[]{:S(2)}, u32[]{:S(2)}) collective-permute-start(bf16[33,32,128]{2,1,0:T(8,128)(2,1)} %get-tuple-element.25), channel_id=1, source_target_pairs={{0,64},{32,96},{64,0},{96,32},{1,65},{33,97},{65,1},{97,33},{2,66}... | collective-permute-start | bytes 811016 | tf_op jit(solution)/shard_map/ppermute | solution.py:34
  117.5 2.5 %collective-permute-start.4 = (bf16[33,32,128]{2,1,0:T(8,128)(2,1)}, bf16[33,32,128]{2,1,0:T(8,128)(2,1)}, u32[]{:S(2)}, u32[]{:S(2)}) collective-permute-start(bf16[33,32,128]{2,1,0:T(8,128)(2,1)} %get-tuple-element.26), channel_id=1, source_target_pairs={{0,32},{32,64},{64,96},{96,0},{1,33},{33,65},{65,97},{97,1},{2,34}... | collective-permute-start | bytes 811016 | tf_op jit(solution)/shard_map/ppermute | solution.py:34
  120.1 4.5 %collective-permute-start.5 = (bf16[33,32,128]{2,1,0:T(8,128)(2,1)}, bf16[33,32,128]{2,1,0:T(8,128)(2,1)}, u32[]{:S(2)}, u32[]{:S(2)}) collective-permute-start(bf16[33,32,128]{2,1,0:T(8,128)(2,1)} %get-tuple-element.27), channel_id=1, source_target_pairs={{0,96},{32,0},{64,32},{96,64},{1,97},{33,1},{65,33},{97,65},{2,98}... | collective-permute-start | bytes 811016 | tf_op jit(solution)/shard_map/ppermute | solution.py:34
  124.6 0.7 copy-done.8
  125.3 0.7 copy-done.15
  126.0 0.7 copy-done.17
  126.6 1.7 hub_grad_terms.2.refs_0_
  128.3 0.0 copy-start.12
  128.4 6.9 %all-to-all-done.1.arrived_ref = bf16[128,24,128]{2,1,0:T(8,128)(2,1)S(1)} async-done(((bf16[128,24,128]{2,1,0:T(8,128)(2,1)}), bf16[128,24,128]{2,1,0:T(8,128)(2,1)S(1)}, u32[]{:S(2)}, u32[]{:S(2)}) %all-to-all-start.1) | async-done | bytes 786464 | tf_op jit(solution)/shard_map/all_to_all | solution.py:29
  135.3 0.1 convert_reduce_fusion.refs_4_
  135.4 1.5 collective-permute-done.4.refs_2_
  137.0 1.9 %hub_grads_over_x.1 = bf16[32,48,128]{2,1,0:T(8,128)(2,1)} custom-call(bf16[33,32,128]{2,1,0:T(8,128)(2,1)S(1)} %hub_grad_terms.2.refs_0_, bf16[33,32,128]{2,1,0:T(8,128)(2,1)S(1)} %collective-permute-done.3.refs_1_, bf16[33,32,128]{2,1,0:T(8,128)(2,1)} %collective-permute-done.4.refs_2_, bf16[33,32,128]{2,1,0:T(8,128)(2,1)} %collective-permute-done.5.refs_3_, ...), custom_call_target="tpu_custom_call" | custom-call | flops 1048576 | bytes 2097152 | tf_op jit(solution)/shard_map/hub_grads_over_x/pallas_call | solution.py:377
  138.9 10.5 %all-to-all-start.2 = ((bf16[32,48,128]{2,1,0:T(8,128)(2,1)}), bf16[32,48,128]{2,1,0:T(8,128)(2,1)S(1)}, u32[]{:S(2)}, u32[]{:S(2)}) async-start(bf16[32,48,128]{2,1,0:T(8,128)(2,1)} %hub_grads_over_x.1), calls=%async_computation.2 | async-start | bytes 786432 | tf_op jit(solution)/shard_map/all_to_all | solution.py:29
  149.5 3.1 %tail_grads.1.base_ref = f32[64,1024]{1,0:T(8,128)} custom-call(s32[2,2048]{1,0:T(2,128)S(1)} %copy-done.12, bf16[128,24,128]{2,1,0:T(8,128)(2,1)S(1)} %all-to-all-done.1.arrived_ref, bf16[64,256]{1,0:T(8,128)(2,1)S(1)} %copy-done.20, bf16[256,1024]{1,0:T(8,128)(2,1)S(1)} %copy-done.19), custom_call_target="tpu_custom_call" | custom-call | flops 1073741824 | bytes 2097152 | tf_op jit(solution)/shard_map/tail_grads/pallas_call | solution.py:273
  152.6 13.0 %all-to-all-done.2.second_ref = bf16[32,48,128]{2,1,0:T(8,128)(2,1)S(1)} async-done(((bf16[32,48,128]{2,1,0:T(8,128)(2,1)}), bf16[32,48,128]{2,1,0:T(8,128)(2,1)S(1)}, u32[]{:S(2)}, u32[]{:S(2)}) %all-to-all-start.2) | async-done | bytes 393248 | tf_op jit(solution)/shard_map/all_to_all | solution.py:29
  165.6 1.6 gradients.1
  (44 shorter events, 0.1 us)
Async XLA Ops:
  3.0 0.6 copy-start.11
  3.6 0.9 copy-start.4
  5.7 1.1 copy-start.1
  6.9 20.5 %copy-start.22 = (f32[64]{0:T(128)S(1)}, f32[64]{0:T(128)}, u32[]{:S(2)}) copy-start(f32[64]{0:T(128)} %param.23) | copy-start | bytes 772
  6.9 20.6 %copy-start.5 = (bf16[64,1024]{1,0:T(8,128)(2,1)S(1)}, bf16[64,1024]{1,0:T(8,128)(2,1)}, u32[]{:S(2)}) copy-start(bf16[64,1024]{1,0:T(8,128)(2,1)} %feat_ref) | copy-start | bytes 393220
  6.9 20.6 %copy-start.6 = (bf16[64,1024]{1,0:T(8,128)(2,1)S(1)}, bf16[64,1024]{1,0:T(8,128)(2,1)}, u32[]{:S(2)}) copy-start(bf16[64,1024]{1,0:T(8,128)(2,1)} %cot_ref.1) | copy-start | bytes 393220
  6.9 20.6 %copy-start.9 = (bf16[256,64]{0,1:T(8,128)(2,1)S(1)}, bf16[256,64]{0,1:T(8,128)(2,1)}, u32[]{:S(2)}) copy-start(bf16[256,64]{0,1:T(8,128)(2,1)} %param.21) | copy-start | bytes 98308
  6.9 20.6 %copy-start.10 = (bf16[256,64]{0,1:T(8,128)(2,1)S(1)}, bf16[256,64]{0,1:T(8,128)(2,1)}, u32[]{:S(2)}) copy-start(bf16[256,64]{0,1:T(8,128)(2,1)} %param.22) | copy-start | bytes 98308
  6.9 63.2 %copy-start.24 = (s32[4]{0:T(128)S(1)}, s32[4]{0:T(128)}, u32[]{:S(2)}) copy-start(s32[4]{0:T(128)} %constant.25.clone) | copy-start | bytes 52
  6.9 63.7 %copy-start.21 = (s32[1,128,32]{1,2,0:T(8,128)S(1)}, s32[1,128,32]{1,2,0:T(8,128)}, u32[]{:S(2)}) copy-start(s32[1,128,32]{1,2,0:T(8,128)} %param.19) | copy-start | bytes 49156
  6.9 65.6 %copy-start = (bf16[1,128,64,128]{3,2,1,0:T(8,128)(2,1)S(1)}, bf16[1,128,64,128]{3,2,1,0:T(8,128)(2,1)}, u32[]{:S(2)}) copy-start(bf16[1,128,64,128]{3,2,1,0:T(8,128)(2,1)} %param.14) | copy-start | bytes 6291460
  6.9 65.6 %copy-start.14 = (s32[1,128]{1,0:T(1,128)S(1)}, s32[1,128]{1,0:T(1,128)}, u32[]{:S(2)}) copy-start(s32[1,128]{1,0:T(1,128)} %param.15) | copy-start | bytes 1540
  6.9 65.6 %copy-start.16 = (s32[1,128]{1,0:T(1,128)S(1)}, s32[1,128]{1,0:T(1,128)}, u32[]{:S(2)}) copy-start(s32[1,128]{1,0:T(1,128)} %param.16) | copy-start | bytes 1540
  7.0 65.6 %copy-start.18 = (s32[1024]{0:T(1024)S(1)}, s32[1024]{0:T(1024)}, u32[]{:S(2)}) copy-start(s32[1024]{0:T(1024)} %param.20) | copy-start | bytes 12292
  7.0 65.5 %all-to-all-start = ((bf16[128,48,128]{2,1,0:T(8,128)(2,1)}), bf16[128,48,128]{2,1,0:T(8,128)(2,1)}, u32[]{:S(2)}, u32[]{:S(2)}) async-start(bf16[128,48,128]{2,1,0:T(8,128)(2,1)} %copy-done.1), calls=%async_computation | async-start | bytes 3145728 | tf_op jit(solution)/shard_map/all_to_all | solution.py:29
  27.6 52.2 %copy-start.3 = (bf16[64,2688]{1,0:T(8,128)(2,1)}, bf16[64,2688]{1,0:T(8,128)(2,1)S(1)}, u32[]{:S(2)}) copy-start(bf16[64,2688]{1,0:T(8,128)(2,1)S(1)} %own_block.1.refs_0_) | copy-start | bytes 1032196
  27.6 40.6 %collective-permute-start = (bf16[64,2688]{1,0:T(8,128)(2,1)S(1)}, bf16[64,2688]{1,0:T(8,128)(2,1)S(1)}, u32[]{:S(2)}, u32[]{:S(2)}) collective-permute-start(bf16[64,2688]{1,0:T(8,128)(2,1)S(1)} %own_block.1.refs_0_), channel_id=1, source_target_pairs={{0,2},{2,0},{1,3},{3,1},{4,6},{6,4},{5,7},{7,5},{8,10},{10,8},{9,1... | collective-permute-start | bytes 1032200 | tf_op jit(solution)/shard_map/ppermute | solution.py:34
  30.2 56.5 %collective-permute-start.1 = (bf16[64,2688]{1,0:T(8,128)(2,1)S(1)}, bf16[64,2688]{1,0:T(8,128)(2,1)}, u32[]{:S(2)}, u32[]{:S(2)}) collective-permute-start(bf16[64,2688]{1,0:T(8,128)(2,1)S(1)} %own_block.1.refs_0_), channel_id=1, source_target_pairs={{0,1},{1,0},{2,3},{3,2},{4,5},{5,4},{6,7},{7,6},{8,9},{9,8},{10,11... | collective-permute-start | bytes 1032200 | tf_op jit(solution)/shard_map/ppermute | solution.py:34
  68.2 11.5 %copy-start.23 = (bf16[64,2688]{1,0:T(8,128)(2,1)}, bf16[64,2688]{1,0:T(8,128)(2,1)S(1)}, u32[]{:S(2)}) copy-start(bf16[64,2688]{1,0:T(8,128)(2,1)S(1)} %collective-permute-done.refs_1_) | copy-start | bytes 1032196
  68.2 18.5 %collective-permute-start.2 = (bf16[64,2688]{1,0:T(8,128)(2,1)S(1)}, bf16[64,2688]{1,0:T(8,128)(2,1)}, u32[]{:S(2)}, u32[]{:S(2)}) collective-permute-start(bf16[64,2688]{1,0:T(8,128)(2,1)S(1)} %collective-permute-done.refs_1_), channel_id=1, source_target_pairs={{0,1},{1,0},{2,3},{3,2},{4,5},{5,4},{6,7},{7,6},{8,9},{9,8},{10,11... | collective-permute-start | bytes 1032200 | tf_op jit(solution)/shard_map/ppermute | solution.py:34
  70.9 8.9 %copy-start.13 = (s32[2,2048]{1,0:T(2,128)}, s32[2,2048]{1,0:T(2,128)S(1)}, u32[]{:S(2)}) copy-start(s32[2,2048]{1,0:T(2,128)S(1)} %reshape.41.index_ref) | copy-start | bytes 49156
  92.2 15.7 %copy-start.2 = (bf16[64,1024]{1,0:T(8,128)(2,1)S(1)}, bf16[64,1024]{1,0:T(8,128)(2,1)}, u32[]{:S(2)}) copy-start(bf16[64,1024]{1,0:T(8,128)(2,1)} %get-tuple-element.23.grad_ref) | copy-start | bytes 393220
  92.2 15.7 %copy-start.7 = (bf16[32,128]{1,0:T(8,128)(2,1)S(1)}, bf16[32,128]{1,0:T(8,128)(2,1)}, u32[]{:S(2)}) copy-start(bf16[32,128]{1,0:T(8,128)(2,1)} %get-tuple-element.24.bias_ref) | copy-start | bytes 24580
  92.2 43.1 %all-to-all-start.1 = ((bf16[128,24,128]{2,1,0:T(8,128)(2,1)}), bf16[128,24,128]{2,1,0:T(8,128)(2,1)S(1)}, u32[]{:S(2)}, u32[]{:S(2)}) async-start(bf16[128,24,128]{2,1,0:T(8,128)(2,1)} %bitcast.37), calls=%async_computation.1 | async-start | bytes 1572864 | tf_op jit(solution)/shard_map/all_to_all | solution.py:29
  112.6 22.9 %collective-permute-start.3 = (bf16[33,32,128]{2,1,0:T(8,128)(2,1)}, bf16[33,32,128]{2,1,0:T(8,128)(2,1)S(1)}, u32[]{:S(2)}, u32[]{:S(2)}) collective-permute-start(bf16[33,32,128]{2,1,0:T(8,128)(2,1)} %get-tuple-element.25), channel_id=1, source_target_pairs={{0,64},{32,96},{64,0},{96,32},{1,65},{33,97},{65,1},{97,33},{2,66}... | collective-permute-start | bytes 811016 | tf_op jit(solution)/shard_map/ppermute | solution.py:34
  117.5 19.4 %collective-permute-start.4 = (bf16[33,32,128]{2,1,0:T(8,128)(2,1)}, bf16[33,32,128]{2,1,0:T(8,128)(2,1)}, u32[]{:S(2)}, u32[]{:S(2)}) collective-permute-start(bf16[33,32,128]{2,1,0:T(8,128)(2,1)} %get-tuple-element.26), channel_id=1, source_target_pairs={{0,32},{32,64},{64,96},{96,0},{1,33},{33,65},{65,97},{97,1},{2,34}... | collective-permute-start | bytes 811016 | tf_op jit(solution)/shard_map/ppermute | solution.py:34
  120.1 16.9 %collective-permute-start.5 = (bf16[33,32,128]{2,1,0:T(8,128)(2,1)}, bf16[33,32,128]{2,1,0:T(8,128)(2,1)}, u32[]{:S(2)}, u32[]{:S(2)}) collective-permute-start(bf16[33,32,128]{2,1,0:T(8,128)(2,1)} %get-tuple-element.27), channel_id=1, source_target_pairs={{0,96},{32,0},{64,32},{96,64},{1,97},{33,1},{65,33},{97,65},{2,98}... | collective-permute-start | bytes 811016 | tf_op jit(solution)/shard_map/ppermute | solution.py:34
  124.6 0.7 copy-start.8
  125.3 0.7 copy-start.15
  126.0 0.7 copy-start.17
  128.3 21.1 %copy-start.12 = (s32[2,2048]{1,0:T(2,128)S(1)}, s32[2,2048]{1,0:T(2,128)}, u32[]{:S(2)}) copy-start(s32[2,2048]{1,0:T(2,128)} %copy-done.11) | copy-start | bytes 49156
  128.3 21.1 %copy-start.19 = (bf16[256,1024]{1,0:T(8,128)(2,1)S(1)}, bf16[256,1024]{1,0:T(8,128)(2,1)}, u32[]{:S(2)}) copy-start(bf16[256,1024]{1,0:T(8,128)(2,1)} %get-tuple-element.30.d_ref) | copy-start | bytes 1572868
  128.3 21.1 %copy-start.20 = (bf16[64,256]{1,0:T(8,128)(2,1)S(1)}, bf16[64,256]{1,0:T(8,128)(2,1)}, u32[]{:S(2)}) copy-start(bf16[64,256]{1,0:T(8,128)(2,1)} %get-tuple-element.29.weight_ref) | copy-start | bytes 98308
  138.9 26.7 %all-to-all-start.2 = ((bf16[32,48,128]{2,1,0:T(8,128)(2,1)}), bf16[32,48,128]{2,1,0:T(8,128)(2,1)S(1)}, u32[]{:S(2)}, u32[]{:S(2)}) async-start(bf16[32,48,128]{2,1,0:T(8,128)(2,1)} %hub_grads_over_x.1), calls=%async_computation.2 | async-start | bytes 786432 | tf_op jit(solution)/shard_map/all_to_all | solution.py:29

commit v10 on v8

--- a/solution.py
+++ b/solution.py
@@ -34,7 +34,7 @@
     return lax.ppermute(values, axis, [(i, (i + step) % size) for i in range(size)])
 
 
-def call(kernel, out_shape, in_specs, scratch, name, flops, mib, limit=VMEM_LIMIT):
+def call(kernel, out_shape, in_specs, scratch, name, flops, mib):
     outs = VMEM if isinstance(out_shape, jax.ShapeDtypeStruct) else [VMEM] * len(out_shape)
     return pl.pallas_call(
         kernel,
@@ -42,7 +42,7 @@
         in_specs=in_specs,
         out_specs=outs,
         scratch_shapes=scratch,
-        compiler_params=pltpu.CompilerParams(vmem_limit_bytes=limit),
+        compiler_params=pltpu.CompilerParams(vmem_limit_bytes=VMEM_LIMIT),
         cost_estimate=pl.CostEstimate(flops=flops, bytes_accessed=mib * MIB, transcendentals=0),
         name=name,
     )
@@ -374,7 +374,6 @@
         "hub_grad_terms",
         tiles.size * width * len(steps),
         4,
-        60 * MIB,
     )(x_index, block, mask, grad, bias, tiles)
 
 
@@ -493,13 +492,11 @@
     arrived = swap(tail_send, DOM)
     hub_all = [hub_plane] + [shift(hub_plane, "x", k) for k in range(1, x_size)]
     near = shift(own, "yl", 1)
+    own_blocks = [own, near, across, shift(near, "core", 1)]
     place = lax.axis_index(REP) ^ jnp.array([0, 2, 1, 3], jnp.int32)
 
     fold = partial(fold_hubs, *hub_at, tiles=tiles, sizes=sizes, blocks=blocks)
-    hub_sum = fold(hub_all[:2], (0, 1), base=None)
-    hub_sum, near = lax.optimization_barrier((hub_sum, near))
-    own_blocks = [own, near, across, shift(near, "core", 1)]
-    hub_sum = fold(hub_all[2:], (2, 3), base=hub_sum)
+    hub_sum = fold(hub_all, tuple(range(x_size)), base=None)
     mixed = mixed_sums(recv_index, arrived, hub_sum, degree)
     full_mixed = lax.all_gather(mixed, REP, axis=0, tiled=True)
 

time: 166 us -> 167 us (level)
  the two profiles are of different devices: /device:TPU:8 before, /device:TPU:16 now
where the time goes in v10:
time: 167 us; the launch traced here: 165 us
  starting transfers between devices  79.6 us (48%)
  waiting for transfers between devices  37.3 us (22%)
  Pallas kernels  27.2 us (16%)
  local copies, waits for them, and re-layouts  10.5 us (6%)
  blocking collectives  7.45 us (4%)
  other arithmetic  2.16 us (1%)
    all_to_all x4, starting transfers between devices, swap(): return lax.all_to_all(pieces, axis, split_axis=0, concat_axis=0, tiled=True)  50.9 us
    ppermute x9, starting transfers between devices, shift(): lax.ppermute(values, axis, [(i, (i + step) % size) for i in range(size)])  28.7 us
    all_to_all x4, waiting for transfers between devices, swap(): return lax.all_to_all(pieces, axis, split_axis=0, concat_axis=0, tiled=True)  23.3 us
    ppermute x9, waiting for transfers between devices, shift(): lax.ppermute(values, axis, [(i, (i + step) % size) for i in range(size)])  13.9 us
    unnamed x38, local copies, waits for them, and re-layouts  7.77 us
    all_gather x1, blocking collectives, local(): full_mixed = lax.all_gather(mixed, REP, axis=0, tiled=True)  7.45 us
    pallas_call x2, Pallas kernels, hub_grad_terms(): call(partial(hub_grad_kernel, steps, sizes), [jax.ShapeDtypeStruct(shape,...  6.32 us
    pallas_call x1, Pallas kernels, layer(): pl.pallas_call(partial(layer_kernel, sizes), out_shape=[jax.ShapeDtypeStr...  5.46 us
  transfers between devices with their start and end apart: 13, of which 7 were waited for; matrix products, arithmetic and copies ran while one was open for 2% of the time, Pallas kernels for 11%

profile of v10, /device:TPU:16, one launch (start us, length us, event | category | flops | bytes accessed | tf_op | source)
XLA Modules:
  0.0 165.2 jit_solution(959996076378387747)
XLA Ops:
  0.7 0.8 fusion.4
  1.5 0.7 broadcast_in_dim.17
  2.2 16.1 %all-to-all-start = ((bf16[32,32,128]{2,1,0:T(8,128)(2,1)}), bf16[32,32,128]{2,1,0:T(8,128)(2,1)S(1)}, u32[]{:S(2)}, u32[]{:S(2)}) async-start(bf16[32,32,128]{2,1,0:T(8,128)(2,1)} %broadcast_in_dim.17), calls=%async_computation | async-start | bytes 524288 | tf_op jit(solution)/shard_map/all_to_all | solution.py:29
  18.3 0.7 fusion
  19.1 0.8 copy.29
  20.0 0.8 select_bitcast_fusion
  20.7 0.1 reshape.37.index_ref
  20.9 1.0 copy-done.5
  21.9 0.9 copy-done.7
  22.8 0.8 copy-done.9
  23.6 0.8 copy-done.10
  24.4 1.9 %collective-permute-start = (bf16[64,2688]{1,0:T(8,128)(2,1)S(1)}, bf16[64,2688]{1,0:T(8,128)(2,1)}, u32[]{:S(2)}, u32[]{:S(2)}) collective-permute-start(bf16[64,2688]{1,0:T(8,128)(2,1)S(1)} %own_block.1.refs_0_), channel_id=1, source_target_pairs={{0,1},{1,0},{2,3},{3,2},{4,5},{5,4},{6,7},{7,6},{8,9},{9,8},{10,11... | collective-permute-start | bytes 1032200 | tf_op jit(solution)/shard_map/ppermute | solution.py:34
  26.4 0.1 reshape.38.index_ref
  26.5 1.8 %tail_rows_out.1 = bf16[128,16,128]{2,1,0:T(8,128)(2,1)} custom-call(s32[2,2048]{1,0:T(2,128)S(1)} %reshape.37.index_ref, bf16[64,1024]{1,0:T(8,128)(2,1)S(1)} %copy-done.6), custom_call_target="tpu_custom_call" | custom-call | flops 536870912 | bytes 2097152 | tf_op jit(solution)/shard_map/tail_rows_out/pallas_call | solution.py:86
  28.4 3.9 %all-to-all-done.refs_0_ = bf16[32,32,128]{2,1,0:T(8,128)(2,1)S(1)} async-done(((bf16[32,32,128]{2,1,0:T(8,128)(2,1)}), bf16[32,32,128]{2,1,0:T(8,128)(2,1)S(1)}, u32[]{:S(2)}, u32[]{:S(2)}) %all-to-all-start) | async-done | bytes 262176 | tf_op jit(solution)/shard_map/all_to_all | solution.py:29
  32.3 12.0 %all-to-all-start.1 = ((bf16[128,16,128]{2,1,0:T(8,128)(2,1)}), bf16[128,16,128]{2,1,0:T(8,128)(2,1)S(1)}, u32[]{:S(2)}, u32[]{:S(2)}) async-start(bf16[128,16,128]{2,1,0:T(8,128)(2,1)} %tail_rows_out.1), calls=%async_computation.1 | async-start | bytes 1048576 | tf_op jit(solution)/shard_map/all_to_all | solution.py:29
  44.3 2.6 %collective-permute-start.4 = (bf16[64,2688]{1,0:T(8,128)(2,1)S(1)}, bf16[64,2688]{1,0:T(8,128)(2,1)}, u32[]{:S(2)}, u32[]{:S(2)}) collective-permute-start(bf16[64,2688]{1,0:T(8,128)(2,1)S(1)} %own_block.1.refs_0_), channel_id=1, source_target_pairs={{0,2},{2,0},{1,3},{3,1},{4,6},{6,4},{5,7},{7,5},{8,10},{10,8},{9,1... | collective-permute-start | bytes 1032200 | tf_op jit(solution)/shard_map/ppermute | solution.py:34
  46.9 4.7 %collective-permute-start.3 = (bf16[32,32,128]{2,1,0:T(8,128)(2,1)S(1)}, bf16[32,32,128]{2,1,0:T(8,128)(2,1)S(1)}, u32[]{:S(2)}, u32[]{:S(2)}) collective-permute-start(bf16[32,32,128]{2,1,0:T(8,128)(2,1)S(1)} %all-to-all-done.refs_0_), channel_id=1, source_target_pairs={{0,96},{32,0},{64,32},{96,64},{1,97},{33,1},{65,33},{97,65},{2,98}... | collective-permute-start | bytes 786440 | tf_op jit(solution)/shard_map/ppermute | solution.py:34
  51.7 2.7 %collective-permute-start.2 = (bf16[32,32,128]{2,1,0:T(8,128)(2,1)S(1)}, bf16[32,32,128]{2,1,0:T(8,128)(2,1)}, u32[]{:S(2)}, u32[]{:S(2)}) collective-permute-start(bf16[32,32,128]{2,1,0:T(8,128)(2,1)S(1)} %all-to-all-done.refs_0_), channel_id=1, source_target_pairs={{0,64},{32,96},{64,0},{96,32},{1,65},{33,97},{65,1},{97,33},{2,66}... | collective-permute-start | bytes 786440 | tf_op jit(solution)/shard_map/ppermute | solution.py:34
  54.3 2.8 %collective-permute-start.1 = (bf16[32,32,128]{2,1,0:T(8,128)(2,1)S(1)}, bf16[32,32,128]{2,1,0:T(8,128)(2,1)}, u32[]{:S(2)}, u32[]{:S(2)}) collective-permute-start(bf16[32,32,128]{2,1,0:T(8,128)(2,1)S(1)} %all-to-all-done.refs_0_), channel_id=1, source_target_pairs={{0,32},{32,64},{64,96},{96,0},{1,33},{33,65},{65,97},{97,1},{2,34}... | collective-permute-start | bytes 786440 | tf_op jit(solution)/shard_map/ppermute | solution.py:34
  57.2 6.7 %collective-permute-done.4.refs_1_ = bf16[64,2688]{1,0:T(8,128)(2,1)} collective-permute-done((bf16[64,2688]{1,0:T(8,128)(2,1)S(1)}, bf16[64,2688]{1,0:T(8,128)(2,1)}, u32[]{:S(2)}, u32[]{:S(2)}) %collective-permute-start.4) | collective-permute-done | bytes 344096 | tf_op jit(solution)/shard_map/ppermute | solution.py:34
  63.9 1.9 %collective-permute-start.5 = (bf16[64,2688]{1,0:T(8,128)(2,1)}, bf16[64,2688]{1,0:T(8,128)(2,1)}, u32[]{:S(2)}, u32[]{:S(2)}) collective-permute-start(bf16[64,2688]{1,0:T(8,128)(2,1)} %collective-permute-done.4.refs_1_), channel_id=1, source_target_pairs={{0,1},{1,0},{2,3},{3,2},{4,5},{5,4},{6,7},{7,6},{8,9},{9,8},{10,11... | collective-permute-start | bytes 1032200 | tf_op jit(solution)/shard_map/ppermute | solution.py:34
  65.8 0.5 broadcast_xor_fusion.place_ref
  66.3 0.4 collective-permute-done.2.refs_2_
  66.7 4.4 %collective-permute-done.1.refs_1_ = bf16[32,32,128]{2,1,0:T(8,128)(2,1)} collective-permute-done((bf16[32,32,128]{2,1,0:T(8,128)(2,1)S(1)}, bf16[32,32,128]{2,1,0:T(8,128)(2,1)}, u32[]{:S(2)}, u32[]{:S(2)}) %collective-permute-start.1) | collective-permute-done | bytes 262176 | tf_op jit(solution)/shard_map/ppermute | solution.py:34
  71.1 4.5 %hub_sums.1.hub_ref = f32[64,1024]{1,0:T(8,128)S(1)} custom-call(s32[1]{0:T(128)} %bitcast.11.x_ref, s32[128]{0:T(128)S(1)} %bitcast.28, s32[128]{0:T(128)S(1)} %bitcast.31, bf16[32,32,128]{2,1,0:T(8,128)(2,1)S(1)} %all-to-all-done.refs_0_, bf16[32,32,128]{2,1,0:T(8,128)(2,1)} %collective-permute-done.1.refs_1_, ...), custom_call_target="tpu_custom_call" | custom-call | flops 268435456 | bytes 4194304 | tf_op jit(solution)/shard_map/hub_sums/pallas_call | solution.py:325
  75.7 0.7 copy-done.3
  76.4 0.9 copy-done.4
  77.3 2.4 %mixed.1 = bf16[64,1024]{1,0:T(8,128)(2,1)S(1)} custom-call(s32[2,2048]{1,0:T(2,128)S(1)} %reshape.38.index_ref, bf16[128,16,128]{2,1,0:T(8,128)(2,1)S(1)} %all-to-all-done.1.arrived_ref, f32[64,1024]{1,0:T(8,128)S(1)} %copy-done.4, s32[1,1024]{1,0:T(1,128)S(1)} %bitcast.35), custom_call_target="tpu_custom_call" | custom-call | flops 1073741824 | bytes 2097152 | tf_op jit(solution)/shard_map/mixed/pallas_call | solution.py:223
  79.7 7.5 %all_gather.3.mixed_ref = bf16[256,1024]{1,0:T(8,128)(2,1)} all-gather(bf16[64,1024]{1,0:T(8,128)(2,1)S(1)} %mixed.1), channel_id=1, replica_groups=mesh['yh'=4,'x'=4,'z'=8,'yl'=2,'core'=2] {'yl','core'}, dimensions={0}, use_global_device_ids=true | all-gather | bytes 655360 | tf_op jit(solution)/shard_map/all_gather | solution.py:501
  87.2 5.5 %layer.1 = (bf16[64,1024]{1,0:T(8,128)(2,1)}, bf16[256,1024]{1,0:T(8,128)(2,1)}, bf16[64,1024]{1,0:T(8,128)(2,1)}, bf16[64,48,128]{2,1,0:T(8,128)(2,1)}, bf16[64...) custom-call(s32[4]{0:T(128)} %broadcast_xor_fusion.place_ref, s32[2,2048]{1,0:T(2,128)} %copy-done.11, s32[1,1024]{1,0:T(1,128)} %bitcast.34, ...), custom_call_target="tpu_custom_call" | custom-call | flops 1048576000 | bytes 4194304 | tf_op jit(solution)/shard_map/layer/pallas_call | solution.py:184
  92.6 12.3 %all-to-all-start.2 = ((bf16[128,24,128]{2,1,0:T(8,128)(2,1)}), bf16[128,24,128]{2,1,0:T(8,128)(2,1)S(1)}, u32[]{:S(2)}, u32[]{:S(2)}) async-start(bf16[128,24,128]{2,1,0:T(8,128)(2,1)} %bitcast.36), calls=%async_computation.2 | async-start | bytes 1572864 | tf_op jit(solution)/shard_map/all_to_all | solution.py:29
  105.0 0.9 copy-done.1
  105.9 0.7 copy-done.8
  106.6 4.6 %hub_grad_terms.3 = (bf16[33,32,128]{2,1,0:T(8,128)(2,1)}, bf16[33,32,128]{2,1,0:T(8,128)(2,1)}, bf16[33,32,128]{2,1,0:T(8,128)(2,1)}) custom-call(s32[1]{0:T(128)} %bitcast.11.x_ref, s32[128]{0:T(128)S(1)} %bitcast.29, s32[128]{0:T(128)S(1)} %bitcast.32, bf16[64,1024]{1,0:T(8,128)(2,1)S(1)} %copy-done.1, bf16[32,128]{1,0:T(8,128)(2,1)S(1)} %copy-done.8, ...), custom_call_target="tpu_custom_call" | custom-call | flops 201326592 | bytes 4194304 | tf_op jit(solution)/shard_map/hub_grad_terms/pallas_call | solution.py:369
  111.2 5.0 %collective-permute-start.6 = (bf16[33,32,128]{2,1,0:T(8,128)(2,1)}, bf16[33,32,128]{2,1,0:T(8,128)(2,1)S(1)}, u32[]{:S(2)}, u32[]{:S(2)}) collective-permute-start(bf16[33,32,128]{2,1,0:T(8,128)(2,1)} %get-tuple-element.35), channel_id=1, source_target_pairs={{0,64},{32,96},{64,0},{96,32},{1,65},{33,97},{65,1},{97,33},{2,66}... | collective-permute-start | bytes 811016 | tf_op jit(solution)/shard_map/ppermute | solution.py:34
  116.2 2.5 %collective-permute-start.7 = (bf16[33,32,128]{2,1,0:T(8,128)(2,1)}, bf16[33,32,128]{2,1,0:T(8,128)(2,1)}, u32[]{:S(2)}, u32[]{:S(2)}) collective-permute-start(bf16[33,32,128]{2,1,0:T(8,128)(2,1)} %get-tuple-element.36), channel_id=1, source_target_pairs={{0,32},{32,64},{64,96},{96,0},{1,33},{33,65},{65,97},{97,1},{2,34}... | collective-permute-start | bytes 811016 | tf_op jit(solution)/shard_map/ppermute | solution.py:34
  118.7 4.5 %collective-permute-start.8 = (bf16[33,32,128]{2,1,0:T(8,128)(2,1)}, bf16[33,32,128]{2,1,0:T(8,128)(2,1)}, u32[]{:S(2)}, u32[]{:S(2)}) collective-permute-start(bf16[33,32,128]{2,1,0:T(8,128)(2,1)} %get-tuple-element.37), channel_id=1, source_target_pairs={{0,96},{32,0},{64,32},{96,64},{1,97},{33,1},{65,33},{97,65},{2,98}... | collective-permute-start | bytes 811016 | tf_op jit(solution)/shard_map/ppermute | solution.py:34
  123.3 1.7 %hub_grad_terms.2.refs_0_ = bf16[33,32,128]{2,1,0:T(8,128)(2,1)S(1)} custom-call(s32[1]{0:T(128)} %bitcast.11.x_ref, s32[128]{0:T(128)S(1)} %bitcast.30, s32[128]{0:T(128)S(1)} %bitcast.33, bf16[64,1024]{1,0:T(8,128)(2,1)S(1)} %copy-done.1, bf16[32,128]{1,0:T(8,128)(2,1)S(1)} %copy-done.8, bf16[128,64,128]{2,1,0:T(8,128)(2,1)S(1)} %bitcast.25), custom_call_target="tpu_custom_call" | custom-call | flops 67108864 | bytes 4194304 | tf_op jit(solution)/shard_map/hub_grad_terms/pallas_call | solution.py:369
  125.0 7.0 %all-to-all-done.2.arrived_ref = bf16[128,24,128]{2,1,0:T(8,128)(2,1)S(1)} async-done(((bf16[128,24,128]{2,1,0:T(8,128)(2,1)}), bf16[128,24,128]{2,1,0:T(8,128)(2,1)S(1)}, u32[]{:S(2)}, u32[]{:S(2)}) %all-to-all-start.2) | async-done | bytes 786464 | tf_op jit(solution)/shard_map/all_to_all | solution.py:29
  132.0 0.1 convert_reduce_fusion.refs_4_
  132.1 2.5 %collective-permute-done.7.refs_2_ = bf16[33,32,128]{2,1,0:T(8,128)(2,1)} collective-permute-done((bf16[33,32,128]{2,1,0:T(8,128)(2,1)}, bf16[33,32,128]{2,1,0:T(8,128)(2,1)}, u32[]{:S(2)}, u32[]{:S(2)}) %collective-permute-start.7) | collective-permute-done | bytes 270368 | tf_op jit(solution)/shard_map/ppermute | solution.py:34
  134.6 1.9 %hub_grads_over_x.1 = bf16[32,48,128]{2,1,0:T(8,128)(2,1)} custom-call(bf16[33,32,128]{2,1,0:T(8,128)(2,1)S(1)} %hub_grad_terms.2.refs_0_, bf16[33,32,128]{2,1,0:T(8,128)(2,1)S(1)} %collective-permute-done.6.refs_1_, bf16[33,32,128]{2,1,0:T(8,128)(2,1)} %collective-permute-done.7.refs_2_, bf16[33,32,128]{2,1,0:T(8,128)(2,1)} %collective-permute-done.8.refs_3_, ...), custom_call_target="tpu_custom_call" | custom-call | flops 1048576 | bytes 2097152 | tf_op jit(solution)/shard_map/hub_grads_over_x/pallas_call | solution.py:398
  136.5 10.6 %all-to-all-start.3 = ((bf16[32,48,128]{2,1,0:T(8,128)(2,1)}), bf16[32,48,128]{2,1,0:T(8,128)(2,1)S(1)}, u32[]{:S(2)}, u32[]{:S(2)}) async-start(bf16[32,48,128]{2,1,0:T(8,128)(2,1)} %hub_grads_over_x.1), calls=%async_computation.3 | async-start | bytes 786432 | tf_op jit(solution)/shard_map/all_to_all | solution.py:29
  147.1 1.0 copy-done.15
  148.2 3.1 %tail_grads.1.base_ref = f32[64,1024]{1,0:T(8,128)} custom-call(s32[2,2048]{1,0:T(2,128)S(1)} %reshape.37.index_ref, bf16[128,24,128]{2,1,0:T(8,128)(2,1)S(1)} %all-to-all-done.2.arrived_ref, bf16[64,256]{1,0:T(8,128)(2,1)S(1)} %copy-done.16, bf16[256,1024]{1,0:T(8,128)(2,1)S(1)} %copy-done.15), custom_call_target="tpu_custom_call" | custom-call | flops 1073741824 | bytes 2097152 | tf_op jit(solution)/shard_map/tail_grads/pallas_call | solution.py:246
  151.3 12.4 %all-to-all-done.3.second_ref = bf16[32,48,128]{2,1,0:T(8,128)(2,1)S(1)} async-done(((bf16[32,48,128]{2,1,0:T(8,128)(2,1)}), bf16[32,48,128]{2,1,0:T(8,128)(2,1)S(1)}, u32[]{:S(2)}, u32[]{:S(2)}) %all-to-all-start.3) | async-done | bytes 393248 | tf_op jit(solution)/shard_map/all_to_all | solution.py:29
  163.7 1.6 gradients.1
  (42 shorter events, 0.4 us)
Async XLA Ops:
  0.6 25.9 %copy-start.6 = (bf16[64,1024]{1,0:T(8,128)(2,1)S(1)}, bf16[64,1024]{1,0:T(8,128)(2,1)}, u32[]{:S(2)}) copy-start(bf16[64,1024]{1,0:T(8,128)(2,1)} %feat_ref) | copy-start | bytes 393220
  0.6 25.6 %copy-start.17 = (s32[1,128,32]{1,2,0:T(8,128)S(1)}, s32[1,128,32]{1,2,0:T(8,128)}, u32[]{:S(2)}) copy-start(s32[1,128,32]{1,2,0:T(8,128)} %param.19) | copy-start | bytes 49156
  2.2 30.1 %all-to-all-start = ((bf16[32,32,128]{2,1,0:T(8,128)(2,1)}), bf16[32,32,128]{2,1,0:T(8,128)(2,1)S(1)}, u32[]{:S(2)}, u32[]{:S(2)}) async-start(bf16[32,32,128]{2,1,0:T(8,128)(2,1)} %broadcast_in_dim.17), calls=%async_computation | async-start | bytes 524288 | tf_op jit(solution)/shard_map/all_to_all | solution.py:29
  19.9 45.9 %copy-start.18 = (s32[4]{0:T(128)S(1)}, s32[4]{0:T(128)}, u32[]{:S(2)}) copy-start(s32[4]{0:T(128)} %constant.25.clone) | copy-start | bytes 52
  19.9 51.1 %copy-start.12 = (s32[1,128]{1,0:T(1,128)S(1)}, s32[1,128]{1,0:T(1,128)}, u32[]{:S(2)}) copy-start(s32[1,128]{1,0:T(1,128)} %param.15) | copy-start | bytes 1540
  20.0 51.1 %copy-start.13 = (s32[1,128]{1,0:T(1,128)S(1)}, s32[1,128]{1,0:T(1,128)}, u32[]{:S(2)}) copy-start(s32[1,128]{1,0:T(1,128)} %param.16) | copy-start | bytes 1540
  20.7 50.4 %copy-start = (bf16[1,128,64,128]{3,2,1,0:T(8,128)(2,1)S(1)}, bf16[1,128,64,128]{3,2,1,0:T(8,128)(2,1)}, u32[]{:S(2)}) copy-start(bf16[1,128,64,128]{3,2,1,0:T(8,128)(2,1)} %param.14) | copy-start | bytes 6291460
  20.9 1.0 copy-start.5
  21.9 0.9 copy-start.7
  22.8 0.8 copy-start.9
  23.6 0.8 copy-start.10
  24.4 51.3 %copy-start.2 = (bf16[64,2688]{1,0:T(8,128)(2,1)}, bf16[64,2688]{1,0:T(8,128)(2,1)S(1)}, u32[]{:S(2)}) copy-start(bf16[64,2688]{1,0:T(8,128)(2,1)S(1)} %own_block.1.refs_0_) | copy-start | bytes 1032196
  24.4 4.0 %collective-permute-start = (bf16[64,2688]{1,0:T(8,128)(2,1)S(1)}, bf16[64,2688]{1,0:T(8,128)(2,1)}, u32[]{:S(2)}, u32[]{:S(2)}) collective-permute-start(bf16[64,2688]{1,0:T(8,128)(2,1)S(1)} %own_block.1.refs_0_), channel_id=1, source_target_pairs={{0,1},{1,0},{2,3},{3,2},{4,5},{5,4},{6,7},{7,6},{8,9},{9,8},{10,11... | collective-permute-start | bytes 1032200 | tf_op jit(solution)/shard_map/ppermute | solution.py:34
  26.5 49.8 %copy-start.11 = (s32[2,2048]{1,0:T(2,128)}, s32[2,2048]{1,0:T(2,128)S(1)}, u32[]{:S(2)}) copy-start(s32[2,2048]{1,0:T(2,128)S(1)} %reshape.38.index_ref) | copy-start | bytes 49156
  28.4 48.0 %copy-start.14 = (s32[1024]{0:T(1024)S(1)}, s32[1024]{0:T(1024)}, u32[]{:S(2)}) copy-start(s32[1024]{0:T(1024)} %param.20) | copy-start | bytes 12292
  32.3 44.0 %all-to-all-start.1 = ((bf16[128,16,128]{2,1,0:T(8,128)(2,1)}), bf16[128,16,128]{2,1,0:T(8,128)(2,1)S(1)}, u32[]{:S(2)}, u32[]{:S(2)}) async-start(bf16[128,16,128]{2,1,0:T(8,128)(2,1)} %tail_rows_out.1), calls=%async_computation.1 | async-start | bytes 1048576 | tf_op jit(solution)/shard_map/all_to_all | solution.py:29
  44.3 19.6 %collective-permute-start.4 = (bf16[64,2688]{1,0:T(8,128)(2,1)S(1)}, bf16[64,2688]{1,0:T(8,128)(2,1)}, u32[]{:S(2)}, u32[]{:S(2)}) collective-permute-start(bf16[64,2688]{1,0:T(8,128)(2,1)S(1)} %own_block.1.refs_0_), channel_id=1, source_target_pairs={{0,2},{2,0},{1,3},{3,1},{4,6},{6,4},{5,7},{7,5},{8,10},{10,8},{9,1... | collective-permute-start | bytes 1032200 | tf_op jit(solution)/shard_map/ppermute | solution.py:34
  46.9 19.4 %collective-permute-start.3 = (bf16[32,32,128]{2,1,0:T(8,128)(2,1)S(1)}, bf16[32,32,128]{2,1,0:T(8,128)(2,1)S(1)}, u32[]{:S(2)}, u32[]{:S(2)}) collective-permute-start(bf16[32,32,128]{2,1,0:T(8,128)(2,1)S(1)} %all-to-all-done.refs_0_), channel_id=1, source_target_pairs={{0,96},{32,0},{64,32},{96,64},{1,97},{33,1},{65,33},{97,65},{2,98}... | collective-permute-start | bytes 786440 | tf_op jit(solution)/shard_map/ppermute | solution.py:34
  51.7 15.0 %collective-permute-start.2 = (bf16[32,32,128]{2,1,0:T(8,128)(2,1)S(1)}, bf16[32,32,128]{2,1,0:T(8,128)(2,1)}, u32[]{:S(2)}, u32[]{:S(2)}) collective-permute-start(bf16[32,32,128]{2,1,0:T(8,128)(2,1)S(1)} %all-to-all-done.refs_0_), channel_id=1, source_target_pairs={{0,64},{32,96},{64,0},{96,32},{1,65},{33,97},{65,1},{97,33},{2,66}... | collective-permute-start | bytes 786440 | tf_op jit(solution)/shard_map/ppermute | solution.py:34
  54.3 16.7 %collective-permute-start.1 = (bf16[32,32,128]{2,1,0:T(8,128)(2,1)S(1)}, bf16[32,32,128]{2,1,0:T(8,128)(2,1)}, u32[]{:S(2)}, u32[]{:S(2)}) collective-permute-start(bf16[32,32,128]{2,1,0:T(8,128)(2,1)S(1)} %all-to-all-done.refs_0_), channel_id=1, source_target_pairs={{0,32},{32,64},{64,96},{96,0},{1,33},{33,65},{65,97},{97,1},{2,34}... | collective-permute-start | bytes 786440 | tf_op jit(solution)/shard_map/ppermute | solution.py:34
  63.9 23.3 %collective-permute-start.5 = (bf16[64,2688]{1,0:T(8,128)(2,1)}, bf16[64,2688]{1,0:T(8,128)(2,1)}, u32[]{:S(2)}, u32[]{:S(2)}) collective-permute-start(bf16[64,2688]{1,0:T(8,128)(2,1)} %collective-permute-done.4.refs_1_), channel_id=1, source_target_pairs={{0,1},{1,0},{2,3},{3,2},{4,5},{5,4},{6,7},{7,6},{8,9},{9,8},{10,11... | collective-permute-start | bytes 1032200 | tf_op jit(solution)/shard_map/ppermute | solution.py:34
  75.6 0.7 copy-start.3
  76.4 1.0 copy-start.4
  92.6 39.3 %all-to-all-start.2 = ((bf16[128,24,128]{2,1,0:T(8,128)(2,1)}), bf16[128,24,128]{2,1,0:T(8,128)(2,1)S(1)}, u32[]{:S(2)}, u32[]{:S(2)}) async-start(bf16[128,24,128]{2,1,0:T(8,128)(2,1)} %bitcast.36), calls=%async_computation.2 | async-start | bytes 1572864 | tf_op jit(solution)/shard_map/all_to_all | solution.py:29
  105.0 0.9 copy-start.1
  105.9 0.7 copy-start.8
  111.2 20.9 %collective-permute-start.6 = (bf16[33,32,128]{2,1,0:T(8,128)(2,1)}, bf16[33,32,128]{2,1,0:T(8,128)(2,1)S(1)}, u32[]{:S(2)}, u32[]{:S(2)}) collective-permute-start(bf16[33,32,128]{2,1,0:T(8,128)(2,1)} %get-tuple-element.35), channel_id=1, source_target_pairs={{0,64},{32,96},{64,0},{96,32},{1,65},{33,97},{65,1},{97,33},{2,66}... | collective-permute-start | bytes 811016 | tf_op jit(solution)/shard_map/ppermute | solution.py:34
  116.2 18.4 %collective-permute-start.7 = (bf16[33,32,128]{2,1,0:T(8,128)(2,1)}, bf16[33,32,128]{2,1,0:T(8,128)(2,1)}, u32[]{:S(2)}, u32[]{:S(2)}) collective-permute-start(bf16[33,32,128]{2,1,0:T(8,128)(2,1)} %get-tuple-element.36), channel_id=1, source_target_pairs={{0,32},{32,64},{64,96},{96,0},{1,33},{33,65},{65,97},{97,1},{2,34}... | collective-permute-start | bytes 811016 | tf_op jit(solution)/shard_map/ppermute | solution.py:34
  118.7 28.4 %copy-start.16 = (bf16[64,256]{1,0:T(8,128)(2,1)S(1)}, bf16[64,256]{1,0:T(8,128)(2,1)}, u32[]{:S(2)}) copy-start(bf16[64,256]{1,0:T(8,128)(2,1)} %get-tuple-element.39.weight_ref) | copy-start | bytes 98308
  118.7 15.9 %collective-permute-start.8 = (bf16[33,32,128]{2,1,0:T(8,128)(2,1)}, bf16[33,32,128]{2,1,0:T(8,128)(2,1)}, u32[]{:S(2)}, u32[]{:S(2)}) collective-permute-start(bf16[33,32,128]{2,1,0:T(8,128)(2,1)} %get-tuple-element.37), channel_id=1, source_target_pairs={{0,96},{32,0},{64,32},{96,64},{1,97},{33,1},{65,33},{97,65},{2,98}... | collective-permute-start | bytes 811016 | tf_op jit(solution)/shard_map/ppermute | solution.py:34
  136.5 27.1 %all-to-all-start.3 = ((bf16[32,48,128]{2,1,0:T(8,128)(2,1)}), bf16[32,48,128]{2,1,0:T(8,128)(2,1)S(1)}, u32[]{:S(2)}, u32[]{:S(2)}) async-start(bf16[32,48,128]{2,1,0:T(8,128)(2,1)} %hub_grads_over_x.1), calls=%async_computation.3 | async-start | bytes 786432 | tf_op jit(solution)/shard_map/all_to_all | solution.py:29
  147.1 1.0 copy-start.15

commit v11 on v8

--- a/solution.py
+++ b/solution.py
@@ -374,7 +374,6 @@
         "hub_grad_terms",
         tiles.size * width * len(steps),
         4,
-        60 * MIB,
     )(x_index, block, mask, grad, bias, tiles)
 
 

time: 166 us -> 167 us (level)
  Pallas kernels: 30.1 us -> 28.1 us
  local copies, waits for them, and re-layouts: 7.96 us -> 9.63 us
    pallas_call x2, Pallas kernels: 9.34 us -> 6.33 us  [hub_grad_terms(): call(partial(hub_grad_kernel, steps, sizes), [jax.ShapeDtypeStruct(shape,...]
    unnamed x34 -> x36, local copies, waits for them, and re-layouts: 5.19 us -> 6.86 us
  transfers between devices with their start and end apart: 13 -> 13, of which waited for: 6 -> 6; matrix products, arithmetic and copies ran while one was open for 2% -> 2% of each run, Pallas kernels for 13% -> 12%
where the time goes in v11:
time: 167 us; the launch traced here: 165 us
  starting transfers between devices  84.7 us (51%)
  waiting for transfers between devices  32.7 us (20%)
  Pallas kernels  28.1 us (17%)
  local copies, waits for them, and re-layouts  9.63 us (6%)
  blocking collectives  7.1 us (4%)
  other arithmetic  2.16 us (1%)
    all_to_all x4, starting transfers between devices, swap(): return lax.all_to_all(pieces, axis, split_axis=0, concat_axis=0, tiled=True)  55.7 us
    ppermute x9, starting transfers between devices, shift(): lax.ppermute(values, axis, [(i, (i + step) % size) for i in range(size)])  28.9 us
    all_to_all x4, waiting for transfers between devices, swap(): return lax.all_to_all(pieces, axis, split_axis=0, concat_axis=0, tiled=True)  25.3 us
    ppermute x9, waiting for transfers between devices, shift(): lax.ppermute(values, axis, [(i, (i + step) % size) for i in range(size)])  7.42 us
    all_gather x1, blocking collectives, local(): full_mixed = lax.all_gather(mixed, REP, axis=0, tiled=True)  7.1 us
    unnamed x36, local copies, waits for them, and re-layouts  6.86 us
    pallas_call x2, Pallas kernels, hub_grad_terms(): call(partial(hub_grad_kernel, steps, sizes), [jax.ShapeDtypeStruct(shape,...  6.33 us
    pallas_call x1, Pallas kernels, layer(): pl.pallas_call(partial(layer_kernel, sizes), out_shape=[jax.ShapeDtypeStr...  5.46 us
  transfers between devices with their start and end apart: 13, of which 6 were waited for; matrix products, arithmetic and copies ran while one was open for 2% of the time, Pallas kernels for 12%

profile of v11, /device:TPU:8, one launch (start us, length us, event | category | flops | bytes accessed | tf_op | source)
XLA Modules:
  0.0 165.4 jit_solution(16102684655391116999)
XLA Ops:
  0.7 0.8 fusion.4
  1.5 0.7 broadcast_in_dim.17
  2.2 15.1 %all-to-all-start = ((bf16[32,32,128]{2,1,0:T(8,128)(2,1)}), bf16[32,32,128]{2,1,0:T(8,128)(2,1)S(1)}, u32[]{:S(2)}, u32[]{:S(2)}) async-start(bf16[32,32,128]{2,1,0:T(8,128)(2,1)} %broadcast_in_dim.17), calls=%async_computation | async-start | bytes 524288 | tf_op jit(solution)/shard_map/all_to_all | solution.py:29
  17.3 0.7 fusion
  18.0 0.1 copy.31
  18.1 0.8 copy.29
  19.0 0.7 select_bitcast_fusion
  19.7 0.1 reshape.37.index_ref
  19.9 1.0 copy-done.3
  20.9 0.9 copy-done.5
  21.8 0.8 copy-done.7
  22.5 0.8 copy-done.8
  23.3 1.9 %collective-permute-start = (bf16[64,2688]{1,0:T(8,128)(2,1)S(1)}, bf16[64,2688]{1,0:T(8,128)(2,1)}, u32[]{:S(2)}, u32[]{:S(2)}) collective-permute-start(bf16[64,2688]{1,0:T(8,128)(2,1)S(1)} %own_block.1.refs_0_), channel_id=1, source_target_pairs={{0,1},{1,0},{2,3},{3,2},{4,5},{5,4},{6,7},{7,6},{8,9},{9,8},{10,11... | collective-permute-start | bytes 1032200 | tf_op jit(solution)/shard_map/ppermute | solution.py:34
  25.4 0.1 reshape.38.index_ref
  25.5 1.8 %tail_rows_out.1 = bf16[128,16,128]{2,1,0:T(8,128)(2,1)} custom-call(s32[2,2048]{1,0:T(2,128)S(1)} %reshape.37.index_ref, bf16[64,1024]{1,0:T(8,128)(2,1)S(1)} %copy-done.4), custom_call_target="tpu_custom_call" | custom-call | flops 536870912 | bytes 2097152 | tf_op jit(solution)/shard_map/tail_rows_out/pallas_call | solution.py:86
  27.4 3.9 %all-to-all-done.refs_0_ = bf16[32,32,128]{2,1,0:T(8,128)(2,1)S(1)} async-done(((bf16[32,32,128]{2,1,0:T(8,128)(2,1)}), bf16[32,32,128]{2,1,0:T(8,128)(2,1)S(1)}, u32[]{:S(2)}, u32[]{:S(2)}) %all-to-all-start) | async-done | bytes 262176 | tf_op jit(solution)/shard_map/all_to_all | solution.py:29
  31.3 12.6 %all-to-all-start.1 = ((bf16[128,16,128]{2,1,0:T(8,128)(2,1)}), bf16[128,16,128]{2,1,0:T(8,128)(2,1)S(1)}, u32[]{:S(2)}, u32[]{:S(2)}) async-start(bf16[128,16,128]{2,1,0:T(8,128)(2,1)} %tail_rows_out.1), calls=%async_computation.1 | async-start | bytes 1048576 | tf_op jit(solution)/shard_map/all_to_all | solution.py:29
  43.9 3.3 %collective-permute-start.4 = (bf16[64,2688]{1,0:T(8,128)(2,1)S(1)}, bf16[64,2688]{1,0:T(8,128)(2,1)}, u32[]{:S(2)}, u32[]{:S(2)}) collective-permute-start(bf16[64,2688]{1,0:T(8,128)(2,1)S(1)} %own_block.1.refs_0_), channel_id=1, source_target_pairs={{0,2},{2,0},{1,3},{3,1},{4,6},{6,4},{5,7},{7,5},{8,10},{10,8},{9,1... | collective-permute-start | bytes 1032200 | tf_op jit(solution)/shard_map/ppermute | solution.py:34
  47.1 3.0 %collective-permute-start.3 = (bf16[32,32,128]{2,1,0:T(8,128)(2,1)S(1)}, bf16[32,32,128]{2,1,0:T(8,128)(2,1)}, u32[]{:S(2)}, u32[]{:S(2)}) collective-permute-start(bf16[32,32,128]{2,1,0:T(8,128)(2,1)S(1)} %all-to-all-done.refs_0_), channel_id=1, source_target_pairs={{0,32},{32,64},{64,96},{96,0},{1,33},{33,65},{65,97},{97,1},{2,34}... | collective-permute-start | bytes 786440 | tf_op jit(solution)/shard_map/ppermute | solution.py:34
  50.2 4.0 %collective-permute-start.2 = (bf16[32,32,128]{2,1,0:T(8,128)(2,1)S(1)}, bf16[32,32,128]{2,1,0:T(8,128)(2,1)S(1)}, u32[]{:S(2)}, u32[]{:S(2)}) collective-permute-start(bf16[32,32,128]{2,1,0:T(8,128)(2,1)S(1)} %all-to-all-done.refs_0_), channel_id=1, source_target_pairs={{0,96},{32,0},{64,32},{96,64},{1,97},{33,1},{65,33},{97,65},{2,98}... | collective-permute-start | bytes 786440 | tf_op jit(solution)/shard_map/ppermute | solution.py:34
  54.2 3.3 %collective-permute-start.1 = (bf16[32,32,128]{2,1,0:T(8,128)(2,1)S(1)}, bf16[32,32,128]{2,1,0:T(8,128)(2,1)}, u32[]{:S(2)}, u32[]{:S(2)}) collective-permute-start(bf16[32,32,128]{2,1,0:T(8,128)(2,1)S(1)} %all-to-all-done.refs_0_), channel_id=1, source_target_pairs={{0,64},{32,96},{64,0},{96,32},{1,65},{33,97},{65,1},{97,33},{2,66}... | collective-permute-start | bytes 786440 | tf_op jit(solution)/shard_map/ppermute | solution.py:34
  57.6 4.7 %collective-permute-done.3.refs_1_ = bf16[32,32,128]{2,1,0:T(8,128)(2,1)} collective-permute-done((bf16[32,32,128]{2,1,0:T(8,128)(2,1)S(1)}, bf16[32,32,128]{2,1,0:T(8,128)(2,1)}, u32[]{:S(2)}, u32[]{:S(2)}) %collective-permute-start.3) | collective-permute-done | bytes 262176 | tf_op jit(solution)/shard_map/ppermute | solution.py:34
  62.3 2.7 %hub_sums.2.refs_3_ = f32[64,1024]{1,0:T(8,128)S(1)} custom-call(s32[1]{0:T(128)} %bitcast.11.x_ref, s32[128]{0:T(128)S(1)} %bitcast.29, s32[128]{0:T(128)S(1)} %bitcast.33, bf16[32,32,128]{2,1,0:T(8,128)(2,1)S(1)} %all-to-all-done.refs_0_, bf16[32,32,128]{2,1,0:T(8,128)(2,1)} %collective-permute-done.3.refs_1_, bf16[128,64,128]{2,1,0:T(8,128)(2,1)S(1)} %bitcast.23), custom_call_target="tpu_custom_call" | custom-call | flops 134217728 | bytes 4194304 | tf_op jit(solution)/shard_map/hub_sums/pallas_call | solution.py:325
  65.1 1.9 %collective-permute-start.5 = (bf16[64,2688]{1,0:T(8,128)(2,1)}, bf16[64,2688]{1,0:T(8,128)(2,1)S(1)}, u32[]{:S(2)}, u32[]{:S(2)}) collective-permute-start(bf16[64,2688]{1,0:T(8,128)(2,1)} %collective-permute-done.4.refs_1_), channel_id=1, source_target_pairs={{0,1},{1,0},{2,3},{3,2},{4,5},{5,4},{6,7},{7,6},{8,9},{9,8},{10,11... | collective-permute-start | bytes 1032200 | tf_op jit(solution)/shard_map/ppermute | solution.py:34
  67.0 0.5 broadcast_xor_fusion.place_ref
  67.5 1.0 collective-permute-done.1.refs_0_
  68.6 2.7 %hub_sums.3.hub_ref = f32[64,1024]{1,0:T(8,128)S(1)} custom-call(s32[1]{0:T(128)} %bitcast.11.x_ref, s32[128]{0:T(128)S(1)} %bitcast.30, s32[128]{0:T(128)S(1)} %bitcast.34, bf16[32,32,128]{2,1,0:T(8,128)(2,1)} %collective-permute-done.1.refs_0_, bf16[32,32,128]{2,1,0:T(8,128)(2,1)S(1)} %collective-permute-done.2.refs_1_, ...), custom_call_target="tpu_custom_call" | custom-call | flops 134217728 | bytes 4194304 | tf_op jit(solution)/shard_map/hub_sums/pallas_call | solution.py:325
  71.3 2.4 %mixed.1 = bf16[64,1024]{1,0:T(8,128)(2,1)S(1)} custom-call(s32[2,2048]{1,0:T(2,128)S(1)} %reshape.38.index_ref, bf16[128,16,128]{2,1,0:T(8,128)(2,1)S(1)} %all-to-all-done.1.arrived_ref, f32[64,1024]{1,0:T(8,128)S(1)} %hub_sums.3.hub_ref, s32[1,1024]{1,0:T(1,128)S(1)} %bitcast.38), custom_call_target="tpu_custom_call" | custom-call | flops 1073741824 | bytes 2097152 | tf_op jit(solution)/shard_map/mixed/pallas_call | solution.py:223
  73.7 7.1 %all_gather.3.mixed_ref = bf16[256,1024]{1,0:T(8,128)(2,1)} all-gather(bf16[64,1024]{1,0:T(8,128)(2,1)S(1)} %mixed.1), channel_id=1, replica_groups=mesh['yh'=4,'x'=4,'z'=8,'yl'=2,'core'=2] {'yl','core'}, dimensions={0}, use_global_device_ids=true | all-gather | bytes 655360 | tf_op jit(solution)/shard_map/all_gather | solution.py:503
  80.8 0.7 copy-done.16
  81.6 5.5 %layer.1 = (bf16[64,1024]{1,0:T(8,128)(2,1)}, bf16[256,1024]{1,0:T(8,128)(2,1)}, bf16[64,1024]{1,0:T(8,128)(2,1)}, bf16[64,48,128]{2,1,0:T(8,128)(2,1)}, bf16[64...) custom-call(s32[4]{0:T(128)} %broadcast_xor_fusion.place_ref, s32[2,2048]{1,0:T(2,128)} %copy-done.9, s32[1,1024]{1,0:T(1,128)} %bitcast.37, ...), custom_call_target="tpu_custom_call" | custom-call | flops 1048576000 | bytes 4194304 | tf_op jit(solution)/shard_map/layer/pallas_call | solution.py:184
  87.0 18.6 %all-to-all-start.2 = ((bf16[128,24,128]{2,1,0:T(8,128)(2,1)}), bf16[128,24,128]{2,1,0:T(8,128)(2,1)S(1)}, u32[]{:S(2)}, u32[]{:S(2)}) async-start(bf16[128,24,128]{2,1,0:T(8,128)(2,1)} %bitcast.39), calls=%async_computation.2 | async-start | bytes 1572864 | tf_op jit(solution)/shard_map/all_to_all | solution.py:29
  105.7 0.9 copy-done.1
  106.6 0.7 copy-done.6
  107.2 4.6 %hub_grad_terms.3 = (bf16[33,32,128]{2,1,0:T(8,128)(2,1)}, bf16[33,32,128]{2,1,0:T(8,128)(2,1)}, bf16[33,32,128]{2,1,0:T(8,128)(2,1)}) custom-call(s32[1]{0:T(128)} %bitcast.11.x_ref, s32[128]{0:T(128)S(1)} %bitcast.31, s32[128]{0:T(128)S(1)} %bitcast.35, bf16[64,1024]{1,0:T(8,128)(2,1)S(1)} %copy-done.1, bf16[32,128]{1,0:T(8,128)(2,1)S(1)} %copy-done.6, ...), custom_call_target="tpu_custom_call" | custom-call | flops 201326592 | bytes 4194304 | tf_op jit(solution)/shard_map/hub_grad_terms/pallas_call | solution.py:369
  111.9 4.4 %collective-permute-start.6 = (bf16[33,32,128]{2,1,0:T(8,128)(2,1)}, bf16[33,32,128]{2,1,0:T(8,128)(2,1)S(1)}, u32[]{:S(2)}, u32[]{:S(2)}) collective-permute-start(bf16[33,32,128]{2,1,0:T(8,128)(2,1)} %get-tuple-element.39), channel_id=1, source_target_pairs={{0,64},{32,96},{64,0},{96,32},{1,65},{33,97},{65,1},{97,33},{2,66}... | collective-permute-start | bytes 811016 | tf_op jit(solution)/shard_map/ppermute | solution.py:34
  116.3 2.5 %collective-permute-start.7 = (bf16[33,32,128]{2,1,0:T(8,128)(2,1)}, bf16[33,32,128]{2,1,0:T(8,128)(2,1)}, u32[]{:S(2)}, u32[]{:S(2)}) collective-permute-start(bf16[33,32,128]{2,1,0:T(8,128)(2,1)} %get-tuple-element.40), channel_id=1, source_target_pairs={{0,32},{32,64},{64,96},{96,0},{1,33},{33,65},{65,97},{97,1},{2,34}... | collective-permute-start | bytes 811016 | tf_op jit(solution)/shard_map/ppermute | solution.py:34
  118.8 4.5 %collective-permute-start.8 = (bf16[33,32,128]{2,1,0:T(8,128)(2,1)}, bf16[33,32,128]{2,1,0:T(8,128)(2,1)}, u32[]{:S(2)}, u32[]{:S(2)}) collective-permute-start(bf16[33,32,128]{2,1,0:T(8,128)(2,1)} %get-tuple-element.41), channel_id=1, source_target_pairs={{0,96},{32,0},{64,32},{96,64},{1,97},{33,1},{65,33},{97,65},{2,98}... | collective-permute-start | bytes 811016 | tf_op jit(solution)/shard_map/ppermute | solution.py:34
  123.4 1.7 %hub_grad_terms.2.refs_0_ = bf16[33,32,128]{2,1,0:T(8,128)(2,1)S(1)} custom-call(s32[1]{0:T(128)} %bitcast.11.x_ref, s32[128]{0:T(128)S(1)} %bitcast.32, s32[128]{0:T(128)S(1)} %bitcast.36, bf16[64,1024]{1,0:T(8,128)(2,1)S(1)} %copy-done.1, bf16[32,128]{1,0:T(8,128)(2,1)S(1)} %copy-done.6, bf16[128,64,128]{2,1,0:T(8,128)(2,1)S(1)} %bitcast.26), custom_call_target="tpu_custom_call" | custom-call | flops 67108864 | bytes 4194304 | tf_op jit(solution)/shard_map/hub_grad_terms/pallas_call | solution.py:369
  125.0 9.2 %all-to-all-done.2.arrived_ref = bf16[128,24,128]{2,1,0:T(8,128)(2,1)S(1)} async-done(((bf16[128,24,128]{2,1,0:T(8,128)(2,1)}), bf16[128,24,128]{2,1,0:T(8,128)(2,1)S(1)}, u32[]{:S(2)}, u32[]{:S(2)}) %all-to-all-start.2) | async-done | bytes 786464 | tf_op jit(solution)/shard_map/all_to_all | solution.py:29
  134.2 0.1 convert_reduce_fusion.refs_4_
  134.3 1.6 collective-permute-done.7.refs_2_
  136.0 1.9 %hub_grads_over_x.1 = bf16[32,48,128]{2,1,0:T(8,128)(2,1)} custom-call(bf16[33,32,128]{2,1,0:T(8,128)(2,1)S(1)} %hub_grad_terms.2.refs_0_, bf16[33,32,128]{2,1,0:T(8,128)(2,1)S(1)} %collective-permute-done.6.refs_1_, bf16[33,32,128]{2,1,0:T(8,128)(2,1)} %collective-permute-done.7.refs_2_, bf16[33,32,128]{2,1,0:T(8,128)(2,1)} %collective-permute-done.8.refs_3_, ...), custom_call_target="tpu_custom_call" | custom-call | flops 1048576 | bytes 2097152 | tf_op jit(solution)/shard_map/hub_grads_over_x/pallas_call | solution.py:398
  137.9 9.5 %all-to-all-start.3 = ((bf16[32,48,128]{2,1,0:T(8,128)(2,1)}), bf16[32,48,128]{2,1,0:T(8,128)(2,1)S(1)}, u32[]{:S(2)}, u32[]{:S(2)}) async-start(bf16[32,48,128]{2,1,0:T(8,128)(2,1)} %hub_grads_over_x.1), calls=%async_computation.3 | async-start | bytes 786432 | tf_op jit(solution)/shard_map/all_to_all | solution.py:29
  147.5 1.0 copy-done.13
  148.5 3.1 %tail_grads.1.base_ref = f32[64,1024]{1,0:T(8,128)} custom-call(s32[2,2048]{1,0:T(2,128)S(1)} %reshape.37.index_ref, bf16[128,24,128]{2,1,0:T(8,128)(2,1)S(1)} %all-to-all-done.2.arrived_ref, bf16[64,256]{1,0:T(8,128)(2,1)S(1)} %copy-done.14, bf16[256,1024]{1,0:T(8,128)(2,1)S(1)} %copy-done.13), custom_call_target="tpu_custom_call" | custom-call | flops 1073741824 | bytes 2097152 | tf_op jit(solution)/shard_map/tail_grads/pallas_call | solution.py:246
  151.6 12.2 %all-to-all-done.3.second_ref = bf16[32,48,128]{2,1,0:T(8,128)(2,1)S(1)} async-done(((bf16[32,48,128]{2,1,0:T(8,128)(2,1)}), bf16[32,48,128]{2,1,0:T(8,128)(2,1)S(1)}, u32[]{:S(2)}, u32[]{:S(2)}) %all-to-all-start.3) | async-done | bytes 393248 | tf_op jit(solution)/shard_map/all_to_all | solution.py:29
  163.9 1.6 gradients.1
  (41 shorter events, 0.3 us)
Async XLA Ops:
  0.6 24.9 %copy-start.4 = (bf16[64,1024]{1,0:T(8,128)(2,1)S(1)}, bf16[64,1024]{1,0:T(8,128)(2,1)}, u32[]{:S(2)}) copy-start(bf16[64,1024]{1,0:T(8,128)(2,1)} %feat_ref) | copy-start | bytes 393220
  0.6 24.6 %copy-start.15 = (s32[1,128,32]{1,2,0:T(8,128)S(1)}, s32[1,128,32]{1,2,0:T(8,128)}, u32[]{:S(2)}) copy-start(s32[1,128,32]{1,2,0:T(8,128)} %param.19) | copy-start | bytes 49156
  2.2 29.1 %all-to-all-start = ((bf16[32,32,128]{2,1,0:T(8,128)(2,1)}), bf16[32,32,128]{2,1,0:T(8,128)(2,1)S(1)}, u32[]{:S(2)}, u32[]{:S(2)}) async-start(bf16[32,32,128]{2,1,0:T(8,128)(2,1)} %broadcast_in_dim.17), calls=%async_computation | async-start | bytes 524288 | tf_op jit(solution)/shard_map/all_to_all | solution.py:29
  18.9 43.4 %copy-start.10 = (s32[1,128]{1,0:T(1,128)S(1)}, s32[1,128]{1,0:T(1,128)}, u32[]{:S(2)}) copy-start(s32[1,128]{1,0:T(1,128)} %param.15) | copy-start | bytes 1540
  18.9 43.4 %copy-start.11 = (s32[1,128]{1,0:T(1,128)S(1)}, s32[1,128]{1,0:T(1,128)}, u32[]{:S(2)}) copy-start(s32[1,128]{1,0:T(1,128)} %param.16) | copy-start | bytes 1540
  19.7 42.6 %copy-start = (bf16[1,128,64,128]{3,2,1,0:T(8,128)(2,1)S(1)}, bf16[1,128,64,128]{3,2,1,0:T(8,128)(2,1)}, u32[]{:S(2)}) copy-start(bf16[1,128,64,128]{3,2,1,0:T(8,128)(2,1)} %param.14) | copy-start | bytes 6291460
  19.9 1.0 copy-start.3
  20.9 0.9 copy-start.5
  21.8 0.8 copy-start.7
  22.5 0.8 copy-start.8
  23.3 41.7 %copy-start.2 = (bf16[64,2688]{1,0:T(8,128)(2,1)}, bf16[64,2688]{1,0:T(8,128)(2,1)S(1)}, u32[]{:S(2)}) copy-start(bf16[64,2688]{1,0:T(8,128)(2,1)S(1)} %own_block.1.refs_0_) | copy-start | bytes 1032196
  23.3 4.0 %collective-permute-start = (bf16[64,2688]{1,0:T(8,128)(2,1)S(1)}, bf16[64,2688]{1,0:T(8,128)(2,1)}, u32[]{:S(2)}, u32[]{:S(2)}) collective-permute-start(bf16[64,2688]{1,0:T(8,128)(2,1)S(1)} %own_block.1.refs_0_), channel_id=1, source_target_pairs={{0,1},{1,0},{2,3},{3,2},{4,5},{5,4},{6,7},{7,6},{8,9},{9,8},{10,11... | collective-permute-start | bytes 1032200 | tf_op jit(solution)/shard_map/ppermute | solution.py:34
  25.5 45.8 %copy-start.9 = (s32[2,2048]{1,0:T(2,128)}, s32[2,2048]{1,0:T(2,128)S(1)}, u32[]{:S(2)}) copy-start(s32[2,2048]{1,0:T(2,128)S(1)} %reshape.38.index_ref) | copy-start | bytes 49156
  27.3 39.7 %copy-start.17 = (s32[4]{0:T(128)S(1)}, s32[4]{0:T(128)}, u32[]{:S(2)}) copy-start(s32[4]{0:T(128)} %constant.25.clone) | copy-start | bytes 52
  31.3 40.0 %all-to-all-start.1 = ((bf16[128,16,128]{2,1,0:T(8,128)(2,1)}), bf16[128,16,128]{2,1,0:T(8,128)(2,1)S(1)}, u32[]{:S(2)}, u32[]{:S(2)}) async-start(bf16[128,16,128]{2,1,0:T(8,128)(2,1)} %tail_rows_out.1), calls=%async_computation.1 | async-start | bytes 1048576 | tf_op jit(solution)/shard_map/all_to_all | solution.py:29
  43.9 21.2 %collective-permute-start.4 = (bf16[64,2688]{1,0:T(8,128)(2,1)S(1)}, bf16[64,2688]{1,0:T(8,128)(2,1)}, u32[]{:S(2)}, u32[]{:S(2)}) collective-permute-start(bf16[64,2688]{1,0:T(8,128)(2,1)S(1)} %own_block.1.refs_0_), channel_id=1, source_target_pairs={{0,2},{2,0},{1,3},{3,1},{4,6},{6,4},{5,7},{7,5},{8,10},{10,8},{9,1... | collective-permute-start | bytes 1032200 | tf_op jit(solution)/shard_map/ppermute | solution.py:34
  47.1 15.2 %collective-permute-start.3 = (bf16[32,32,128]{2,1,0:T(8,128)(2,1)S(1)}, bf16[32,32,128]{2,1,0:T(8,128)(2,1)}, u32[]{:S(2)}, u32[]{:S(2)}) collective-permute-start(bf16[32,32,128]{2,1,0:T(8,128)(2,1)S(1)} %all-to-all-done.refs_0_), channel_id=1, source_target_pairs={{0,32},{32,64},{64,96},{96,0},{1,33},{33,65},{65,97},{97,1},{2,34}... | collective-permute-start | bytes 786440 | tf_op jit(solution)/shard_map/ppermute | solution.py:34
  50.2 17.3 %collective-permute-start.2 = (bf16[32,32,128]{2,1,0:T(8,128)(2,1)S(1)}, bf16[32,32,128]{2,1,0:T(8,128)(2,1)S(1)}, u32[]{:S(2)}, u32[]{:S(2)}) collective-permute-start(bf16[32,32,128]{2,1,0:T(8,128)(2,1)S(1)} %all-to-all-done.refs_0_), channel_id=1, source_target_pairs={{0,96},{32,0},{64,32},{96,64},{1,97},{33,1},{65,33},{97,65},{2,98}... | collective-permute-start | bytes 786440 | tf_op jit(solution)/shard_map/ppermute | solution.py:34
  54.2 14.4 %collective-permute-start.1 = (bf16[32,32,128]{2,1,0:T(8,128)(2,1)S(1)}, bf16[32,32,128]{2,1,0:T(8,128)(2,1)}, u32[]{:S(2)}, u32[]{:S(2)}) collective-permute-start(bf16[32,32,128]{2,1,0:T(8,128)(2,1)S(1)} %all-to-all-done.refs_0_), channel_id=1, source_target_pairs={{0,64},{32,96},{64,0},{96,32},{1,65},{33,97},{65,1},{97,33},{2,66}... | collective-permute-start | bytes 786440 | tf_op jit(solution)/shard_map/ppermute | solution.py:34
  65.0 6.3 %copy-start.12 = (s32[1024]{0:T(1024)S(1)}, s32[1024]{0:T(1024)}, u32[]{:S(2)}) copy-start(s32[1024]{0:T(1024)} %param.20) | copy-start | bytes 12292
  65.1 15.8 %collective-permute-start.5 = (bf16[64,2688]{1,0:T(8,128)(2,1)}, bf16[64,2688]{1,0:T(8,128)(2,1)S(1)}, u32[]{:S(2)}, u32[]{:S(2)}) collective-permute-start(bf16[64,2688]{1,0:T(8,128)(2,1)} %collective-permute-done.4.refs_1_), channel_id=1, source_target_pairs={{0,1},{1,0},{2,3},{3,2},{4,5},{5,4},{6,7},{7,6},{8,9},{9,8},{10,11... | collective-permute-start | bytes 1032200 | tf_op jit(solution)/shard_map/ppermute | solution.py:34
  80.8 0.7 copy-start.16
  87.0 47.2 %all-to-all-start.2 = ((bf16[128,24,128]{2,1,0:T(8,128)(2,1)}), bf16[128,24,128]{2,1,0:T(8,128)(2,1)S(1)}, u32[]{:S(2)}, u32[]{:S(2)}) async-start(bf16[128,24,128]{2,1,0:T(8,128)(2,1)} %bitcast.39), calls=%async_computation.2 | async-start | bytes 1572864 | tf_op jit(solution)/shard_map/all_to_all | solution.py:29
  105.6 0.9 copy-start.1
  106.6 0.7 copy-start.6
  111.9 22.4 %collective-permute-start.6 = (bf16[33,32,128]{2,1,0:T(8,128)(2,1)}, bf16[33,32,128]{2,1,0:T(8,128)(2,1)S(1)}, u32[]{:S(2)}, u32[]{:S(2)}) collective-permute-start(bf16[33,32,128]{2,1,0:T(8,128)(2,1)} %get-tuple-element.39), channel_id=1, source_target_pairs={{0,64},{32,96},{64,0},{96,32},{1,65},{33,97},{65,1},{97,33},{2,66}... | collective-permute-start | bytes 811016 | tf_op jit(solution)/shard_map/ppermute | solution.py:34
  116.3 19.7 %collective-permute-start.7 = (bf16[33,32,128]{2,1,0:T(8,128)(2,1)}, bf16[33,32,128]{2,1,0:T(8,128)(2,1)}, u32[]{:S(2)}, u32[]{:S(2)}) collective-permute-start(bf16[33,32,128]{2,1,0:T(8,128)(2,1)} %get-tuple-element.40), channel_id=1, source_target_pairs={{0,32},{32,64},{64,96},{96,0},{1,33},{33,65},{65,97},{97,1},{2,34}... | collective-permute-start | bytes 811016 | tf_op jit(solution)/shard_map/ppermute | solution.py:34
  118.8 28.7 %copy-start.14 = (bf16[64,256]{1,0:T(8,128)(2,1)S(1)}, bf16[64,256]{1,0:T(8,128)(2,1)}, u32[]{:S(2)}) copy-start(bf16[64,256]{1,0:T(8,128)(2,1)} %get-tuple-element.43.weight_ref) | copy-start | bytes 98308
  118.8 17.2 %collective-permute-start.8 = (bf16[33,32,128]{2,1,0:T(8,128)(2,1)}, bf16[33,32,128]{2,1,0:T(8,128)(2,1)}, u32[]{:S(2)}, u32[]{:S(2)}) collective-permute-start(bf16[33,32,128]{2,1,0:T(8,128)(2,1)} %get-tuple-element.41), channel_id=1, source_target_pairs={{0,96},{32,0},{64,32},{96,64},{1,97},{33,1},{65,33},{97,65},{2,98}... | collective-permute-start | bytes 811016 | tf_op jit(solution)/shard_map/ppermute | solution.py:34
  137.9 25.9 %all-to-all-start.3 = ((bf16[32,48,128]{2,1,0:T(8,128)(2,1)}), bf16[32,48,128]{2,1,0:T(8,128)(2,1)S(1)}, u32[]{:S(2)}, u32[]{:S(2)}) async-start(bf16[32,48,128]{2,1,0:T(8,128)(2,1)} %hub_grads_over_x.1), calls=%async_computation.3 | async-start | bytes 786432 | tf_op jit(solution)/shard_map/all_to_all | solution.py:29
  147.5 1.0 copy-start.13
